TPU v7x, 32 devices: a whole 2x2x4 slice. The times are simulated.
32 devices in a mesh: dp: 4 (over y, x), seq: 8 (over z, core).
Axes of the slice: x: 2, y: 2, z: 4, core: 2. Of those that a mesh axis runs over, the one named last changes fastest.
Arguments:
- series: bfloat16 [4, 4096, 128], P('dp', 'seq'), may hold values from -6 to 6
- cotangent: bfloat16 [4, 4096, 128], P('dp', 'seq'), may hold values from -6 to 6
- w_in: bfloat16 [128, 384], replicated, may hold values from -0.5 to 0.5
- w_out: bfloat16 [128, 128], replicated, may hold values from -0.5 to 0.5
- taps: float32 [3, 384], replicated, may hold values from -3 to 3
- skip_one: float32 [128], replicated, may hold values from 0.5 to 1.5
- skip_two: float32 [128], replicated, may hold values from 0.5 to 1.5
- filter_one: float32 [8, 4096], P(None, 'seq'), may hold values from -0.09375 to 0.09375
- filter_two: float32 [8, 4096], P(None, 'seq'), may hold values from -0.09375 to 0.09375
Outputs:
- output: bfloat16 [4, 4096, 128], P('dp', 'seq')
- d_series: bfloat16 [4, 4096, 128], P('dp', 'seq')
- grad_w_in: float32 [128, 384], replicated
- grad_w_out: float32 [128, 128], replicated
- grad_taps: float32 [3, 384], replicated
- grad_skip_one: float32 [128], replicated
- grad_skip_two: float32 [128], replicated
- grad_filter_one: float32 [8, 4096], P(None, 'seq')
- grad_filter_two: float32 [8, 4096], P(None, 'seq')
All inputs are finite; a program needn't handle non-finite values.
Results may differ from a plain program's by a relative error of at most 0.015.
Values may be sent and summed in bfloat16 or wider, within the bound.
No kernel may reach another device: no remote copies, remote signals or barrier semaphores. Data moves between devices by JAX's collectives and lax.ppermute only.
A program may use at most 128 MiB of HBM per device.

v0:
```python
import math

import jax
import jax.numpy as jnp
from jax import lax
from jax.sharding import PartitionSpec as P

FACTOR = 32


def passed_along(block, axis, distance):
    devices = range(lax.axis_size(axis))
    route = [(i - distance, i) for i in devices if i - distance in devices]
    return lax.ppermute(block, axis, route)


def grid_index(shape_pair, along):
    return lax.broadcasted_iota(jnp.int32, shape_pair, along)


def twiddle(row_index, col_index, period, direction):
    angle = (
        direction * 2.0 * math.pi / period * (row_index * col_index % period).astype(jnp.float32)
    )
    return (jnp.cos(angle), jnp.sin(angle))


def complex_mul(left_real, left_imag, right_real, right_imag):
    return (
        left_real * right_real - left_imag * right_imag,
        left_real * right_imag + left_imag * right_real,
    )


def complex_dft(real_part, imag_part, table_real, table_imag, pattern):
    highest = lax.Precision.HIGHEST
    first = jnp.einsum(pattern, table_real, real_part, precision=highest)
    second = jnp.einsum(pattern, table_imag, imag_part, precision=highest)
    third = jnp.einsum(pattern, table_real, imag_part, precision=highest)
    fourth = jnp.einsum(pattern, table_imag, real_part, precision=highest)
    return (first - second, third + fourth)


def local_dft(pieces):
    real_part, imag_part = pieces
    series_count, pair_rows, block_rows, channels = real_part.shape
    inner = block_rows // FACTOR
    real_part = real_part.reshape(series_count, pair_rows, FACTOR, inner, channels)
    imag_part = imag_part.reshape(series_count, pair_rows, FACTOR, inner, channels)
    table_real, table_imag = twiddle(
        grid_index((FACTOR, FACTOR), 0), grid_index((FACTOR, FACTOR), 1), FACTOR, -1.0
    )
    real_part, imag_part = complex_dft(
        real_part, imag_part, table_real, table_imag, "ca,erabk->ercbk"
    )
    turn_real, turn_imag = twiddle(
        grid_index((FACTOR, inner), 0), grid_index((FACTOR, inner), 1), block_rows, -1.0
    )
    real_part, imag_part = complex_mul(
        real_part, imag_part, turn_real[:, :, None], turn_imag[:, :, None]
    )
    table_real, table_imag = twiddle(
        grid_index((inner, inner), 0), grid_index((inner, inner), 1), inner, -1.0
    )
    return complex_dft(real_part, imag_part, table_real, table_imag, "db,ercbk->ercdk")


def local_inverse(real_part, imag_part):
    series_count, pair_rows, outer, inner, channels = real_part.shape
    block_rows = outer * inner
    table_real, table_imag = twiddle(
        grid_index((inner, inner), 0), grid_index((inner, inner), 1), inner, 1.0
    )
    real_part, imag_part = complex_dft(
        real_part, imag_part, table_real, table_imag, "bd,ercdk->ercbk"
    )
    turn_real, turn_imag = twiddle(
        grid_index((outer, inner), 0), grid_index((outer, inner), 1), block_rows, 1.0
    )
    real_part, imag_part = complex_mul(
        real_part, imag_part, turn_real[:, :, None], turn_imag[:, :, None]
    )
    table_real, table_imag = twiddle(
        grid_index((outer, outer), 0), grid_index((outer, outer), 1), outer, 1.0
    )
    real_part, imag_part = complex_dft(
        real_part, imag_part, table_real, table_imag, "ac,ercbk->erabk"
    )
    return (
        real_part.reshape(series_count, pair_rows, block_rows, channels),
        imag_part.reshape(series_count, pair_rows, block_rows, channels),
    )


def first_section(columns):
    highest = lax.Precision.HIGHEST
    groups = lax.axis_size("seq")
    column_width = columns.shape[2]
    period = 2 * groups * groups * column_width
    offset = lax.axis_index("seq") * column_width
    table_real, table_imag = twiddle(
        grid_index((2 * groups, groups), 0), grid_index((2 * groups, groups), 1), 2 * groups, -1.0
    )
    real_part = jnp.einsum("kn,enjc->ekjc", table_real, columns, precision=highest)
    imag_part = jnp.einsum("kn,enjc->ekjc", table_imag, columns, precision=highest)
    turn_real, turn_imag = twiddle(
        grid_index((2 * groups, column_width), 0),
        grid_index((2 * groups, column_width), 1) + offset,
        period,
        -1.0,
    )
    return complex_mul(real_part, imag_part, turn_real[:, :, None], turn_imag[:, :, None])


def last_section(pieces):
    highest = lax.Precision.HIGHEST
    part_real, part_imag = pieces
    groups = lax.axis_size("seq")
    column_width = part_real.shape[2]
    period = 2 * groups * groups * column_width
    offset = lax.axis_index("seq") * column_width
    turn_real, turn_imag = twiddle(
        grid_index((2 * groups, column_width), 0),
        grid_index((2 * groups, column_width), 1) + offset,
        period,
        1.0,
    )
    part_real, part_imag = complex_mul(
        part_real, part_imag, turn_real[:, :, None], turn_imag[:, :, None]
    )
    table_real, table_imag = twiddle(
        grid_index((groups, 2 * groups), 0), grid_index((groups, 2 * groups), 1), 2 * groups, 1.0
    )
    summed = jnp.einsum("nk,ekjc->enjc", table_real, part_real, precision=highest) - jnp.einsum(
        "nk,ekjc->enjc", table_imag, part_imag, precision=highest
    )
    return summed * (1.0 / period)


def to_frequency(real_part, imag_part):
    return local_dft(
        (
            lax.all_to_all(real_part, "seq", split_axis=1, concat_axis=2, tiled=True),
            lax.all_to_all(imag_part, "seq", split_axis=1, concat_axis=2, tiled=True),
        )
    )


def spectrum(field):
    real_part, imag_part = first_section(
        lax.all_to_all(field, "seq", split_axis=2, concat_axis=1, tiled=True)
    )
    return to_frequency(real_part, imag_part)


def signal(real_part, imag_part):
    real_part, imag_part = local_inverse(real_part, imag_part)
    columns = last_section(
        (
            lax.all_to_all(real_part, "seq", split_axis=2, concat_axis=1, tiled=True),
            lax.all_to_all(imag_part, "seq", split_axis=2, concat_axis=1, tiled=True),
        )
    )
    return lax.all_to_all(columns, "seq", split_axis=1, concat_axis=2, tiled=True)


def order_spectrum(real_part, imag_part):
    series_count, pair_rows, outer, inner, channels = real_part.shape
    block_rows = outer * inner
    real_part = jnp.swapaxes(real_part, 2, 3).reshape(series_count, pair_rows, block_rows, channels)
    imag_part = jnp.swapaxes(imag_part, 2, 3).reshape(series_count, pair_rows, block_rows, channels)
    real_part, imag_part = (
        lax.all_to_all(real_part, "seq", split_axis=2, concat_axis=1, tiled=True),
        lax.all_to_all(imag_part, "seq", split_axis=2, concat_axis=1, tiled=True),
    )
    return (jnp.swapaxes(real_part, 1, 2), jnp.swapaxes(imag_part, 1, 2))


def restore_spectrum(real_part, imag_part):
    real_part = jnp.swapaxes(real_part, 1, 2)
    imag_part = jnp.swapaxes(imag_part, 1, 2)
    real_part, imag_part = (
        lax.all_to_all(real_part, "seq", split_axis=1, concat_axis=2, tiled=True),
        lax.all_to_all(imag_part, "seq", split_axis=1, concat_axis=2, tiled=True),
    )
    series_count, pair_rows, block_rows, channels = real_part.shape
    inner = block_rows // FACTOR
    real_part = jnp.swapaxes(
        real_part.reshape(series_count, pair_rows, inner, FACTOR, channels), 2, 3
    )
    imag_part = jnp.swapaxes(
        imag_part.reshape(series_count, pair_rows, inner, FACTOR, channels), 2, 3
    )
    return (real_part, imag_part)


def transform(field):
    real_part, imag_part = spectrum(field)
    real_part, imag_part = order_spectrum(real_part, imag_part)
    return (real_part, imag_part)


def untransform(real_part, imag_part, in_columns):
    real_part, imag_part = restore_spectrum(real_part, imag_part)
    return signal(real_part, imag_part)


def widen_groups(pieces, channels):
    real_part, imag_part = pieces
    repeat_count = channels // real_part.shape[-1]
    return (
        jnp.repeat(real_part, repeat_count, axis=-1),
        jnp.repeat(imag_part, repeat_count, axis=-1),
    )


def group_sum(pieces, filters):
    result = []
    for piece in pieces:
        channels = piece.shape[-1]
        reshaped = piece.reshape(piece.shape[:-1] + (filters, channels // filters))
        result.append(jnp.sum(jnp.sum(reshaped, axis=-1), axis=0, keepdims=True))
    return (result[0], result[1])


def rows_before(field):
    return passed_along(field[:, :, -2:], "seq", 1)


def rows_after(field):
    return passed_along(field[:, :, :2], "seq", -1)


def filter_blocks(filter_rows):
    return filter_rows.T.reshape(1, 1, filter_rows.shape[1], filter_rows.shape[0])


def shards(series, cotangent, w_in, w_out, taps, skip_one, skip_two, filter_one, filter_two):
    series_count, block_rows, width_d = series.shape
    filters = filter_one.shape[0]
    token_total = series_count * lax.axis_size("dp") * block_rows * lax.axis_size("seq")
    grad_scale = 1.0 / math.sqrt(token_total)
    series_four = series.reshape(series_count, 1, block_rows, width_d)
    cot_four = cotangent.reshape(series_count, 1, block_rows, width_d)
    series_here, cot_here = (series_four, cot_four)
    projected = jnp.einsum("entd,dc->entc", series_here, w_in, preferred_element_type=jnp.float32)
    before = rows_before(projected)
    extended = jnp.concatenate([before, projected], axis=2)
    run_rows = projected.shape[2]
    convolved = (
        taps[0] * extended[:, :, 2:]
        + taps[1] * extended[:, :, 1:-1]
        + taps[2] * extended[:, :, :-2]
    )
    value_part = convolved[..., :width_d]
    gate_one = convolved[..., width_d : 2 * width_d]
    gate_two = convolved[..., 2 * width_d :]
    spec_one = transform(filter_blocks(filter_one))
    spec_two = transform(filter_blocks(filter_two))
    one_real, one_imag = widen_groups(spec_one, width_d)
    two_real, two_imag = widen_groups(spec_two, width_d)
    value_real, value_imag = transform(value_part)
    y_one = (
        untransform(*complex_mul(one_real, one_imag, value_real, value_imag), False)
        + skip_one * value_part
    )
    gated_mid = gate_one * y_one
    mid_real, mid_imag = transform(gated_mid)
    y_two = (
        untransform(*complex_mul(two_real, two_imag, mid_real, mid_imag), False)
        + skip_two * gated_mid
    )
    product = (gate_two * y_two).astype(jnp.bfloat16)
    output = jnp.einsum("entc,cd->entd", product, w_out, preferred_element_type=jnp.float32).astype(
        jnp.bfloat16
    )
    d_product = jnp.einsum("entd,cd->entc", cot_here, w_out, preferred_element_type=jnp.float32)
    grad_two = d_product * gate_two
    d_gate_two = d_product * y_two
    gtwo_real, gtwo_imag = transform(grad_two)
    d_mid = (
        untransform(*complex_mul(two_real, -two_imag, gtwo_real, gtwo_imag), False)
        + skip_two * grad_two
    )
    filter_two_spec = group_sum(complex_mul(mid_real, -mid_imag, gtwo_real, gtwo_imag), filters)
    filter_two_time = untransform(filter_two_spec[0], filter_two_spec[1], False)[0, 0].T
    grad_one = d_mid * gate_one
    d_gate_one = d_mid * y_one
    gone_real, gone_imag = transform(grad_one)
    d_value = (
        untransform(*complex_mul(one_real, -one_imag, gone_real, gone_imag), False)
        + skip_one * grad_one
    )
    filter_one_spec = group_sum(complex_mul(value_real, -value_imag, gone_real, gone_imag), filters)
    filter_one_time = untransform(filter_one_spec[0], filter_one_spec[1], False)[0, 0].T
    d_convolved = jnp.concatenate([d_value, d_gate_one, d_gate_two], axis=3)
    after = rows_after(d_convolved)
    extended_back = jnp.concatenate([d_convolved, after], axis=2)
    d_projected = (
        taps[0] * extended_back[:, :, :-2]
        + taps[1] * extended_back[:, :, 1:-1]
        + taps[2] * extended_back[:, :, 2:]
    ).astype(jnp.bfloat16)
    d_series = jnp.einsum(
        "entc,dc->entd", d_projected, w_in, preferred_element_type=jnp.float32
    ).astype(jnp.bfloat16)
    local_w_in = jnp.einsum(
        "entd,entc->dc", series_here, d_projected, preferred_element_type=jnp.float32
    )
    local_w_out = jnp.einsum("entc,entd->cd", product, cot_here, preferred_element_type=jnp.float32)
    local_taps = jnp.stack(
        [
            jnp.sum(
                d_convolved * extended[:, :, 2 - offset : 2 - offset + run_rows], axis=(0, 1, 2)
            )
            for offset in range(3)
        ]
    )
    local_skip_one = jnp.sum(grad_one * value_part, axis=(0, 1, 2))
    local_skip_two = jnp.sum(grad_two * gated_mid, axis=(0, 1, 2))
    grad_w_in, grad_w_out, grad_taps, grad_skip_one, grad_skip_two = lax.psum(
        (local_w_in, local_w_out, local_taps, local_skip_one, local_skip_two), ("dp", "seq")
    )
    grad_filter_one, grad_filter_two = (
        lax.psum(filter_one_time.astype(jnp.bfloat16), "dp").astype(jnp.float32),
        lax.psum(filter_two_time.astype(jnp.bfloat16), "dp").astype(jnp.float32),
    )
    output = output.reshape(series_count, block_rows, width_d)
    d_series = d_series.reshape(series_count, block_rows, width_d)
    return (
        output,
        d_series,
        grad_scale * grad_w_in,
        grad_scale * grad_w_out,
        grad_scale * grad_taps,
        grad_scale * grad_skip_one,
        grad_scale * grad_skip_two,
        grad_scale * grad_filter_one,
        grad_scale * grad_filter_two,
    )


def solution(mesh):
    in_specs = (
        P("dp", "seq", None),
        P("dp", "seq", None),
        P(),
        P(),
        P(),
        P(),
        P(),
        P(None, "seq"),
        P(None, "seq"),
    )
    out_specs = (
        P("dp", "seq", None),
        P("dp", "seq", None),
        P(),
        P(),
        P(),
        P(),
        P(),
        P(None, "seq"),
        P(None, "seq"),
    )
    return jax.shard_map(shards, mesh=mesh, in_specs=in_specs, out_specs=out_specs, check_vma=False)
```

profile of v0, /device:TPU:0, one launch (start us, length us, event | category | flops | bytes accessed | tf_op | source)
XLA Modules:
  0.0 1217.3 jit_solution(9999531200184390576)
XLA Ops:
  75.3 10.0 all-to-all-done.9
  94.4 9.8 all-to-all-done.10
  129.6 12.1 all-to-all-done.11
  152.2 9.4 all-to-all-done.13
  173.8 13.0 %all-to-all-done.15 = f32[1,16,64,128]{3,2,0,1:T(8,128)S(1)} async-done(((f32[1,16,64,128]{3,2,0,1:T(8,128)}), f32[1,16,64,128]{3,2,0,1:T(8,128)S(1)}, u32[]{:S(2)}, u32[]{:S(2)}) %all-to-all-start.15) | async-done | bytes 524320 | tf_op jit(solution)/shard_map/all_to_all | solution.py:184
  194.2 12.8 %all-to-all-done.14 = f32[1,16,64,128]{3,2,0,1:T(8,128)} async-done(((f32[1,16,64,128]{3,2,0,1:T(8,128)}), f32[1,16,64,128]{3,2,0,1:T(8,128)}, u32[]{:S(2)}, u32[]{:S(2)}) %all-to-all-start.14) | async-done | bytes 524320 | tf_op jit(solution)/shard_map/all_to_all | solution.py:183
  223.3 11.3 all-to-all-done.16
  240.2 13.4 %all-to-all-done.17 = f32[1,2,512,128]{3,1,0,2:T(2,128)S(1)} async-done(((f32[1,2,512,128]{3,1,0,2:T(2,128)}), f32[1,2,512,128]{3,1,0,2:T(2,128)S(1)}, u32[]{:S(2)}, u32[]{:S(2)}) %all-to-all-start.17) | async-done | bytes 524320 | tf_op jit(solution)/shard_map/all_to_all | solution.py:161
  256.5 12.3 %all_to_all.912 = f32[1,8,64,128]{3,2,0,1:T(8,128)S(1)} all-to-all(f32[1,8,64,128]{3,2,0,1:T(8,128)S(1)} %copy.658), channel_id=1, replica_groups=mesh['dp'=4,'seq'=8] {'seq'}, dimensions={1} | all-to-all | bytes 524288 | tf_op jit(solution)/shard_map/all_to_all | solution.py:164
  272.1 12.1 all_to_all.913
  322.3 14.4 %all-to-all-done.31 = f32[1,16,64,128]{3,2,0,1:T(8,128)} async-done(((f32[1,16,64,128]{3,2,0,1:T(8,128)}), f32[1,16,64,128]{3,2,0,1:T(8,128)}, u32[]{:S(2)}, u32[]{:S(2)}) %all-to-all-start.31) | async-done | bytes 524320 | tf_op jit(solution)/shard_map/all_to_all | solution.py:143
  348.5 7.8 all-to-all-done.32
  387.8 7.7 all-to-all-done.20
  426.8 11.1 all-to-all-done.34
  445.3 12.0 all-to-all-done.33
  465.7 11.2 all-to-all-done.24
  518.3 13.0 %all-to-all-done.26 = f32[1,16,64,128]{3,2,0,1:T(8,128)S(1)} async-done(((f32[1,16,64,128]{3,2,0,1:T(8,128)}), f32[1,16,64,128]{3,2,0,1:T(8,128)S(1)}, u32[]{:S(2)}, u32[]{:S(2)}) %all-to-all-start.26) | async-done | bytes 524320 | tf_op jit(solution)/shard_map/all_to_all | solution.py:184
  537.8 13.0 %all-to-all-done.25 = f32[1,16,64,128]{3,2,0,1:T(8,128)} async-done(((f32[1,16,64,128]{3,2,0,1:T(8,128)}), f32[1,16,64,128]{3,2,0,1:T(8,128)}, u32[]{:S(2)}, u32[]{:S(2)}) %all-to-all-start.25) | async-done | bytes 524320 | tf_op jit(solution)/shard_map/all_to_all | solution.py:183
  557.3 13.0 %all-to-all-done.36 = f32[1,16,64,128]{3,2,0,1:T(8,128)} async-done(((f32[1,16,64,128]{3,2,0,1:T(8,128)}), f32[1,16,64,128]{3,2,0,1:T(8,128)}, u32[]{:S(2)}, u32[]{:S(2)}) %all-to-all-start.36) | async-done | bytes 524320 | tf_op jit(solution)/shard_map/all_to_all | solution.py:184
  608.1 11.2 all-to-all-done.37
  626.8 12.0 all-to-all-done.38
  647.0 11.3 all-to-all-done.28
  667.5 9.5 all-to-all-done.27
  688.4 7.2 all-to-all-done.39
  695.7 12.3 %all_to_all.914 = f32[1,8,64,128]{3,2,0,1:T(8,128)S(1)} all-to-all(f32[1,8,64,128]{3,2,0,1:T(8,128)S(1)} %copy.705), channel_id=1, replica_groups=mesh['dp'=4,'seq'=8] {'seq'}, dimensions={1} | all-to-all | bytes 524288 | tf_op jit(solution)/shard_map/all_to_all | solution.py:164
  711.3 12.5 %all_to_all.915 = f32[1,1,512,128]{3,1,0,2:T(1,128)S(1)} all-to-all(f32[1,1,512,128]{3,1,0,2:T(1,128)S(1)} %bitcast.1363), channel_id=1, replica_groups=mesh['dp'=4,'seq'=8] {'seq'}, dimensions={2} | all-to-all | bytes 524288 | tf_op jit(solution)/shard_map/all_to_all | solution.py:151
  733.4 13.3 %all-to-all-done.41 = f32[1,16,64,128]{3,2,0,1:T(8,128)} async-done(((f32[1,16,64,128]{3,2,0,1:T(8,128)}), f32[1,16,64,128]{3,2,0,1:T(8,128)}, u32[]{:S(2)}, u32[]{:S(2)}) %all-to-all-start.41) | async-done | bytes 524320 | tf_op jit(solution)/shard_map/all_to_all | solution.py:143
  893.9 7.7 all-to-all-done.45
  979.8 12.9 %all-to-all-done.48 = f32[1,2,512,128]{3,1,0,2:T(2,128)S(1)} async-done(((f32[1,2,512,128]{3,1,0,2:T(2,128)}), f32[1,2,512,128]{3,1,0,2:T(2,128)S(1)}, u32[]{:S(2)}, u32[]{:S(2)}) %all-to-all-start.48) | async-done | bytes 524320 | tf_op jit(solution)/shard_map/all_to_all | solution.py:161
  1016.5 16.0 %all-reduce.2 = (bf16[8,512]{1,0:T(8,128)(2,1)S(1)}, bf16[8,512]{1,0:T(8,128)(2,1)S(1)}) all-reduce(bf16[8,512]{1,0:T(8,128)(2,1)S(1)} %bitcast.1464, bf16[8,512]{1,0:T(8,128)(2,1)S(1)} %bitcast.1463), channel_id=1, replica_groups=mesh['dp'=4,'seq'=8] {'dp'}, use_global_device_ids=true, to_apply=%region_12.13 | all-reduce | flops 8192 | bytes 32768 | tf_op jit(solution)/shard_map/psum | solution.py:325
  1038.8 40.0 %all-reduce = (f32[3,384]{1,0:T(4,128)S(1)}, f32[128]{0:T(128)S(1)}, f32[128]{0:T(128)S(1)}) all-reduce(f32[3,384]{1,0:T(4,128)S(1)} %pad_maximum_fusion.3, f32[128]{0:T(128)S(1)} %copy-done.109, f32[128]{0:T(128)S(1)} %copy-done.108), channel_id=1, replica_groups=mesh['dp'=4,'seq'=8] {'dp','seq'}, use_global_device_ids=true, to_apply=%region_5.6 | all-reduce | flops 1408 | bytes 11264 | tf_op jit(solution)/shard_map/psum | solution.py:321
  1083.3 124.3 %all-reduce.5.cloned.1.call-done = (f32[128,384]{0,1:T(8,128)}, f32[128,128]{1,0:T(8,128)}) async-done(((f32[128,384]{0,1:T(8,128)}, f32[128,128]{1,0:T(8,128)}), (f32[128,384]{0,1:T(8,128)}, f32[128,128]{1,0:T(8,128)})) %all-reduce.5.cloned.1.call-update) | async-done | bytes 262160 | tf_op jit(solution)/shard_map/psum | solution.py:321
  (702 shorter events, 690.2 us)
Async XLA Ops:
  66.5 18.8 %all-to-all-start.9 = ((f32[1,16,64,128]{3,2,0,1:T(8,128)}), f32[1,16,64,128]{3,2,0,1:T(8,128)S(1)}, u32[]{:S(2)}, u32[]{:S(2)}) async-start(f32[1,16,64,128]{3,2,0,1:T(8,128)} %copy.613), calls=%async_computation.9 | async-start | bytes 1048576 | tf_op jit(solution)/shard_map/all_to_all | solution.py:143
  85.3 19.0 %all-to-all-start.10 = ((f32[1,16,64,128]{3,2,0,1:T(8,128)}), f32[1,16,64,128]{3,2,0,1:T(8,128)S(1)}, u32[]{:S(2)}, u32[]{:S(2)}) async-start(f32[1,16,64,128]{3,2,0,1:T(8,128)} %copy.616), calls=%async_computation.10 | async-start | bytes 1048576 | tf_op jit(solution)/shard_map/all_to_all | solution.py:144
  123.0 18.8 %all-to-all-start.11 = ((f32[1,2,512,128]{3,1,0,2:T(2,128)}), f32[1,2,512,128]{3,1,0,2:T(2,128)S(1)}, u32[]{:S(2)}, u32[]{:S(2)}) async-start(f32[1,2,512,128]{3,1,0,2:T(2,128)} %copy.624), calls=%async_computation.11 | async-start | bytes 1048576 | tf_op jit(solution)/shard_map/all_to_all | solution.py:173
  141.8 19.9 %all-to-all-start.13 = ((f32[1,2,512,128]{3,1,0,2:T(2,128)}), f32[1,2,512,128]{3,1,0,2:T(2,128)}, u32[]{:S(2)}, u32[]{:S(2)}) async-start(f32[1,2,512,128]{3,1,0,2:T(2,128)} %copy.633), calls=%async_computation.13 | async-start | bytes 1048576 | tf_op jit(solution)/shard_map/all_to_all | solution.py:174
  187.6 19.5 %all-to-all-start.14 = ((f32[1,16,64,128]{3,2,0,1:T(8,128)}), f32[1,16,64,128]{3,2,0,1:T(8,128)}, u32[]{:S(2)}, u32[]{:S(2)}) async-start(f32[1,16,64,128]{3,2,0,1:T(8,128)} %copy.636), calls=%async_computation.14 | async-start | bytes 1048576 | tf_op jit(solution)/shard_map/all_to_all | solution.py:183
  215.1 19.5 %all-to-all-start.16 = ((f32[1,2,512,128]{3,1,0,2:T(2,128)}), f32[1,2,512,128]{3,1,0,2:T(2,128)}, u32[]{:S(2)}, u32[]{:S(2)}) async-start(f32[1,2,512,128]{3,1,0,2:T(2,128)} %copy.647), calls=%async_computation.16 | async-start | bytes 1048576 | tf_op jit(solution)/shard_map/all_to_all | solution.py:160
  234.6 18.9 %all-to-all-start.17 = ((f32[1,2,512,128]{3,1,0,2:T(2,128)}), f32[1,2,512,128]{3,1,0,2:T(2,128)S(1)}, u32[]{:S(2)}, u32[]{:S(2)}) async-start(f32[1,2,512,128]{3,1,0,2:T(2,128)} %copy.653), calls=%async_computation.17 | async-start | bytes 1048576 | tf_op jit(solution)/shard_map/all_to_all | solution.py:161
  317.2 19.5 %all-to-all-start.31 = ((f32[1,16,64,128]{3,2,0,1:T(8,128)}), f32[1,16,64,128]{3,2,0,1:T(8,128)}, u32[]{:S(2)}, u32[]{:S(2)}) async-start(f32[1,16,64,128]{3,2,0,1:T(8,128)} %copy.709), calls=%async_computation.31 | async-start | bytes 1048576 | tf_op jit(solution)/shard_map/all_to_all | solution.py:143
  336.7 19.5 %all-to-all-start.32 = ((f32[1,16,64,128]{3,2,0,1:T(8,128)}), f32[1,16,64,128]{3,2,0,1:T(8,128)}, u32[]{:S(2)}, u32[]{:S(2)}) async-start(f32[1,16,64,128]{3,2,0,1:T(8,128)} %copy.712), calls=%async_computation.32 | async-start | bytes 1048576 | tf_op jit(solution)/shard_map/all_to_all | solution.py:144
  356.3 19.7 %all-to-all-start.21 = ((f32[1,16,64,128]{3,2,0,1:T(8,128)}), f32[1,16,64,128]{3,2,0,1:T(8,128)}, u32[]{:S(2)}, u32[]{:S(2)}) async-start(f32[1,16,64,128]{3,2,0,1:T(8,128)} %copy.665), calls=%async_computation.21 | async-start | bytes 1048576 | tf_op jit(solution)/shard_map/all_to_all | solution.py:144
  376.0 19.5 %all-to-all-start.20 = ((f32[1,16,64,128]{3,2,0,1:T(8,128)}), f32[1,16,64,128]{3,2,0,1:T(8,128)}, u32[]{:S(2)}, u32[]{:S(2)}) async-start(f32[1,16,64,128]{3,2,0,1:T(8,128)} %copy.662), calls=%async_computation.20 | async-start | bytes 1048576 | tf_op jit(solution)/shard_map/all_to_all | solution.py:143
  418.3 19.5 %all-to-all-start.34 = ((f32[1,2,512,128]{3,1,0,2:T(2,128)}), f32[1,2,512,128]{3,1,0,2:T(2,128)}, u32[]{:S(2)}, u32[]{:S(2)}) async-start(f32[1,2,512,128]{3,1,0,2:T(2,128)} %copy.726), calls=%async_computation.34 | async-start | bytes 1048576 | tf_op jit(solution)/shard_map/all_to_all | solution.py:174
  437.8 19.5 %all-to-all-start.33 = ((f32[1,2,512,128]{3,1,0,2:T(2,128)}), f32[1,2,512,128]{3,1,0,2:T(2,128)}, u32[]{:S(2)}, u32[]{:S(2)}) async-start(f32[1,2,512,128]{3,1,0,2:T(2,128)} %copy.720), calls=%async_computation.33 | async-start | bytes 1048576 | tf_op jit(solution)/shard_map/all_to_all | solution.py:173
  457.4 19.5 %all-to-all-start.24 = ((f32[1,2,512,128]{3,1,0,2:T(2,128)}), f32[1,2,512,128]{3,1,0,2:T(2,128)}, u32[]{:S(2)}, u32[]{:S(2)}) async-start(f32[1,2,512,128]{3,1,0,2:T(2,128)} %copy.682), calls=%async_computation.24 | async-start | bytes 1048576 | tf_op jit(solution)/shard_map/all_to_all | solution.py:174
  476.9 23.4 %all-to-all-start.22 = ((f32[1,2,512,128]{3,1,0,2:T(2,128)}), f32[1,2,512,128]{3,1,0,2:T(2,128)}, u32[]{:S(2)}, u32[]{:S(2)}) async-start(f32[1,2,512,128]{3,1,0,2:T(2,128)} %copy.673), calls=%async_computation.22 | async-start | bytes 1048576 | tf_op jit(solution)/shard_map/all_to_all | solution.py:173
  511.0 20.4 %all-to-all-start.26 = ((f32[1,16,64,128]{3,2,0,1:T(8,128)}), f32[1,16,64,128]{3,2,0,1:T(8,128)S(1)}, u32[]{:S(2)}, u32[]{:S(2)}) async-start(f32[1,16,64,128]{3,2,0,1:T(8,128)} %copy.688), calls=%async_computation.26 | async-start | bytes 1048576 | tf_op jit(solution)/shard_map/all_to_all | solution.py:184
  531.3 19.5 %all-to-all-start.25 = ((f32[1,16,64,128]{3,2,0,1:T(8,128)}), f32[1,16,64,128]{3,2,0,1:T(8,128)}, u32[]{:S(2)}, u32[]{:S(2)}) async-start(f32[1,16,64,128]{3,2,0,1:T(8,128)} %copy.685), calls=%async_computation.25 | async-start | bytes 1048576 | tf_op jit(solution)/shard_map/all_to_all | solution.py:183
  550.8 19.5 %all-to-all-start.36 = ((f32[1,16,64,128]{3,2,0,1:T(8,128)}), f32[1,16,64,128]{3,2,0,1:T(8,128)}, u32[]{:S(2)}, u32[]{:S(2)}) async-start(f32[1,16,64,128]{3,2,0,1:T(8,128)} %copy.732), calls=%async_computation.36 | async-start | bytes 1048576 | tf_op jit(solution)/shard_map/all_to_all | solution.py:184
  570.3 19.7 %all-to-all-start.35 = ((f32[1,16,64,128]{3,2,0,1:T(8,128)}), f32[1,16,64,128]{3,2,0,1:T(8,128)}, u32[]{:S(2)}, u32[]{:S(2)}) async-start(f32[1,16,64,128]{3,2,0,1:T(8,128)} %copy.729), calls=%async_computation.35 | async-start | bytes 1048576 | tf_op jit(solution)/shard_map/all_to_all | solution.py:183
  599.6 19.7 %all-to-all-start.37 = ((f32[1,2,512,128]{3,1,0,2:T(2,128)}), f32[1,2,512,128]{3,1,0,2:T(2,128)}, u32[]{:S(2)}, u32[]{:S(2)}) async-start(f32[1,2,512,128]{3,1,0,2:T(2,128)} %copy.738), calls=%async_computation.37 | async-start | bytes 1048576 | tf_op jit(solution)/shard_map/all_to_all | solution.py:160
  619.3 19.5 %all-to-all-start.38 = ((f32[1,2,512,128]{3,1,0,2:T(2,128)}), f32[1,2,512,128]{3,1,0,2:T(2,128)}, u32[]{:S(2)}, u32[]{:S(2)}) async-start(f32[1,2,512,128]{3,1,0,2:T(2,128)} %copy.744), calls=%async_computation.38 | async-start | bytes 1048576 | tf_op jit(solution)/shard_map/all_to_all | solution.py:161
  638.8 19.5 %all-to-all-start.28 = ((f32[1,2,512,128]{3,1,0,2:T(2,128)}), f32[1,2,512,128]{3,1,0,2:T(2,128)}, u32[]{:S(2)}, u32[]{:S(2)}) async-start(f32[1,2,512,128]{3,1,0,2:T(2,128)} %copy.700), calls=%async_computation.28 | async-start | bytes 1048576 | tf_op jit(solution)/shard_map/all_to_all | solution.py:161
  727.2 19.5 %all-to-all-start.41 = ((f32[1,16,64,128]{3,2,0,1:T(8,128)}), f32[1,16,64,128]{3,2,0,1:T(8,128)}, u32[]{:S(2)}, u32[]{:S(2)}) async-start(f32[1,16,64,128]{3,2,0,1:T(8,128)} %copy.753), calls=%async_computation.41 | async-start | bytes 1048576 | tf_op jit(solution)/shard_map/all_to_all | solution.py:143
  746.7 19.5 %all-to-all-start.42 = ((f32[1,16,64,128]{3,2,0,1:T(8,128)}), f32[1,16,64,128]{3,2,0,1:T(8,128)}, u32[]{:S(2)}, u32[]{:S(2)}) async-start(f32[1,16,64,128]{3,2,0,1:T(8,128)} %copy.756), calls=%async_computation.42 | async-start | bytes 1048576 | tf_op jit(solution)/shard_map/all_to_all | solution.py:144
  788.4 21.7 %all-to-all-start.43 = ((f32[1,2,512,128]{3,1,0,2:T(2,128)}), f32[1,2,512,128]{3,1,0,2:T(2,128)}, u32[]{:S(2)}, u32[]{:S(2)}) async-start(f32[1,2,512,128]{3,1,0,2:T(2,128)} %copy.764), calls=%async_computation.43 | async-start | bytes 1048576 | tf_op jit(solution)/shard_map/all_to_all | solution.py:173
  810.1 20.6 %all-to-all-start.44 = ((f32[1,2,512,128]{3,1,0,2:T(2,128)}), f32[1,2,512,128]{3,1,0,2:T(2,128)}, u32[]{:S(2)}, u32[]{:S(2)}) async-start(f32[1,2,512,128]{3,1,0,2:T(2,128)} %copy.770), calls=%async_computation.44 | async-start | bytes 1048576 | tf_op jit(solution)/shard_map/all_to_all | solution.py:174
  863.1 19.5 %all-to-all-start.46 = ((f32[1,16,64,128]{3,2,0,1:T(8,128)}), f32[1,16,64,128]{3,2,0,1:T(8,128)}, u32[]{:S(2)}, u32[]{:S(2)}) async-start(f32[1,16,64,128]{3,2,0,1:T(8,128)} %copy.776), calls=%async_computation.46 | async-start | bytes 1048576 | tf_op jit(solution)/shard_map/all_to_all | solution.py:184
  882.6 19.0 %all-to-all-start.45 = ((f32[1,16,64,128]{3,2,0,1:T(8,128)}), f32[1,16,64,128]{3,2,0,1:T(8,128)S(1)}, u32[]{:S(2)}, u32[]{:S(2)}) async-start(f32[1,16,64,128]{3,2,0,1:T(8,128)} %copy.773), calls=%async_computation.45 | async-start | bytes 1048576 | tf_op jit(solution)/shard_map/all_to_all | solution.py:183
  940.4 31.7 %all-to-all-start.47 = ((f32[1,2,512,128]{3,1,0,2:T(2,128)}), f32[1,2,512,128]{3,1,0,2:T(2,128)S(1)}, u32[]{:S(2)}, u32[]{:S(2)}) async-start(f32[1,2,512,128]{3,1,0,2:T(2,128)} %copy.782), calls=%async_computation.47 | async-start | bytes 1048576 | tf_op jit(solution)/shard_map/all_to_all | solution.py:160
  972.1 20.6 %all-to-all-start.48 = ((f32[1,2,512,128]{3,1,0,2:T(2,128)}), f32[1,2,512,128]{3,1,0,2:T(2,128)S(1)}, u32[]{:S(2)}, u32[]{:S(2)}) async-start(f32[1,2,512,128]{3,1,0,2:T(2,128)} %copy.788), calls=%async_computation.48 | async-start | bytes 1048576 | tf_op jit(solution)/shard_map/all_to_all | solution.py:161
  1011.1 22.7 %all-to-all-start.49 = ((f32[1,8,64,128]{3,2,0,1:T(8,128)}), f32[1,8,64,128]{3,2,0,1:T(8,128)S(1)}, u32[]{:S(2)}, u32[]{:S(2)}) async-start(f32[1,8,64,128]{3,2,0,1:T(8,128)} %copy.793), calls=%async_computation.49 | async-start | bytes 524288 | tf_op jit(solution)/shard_map/all_to_all | solution.py:164
  1014.5 193.1 %all-reduce.5.cloned.1.call-start = ((), (), s32[]{:S(2)}) async-start(), calls=%async_computation.60 | async-start | bytes 524288 | tf_op jit(solution)/shard_map/psum | solution.py:321
  (138 other events, 790.5 us)
Sparse Core Ops, SparseCore 0:
  1081.6 125.9 all-reduce.4
where the time goes:
time: 1230 us; the launch traced here: 1220 us
  waiting for transfers between devices  496 us (40%)
  starting transfers between devices  231 us (19%)
  local copies, waits for them, and re-layouts  190 us (15%)
  matrix products  119 us (10%)
  blocking collectives  105 us (9%)
  other arithmetic  58 us (5%)
  between operations  17.3 us (1%)
    psum x1, waiting for transfers between devices, shards(): lax.psum((local_w_in, local_w_out, local_taps, local_skip_one, local_skip...  124 us
    unnamed x270, local copies, waits for them, and re-layouts  63.8 us
    all_to_all x6, waiting for transfers between devices, signal(): lax.all_to_all(imag_part, 'seq', split_axis=2, concat_axis=1, tiled=True)  56.7 us
    all_to_all x6, waiting for transfers between devices, to_frequency(): lax.all_to_all(real_part, 'seq', split_axis=1, concat_axis=2, tiled=True)  53.5 us
    all_to_all x6, waiting for transfers between devices, restore_spectrum(): lax.all_to_all(imag_part, 'seq', split_axis=1, concat_axis=2, tiled=True)  49.4 us
    all_to_all x6, waiting for transfers between devices, restore_spectrum(): lax.all_to_all(real_part, 'seq', split_axis=1, concat_axis=2, tiled=True)  47.1 us
    all_to_all x6, waiting for transfers between devices, order_spectrum(): lax.all_to_all(imag_part, 'seq', split_axis=2, concat_axis=1, tiled=True)  44.1 us
    all_to_all x6, waiting for transfers between devices, signal(): lax.all_to_all(real_part, 'seq', split_axis=2, concat_axis=1, tiled=True)  40 us
  transfers between devices with their start and end apart: 59, of which 51 were waited for; matrix products, arithmetic and copies ran while one was open for 23% of the time, Pallas kernels for 0%

commit v1 on v0

v1 whole, which is shorter than its diff:
```python
import functools
import math

import jax
import jax.numpy as jnp
from jax import lax
from jax.experimental import pallas as pl
from jax.experimental.pallas import tpu as pltpu
from jax.sharding import PartitionSpec as P

W = 256
F32 = jnp.float32
BF16 = jnp.bfloat16
NT = (((1,), (1,)), ((), ()))
VMEM_LIMIT = 56 * 1024 * 1024


def call(body, out_shape, scratch=(), flops=0, moved=0):
    return pl.pallas_call(
        body,
        out_shape=out_shape,
        scratch_shapes=list(scratch),
        compiler_params=pltpu.CompilerParams(vmem_limit_bytes=VMEM_LIMIT),
        cost_estimate=pl.CostEstimate(flops=flops, bytes_accessed=moved, transcendentals=0),
    )


def dot(a, b):
    return jnp.dot(a, b, preferred_element_type=F32)


def dot_nt(a, b):
    return lax.dot_general(a, b, NT, preferred_element_type=F32)


def project_kernel(units, series_ref, cot_ref, w_in_ref, w_out_ref, out_ref):
    count, block, width = series_ref.shape
    group = width // units
    parts = block // W
    w_in_t = w_in_ref[...].T
    w_out = w_out_ref[...]
    for e in range(count):
        for part in range(parts):
            rows = pl.ds(part * W, W)
            proj = dot_nt(w_in_t, series_ref[e, rows, :]).astype(BF16)
            d_prod = dot_nt(w_out, cot_ref[e, rows, :]).astype(BF16)
            for kind in range(4):
                field = proj[kind * width : (kind + 1) * width] if kind < 3 else d_prod
                out_ref[
                    e * units : (e + 1) * units,
                    (kind * parts + part) * group : (kind * parts + part + 1) * group,
                    :,
                ] = field.reshape(units, group, W)


def toeplitz_kernel(taps_ref, out_ref, base_ref):
    sources, chunk_rows, lanes = taps_ref.shape
    chunks = chunk_rows // 2
    length = sources * chunks * lanes
    blocks = length // W
    row = lax.broadcasted_iota(jnp.int32, (8, length), 0)
    for m in range(2):
        for s in range(sources):
            for q in range(chunks):
                at = (s * chunks + q) * lanes
                base_ref[:, at : at + lanes] = jnp.broadcast_to(
                    taps_ref[s, m * chunks + q : m * chunks + q + 1, :], (8, lanes)
                )
        base = base_ref[...]
        for bit in (1, 2, 4):
            base = jnp.where((row & bit) != 0, pltpu.roll(base, bit, 1), base)

        def step(q, base, m=m):
            start = pl.multiple_of(q * 16, 16)
            both = jnp.concatenate([base, pltpu.roll(base, 8, 1)], axis=0)
            b = lax.broadcasted_iota(jnp.int32, (16, W), 0) + start
            r = lax.broadcasted_iota(jnp.int32, (16, W), 1)
            first = jnp.where(r >= b, both[:, :W], 0.0)
            out_ref[m, 0, pl.ds(start, 16), :] = first.astype(BF16)
            for d in range(1, blocks):
                out_ref[m, d, pl.ds(start, 16), :] = both[:, d * W : (d + 1) * W].astype(BF16)
            return pltpu.roll(base, 16, 1)

        lax.fori_loop(0, W // 16, step, base)


def earlier(field, j, group):
    if j == 0:
        return field
    turned = pltpu.roll(field, j, 1)
    above = jnp.concatenate([jnp.zeros((group, W), F32), turned[:-group]], axis=0)
    lane = lax.broadcasted_iota(jnp.int32, field.shape, 1)
    return jnp.where(lane < j, above, turned)


def later(field, j, group):
    if j == 0:
        return field
    turned = pltpu.roll(field, W - j, 1)
    below = jnp.concatenate([turned[group:], jnp.zeros((group, W), F32)], axis=0)
    lane = lax.broadcasted_iota(jnp.int32, field.shape, 1)
    return jnp.where(lane >= W - j, below, turned)


def own_lanes(f, group, width):
    lane = lax.broadcasted_iota(jnp.int32, (group, width), 1)
    channel = lax.broadcasted_iota(jnp.int32, (group, width), 0)
    return lane == f * group + channel


def pick(ref, kind, received):
    rows = received // 4
    field = ref[:, kind * rows : (kind + 1) * rows, :]
    return field.reshape(field.shape[0] * rows, W).astype(F32)


def operator_kernel(
    units, fields_ref, toep_ref, taps_ref, skip_one_ref, skip_two_ref, out_ref, kept_ref, pad_ref
):
    sources, received, _ = fields_ref.shape
    width = taps_ref.shape[1] // 3
    group = width // units
    rows = sources * received // 4
    blocks = rows // group
    f = lax.rem(lax.axis_index("seq"), units)
    mine = own_lanes(f, group, width)

    def column(values):
        col = jnp.sum(jnp.where(mine, values, 0.0), axis=1, keepdims=True)
        return jnp.broadcast_to(col, (group, W))

    def scaled(field, col):
        return (field.reshape(blocks, group, W) * col[None]).reshape(rows, W)

    zeros = jnp.zeros((rows, W), BF16)
    pad_ref[0:rows, :] = zeros
    pad_ref[2 * rows : 3 * rows, :] = zeros

    def causal(m, field):
        pad_ref[rows : 2 * rows, :] = field
        left = jnp.concatenate(
            [pad_ref[rows - group * d : 2 * rows - group * d, :] for d in range(blocks)], axis=1
        )
        return dot(left, toep_ref[m].reshape(blocks * W, W))

    def anticausal(m, field):
        pad_ref[rows : 2 * rows, :] = field
        left = jnp.concatenate(
            [pad_ref[rows + group * d : 2 * rows + group * d, :] for d in range(blocks)], axis=1
        )
        right = jnp.concatenate([toep_ref[m, d] for d in range(blocks)], axis=1)
        return dot_nt(left, right)

    tap = [
        [
            column(taps_ref[j : j + 1, kind * width : (kind + 1) * width])
            for j in range(3)
        ]
        for kind in range(3)
    ]
    skip_one = column(skip_one_ref[...])
    skip_two = column(skip_two_ref[...])

    def short(kind):
        field = pick(fields_ref, kind, received)
        total = scaled(field, tap[kind][0])
        for j in (1, 2):
            total = total + scaled(earlier(field, j, group), tap[kind][j])
        return total

    def keep(slot, field):
        low = field.astype(BF16)
        kept_ref[slot] = low
        return low

    def send(kind, field):
        part_rows = received // 4
        out_ref[:, kind * part_rows : (kind + 1) * part_rows, :] = field.astype(BF16).reshape(
            sources, part_rows, W
        )

    def send_back(kind, field):
        total = scaled(field, tap[kind][0])
        for j in (1, 2):
            total = total + scaled(later(field, j, group), tap[kind][j])
        send(kind, total)

    value = short(0)
    y_one = causal(0, keep(0, value)) + scaled(value, skip_one)
    gate_one = short(1)
    mid = gate_one * y_one
    y_two = causal(1, keep(1, mid)) + scaled(mid, skip_two)
    gate_two = short(2)
    send(3, gate_two * y_two)
    d_product = pick(fields_ref, 3, received)
    grad_two = d_product * gate_two
    d_gate_two = d_product * y_two
    keep(6, d_gate_two)
    send_back(2, d_gate_two)
    d_mid = anticausal(1, keep(3, grad_two)) + scaled(grad_two, skip_two)
    grad_one = d_mid * gate_one
    d_gate_one = d_mid * y_one
    keep(5, d_gate_one)
    send_back(1, d_gate_one)
    d_value = anticausal(0, keep(2, grad_one)) + scaled(grad_one, skip_one)
    keep(4, d_value)
    send_back(0, d_value)


def gradient_kernel(
    units,
    fields_ref,
    sent_ref,
    kept_ref,
    series_ref,
    cot_ref,
    out_ref,
    pad_ref,
    corr_ref,
    total_ref,
):
    sources, received, _ = fields_ref.shape
    width = series_ref.shape[3]
    group = width // units
    rows = sources * received // 4
    blocks = rows // group
    parts = blocks // sources
    length = blocks * W
    me = lax.axis_index("seq")
    f = lax.rem(me, units)
    e = me // units
    mine = own_lanes(f, group, width)

    def wide(ref):
        return jnp.concatenate([ref[s, e] for s in range(sources)], axis=0)

    def long_rows(kind):
        return jnp.concatenate(
            [
                sent_ref[s, (kind * parts + p) * group : (kind * parts + p + 1) * group, :]
                for s in range(sources)
                for p in range(parts)
            ],
            axis=1,
        )

    left = jnp.concatenate([long_rows(k) for k in range(3)], axis=0)
    total_ref[0 : 3 * group, :] = dot(left, wide(series_ref))
    total_ref[3 * group : 4 * group, :] = dot(long_rows(3), wide(cot_ref))

    zeros = jnp.zeros((rows, W), BF16)
    pad_ref[rows : 2 * rows, :] = zeros
    row8 = lax.broadcasted_iota(jnp.int32, (8, length), 0)
    for m in range(2):
        pad_ref[0:rows, :] = kept_ref[2 + m]
        right = jnp.concatenate(
            [pad_ref[group * d : rows + group * d, :] for d in range(blocks)], axis=1
        )
        held = kept_ref[m].astype(F32).T.astype(BF16)
        corr_ref[...] = dot(held, right)
        b = lax.broadcasted_iota(jnp.int32, (W, W), 0)
        r = lax.broadcasted_iota(jnp.int32, (W, W), 1)
        corr_ref[:, 0:W] = jnp.where(r >= b, corr_ref[:, 0:W], 0.0)

        def step(i, acc):
            start = pl.multiple_of((W // 8 - 1 - i) * 8, 8)
            return pltpu.roll(acc, length - 8, 1) + corr_ref[pl.ds(start, 8), :]

        acc = lax.fori_loop(0, W // 8, step, jnp.zeros((8, length), F32))
        for bit in (1, 2, 4):
            acc = jnp.where((row8 & bit) != 0, pltpu.roll(acc, length - bit, 1), acc)
        line = jnp.sum(acc, axis=0, keepdims=True)
        for q in range(length // width):
            at = 4 * group + m * (length // width) + q
            total_ref[at : at + 1, :] = line[:, q * width : (q + 1) * width]

    def spread(products):
        by_channel = jnp.sum(products.reshape(blocks, group, W), axis=0)
        col = jnp.sum(by_channel, axis=1, keepdims=True)
        return jnp.sum(jnp.where(mine, col, 0.0), axis=0, keepdims=True)

    small = []
    for j in range(3):
        for kind in range(3):
            field = pick(fields_ref, kind, received)
            small.append(spread(kept_ref[4 + kind].astype(F32) * earlier(field, j, group)))
    for m in range(2):
        small.append(spread(kept_ref[2 + m].astype(F32) * kept_ref[m].astype(F32)))
    base = 4 * group + 2 * (length // width)
    total_ref[base : base + 16, :] = jnp.zeros((16, width), F32)
    for n, line in enumerate(small):
        total_ref[base + n : base + n + 1, :] = line

    total = total_ref[...].astype(BF16)
    for i in range(out_ref.shape[0]):
        out_ref[i] = total


def spread_kernel(units, in_ref, out_ref, sum_ref):
    width = in_ref.shape[2]
    group = width // units
    targets = out_ref.shape[0]
    total = in_ref[0].astype(F32)
    for i in range(1, in_ref.shape[0]):
        total = total + in_ref[i].astype(F32)
    sum_ref[...] = total
    base = 4 * group
    lines = (total.shape[0] - base - 16) // 2
    each = lines // targets
    for s in range(targets):
        out_ref[s] = jnp.concatenate(
            [
                sum_ref[0:base, :],
                sum_ref[base + s * each : base + (s + 1) * each, :],
                sum_ref[base + lines + s * each : base + lines + (s + 1) * each, :],
                sum_ref[base + 2 * lines : base + 2 * lines + 16, :],
                jnp.zeros((16 - 2 * each, width), F32),
            ],
            axis=0,
        ).astype(BF16)


def parameter_kernel(
    units, scale, in_ref, w_in_ref, w_out_ref, taps_ref, skip_one_ref, skip_two_ref, one_ref, two_ref
):
    sources, _, width = in_ref.shape
    group = width // units
    count = sources // units
    each = one_ref.shape[1] // width

    def total(first, last):
        parts = [in_ref[e * units : (e + 1) * units, first:last, :] for e in range(count)]
        result = parts[0].astype(F32)
        for part in parts[1:]:
            result = result + part.astype(F32)
        return result

    blocks = total(0, 4 * group) * scale
    for kind in range(3):
        rows = blocks[:, kind * group : (kind + 1) * group, :].reshape(width, width)
        w_in_ref[:, kind * width : (kind + 1) * width] = rows.T
    w_out_ref[...] = blocks[:, 3 * group : 4 * group, :].reshape(width, width)
    rest = total(4 * group, in_ref.shape[1]) * scale
    filters = one_ref.shape[0]
    for q in range(each):
        for ref, at in ((one_ref, q), (two_ref, each + q)):
            by_unit = rest[:, at, :].reshape(filters, units // filters, width)
            ref[:, q * width : (q + 1) * width] = jnp.sum(by_unit, axis=1)
    small = jnp.sum(rest[:, 2 * each : 2 * each + 16, :], axis=0)
    for j in range(3):
        for kind in range(3):
            n = 3 * j + kind
            taps_ref[j : j + 1, kind * width : (kind + 1) * width] = small[n : n + 1]
    skip_one_ref[...] = small[9:10]
    skip_two_ref[...] = small[10:11]


def output_kernel(units, in_ref, w_in_ref, w_out_ref, out_ref, d_series_ref):
    count, block, width = out_ref.shape
    group = width // units
    parts = block // W
    w_in = w_in_ref[...]
    w_out_t = w_out_ref[...].T

    def field(e, kind, part):
        at = (kind * parts + part) * group
        return in_ref[e * units : (e + 1) * units, at : at + group, :].reshape(width, W)

    for e in range(count):
        for part in range(parts):
            rows = pl.ds(part * W, W)
            out_ref[e, rows, :] = dot(w_out_t, field(e, 3, part)).T.astype(BF16)
            grads = jnp.concatenate([field(e, kind, part) for kind in range(3)], axis=0)
            d_series_ref[e, rows, :] = dot(w_in, grads).T.astype(BF16)


def all_to_all(blocks, axis):
    return lax.all_to_all(blocks, axis, split_axis=0, concat_axis=0, tiled=True)


def shards(series, cotangent, w_in, w_out, taps, skip_one, skip_two, filter_one, filter_two):
    count, block, width = series.shape
    filters = filter_one.shape[0]
    sources = lax.axis_size("seq")
    copies = lax.axis_size("dp")
    length = block * sources
    units = sources // count
    group = width // units
    assert sources == count * units and units % filters == 0 and block % W == 0
    blocks = length // W
    rows = blocks * group
    scale = 1.0 / math.sqrt(count * copies * length)
    shape = jax.ShapeDtypeStruct

    slices = jnp.concatenate(
        [
            filter_one.reshape(filters, block // width, width),
            filter_two.reshape(filters, block // width, width),
        ],
        axis=1,
    )
    slices = jnp.concatenate([jnp.repeat(slices, units // filters, axis=0)] * count, axis=0)
    lines = all_to_all(slices, "seq")

    all_series = lax.all_gather(series, "seq")
    all_cot = lax.all_gather(cotangent, "seq")

    packed = 4 * (block // W) * group
    fields = call(
        functools.partial(project_kernel, units),
        shape((sources, packed, W), BF16),
        flops=2 * count * block * width * 4 * width,
        moved=8 * count * block * width * 4,
    )(series, cotangent, w_in, w_out)
    fields = all_to_all(fields, "seq")

    toeplitz = call(
        toeplitz_kernel,
        shape((2, blocks, W, W), BF16),
        [pltpu.VMEM((8, length), F32)],
        flops=2 * W * length * 200,
        moved=2 * W * length * 2,
    )(lines)

    sent, kept = call(
        functools.partial(operator_kernel, units),
        (shape((sources, packed, W), BF16), shape((7, rows, W), BF16)),
        [pltpu.VMEM((3 * rows, W), BF16)],
        flops=4 * 2 * rows * length * W,
        moved=2 * W * length * 2 * 2,
    )(fields, toeplitz, taps, skip_one.reshape(1, width), skip_two.reshape(1, width))

    back = all_to_all(sent, "seq")

    total_rows = 4 * group + 2 * (length // width) + 16
    sums = call(
        functools.partial(gradient_kernel, units),
        shape((copies, total_rows, width), BF16),
        [
            pltpu.VMEM((2 * rows, W), BF16),
            pltpu.VMEM((W, length), F32),
            pltpu.VMEM((total_rows, width), F32),
        ],
        flops=2 * 2 * rows * length * W,
        moved=2 * length * width * 2,
    )(fields, sent, kept, all_series, all_cot)
    sums = all_to_all(sums, "dp")

    spread_rows = 4 * group + 32
    sums = call(
        functools.partial(spread_kernel, units),
        shape((sources, spread_rows, width), BF16),
        [pltpu.VMEM((total_rows, width), F32)],
        flops=copies * total_rows * width,
        moved=2 * sources * spread_rows * width,
    )(sums)
    sums = all_to_all(sums, "seq")

    output, d_series = call(
        functools.partial(output_kernel, units),
        (shape(series.shape, BF16), shape(series.shape, BF16)),
        flops=2 * count * block * width * 4 * width,
        moved=2 * count * block * width * 6,
    )(back, w_in, w_out)

    grads = call(
        functools.partial(parameter_kernel, units, scale),
        (
            shape(w_in.shape, F32),
            shape(w_out.shape, F32),
            shape(taps.shape, F32),
            shape((1, width), F32),
            shape((1, width), F32),
            shape(filter_one.shape, F32),
            shape(filter_two.shape, F32),
        ),
        flops=sources * spread_rows * width,
        moved=2 * sources * spread_rows * width,
    )(sums)
    grad_w_in, grad_w_out, grad_taps, grad_skip_one, grad_skip_two, grad_one, grad_two = grads
    return (
        output,
        d_series,
        grad_w_in,
        grad_w_out,
        grad_taps,
        grad_skip_one.reshape(width),
        grad_skip_two.reshape(width),
        grad_one,
        grad_two,
    )


def solution(mesh):
    specs = (
        P("dp", "seq", None),
        P("dp", "seq", None),
        P(),
        P(),
        P(),
        P(),
        P(),
        P(None, "seq"),
        P(None, "seq"),
    )
    return jax.shard_map(shards, mesh=mesh, in_specs=specs, out_specs=specs, check_vma=False)
```

time: 1230 us -> 125 us (0.10)
  waiting for transfers between devices: 496 us -> 45.6 us
  starting transfers between devices: 231 us -> 16.9 us
  local copies, waits for them, and re-layouts: 190 us -> 2.98 us
  matrix products: 119 us -> 0 us
  blocking collectives: 105 us -> 9.48 us
  other arithmetic: 58 us -> 0.62 us
  Pallas kernels: 0 us -> 34 us
    all_to_all x56 -> x4, waiting for transfers between devices: 370 us -> 33.9 us  [all_to_all(): return lax.all_to_all(blocks, axis, split_axis=0, concat_axis=0, tiled=True)]
    all_to_all x56 -> x4, starting transfers between devices: 228 us -> 16.8 us  [all_to_all(): return lax.all_to_all(blocks, axis, split_axis=0, concat_axis=0, tiled=True)]
    psum x1 -> x0, waiting for transfers between devices: 124 us -> none  [shards(): lax.psum((local_w_in, local_w_out, local_taps, local_skip_one, local_skip...]
    dot_general x126 -> x0, matrix products: 119 us -> none  [the longest x24 24.3 us: complex_dft(): first = jnp.einsum(pattern, table_real, real_part, precision=highest)]
    unnamed x270 -> x8, local copies, waits for them, and re-layouts: 63.8 us -> 1.52 us
    all_to_all x72 -> x0, local copies, waits for them, and re-layouts: 60.4 us -> none  [the longest x12 13.7 us: order_spectrum(): lax.all_to_all(imag_part, 'seq', split_axis=2, concat_axis=1, tiled=True)]
    psum x2 -> x0, blocking collectives: 56 us -> none  [the longest x1 40 us: shards(): lax.psum((local_w_in, local_w_out, local_taps, local_skip_one, local_skip...]
    all_to_all x4 -> x1, blocking collectives: 49.2 us -> 9.48 us  [all_to_all(): return lax.all_to_all(blocks, axis, split_axis=0, concat_axis=0, tiled=True)]
  transfers between devices with their start and end apart: 59 -> 6, of which waited for: 51 -> 5; matrix products, arithmetic and copies ran while one was open for 23% -> 2% of each run, Pallas kernels for 0% -> 16%
where the time goes in v1:
time: 125 us; the launch traced here: 124 us
  waiting for transfers between devices  45.6 us (36%)
  Pallas kernels  34 us (27%)
  starting transfers between devices  16.9 us (14%)
  between operations  14.1 us (11%)
  blocking collectives  9.48 us (8%)
  local copies, waits for them, and re-layouts  2.98 us (2%)
    all_to_all x4, waiting for transfers between devices, all_to_all(): return lax.all_to_all(blocks, axis, split_axis=0, concat_axis=0, tiled=True)  33.9 us
    all_to_all x4, starting transfers between devices, all_to_all(): return lax.all_to_all(blocks, axis, split_axis=0, concat_axis=0, tiled=True)  16.8 us
    pallas_call x1, Pallas kernels, shards(): call(functools.partial(gradient_kernel, units), shape((copies, total_rows...  12.2 us
    all_gather x1, waiting for transfers between devices, shards(): all_cot = lax.all_gather(cotangent, 'seq')  10.3 us
    all_to_all x1, blocking collectives, all_to_all(): return lax.all_to_all(blocks, axis, split_axis=0, concat_axis=0, tiled=True)  9.48 us
    pallas_call x1, Pallas kernels, shards(): call(functools.partial(operator_kernel, units), (shape((sources, packed,...  7.11 us
    pallas_call x1, Pallas kernels, shards(): call(toeplitz_kernel, shape((2, blocks, W, W), BF16), [pltpu.VMEM((8, len...  7.03 us
  transfers between devices with their start and end apart: 6, of which 5 were waited for; matrix products, arithmetic and copies ran while one was open for 2% of the time, Pallas kernels for 16%

profile of v1, /device:TPU:0, one launch (start us, length us, event | category | flops | bytes accessed | tf_op | source)
XLA Modules:
  0.0 123.7 jit_solution(5278648319586058334)
XLA Ops:
  7.2 0.0 all-gather.5.cloned.1.call-start
  7.2 0.7 all-gather.5.cloned.1.call-update
  7.9 0.0 all-gather.7.cloned.1.call-start
  8.0 0.7 all-gather.7.cloned.1.call-update
  8.7 0.7 reshape.36
  9.4 0.7 reshape.37
  10.1 0.6 pad_maximum_fusion
  10.7 6.3 %all-to-all-start.1 = ((f32[8,8,128]{2,1,0:T(8,128)}), f32[8,8,128]{2,1,0:T(8,128)S(1)}, u32[]{:S(2)}, u32[]{:S(2)}) async-start(f32[8,8,128]{2,1,0:T(8,128)} %pad_maximum_fusion), calls=%async_computation.1 | async-start | bytes 65536 | tf_op jit(solution)/shard_map/all_to_all | solution.py:378
  17.1 2.1 %shard_map.160 = bf16[8,128,256]{2,1,0:T(8,128)(2,1)} custom-call(bf16[1,512,128]{2,1,0:T(8,128)(2,1)} %series_ref.1, bf16[1,512,128]{2,1,0:T(8,128)(2,1)} %cot_ref.1, bf16[128,384]{1,0:T(8,128)(2,1)} %w_in_ref.3, bf16[128,128]{1,0:T(8,128)(2,1)} %w_out_ref.3), custom_call_target="tpu_custom_call" | custom-call | flops 67108864 | bytes 2097152 | tf_op jit(solution)/shard_map/pallas_call | solution.py:409
  19.2 3.7 %all-to-all-done.1.taps_ref = f32[8,8,128]{2,1,0:T(8,128)S(1)} async-done(((f32[8,8,128]{2,1,0:T(8,128)}), f32[8,8,128]{2,1,0:T(8,128)S(1)}, u32[]{:S(2)}, u32[]{:S(2)}) %all-to-all-start.1) | async-done | bytes 32800 | tf_op jit(solution)/shard_map/all_to_all | solution.py:378
  22.9 0.0 copy-start.3
  22.9 3.5 %all-to-all-start = ((bf16[8,128,256]{2,1,0:T(8,128)(2,1)}), bf16[8,128,256]{2,1,0:T(8,128)(2,1)S(1)}, u32[]{:S(2)}, u32[]{:S(2)}) async-start(bf16[8,128,256]{2,1,0:T(8,128)(2,1)} %shard_map.160), calls=%async_computation | async-start | bytes 1048576 | tf_op jit(solution)/shard_map/all_to_all | solution.py:378
  26.4 0.0 copy-done.3
  26.4 7.0 %shard_map.161.toep_ref = bf16[2,16,256,256]{3,2,1,0:T(8,128)(2,1)} custom-call(f32[8,8,128]{2,1,0:T(8,128)} %copy-done.3), custom_call_target="tpu_custom_call" | custom-call | flops 419430400 | bytes 4194304 | tf_op jit(solution)/shard_map/pallas_call | solution.py:417
  33.4 10.4 %all-to-all-done.fields_ref = bf16[8,128,256]{2,1,0:T(8,128)(2,1)S(1)} async-done(((bf16[8,128,256]{2,1,0:T(8,128)(2,1)}), bf16[8,128,256]{2,1,0:T(8,128)(2,1)S(1)}, u32[]{:S(2)}, u32[]{:S(2)}) %all-to-all-start) | async-done | bytes 524320 | tf_op jit(solution)/shard_map/all_to_all | solution.py:378
  43.8 0.0 copy-start.1
  43.8 0.8 copy-done.1
  44.7 7.1 %shard_map.162 = (bf16[8,128,256]{2,1,0:T(8,128)(2,1)}, bf16[7,256,256]{2,1,0:T(8,128)(2,1)}) custom-call(bf16[8,128,256]{2,1,0:T(8,128)(2,1)} %copy-done.1, bf16[2,16,256,256]{3,2,1,0:T(8,128)(2,1)} %shard_map.161.toep_ref, f32[3,384]{1,0:T(4,128)} %taps_ref.1, f32[1,128]{1,0:T(1,128)} %bitcast.8, f32[1,128]{1,0:T(1,128)} %bitcast.9), custom_call_target="tpu_custom_call" | custom-call | flops 2147483648 | bytes 8388608 | tf_op jit(solution)/shard_map/pallas_call | solution.py:425
  51.8 0.0 all-gather.5.cloned.1.call-done
  51.8 10.3 %all-gather.7.cloned.1.call-done = bf16[8,512,128]{2,1,0:T(8,128)(2,1)} async-done(((bf16[1,512,128]{2,1,0:T(8,128)(2,1)}), bf16[8,512,128]{2,1,0:T(8,128)(2,1)}) %all-gather.7.cloned.1.call-update) | async-done | bytes 1048592 | tf_op jit(solution)/shard_map/all_gather | solution.py:406
  62.1 12.2 %shard_map.164 = bf16[4,144,128]{2,1,0:T(8,128)(2,1)} custom-call(bf16[8,128,256]{2,1,0:T(8,128)(2,1)} %copy-done.1, bf16[8,128,256]{2,1,0:T(8,128)(2,1)} %get-tuple-element.20.sent_ref, bf16[7,256,256]{2,1,0:T(8,128)(2,1)} %get-tuple-element.23.kept_ref, bf16[8,1,512,128]{3,2,1,0:T(8,128)(2,1)} %bitcast.6, bf16[8,1,512,128]{3,2,1,0:T(8,128)(2,1)} %bitcast.7), custom_call_target="tpu_custom_call" | custom-call | flops 1073741824 | bytes 2097152 | tf_op jit(solution)/shard_map/pallas_call | solution.py:436
  74.3 9.5 %all_to_all.25.in_ref = bf16[4,144,128]{2,1,0:T(8,128)(2,1)} all-to-all(bf16[4,144,128]{2,1,0:T(8,128)(2,1)} %shard_map.164), channel_id=1, replica_groups=mesh['dp'=4,'seq'=8] {'dp'}, dimensions={0} | all-to-all | bytes 294912 | tf_op jit(solution)/shard_map/all_to_all | solution.py:378
  83.8 3.6 %all-to-all-start.2 = ((bf16[8,128,256]{2,1,0:T(8,128)(2,1)}), bf16[8,128,256]{2,1,0:T(8,128)(2,1)S(1)}, u32[]{:S(2)}, u32[]{:S(2)}) async-start(bf16[8,128,256]{2,1,0:T(8,128)(2,1)} %get-tuple-element.20.sent_ref), calls=%async_computation.2 | async-start | bytes 1048576 | tf_op jit(solution)/shard_map/all_to_all | solution.py:378
  87.4 1.6 %shard_map.165 = bf16[8,96,128]{2,1,0:T(8,128)(2,1)} custom-call(bf16[4,144,128]{2,1,0:T(8,128)(2,1)} %all_to_all.25.in_ref), custom_call_target="tpu_custom_call" | custom-call | flops 73728 | bytes 196608 | tf_op jit(solution)/shard_map/pallas_call | solution.py:450
  89.0 13.7 %all-to-all-done.2.in_ref = bf16[8,128,256]{2,1,0:T(8,128)(2,1)S(1)} async-done(((bf16[8,128,256]{2,1,0:T(8,128)(2,1)}), bf16[8,128,256]{2,1,0:T(8,128)(2,1)S(1)}, u32[]{:S(2)}, u32[]{:S(2)}) %all-to-all-start.2) | async-done | bytes 524320 | tf_op jit(solution)/shard_map/all_to_all | solution.py:378
  102.8 0.0 copy-start
  102.8 3.4 %all-to-all-start.4 = ((bf16[8,96,128]{2,1,0:T(8,128)(2,1)}), bf16[8,96,128]{2,1,0:T(8,128)(2,1)S(1)}, u32[]{:S(2)}, u32[]{:S(2)}) async-start(bf16[8,96,128]{2,1,0:T(8,128)(2,1)} %shard_map.165), calls=%async_computation.4 | async-start | bytes 393216 | tf_op jit(solution)/shard_map/all_to_all | solution.py:378
  106.2 0.0 copy-done
  106.2 2.2 %shard_map.163 = (bf16[1,512,128]{2,1,0:T(8,128)(2,1)}, bf16[1,512,128]{2,1,0:T(8,128)(2,1)}) custom-call(bf16[8,128,256]{2,1,0:T(8,128)(2,1)} %copy-done, bf16[128,384]{1,0:T(8,128)(2,1)} %w_in_ref.3, bf16[128,128]{1,0:T(8,128)(2,1)} %w_out_ref.3), custom_call_target="tpu_custom_call" | custom-call | flops 67108864 | bytes 786432 | tf_op jit(solution)/shard_map/pallas_call | solution.py:459
  108.3 6.1 %all-to-all-done.4.in_ref = bf16[8,96,128]{2,1,0:T(8,128)(2,1)S(1)} async-done(((bf16[8,96,128]{2,1,0:T(8,128)(2,1)}), bf16[8,96,128]{2,1,0:T(8,128)(2,1)S(1)}, u32[]{:S(2)}, u32[]{:S(2)}) %all-to-all-start.4) | async-done | bytes 196640 | tf_op jit(solution)/shard_map/all_to_all | solution.py:378
  114.4 0.7 copy-done.2
  115.1 1.7 %shard_map.166 = (f32[128,384]{1,0:T(8,128)}, f32[128,128]{1,0:T(8,128)}, f32[3,384]{1,0:T(4,128)}, f32[1,128]{1,0:T(1,128)}, f32[1,128]{1,0:T(1,128)}, /*index=5*/f32[8,512]{1,0:T(8,128)}, f32[8,512]{1,0:T(8,128)}) custom-call(bf16[8,96,128]{2,1,0:T(8,128)(2,1)} %copy-done.2), custom_call_target="tpu_custom_call" | custom-call | flops 98304 | bytes 196608 | tf_op jit(solution)/shard_map/pallas_call | solution.py:466
  (1 shorter events, 0.0 us)
Async XLA Ops:
  7.2 44.6 %all-gather.5.cloned.1.call-start = ((), (), s32[]{:S(2)}) async-start(), calls=%async_computation.5 | async-start | bytes 1179648 | tf_op jit(solution)/shard_map/all_gather | solution.py:405
  7.9 54.2 %all-gather.7.cloned.1.call-start = ((), (), s32[]{:S(2)}) async-start(), calls=%async_computation.6 | async-start | bytes 1179648 | tf_op jit(solution)/shard_map/all_gather | solution.py:406
  10.7 12.1 %all-to-all-start.1 = ((f32[8,8,128]{2,1,0:T(8,128)}), f32[8,8,128]{2,1,0:T(8,128)S(1)}, u32[]{:S(2)}, u32[]{:S(2)}) async-start(f32[8,8,128]{2,1,0:T(8,128)} %pad_maximum_fusion), calls=%async_computation.1 | async-start | bytes 65536 | tf_op jit(solution)/shard_map/all_to_all | solution.py:378
  22.9 3.5 %copy-start.3 = (f32[8,8,128]{2,1,0:T(8,128)}, f32[8,8,128]{2,1,0:T(8,128)S(1)}, u32[]{:S(2)}) copy-start(f32[8,8,128]{2,1,0:T(8,128)S(1)} %all-to-all-done.1.taps_ref) | copy-start | bytes 98308
  22.9 20.9 %all-to-all-start = ((bf16[8,128,256]{2,1,0:T(8,128)(2,1)}), bf16[8,128,256]{2,1,0:T(8,128)(2,1)S(1)}, u32[]{:S(2)}, u32[]{:S(2)}) async-start(bf16[8,128,256]{2,1,0:T(8,128)(2,1)} %shard_map.160), calls=%async_computation | async-start | bytes 1048576 | tf_op jit(solution)/shard_map/all_to_all | solution.py:378
  43.8 0.8 copy-start.1
  83.8 19.0 %all-to-all-start.2 = ((bf16[8,128,256]{2,1,0:T(8,128)(2,1)}), bf16[8,128,256]{2,1,0:T(8,128)(2,1)S(1)}, u32[]{:S(2)}, u32[]{:S(2)}) async-start(bf16[8,128,256]{2,1,0:T(8,128)(2,1)} %get-tuple-element.20.sent_ref), calls=%async_computation.2 | async-start | bytes 1048576 | tf_op jit(solution)/shard_map/all_to_all | solution.py:378
  102.8 3.4 %copy-start = (bf16[8,128,256]{2,1,0:T(8,128)(2,1)}, bf16[8,128,256]{2,1,0:T(8,128)(2,1)S(1)}, u32[]{:S(2)}) copy-start(bf16[8,128,256]{2,1,0:T(8,128)(2,1)S(1)} %all-to-all-done.2.in_ref) | copy-start | bytes 1572868
  102.8 11.7 %all-to-all-start.4 = ((bf16[8,96,128]{2,1,0:T(8,128)(2,1)}), bf16[8,96,128]{2,1,0:T(8,128)(2,1)S(1)}, u32[]{:S(2)}, u32[]{:S(2)}) async-start(bf16[8,96,128]{2,1,0:T(8,128)(2,1)} %shard_map.165), calls=%async_computation.4 | async-start | bytes 393216 | tf_op jit(solution)/shard_map/all_to_all | solution.py:378
  114.4 0.7 copy-start.2
Sparse Core Ops, SparseCore 0:
  9.6 27.2 all-gather.4
  38.5 23.5 all-gather.6

commit v2 on v1

v2 whole, which is shorter than its diff:
```python
import functools
import math

import jax
import jax.numpy as jnp
from jax import lax
from jax.experimental import pallas as pl
from jax.experimental.pallas import tpu as pltpu
from jax.sharding import PartitionSpec as P

W = 256
F32 = jnp.float32
BF16 = jnp.bfloat16
NT = (((1,), (1,)), ((), ()))
VMEM_LIMIT = 56 * 1024 * 1024


def call(body, out_shape, scratch=(), flops=0, moved=0):
    return pl.pallas_call(
        body,
        out_shape=out_shape,
        scratch_shapes=list(scratch),
        compiler_params=pltpu.CompilerParams(vmem_limit_bytes=VMEM_LIMIT),
        cost_estimate=pl.CostEstimate(flops=flops, bytes_accessed=moved, transcendentals=0),
    )


def dot(a, b):
    return jnp.dot(a, b, preferred_element_type=F32)


def dot_nt(a, b):
    return lax.dot_general(a, b, NT, preferred_element_type=F32)


def project_kernel(units, series_ref, cot_ref, w_in_ref, w_out_ref, one_ref, two_ref, out_ref):
    count, block, width = series_ref.shape
    group = width // units
    parts = block // W
    w_in_t = w_in_ref[...].T
    w_out = w_out_ref[...]
    for e in range(count):
        for part in range(parts):
            rows = pl.ds(part * W, W)
            proj = dot_nt(w_in_t, series_ref[e, rows, :]).astype(BF16)
            d_prod = dot_nt(w_out, cot_ref[e, rows, :]).astype(BF16)
            for kind in range(4):
                field = proj[kind * width : (kind + 1) * width] if kind < 3 else d_prod
                out_ref[
                    e * units : (e + 1) * units,
                    (kind * parts + part) * group : (kind * parts + part + 1) * group,
                    :,
                ] = field.reshape(units, group, W)
    lines = [
        ref[:, part * W : (part + 1) * W] for ref in (one_ref, two_ref) for part in range(parts)
    ]
    repeat = units // one_ref.shape[0]
    start = 4 * parts * group
    spare = jnp.zeros((out_ref.shape[1] - start - len(lines), W), F32)
    for u in range(units):
        row = u // repeat
        field = jnp.concatenate([line[row : row + 1] for line in lines] + [spare], axis=0)
        for e in range(count):
            out_ref[e * units + u, start:, :] = field.astype(BF16)


def build_toeplitz(fields_ref, start, toep_ref, base_ref):
    sources = fields_ref.shape[0]
    _, blocks, _, _ = toep_ref.shape
    parts = blocks // sources
    length = blocks * W
    half = W // 2
    row = lax.broadcasted_iota(jnp.int32, (8, length), 0)
    lane = lax.broadcasted_iota(jnp.int32, (16, W), 1)
    channel = lax.broadcasted_iota(jnp.int32, (16, W), 0)
    for m in range(2):
        for s in range(sources):
            lines = fields_ref[s, start : start + 16, :].astype(F32)
            for p in range(parts):
                at = (s * parts + p) * W
                base_ref[:, at : at + W] = jnp.broadcast_to(
                    lines[m * parts + p : m * parts + p + 1, :], (8, W)
                )
        base = base_ref[...]
        for bit in (1, 2, 4):
            base = jnp.where((row & bit) != 0, pltpu.roll(base, bit, 1), base)
        for q in range(half // 16):
            low = pltpu.roll(base, 16 * q, 1) if q else base
            both = jnp.concatenate([low, pltpu.roll(base, 16 * q + 8, 1)], axis=0)
            first = jnp.where(lane >= channel + 16 * q, both[:, :W], 0.0)
            both = jnp.concatenate([first, both[:, W:]], axis=1).astype(BF16)
            at = 16 * q
            moved = jnp.concatenate([jnp.zeros((16, half), BF16), both[:, :-half]], axis=1)
            for d in range(blocks):
                toep_ref[m, d, at : at + 16, :] = both[:, d * W : (d + 1) * W]
                toep_ref[m, d, half + at : half + at + 16, :] = moved[:, d * W : (d + 1) * W]


def earlier(field, j, group):
    if j == 0:
        return field
    turned = pltpu.roll(field, j, 1)
    above = jnp.concatenate([jnp.zeros((group, W), F32), turned[:-group]], axis=0)
    lane = lax.broadcasted_iota(jnp.int32, field.shape, 1)
    return jnp.where(lane < j, above, turned)


def later(field, j, group):
    if j == 0:
        return field
    turned = pltpu.roll(field, W - j, 1)
    below = jnp.concatenate([turned[group:], jnp.zeros((group, W), F32)], axis=0)
    lane = lax.broadcasted_iota(jnp.int32, field.shape, 1)
    return jnp.where(lane >= W - j, below, turned)


def own_lanes(f, group, width):
    lane = lax.broadcasted_iota(jnp.int32, (group, width), 1)
    channel = lax.broadcasted_iota(jnp.int32, (group, width), 0)
    return lane == f * group + channel


def pick(ref, kind, received):
    rows = received // 4
    field = ref[:, kind * rows : (kind + 1) * rows, :]
    return field.reshape(field.shape[0] * rows, W).astype(F32)


def operator_kernel(
    units,
    fields_ref,
    taps_ref,
    skip_one_ref,
    skip_two_ref,
    out_ref,
    kept_ref,
    pad_ref,
    toep_ref,
    base_ref,
):
    sources, received, _ = out_ref.shape
    build_toeplitz(fields_ref, received, toep_ref, base_ref)
    width = taps_ref.shape[1] // 3
    group = width // units
    rows = sources * received // 4
    blocks = rows // group
    f = lax.rem(lax.axis_index("seq"), units)
    mine = own_lanes(f, group, width)

    def column(values):
        col = jnp.sum(jnp.where(mine, values, 0.0), axis=1, keepdims=True)
        return jnp.broadcast_to(col, (group, W))

    def scaled(field, col):
        return (field.reshape(blocks, group, W) * col[None]).reshape(rows, W)

    zeros = jnp.zeros((rows, W), BF16)
    pad_ref[0:rows, :] = zeros
    pad_ref[2 * rows : 3 * rows, :] = zeros

    def causal(m, field):
        pad_ref[rows : 2 * rows, :] = field
        left = jnp.concatenate(
            [pad_ref[rows - group * d : 2 * rows - group * d, :] for d in range(blocks)], axis=1
        )
        return dot(left, toep_ref[m].reshape(blocks * W, W))

    def anticausal(m, field):
        pad_ref[rows : 2 * rows, :] = field
        left = jnp.concatenate(
            [pad_ref[rows + group * d : 2 * rows + group * d, :] for d in range(blocks)], axis=1
        )
        right = jnp.concatenate([toep_ref[m, d] for d in range(blocks)], axis=1)
        return dot_nt(left, right)

    tap = [
        [
            column(taps_ref[j : j + 1, kind * width : (kind + 1) * width])
            for j in range(3)
        ]
        for kind in range(3)
    ]
    skip_one = column(skip_one_ref[...])
    skip_two = column(skip_two_ref[...])

    def short(kind):
        field = pick(fields_ref, kind, received)
        total = scaled(field, tap[kind][0])
        for j in (1, 2):
            total = total + scaled(earlier(field, j, group), tap[kind][j])
        return total

    def keep(slot, field):
        low = field.astype(BF16)
        kept_ref[slot] = low
        return low

    def send(kind, field):
        part_rows = received // 4
        out_ref[:, kind * part_rows : (kind + 1) * part_rows, :] = field.astype(BF16).reshape(
            sources, part_rows, W
        )

    def send_back(kind, field):
        total = scaled(field, tap[kind][0])
        for j in (1, 2):
            total = total + scaled(later(field, j, group), tap[kind][j])
        send(kind, total)

    value = short(0)
    y_one = causal(0, keep(0, value)) + scaled(value, skip_one)
    gate_one = short(1)
    mid = gate_one * y_one
    y_two = causal(1, keep(1, mid)) + scaled(mid, skip_two)
    gate_two = short(2)
    send(3, gate_two * y_two)
    d_product = pick(fields_ref, 3, received)
    grad_two = d_product * gate_two
    d_gate_two = d_product * y_two
    keep(6, d_gate_two)
    send_back(2, d_gate_two)
    d_mid = anticausal(1, keep(3, grad_two)) + scaled(grad_two, skip_two)
    grad_one = d_mid * gate_one
    d_gate_one = d_mid * y_one
    keep(5, d_gate_one)
    send_back(1, d_gate_one)
    d_value = anticausal(0, keep(2, grad_one)) + scaled(grad_one, skip_one)
    keep(4, d_value)
    send_back(0, d_value)


def gradient_kernel(units, fields_ref, kept_ref, out_ref, pad_ref, corr_ref):
    sources, _, _ = fields_ref.shape
    _, rows, _ = kept_ref.shape
    _, length = corr_ref.shape
    width = out_ref.shape[1]
    blocks = length // W
    group = rows // blocks
    received = 4 * rows // sources
    half = W // 2
    u = lax.rem(lax.axis_index("seq"), units)
    mine = own_lanes(u, group, width)
    lines = length // width

    pad_ref[rows : 2 * rows, :] = jnp.zeros((rows, W), BF16)
    row8 = lax.broadcasted_iota(jnp.int32, (8, length), 0)
    b = lax.broadcasted_iota(jnp.int32, (W, W), 0)
    r = lax.broadcasted_iota(jnp.int32, (W, W), 1)
    for m in range(2):
        pad_ref[0:rows, :] = kept_ref[2 + m]
        right = jnp.concatenate(
            [pad_ref[group * d : rows + group * d, :] for d in range(blocks)], axis=1
        )
        held = kept_ref[m].astype(F32).T.astype(BF16)
        corr_ref[...] = dot(held, right)
        corr_ref[:, 0:W] = jnp.where(r >= b, corr_ref[:, 0:W], 0.0)
        total = None
        for q in range(half // 8):
            upper = corr_ref[half + 8 * q : half + 8 * q + 8, :]
            upper = jnp.concatenate([upper[:, half:], jnp.zeros((8, half), F32)], axis=1)
            both = corr_ref[8 * q : 8 * q + 8, :] + upper
            if q:
                both = pltpu.roll(both, length - 8 * q, 1)
            total = both if total is None else total + both
        for bit in (1, 2, 4):
            total = jnp.where((row8 & bit) != 0, pltpu.roll(total, length - bit, 1), total)
        line = jnp.sum(total, axis=0, keepdims=True)
        for q in range(lines):
            at = m * lines + q
            out_ref[at : at + 1, :] = line[:, q * width : (q + 1) * width]

    def spread(products):
        by_channel = jnp.sum(products.reshape(blocks, group, W), axis=0)
        col = jnp.sum(by_channel, axis=1, keepdims=True)
        return jnp.sum(jnp.where(mine, col, 0.0), axis=0, keepdims=True)

    small = []
    for j in range(3):
        for kind in range(3):
            field = pick(fields_ref, kind, received)
            small.append(spread(kept_ref[4 + kind].astype(F32) * earlier(field, j, group)))
    for m in range(2):
        small.append(spread(kept_ref[2 + m].astype(F32) * kept_ref[m].astype(F32)))
    out_ref[2 * lines : 2 * lines + 16, :] = jnp.concatenate(
        small + [jnp.zeros((16 - len(small), width), F32)], axis=0
    )


def output_kernel(
    units, in_ref, w_in_ref, w_out_ref, series_ref, cot_ref, own_ref, out_ref, d_series_ref, part_ref
):
    count, block, width = out_ref.shape
    group = width // units
    parts = block // W
    w_in = w_in_ref[...]
    w_out_t = w_out_ref[...].T

    def field(e, kind, part):
        at = (kind * parts + part) * group
        return in_ref[e * units : (e + 1) * units, at : at + group, :].reshape(width, W)

    w_in_part = 0.0
    w_out_part = 0.0
    for e in range(count):
        for part in range(parts):
            rows = pl.ds(part * W, W)
            product = field(e, 3, part)
            out_ref[e, rows, :] = dot(w_out_t, product).T.astype(BF16)
            grads = jnp.concatenate([field(e, kind, part) for kind in range(3)], axis=0)
            d_series_ref[e, rows, :] = dot(w_in, grads).T.astype(BF16)
            w_in_part += dot(grads, series_ref[e, rows, :])
            w_out_part += dot(product, cot_ref[e, rows, :])

    weights = jnp.concatenate([w_in_part, w_out_part], axis=0)
    targets, sent, _ = part_ref.shape
    each = weights.shape[0] // targets
    sources = in_ref.shape[0]
    lines = (own_ref.shape[0] - 16) // 2
    slots = lines // sources
    spare = jnp.zeros((sent - each - 2 * slots - 1, width), F32)
    for g in range(targets):
        s = g % sources
        small = 2 * lines + g * 16 // targets
        part_ref[g] = jnp.concatenate(
            [
                weights[g * each : (g + 1) * each],
                own_ref[s * slots : (s + 1) * slots, :],
                own_ref[lines + s * slots : lines + (s + 1) * slots, :],
                own_ref[small : small + 1, :],
                spare,
            ],
            axis=0,
        ).astype(BF16)


def sum_kernel(units, each, scale, in_ref, out_ref, one_ref, two_ref):
    targets, _, width = in_ref.shape
    filters, block = one_ref.shape
    slots = block // width
    total = in_ref[0].astype(F32)
    for g in range(1, targets):
        total = total + in_ref[g].astype(F32)
    weights = total[:each]
    small = total[each + 2 * slots : each + 2 * slots + 1]
    spare = jnp.zeros((out_ref.shape[1] - each - 1, width), F32)
    total = jnp.concatenate([weights, small, spare], axis=0).astype(BF16)
    for g in range(targets):
        out_ref[g] = total
    repeat = units // filters
    for row in range(filters):
        sums = 0.0
        for g in range(targets):
            if g % units // repeat == row:
                sums += in_ref[g, each : each + 2 * slots, :].astype(F32)
        for q in range(slots):
            one_ref[row : row + 1, q * width : (q + 1) * width] = sums[q : q + 1] * scale
            two_ref[row : row + 1, q * width : (q + 1) * width] = sums[slots + q : slots + q + 1] * scale


def weight_kernel(each, scale, in_ref, w_in_ref, w_out_ref, taps_ref, skip_one_ref, skip_two_ref):
    targets, _, width = in_ref.shape
    weights = jnp.concatenate([in_ref[g, 0:each, :].astype(F32) for g in range(targets)], axis=0) * scale
    for kind in range(3):
        w_in_ref[:, kind * width : (kind + 1) * width] = weights[kind * width : (kind + 1) * width].T
    w_out_ref[...] = weights[3 * width :]

    def small(n):
        return in_ref[n * targets // 16, each : each + 1, :].astype(F32) * scale

    for j in range(3):
        for kind in range(3):
            taps_ref[j : j + 1, kind * width : (kind + 1) * width] = small(3 * j + kind)
    skip_one_ref[...] = small(9)
    skip_two_ref[...] = small(10)


def all_to_all(blocks, axis):
    return lax.all_to_all(blocks, axis, split_axis=0, concat_axis=0, tiled=True)


def shards(series, cotangent, w_in, w_out, taps, skip_one, skip_two, filter_one, filter_two):
    count, block, width = series.shape
    filters = filter_one.shape[0]
    sources = lax.axis_size("seq")
    copies = lax.axis_size("dp")
    length = block * sources
    units = sources // count
    group = width // units
    assert sources == count * units and units % filters == 0 and block % W == 0
    blocks = length // W
    rows = blocks * group
    scale = 1.0 / math.sqrt(count * copies * length)
    shape = jax.ShapeDtypeStruct

    devices = sources * copies
    packed = 4 * (block // W) * group
    fields = call(
        functools.partial(project_kernel, units),
        shape((sources, packed + 16, W), BF16),
        flops=2 * count * block * width * 4 * width,
        moved=8 * count * block * width * 4,
    )(series, cotangent, w_in, w_out, filter_one, filter_two)
    fields = all_to_all(fields, "seq")

    sent, kept = call(
        functools.partial(operator_kernel, units),
        (shape((sources, packed, W), BF16), shape((7, rows, W), BF16)),
        [
            pltpu.VMEM((3 * rows, W), BF16),
            pltpu.VMEM((2, blocks, W, W), BF16),
            pltpu.VMEM((8, length), F32),
        ],
        flops=4 * 2 * rows * length * W,
        moved=2 * W * length * 2 * 2,
    )(fields, taps, skip_one.reshape(1, width), skip_two.reshape(1, width))

    back = all_to_all(sent, "seq")

    own = call(
        functools.partial(gradient_kernel, units),
        shape((2 * (length // width) + 16, width), F32),
        [pltpu.VMEM((2 * rows, W), BF16), pltpu.VMEM((W, length), F32)],
        flops=2 * 2 * rows * length * W,
        moved=2 * length * width * 2,
    )(fields, kept)

    each = 4 * width // devices
    sent_rows = -(-(each + 2 * (block // width) + 1) // 16) * 16
    output, d_series, partial = call(
        functools.partial(output_kernel, units),
        (
            shape(series.shape, BF16),
            shape(series.shape, BF16),
            shape((devices, sent_rows, width), BF16),
        ),
        flops=2 * count * block * width * 8 * width,
        moved=2 * count * block * width * 6,
    )(back, w_in, w_out, series, cotangent, own)
    partial = all_to_all(partial, ("dp", "seq"))

    sums, grad_one, grad_two = call(
        functools.partial(sum_kernel, units, each, scale),
        (
            shape((devices, -(-(each + 1) // 16) * 16, width), BF16),
            shape(filter_one.shape, F32),
            shape(filter_two.shape, F32),
        ),
        flops=devices * sent_rows * width,
        moved=4 * devices * sent_rows * width,
    )(partial)
    sums = all_to_all(sums, ("dp", "seq"))

    grad_w_in, grad_w_out, grad_taps, grad_skip_one, grad_skip_two = call(
        functools.partial(weight_kernel, each, scale),
        (
            shape(w_in.shape, F32),
            shape(w_out.shape, F32),
            shape(taps.shape, F32),
            shape((1, width), F32),
            shape((1, width), F32),
        ),
        flops=devices * sent_rows * width,
        moved=2 * devices * sent_rows * width,
    )(sums)
    return (
        output,
        d_series,
        grad_w_in,
        grad_w_out,
        grad_taps,
        grad_skip_one.reshape(width),
        grad_skip_two.reshape(width),
        grad_one,
        grad_two,
    )


def solution(mesh):
    specs = (
        P("dp", "seq", None),
        P("dp", "seq", None),
        P(),
        P(),
        P(),
        P(),
        P(),
        P(None, "seq"),
        P(None, "seq"),
    )
    return jax.shard_map(shards, mesh=mesh, in_specs=specs, out_specs=specs, check_vma=False)
```

time: 125 us -> 87.2 us (0.70)
  blocking collectives: 9.48 us -> 50.8 us
  waiting for transfers between devices: 45.6 us -> 10.8 us
  Pallas kernels: 34 us -> 20.1 us
  between operations: 14.1 us -> 0.66 us
  starting transfers between devices: 16.9 us -> 3.49 us
  local copies, waits for them, and re-layouts: 2.98 us -> 0.79 us
    all_to_all x1 -> x3, blocking collectives: 9.48 us -> 50.8 us  [all_to_all(): return lax.all_to_all(blocks, axis, split_axis=0, concat_axis=0, tiled=True)]
    all_to_all x4 -> x1, waiting for transfers between devices: 33.9 us -> 10.8 us  [all_to_all(): return lax.all_to_all(blocks, axis, split_axis=0, concat_axis=0, tiled=True)]
    pallas_call x5 -> x4, Pallas kernels: 24.7 us -> 10.2 us  [the longest x1 4.52 us: shards(): call(functools.partial(gradient_kernel, units), shape((2 * (length // wid...]
    all_to_all x4 -> x1, starting transfers between devices: 16.8 us -> 3.49 us  [all_to_all(): return lax.all_to_all(blocks, axis, split_axis=0, concat_axis=0, tiled=True)]
    all_gather x2 -> x0, waiting for transfers between devices: 10.3 us -> none  [the longest x1 10.3 us: shards(): all_cot = lax.all_gather(cotangent, 'seq')]
    reshape x2 -> x0, local copies, waits for them, and re-layouts: 1.46 us -> none  [the longest x1 0.73 us: shards(): filter_one.reshape(filters, block // width, width)]
    unnamed x2 -> x0, waiting for transfers between devices: 1.38 us -> none
  transfers between devices with their start and end apart: 6 -> 1, of which waited for: 5 -> 1; matrix products, arithmetic and copies ran while one was open for 2% -> 0% of each run, Pallas kernels for 16% -> 5%
where the time goes in v2:
time: 87.2 us; the launch traced here: 86.6 us
  blocking collectives  50.8 us (58%)
  Pallas kernels  20.1 us (23%)
  waiting for transfers between devices  10.8 us (12%)
  starting transfers between devices  3.49 us (4%)
    all_to_all x3, blocking collectives, all_to_all(): return lax.all_to_all(blocks, axis, split_axis=0, concat_axis=0, tiled=True)  50.8 us
    all_to_all x1, waiting for transfers between devices, all_to_all(): return lax.all_to_all(blocks, axis, split_axis=0, concat_axis=0, tiled=True)  10.8 us
    pallas_call x1, Pallas kernels, shards(): call(functools.partial(operator_kernel, units), (shape((sources, packed,...  7.55 us
    pallas_call x1, Pallas kernels, shards(): call(functools.partial(gradient_kernel, units), shape((2 * (length // wid...  4.52 us
    all_to_all x1, starting transfers between devices, all_to_all(): return lax.all_to_all(blocks, axis, split_axis=0, concat_axis=0, tiled=True)  3.49 us
    pallas_call x1, Pallas kernels, shards(): call(functools.partial(output_kernel, units), (shape(series.shape, BF16),...  2.36 us
    pallas_call x1, Pallas kernels, shards(): call(functools.partial(project_kernel, units), shape((sources, packed + 1...  2.18 us
    pallas_call x1, Pallas kernels, shards(): call(functools.partial(weight_kernel, each, scale), (shape(w_in.shape, F3...  1.77 us
  transfers between devices with their start and end apart: 1, of which 1 were waited for; matrix products, arithmetic and copies ran while one was open for 0% of the time, Pallas kernels for 5%

profile of v2, /device:TPU:0, one launch (start us, length us, event | category | flops | bytes accessed | tf_op | source)
XLA Modules:
  0.0 86.6 jit_solution(12494721865315492)
XLA Ops:
  0.6 2.2 %shard_map.160 = bf16[8,144,256]{2,1,0:T(8,128)(2,1)} custom-call(bf16[1,512,128]{2,1,0:T(8,128)(2,1)} %series_ref.3, bf16[1,512,128]{2,1,0:T(8,128)(2,1)} %cot_ref.3, bf16[128,384]{1,0:T(8,128)(2,1)} %w_in_ref.3, bf16[128,128]{1,0:T(8,128)(2,1)} %w_out_ref.3, f32[8,512]{1,0:T(8,128)} %one_ref.1, f32[8,512]{1,0:T(8,128)} %two_ref.1), custom_call_target="tpu_custom_call" | custom-call | flops 67108864 | bytes 2097152 | tf_op jit(solution)/shard_map/pallas_call | solution.py:397
  2.8 23.2 %all_to_all.20.fields_ref = bf16[8,144,256]{2,1,0:T(8,128)(2,1)} all-to-all(bf16[8,144,256]{2,1,0:T(8,128)(2,1)} %shard_map.160), channel_id=1, replica_groups=mesh['dp'=4,'seq'=8] {'seq'}, dimensions={0} | all-to-all | bytes 1179648 | tf_op jit(solution)/shard_map/all_to_all | solution.py:378
  26.0 7.5 %shard_map.161 = (bf16[8,128,256]{2,1,0:T(8,128)(2,1)}, bf16[7,256,256]{2,1,0:T(8,128)(2,1)}) custom-call(bf16[8,144,256]{2,1,0:T(8,128)(2,1)} %all_to_all.20.fields_ref, f32[3,384]{1,0:T(4,128)} %taps_ref.1, f32[1,128]{1,0:T(1,128)} %bitcast.4, f32[1,128]{1,0:T(1,128)} %bitcast.5), custom_call_target="tpu_custom_call" | custom-call | flops 2147483648 | bytes 8388608 | tf_op jit(solution)/shard_map/pallas_call | solution.py:405
  33.6 3.5 %all-to-all-start.1 = ((bf16[8,128,256]{2,1,0:T(8,128)(2,1)}), bf16[8,128,256]{2,1,0:T(8,128)(2,1)S(1)}, u32[]{:S(2)}, u32[]{:S(2)}) async-start(bf16[8,128,256]{2,1,0:T(8,128)(2,1)} %get-tuple-element.22), calls=%async_computation.1 | async-start | bytes 1048576 | tf_op jit(solution)/shard_map/all_to_all | solution.py:378
  37.1 4.5 %shard_map.162.own_ref = f32[80,128]{1,0:T(8,128)} custom-call(bf16[8,144,256]{2,1,0:T(8,128)(2,1)} %all_to_all.20.fields_ref, bf16[7,256,256]{2,1,0:T(8,128)(2,1)} %get-tuple-element.23.kept_ref), custom_call_target="tpu_custom_call" | custom-call | flops 1073741824 | bytes 2097152 | tf_op jit(solution)/shard_map/pallas_call | solution.py:419
  41.6 10.8 %all-to-all-done.1.in_ref = bf16[8,128,256]{2,1,0:T(8,128)(2,1)S(1)} async-done(((bf16[8,128,256]{2,1,0:T(8,128)(2,1)}), bf16[8,128,256]{2,1,0:T(8,128)(2,1)S(1)}, u32[]{:S(2)}, u32[]{:S(2)}) %all-to-all-start.1) | async-done | bytes 524320 | tf_op jit(solution)/shard_map/all_to_all | solution.py:378
  52.3 0.0 copy-start
  52.3 0.8 copy-done
  53.1 2.4 %shard_map.163 = (bf16[1,512,128]{2,1,0:T(8,128)(2,1)}, bf16[1,512,128]{2,1,0:T(8,128)(2,1)}, bf16[32,32,128]{2,1,0:T(8,128)(2,1)}) custom-call(bf16[8,128,256]{2,1,0:T(8,128)(2,1)} %copy-done, bf16[128,384]{1,0:T(8,128)(2,1)} %w_in_ref.3, bf16[128,128]{1,0:T(8,128)(2,1)} %w_out_ref.3, bf16[1,512,128]{2,1,0:T(8,128)(2,1)} %series_ref.3, ...), custom_call_target="tpu_custom_call" | custom-call | flops 134217728 | bytes 786432 | tf_op jit(solution)/shard_map/pallas_call | solution.py:429
  55.5 14.0 %all_to_all.21.in_ref = bf16[32,32,128]{2,1,0:T(8,128)(2,1)} all-to-all(bf16[32,32,128]{2,1,0:T(8,128)(2,1)} %get-tuple-element.26), channel_id=1, replica_groups=mesh['dp'=4,'seq'=8] {'dp','seq'}, dimensions={0} | all-to-all | bytes 524288 | tf_op jit(solution)/shard_map/all_to_all | solution.py:378
  69.5 1.7 %shard_map.164 = (bf16[32,32,128]{2,1,0:T(8,128)(2,1)}, f32[8,512]{1,0:T(8,128)}, f32[8,512]{1,0:T(8,128)}) custom-call(bf16[32,32,128]{2,1,0:T(8,128)(2,1)} %all_to_all.21.in_ref), custom_call_target="tpu_custom_call" | custom-call | flops 131072 | bytes 524288 | tf_op jit(solution)/shard_map/pallas_call | solution.py:441
  71.2 13.7 %all_to_all.22.in_ref = bf16[32,32,128]{2,1,0:T(8,128)(2,1)} all-to-all(bf16[32,32,128]{2,1,0:T(8,128)(2,1)} %get-tuple-element.27), channel_id=1, replica_groups=mesh['dp'=4,'seq'=8] {'dp','seq'}, dimensions={0} | all-to-all | bytes 524288 | tf_op jit(solution)/shard_map/all_to_all | solution.py:378
  84.9 1.8 %shard_map.165 = (f32[128,384]{1,0:T(8,128)}, f32[128,128]{1,0:T(8,128)}, f32[3,384]{1,0:T(4,128)}, f32[1,128]{1,0:T(1,128)}, f32[1,128]{1,0:T(1,128)}) custom-call(bf16[32,32,128]{2,1,0:T(8,128)(2,1)} %all_to_all.22.in_ref), custom_call_target="tpu_custom_call" | custom-call | flops 131072 | bytes 262144 | tf_op jit(solution)/shard_map/pallas_call | solution.py:453
Async XLA Ops:
  33.6 18.8 %all-to-all-start.1 = ((bf16[8,128,256]{2,1,0:T(8,128)(2,1)}), bf16[8,128,256]{2,1,0:T(8,128)(2,1)S(1)}, u32[]{:S(2)}, u32[]{:S(2)}) async-start(bf16[8,128,256]{2,1,0:T(8,128)(2,1)} %get-tuple-element.22), calls=%async_computation.1 | async-start | bytes 1048576 | tf_op jit(solution)/shard_map/all_to_all | solution.py:378
  52.3 0.8 copy-start

commit v3 on v1

--- a/solution.py
+++ b/solution.py
@@ -33,55 +33,51 @@
     return lax.dot_general(a, b, NT, preferred_element_type=F32)
 
 
-def project_kernel(units, series_ref, cot_ref, w_in_ref, w_out_ref, out_ref):
-    count, block, width = series_ref.shape
-    group = width // units
-    parts = block // W
-    w_in_t = w_in_ref[...].T
-    w_out = w_out_ref[...]
-    for e in range(count):
-        for part in range(parts):
-            rows = pl.ds(part * W, W)
-            proj = dot_nt(w_in_t, series_ref[e, rows, :]).astype(BF16)
-            d_prod = dot_nt(w_out, cot_ref[e, rows, :]).astype(BF16)
-            for kind in range(4):
-                field = proj[kind * width : (kind + 1) * width] if kind < 3 else d_prod
-                out_ref[
-                    e * units : (e + 1) * units,
-                    (kind * parts + part) * group : (kind * parts + part + 1) * group,
-                    :,
-                ] = field.reshape(units, group, W)
-
-
-def toeplitz_kernel(taps_ref, out_ref, base_ref):
-    sources, chunk_rows, lanes = taps_ref.shape
-    chunks = chunk_rows // 2
-    length = sources * chunks * lanes
-    blocks = length // W
+def slice_kernel(units, one_ref, two_ref, out_ref):
+    targets, _, width = out_ref.shape
+    filters, block = one_ref.shape
+    repeat = units // filters
+    for f in range(filters):
+        rows = [
+            ref[f : f + 1, q * width : (q + 1) * width]
+            for ref in (one_ref, two_ref)
+            for q in range(block // width)
+        ]
+        rows = jnp.concatenate(rows, axis=0)
+        for g in range(targets):
+            if g % units // repeat == f:
+                out_ref[g] = rows
+
+
+def toeplitz_kernel(lines_ref, toep_ref, base_ref):
+    sources, rows, width = lines_ref.shape
+    _, blocks, _, _ = toep_ref.shape
+    slots = rows // 2
+    length = blocks * W
+    half = W // 2
     row = lax.broadcasted_iota(jnp.int32, (8, length), 0)
+    lane = lax.broadcasted_iota(jnp.int32, (16, W), 1)
+    channel = lax.broadcasted_iota(jnp.int32, (16, W), 0)
     for m in range(2):
         for s in range(sources):
-            for q in range(chunks):
-                at = (s * chunks + q) * lanes
-                base_ref[:, at : at + lanes] = jnp.broadcast_to(
-                    taps_ref[s, m * chunks + q : m * chunks + q + 1, :], (8, lanes)
+            for q in range(slots):
+                at = (s * slots + q) * width
+                base_ref[:, at : at + width] = jnp.broadcast_to(
+                    lines_ref[s, m * slots + q : m * slots + q + 1, :], (8, width)
                 )
         base = base_ref[...]
         for bit in (1, 2, 4):
             base = jnp.where((row & bit) != 0, pltpu.roll(base, bit, 1), base)
-
-        def step(q, base, m=m):
-            start = pl.multiple_of(q * 16, 16)
-            both = jnp.concatenate([base, pltpu.roll(base, 8, 1)], axis=0)
-            b = lax.broadcasted_iota(jnp.int32, (16, W), 0) + start
-            r = lax.broadcasted_iota(jnp.int32, (16, W), 1)
-            first = jnp.where(r >= b, both[:, :W], 0.0)
-            out_ref[m, 0, pl.ds(start, 16), :] = first.astype(BF16)
-            for d in range(1, blocks):
-                out_ref[m, d, pl.ds(start, 16), :] = both[:, d * W : (d + 1) * W].astype(BF16)
-            return pltpu.roll(base, 16, 1)
-
-        lax.fori_loop(0, W // 16, step, base)
+        for q in range(half // 16):
+            low = pltpu.roll(base, 16 * q, 1) if q else base
+            both = jnp.concatenate([low, pltpu.roll(base, 16 * q + 8, 1)], axis=0)
+            first = jnp.where(lane >= channel + 16 * q, both[:, :W], 0.0)
+            both = jnp.concatenate([first, both[:, W:]], axis=1).astype(BF16)
+            at = 16 * q
+            moved = jnp.concatenate([jnp.zeros((16, half), BF16), both[:, :-half]], axis=1)
+            for d in range(blocks):
+                toep_ref[m, d, at : at + 16, :] = both[:, d * W : (d + 1) * W]
+                toep_ref[m, d, half + at : half + at + 16, :] = moved[:, d * W : (d + 1) * W]
 
 
 def earlier(field, j, group):
@@ -108,22 +104,49 @@
     return lane == f * group + channel
 
 
-def pick(ref, kind, received):
-    rows = received // 4
-    field = ref[:, kind * rows : (kind + 1) * rows, :]
-    return field.reshape(field.shape[0] * rows, W).astype(F32)
-
-
-def operator_kernel(
-    units, fields_ref, toep_ref, taps_ref, skip_one_ref, skip_two_ref, out_ref, kept_ref, pad_ref
-):
-    sources, received, _ = fields_ref.shape
+def places(own, other, other_last):
+    m = len(own)
+    me = lax.axis_index("seq")
+    row, core = me // 2, lax.rem(me, 2)
+    for k in range(m):
+        place = 2 * lax.rem(row - k + m, m)
+        yield place + core, own[k][...]
+        yield place + 1 - core, (other[k] if k < m - 1 else other_last[...])
+
+
+def operator_kernel(units, m, *refs):
+    series = refs[0 : m + 2]
+    cot = refs[m + 2 : 2 * m + 4]
+    toep_ref, w_in_ref, w_out_ref, taps_ref, skip_one_ref, skip_two_ref = refs[2 * m + 4 : 2 * m + 10]
+    out_ref, kept_ref, pad_ref, raw_ref, wide_ref = refs[2 * m + 10 :]
+    sources, received, _ = out_ref.shape
     width = taps_ref.shape[1] // 3
     group = width // units
     rows = sources * received // 4
     blocks = rows // group
-    f = lax.rem(lax.axis_index("seq"), units)
-    mine = own_lanes(f, group, width)
+    parts = blocks // sources
+    u = lax.rem(lax.axis_index("seq"), units)
+    mine = own_lanes(u, group, width)
+
+    wide_ref[0 : 3 * width, :] = w_in_ref[...].astype(F32).T
+    wide_ref[3 * width :, :] = w_out_ref[...].astype(F32)
+
+    def weights(kind):
+        return wide_ref[pl.ds(pl.multiple_of(kind * width + u * group, group), group), :]
+
+    w_in = jnp.concatenate([weights(kind) for kind in range(3)], axis=0).astype(BF16)
+    w_out = weights(3).astype(BF16)
+
+    def project(first, matrix, gathered):
+        for place, block in places(gathered[:m], gathered[m], gathered[m + 1]):
+            for p in range(parts):
+                field = dot_nt(matrix, block[p * W : (p + 1) * W])
+                at = pl.multiple_of((place * parts + p) * group, group)
+                for i in range(field.shape[0] // group):
+                    raw_ref[first + i, pl.ds(at, group), :] = field[i * group : (i + 1) * group]
+
+    project(0, w_in, series)
+    project(3, w_out, cot)
 
     def column(values):
         col = jnp.sum(jnp.where(mine, values, 0.0), axis=1, keepdims=True)
@@ -162,7 +185,8 @@
     skip_two = column(skip_two_ref[...])
 
     def short(kind):
-        field = pick(fields_ref, kind, received)
+        field = raw_ref[kind]
+        kept_ref[7 + kind] = field.astype(BF16)
         total = scaled(field, tap[kind][0])
         for j in (1, 2):
             total = total + scaled(earlier(field, j, group), tap[kind][j])
@@ -192,7 +216,7 @@
     y_two = causal(1, keep(1, mid)) + scaled(mid, skip_two)
     gate_two = short(2)
     send(3, gate_two * y_two)
-    d_product = pick(fields_ref, 3, received)
+    d_product = raw_ref[3]
     grad_two = d_product * gate_two
     d_gate_two = d_product * y_two
     keep(6, d_gate_two)
@@ -207,71 +231,59 @@
     send_back(0, d_value)
 
 
-def gradient_kernel(
-    units,
-    fields_ref,
-    sent_ref,
-    kept_ref,
-    series_ref,
-    cot_ref,
-    out_ref,
-    pad_ref,
-    corr_ref,
-    total_ref,
-):
-    sources, received, _ = fields_ref.shape
-    width = series_ref.shape[3]
-    group = width // units
-    rows = sources * received // 4
-    blocks = rows // group
+def gradient_kernel(units, m, *refs):
+    series = refs[0 : m + 2]
+    cot = refs[m + 2 : 2 * m + 4]
+    sent_ref, kept_ref, out_ref, pad_ref, corr_ref, total_ref = refs[2 * m + 4 :]
+    sources, _, _ = sent_ref.shape
+    _, rows, _ = kept_ref.shape
+    _, length = corr_ref.shape
+    width = out_ref.shape[1]
+    blocks = length // W
+    group = rows // blocks
     parts = blocks // sources
-    length = blocks * W
-    me = lax.axis_index("seq")
-    f = lax.rem(me, units)
-    e = me // units
-    mine = own_lanes(f, group, width)
-
-    def wide(ref):
-        return jnp.concatenate([ref[s, e] for s in range(sources)], axis=0)
-
-    def long_rows(kind):
-        return jnp.concatenate(
-            [
-                sent_ref[s, (kind * parts + p) * group : (kind * parts + p + 1) * group, :]
-                for s in range(sources)
-                for p in range(parts)
-            ],
-            axis=1,
-        )
-
-    left = jnp.concatenate([long_rows(k) for k in range(3)], axis=0)
-    total_ref[0 : 3 * group, :] = dot(left, wide(series_ref))
-    total_ref[3 * group : 4 * group, :] = dot(long_rows(3), wide(cot_ref))
-
-    zeros = jnp.zeros((rows, W), BF16)
-    pad_ref[rows : 2 * rows, :] = zeros
+    half = W // 2
+    u = lax.rem(lax.axis_index("seq"), units)
+    mine = own_lanes(u, group, width)
+    lines = length // width
+
+    def weights(kinds, gathered):
+        left, right = [], []
+        for place, block in places(gathered[:m], gathered[m], gathered[m + 1]):
+            right.append(block)
+            for p in range(parts):
+                at = [(kind * parts + p) * group for kind in kinds]
+                left.append(jnp.concatenate([sent_ref[place, i : i + group, :] for i in at], axis=0))
+        return dot(jnp.concatenate(left, axis=1), jnp.concatenate(right, axis=0))
+
+    total_ref[0 : 3 * group, :] = weights((0, 1, 2), series)
+    total_ref[3 * group : 4 * group, :] = weights((3,), cot)
+
+    pad_ref[rows : 2 * rows, :] = jnp.zeros((rows, W), BF16)
     row8 = lax.broadcasted_iota(jnp.int32, (8, length), 0)
-    for m in range(2):
-        pad_ref[0:rows, :] = kept_ref[2 + m]
+    b = lax.broadcasted_iota(jnp.int32, (W, W), 0)
+    r = lax.broadcasted_iota(jnp.int32, (W, W), 1)
+    for order in range(2):
+        pad_ref[0:rows, :] = kept_ref[2 + order]
         right = jnp.concatenate(
             [pad_ref[group * d : rows + group * d, :] for d in range(blocks)], axis=1
         )
-        held = kept_ref[m].astype(F32).T.astype(BF16)
+        held = kept_ref[order].astype(F32).T.astype(BF16)
         corr_ref[...] = dot(held, right)
-        b = lax.broadcasted_iota(jnp.int32, (W, W), 0)
-        r = lax.broadcasted_iota(jnp.int32, (W, W), 1)
         corr_ref[:, 0:W] = jnp.where(r >= b, corr_ref[:, 0:W], 0.0)
-
-        def step(i, acc):
-            start = pl.multiple_of((W // 8 - 1 - i) * 8, 8)
-            return pltpu.roll(acc, length - 8, 1) + corr_ref[pl.ds(start, 8), :]
-
-        acc = lax.fori_loop(0, W // 8, step, jnp.zeros((8, length), F32))
+        total = None
+        for q in range(half // 8):
+            upper = corr_ref[half + 8 * q : half + 8 * q + 8, :]
+            upper = jnp.concatenate([upper[:, half:], jnp.zeros((8, half), F32)], axis=1)
+            both = corr_ref[8 * q : 8 * q + 8, :] + upper
+            if q:
+                both = pltpu.roll(both, length - 8 * q, 1)
+            total = both if total is None else total + both
         for bit in (1, 2, 4):
-            acc = jnp.where((row8 & bit) != 0, pltpu.roll(acc, length - bit, 1), acc)
-        line = jnp.sum(acc, axis=0, keepdims=True)
-        for q in range(length // width):
-            at = 4 * group + m * (length // width) + q
+            total = jnp.where((row8 & bit) != 0, pltpu.roll(total, length - bit, 1), total)
+        line = jnp.sum(total, axis=0, keepdims=True)
+        for q in range(lines):
+            at = 4 * group + order * lines + q
             total_ref[at : at + 1, :] = line[:, q * width : (q + 1) * width]
 
     def spread(products):
@@ -282,27 +294,24 @@
     small = []
     for j in range(3):
         for kind in range(3):
-            field = pick(fields_ref, kind, received)
+            field = kept_ref[7 + kind].astype(F32)
             small.append(spread(kept_ref[4 + kind].astype(F32) * earlier(field, j, group)))
-    for m in range(2):
-        small.append(spread(kept_ref[2 + m].astype(F32) * kept_ref[m].astype(F32)))
-    base = 4 * group + 2 * (length // width)
-    total_ref[base : base + 16, :] = jnp.zeros((16, width), F32)
-    for n, line in enumerate(small):
-        total_ref[base + n : base + n + 1, :] = line
-
-    total = total_ref[...].astype(BF16)
-    for i in range(out_ref.shape[0]):
-        out_ref[i] = total
-
-
-def spread_kernel(units, in_ref, out_ref, sum_ref):
-    width = in_ref.shape[2]
+    for order in range(2):
+        small.append(spread(kept_ref[2 + order].astype(F32) * kept_ref[order].astype(F32)))
+    total_ref[4 * group + 2 * lines :, :] = jnp.concatenate(
+        small + [jnp.zeros((16 - len(small), width), F32)], axis=0
+    )
+    out_ref[...] = total_ref[...].astype(BF16)
+
+
+def spread_kernel(units, *refs):
+    in_refs, out_ref, sum_ref = refs[:-2], refs[-2], refs[-1]
+    width = out_ref.shape[2]
     group = width // units
     targets = out_ref.shape[0]
-    total = in_ref[0].astype(F32)
-    for i in range(1, in_ref.shape[0]):
-        total = total + in_ref[i].astype(F32)
+    total = in_refs[0][...].astype(F32)
+    for ref in in_refs[1:]:
+        total = total + ref[...].astype(F32)
     sum_ref[...] = total
     base = 4 * group
     lines = (total.shape[0] - base - 16) // 2
@@ -378,6 +387,21 @@
     return lax.all_to_all(blocks, axis, split_axis=0, concat_axis=0, tiled=True)
 
 
+def passed(block, axis, route):
+    return lax.ppermute(block, axis, route)
+
+
+def ring(block):
+    devices = lax.axis_size("seq")
+    onward = [(i, (i + 2) % devices) for i in range(devices)]
+    swap = [(i, i ^ 1) for i in range(devices)]
+    own = [block]
+    for _ in range(devices // 2 - 1):
+        own.append(passed(own[-1], "seq", onward))
+    other = passed(jnp.stack(own[:-1]), "seq", swap)
+    return own + [other, passed(own[-1], "seq", swap)]
+
+
 def shards(series, cotangent, w_in, w_out, taps, skip_one, skip_two, filter_one, filter_two):
     count, block, width = series.shape
     filters = filter_one.shape[0]
@@ -386,34 +410,21 @@
     length = block * sources
     units = sources // count
     group = width // units
-    assert sources == count * units and units % filters == 0 and block % W == 0
+    assert count == 1 and units % filters == 0 and block % W == 0
+    assert sources % 2 == 0
     blocks = length // W
     rows = blocks * group
     scale = 1.0 / math.sqrt(count * copies * length)
     shape = jax.ShapeDtypeStruct
-
-    slices = jnp.concatenate(
-        [
-            filter_one.reshape(filters, block // width, width),
-            filter_two.reshape(filters, block // width, width),
-        ],
-        axis=1,
-    )
-    slices = jnp.concatenate([jnp.repeat(slices, units // filters, axis=0)] * count, axis=0)
+    m = sources // 2
+
+    slices = call(
+        functools.partial(slice_kernel, units),
+        shape((sources, 2 * block // width, width), F32),
+        flops=1000,
+        moved=4 * 4 * filters * block,
+    )(filter_one, filter_two)
     lines = all_to_all(slices, "seq")
-
-    all_series = lax.all_gather(series, "seq")
-    all_cot = lax.all_gather(cotangent, "seq")
-
-    packed = 4 * (block // W) * group
-    fields = call(
-        functools.partial(project_kernel, units),
-        shape((sources, packed, W), BF16),
-        flops=2 * count * block * width * 4 * width,
-        moved=8 * count * block * width * 4,
-    )(series, cotangent, w_in, w_out)
-    fields = all_to_all(fields, "seq")
-
     toeplitz = call(
         toeplitz_kernel,
         shape((2, blocks, W, W), BF16),
@@ -422,20 +433,37 @@
         moved=2 * W * length * 2,
     )(lines)
 
+    all_series = ring(series.reshape(block, width))
+    all_cot = ring(cotangent.reshape(block, width))
+
+    packed = 4 * (block // W) * group
     sent, kept = call(
-        functools.partial(operator_kernel, units),
-        (shape((sources, packed, W), BF16), shape((7, rows, W), BF16)),
-        [pltpu.VMEM((3 * rows, W), BF16)],
+        functools.partial(operator_kernel, units, m),
+        (shape((sources, packed, W), BF16), shape((10, rows, W), BF16)),
+        [
+            pltpu.VMEM((3 * rows, W), BF16),
+            pltpu.VMEM((4, rows, W), F32),
+            pltpu.VMEM((4 * width, width), F32),
+        ],
         flops=4 * 2 * rows * length * W,
         moved=2 * W * length * 2 * 2,
-    )(fields, toeplitz, taps, skip_one.reshape(1, width), skip_two.reshape(1, width))
+    )(
+        *all_series,
+        *all_cot,
+        toeplitz,
+        w_in,
+        w_out,
+        taps,
+        skip_one.reshape(1, width),
+        skip_two.reshape(1, width),
+    )
 
     back = all_to_all(sent, "seq")
 
     total_rows = 4 * group + 2 * (length // width) + 16
-    sums = call(
-        functools.partial(gradient_kernel, units),
-        shape((copies, total_rows, width), BF16),
+    total = call(
+        functools.partial(gradient_kernel, units, m),
+        shape((total_rows, width), BF16),
         [
             pltpu.VMEM((2 * rows, W), BF16),
             pltpu.VMEM((W, length), F32),
@@ -443,8 +471,10 @@
         ],
         flops=2 * 2 * rows * length * W,
         moved=2 * length * width * 2,
-    )(fields, sent, kept, all_series, all_cot)
-    sums = all_to_all(sums, "dp")
+    )(*all_series, *all_cot, sent, kept)
+    totals = [total] + [
+        passed(total, "dp", [(i, (i + d) % copies) for i in range(copies)]) for d in range(1, copies)
+    ]
 
     spread_rows = 4 * group + 32
     sums = call(
@@ -453,7 +483,7 @@
         [pltpu.VMEM((total_rows, width), F32)],
         flops=copies * total_rows * width,
         moved=2 * sources * spread_rows * width,
-    )(sums)
+    )(*totals)
     sums = all_to_all(sums, "seq")
 
     output, d_series = call(

time: 125 us -> 106 us (0.85)
  between operations: 14.1 us -> 0.8 us
  blocking collectives: 9.48 us -> 22 us
  Pallas kernels: 34 us -> 24.7 us
  starting transfers between devices: 16.9 us -> 12.1 us
  waiting for transfers between devices: 45.6 us -> 41.8 us
  other arithmetic: 0.62 us -> 1.99 us
    ppermute x0 -> x13, waiting for transfers between devices: none -> 28.2 us  [passed(): return lax.ppermute(block, axis, route)]
    all_to_all x4 -> x1, waiting for transfers between devices: 33.9 us -> 13.5 us  [all_to_all(): return lax.all_to_all(blocks, axis, split_axis=0, concat_axis=0, tiled=True)]
    all_to_all x4 -> x1, starting transfers between devices: 16.8 us -> 3.49 us  [all_to_all(): return lax.all_to_all(blocks, axis, split_axis=0, concat_axis=0, tiled=True)]
    all_to_all x1 -> x2, blocking collectives: 9.48 us -> 22 us  [all_to_all(): return lax.all_to_all(blocks, axis, split_axis=0, concat_axis=0, tiled=True)]
    all_gather x2 -> x0, waiting for transfers between devices: 10.3 us -> none  [the longest x1 10.3 us: shards(): all_cot = lax.all_gather(cotangent, 'seq')]
    ppermute x0 -> x13, starting transfers between devices: none -> 8.6 us  [passed(): return lax.ppermute(block, axis, route)]
    pallas_call x3, Pallas kernels: 21.5 us -> 15.4 us  [the longest x1 8.68 us: shards(): call(functools.partial(operator_kernel, units, m), (shape((sources, packe...]
    pallas_call x1, Pallas kernels: 7.03 us -> 3.87 us  [shards(): call(toeplitz_kernel, shape((2, blocks, W, W), BF16), [pltpu.VMEM((8, len...]
  transfers between devices with their start and end apart: 6 -> 14, of which waited for: 5 -> 10; matrix products, arithmetic and copies ran while one was open for 2% -> 2% of each run, Pallas kernels for 16% -> 7%
where the time goes in v3:
time: 106 us
  waiting for transfers between devices  41.8 us (39%)
  Pallas kernels  24.7 us (23%)
  blocking collectives  22 us (21%)
  starting transfers between devices  12.1 us (11%)
  local copies, waits for them, and re-layouts  2.33 us (2%)
  other arithmetic  1.99 us (2%)
    ppermute x13, waiting for transfers between devices, passed(): return lax.ppermute(block, axis, route)  28.2 us
    all_to_all x2, blocking collectives, all_to_all(): return lax.all_to_all(blocks, axis, split_axis=0, concat_axis=0, tiled=True)  22 us
    all_to_all x1, waiting for transfers between devices, all_to_all(): return lax.all_to_all(blocks, axis, split_axis=0, concat_axis=0, tiled=True)  13.5 us
    pallas_call x1, Pallas kernels, shards(): call(functools.partial(operator_kernel, units, m), (shape((sources, packe...  8.68 us
    ppermute x13, starting transfers between devices, passed(): return lax.ppermute(block, axis, route)  8.6 us
    pallas_call x1, Pallas kernels, shards(): call(functools.partial(gradient_kernel, units, m), shape((total_rows, wid...  5.3 us
    pallas_call x1, Pallas kernels, shards(): call(toeplitz_kernel, shape((2, blocks, W, W), BF16), [pltpu.VMEM((8, len...  3.87 us
    all_to_all x1, starting transfers between devices, all_to_all(): return lax.all_to_all(blocks, axis, split_axis=0, concat_axis=0, tiled=True)  3.49 us
  transfers between devices with their start and end apart: 14, of which 10 were waited for; matrix products, arithmetic and copies ran while one was open for 2% of the time, Pallas kernels for 7%

profile of v3, /device:TPU:0, one launch (start us, length us, event | category | flops | bytes accessed | tf_op | source)
XLA Modules:
  0.0 105.7 jit_solution(12999237036322581460)
XLA Ops:
  0.6 3.1 %collective-permute-start = (bf16[512,128]{1,0:T(8,128)(2,1)}, bf16[512,128]{1,0:T(8,128)(2,1)S(1)}, u32[]{:S(2)}, u32[]{:S(2)}) collective-permute-start(bf16[512,128]{1,0:T(8,128)(2,1)} %bitcast.10), channel_id=1, source_target_pairs={{0,2},{1,3},{2,4},{3,5},{4,6},{5,7},{6,0},{7,1},{8,10},{9,11},{10,... | collective-permute-start | bytes 393224 | tf_op jit(solution)/shard_map/ppermute | solution.py:391
  3.7 1.6 %collective-permute-start.5 = (bf16[512,128]{1,0:T(8,128)(2,1)}, bf16[512,128]{1,0:T(8,128)(2,1)S(1)}, u32[]{:S(2)}, u32[]{:S(2)}) collective-permute-start(bf16[512,128]{1,0:T(8,128)(2,1)} %bitcast.13), channel_id=1, source_target_pairs={{0,2},{1,3},{2,4},{3,5},{4,6},{5,7},{6,0},{7,1},{8,10},{9,11},{10,... | collective-permute-start | bytes 393224 | tf_op jit(solution)/shard_map/ppermute | solution.py:391
  5.3 5.0 %collective-permute-done.refs_1_ = bf16[512,128]{1,0:T(8,128)(2,1)S(1)} collective-permute-done((bf16[512,128]{1,0:T(8,128)(2,1)}, bf16[512,128]{1,0:T(8,128)(2,1)S(1)}, u32[]{:S(2)}, u32[]{:S(2)}) %collective-permute-start) | collective-permute-done | bytes 131104 | tf_op jit(solution)/shard_map/ppermute | solution.py:391
  10.3 1.9 %collective-permute-done.5.refs_7_ = bf16[512,128]{1,0:T(8,128)(2,1)S(1)} collective-permute-done((bf16[512,128]{1,0:T(8,128)(2,1)}, bf16[512,128]{1,0:T(8,128)(2,1)S(1)}, u32[]{:S(2)}, u32[]{:S(2)}) %collective-permute-start.5) | collective-permute-done | bytes 131104 | tf_op jit(solution)/shard_map/ppermute | solution.py:391
  12.3 5.8 %collective-permute-done.1.refs_2_ = bf16[512,128]{1,0:T(8,128)(2,1)S(1)} collective-permute-done((bf16[512,128]{1,0:T(8,128)(2,1)S(1)}, bf16[512,128]{1,0:T(8,128)(2,1)S(1)}, u32[]{:S(2)}, u32[]{:S(2)}) %collective-permute-start.1) | collective-permute-done | bytes 131104 | tf_op jit(solution)/shard_map/ppermute | solution.py:391
  18.2 1.0 pad_maximum_fusion
  19.2 0.6 collective-permute-done.6.refs_8_
  19.9 1.0 pad_maximum_fusion.1
  21.1 8.0 %collective-permute-done.2.refs_3_ = bf16[512,128]{1,0:T(8,128)(2,1)S(1)} collective-permute-done((bf16[512,128]{1,0:T(8,128)(2,1)S(1)}, bf16[512,128]{1,0:T(8,128)(2,1)S(1)}, u32[]{:S(2)}, u32[]{:S(2)}) %collective-permute-start.2) | collective-permute-done | bytes 131104 | tf_op jit(solution)/shard_map/ppermute | solution.py:391
  29.1 2.4 %collective-permute-done.7.refs_9_ = bf16[512,128]{1,0:T(8,128)(2,1)S(1)} collective-permute-done((bf16[512,128]{1,0:T(8,128)(2,1)S(1)}, bf16[512,128]{1,0:T(8,128)(2,1)S(1)}, u32[]{:S(2)}, u32[]{:S(2)}) %collective-permute-start.7) | collective-permute-done | bytes 131104 | tf_op jit(solution)/shard_map/ppermute | solution.py:391
  31.4 1.4 %shard_map.160 = f32[8,8,128]{2,1,0:T(8,128)} custom-call(f32[8,512]{1,0:T(8,128)} %one_ref.1, f32[8,512]{1,0:T(8,128)} %two_ref.1), custom_call_target="tpu_custom_call" | custom-call | flops 1000 | bytes 65536 | tf_op jit(solution)/shard_map/pallas_call | solution.py:421
  32.9 9.7 %all_to_all.15.lines_ref = f32[8,8,128]{2,1,0:T(8,128)} all-to-all(f32[8,8,128]{2,1,0:T(8,128)} %shard_map.160), channel_id=1, replica_groups=mesh['dp'=4,'seq'=8] {'seq'}, dimensions={0} | all-to-all | bytes 65536 | tf_op jit(solution)/shard_map/all_to_all | solution.py:387
  42.5 3.9 %shard_map.161.refs_12_ = bf16[2,16,256,256]{3,2,1,0:T(8,128)(2,1)} custom-call(f32[8,8,128]{2,1,0:T(8,128)} %all_to_all.15.lines_ref), custom_call_target="tpu_custom_call" | custom-call | flops 419430400 | bytes 4194304 | tf_op jit(solution)/shard_map/pallas_call | solution.py:428
  46.5 0.5 copy-done.12
  47.1 0.2 copy-done.8
  47.3 0.1 copy-done.9
  47.4 8.7 %shard_map.162 = (bf16[8,128,256]{2,1,0:T(8,128)(2,1)}, bf16[10,256,256]{2,1,0:T(8,128)(2,1)}) custom-call(bf16[512,128]{1,0:T(8,128)(2,1)} %bitcast.11, bf16[512,128]{1,0:T(8,128)(2,1)} %copy-done.1, bf16[512,128]{1,0:T(8,128)(2,1)} %copy-done.3, bf16[512,128]{1,0:T(8,128)(2,1)} %copy-done.10, bf16[3,512,128]{2,1,0:T(8,128)(2,1)} %copy-done.8, ...), custom_call_target="tpu_custom_call" | custom-call | flops 2147483648 | bytes 8388608 | tf_op jit(solution)/shard_map/pallas_call | solution.py:440
  56.1 5.3 %shard_map.164.refs_0_ = bf16[144,128]{1,0:T(8,128)(2,1)} custom-call(bf16[512,128]{1,0:T(8,128)(2,1)} %bitcast.12, bf16[512,128]{1,0:T(8,128)(2,1)} %copy-done.1, bf16[512,128]{1,0:T(8,128)(2,1)} %copy-done.3, bf16[512,128]{1,0:T(8,128)(2,1)} %copy-done.10, bf16[3,512,128]{2,1,0:T(8,128)(2,1)} %copy-done.8, bf16[512,128]{1,0:T(8,128)(2,1)} %copy-done.12, ...), custom_call_target="tpu_custom_call" | custom-call | flops 1073741824 | bytes 2097152 | tf_op jit(solution)/shard_map/pallas_call | solution.py:464
  61.4 2.5 %collective-permute-start.12 = (bf16[144,128]{1,0:T(8,128)(2,1)}, bf16[144,128]{1,0:T(8,128)(2,1)S(1)}, u32[]{:S(2)}, u32[]{:S(2)}) collective-permute-start(bf16[144,128]{1,0:T(8,128)(2,1)} %shard_map.164.refs_0_), channel_id=1, source_target_pairs={{0,24},{8,0},{16,8},{24,16},{1,25},{9,1},{17,9},{25,17},{2,26},{10... | collective-permute-start | bytes 110600 | tf_op jit(solution)/shard_map/ppermute | solution.py:391
  63.9 0.5 collective-permute-start.11
  64.4 0.6 collective-permute-start.10
  65.0 0.9 collective-permute-done.12.refs_3_
  65.8 2.2 %collective-permute-done.11.refs_2_ = bf16[144,128]{1,0:T(8,128)(2,1)S(1)} collective-permute-done((bf16[144,128]{1,0:T(8,128)(2,1)}, bf16[144,128]{1,0:T(8,128)(2,1)S(1)}, u32[]{:S(2)}, u32[]{:S(2)}) %collective-permute-start.11) | collective-permute-done | bytes 36896 | tf_op jit(solution)/shard_map/ppermute | solution.py:391
  68.1 1.4 %collective-permute-done.10.refs_1_ = bf16[144,128]{1,0:T(8,128)(2,1)S(1)} collective-permute-done((bf16[144,128]{1,0:T(8,128)(2,1)}, bf16[144,128]{1,0:T(8,128)(2,1)S(1)}, u32[]{:S(2)}, u32[]{:S(2)}) %collective-permute-start.10) | collective-permute-done | bytes 36896 | tf_op jit(solution)/shard_map/ppermute | solution.py:391
  69.5 0.6 copy-done.7
  70.1 1.5 %shard_map.165 = bf16[8,96,128]{2,1,0:T(8,128)(2,1)} custom-call(bf16[144,128]{1,0:T(8,128)(2,1)} %shard_map.164.refs_0_, bf16[144,128]{1,0:T(8,128)(2,1)} %copy-done.7, bf16[144,128]{1,0:T(8,128)(2,1)} %copy-done.6, bf16[144,128]{1,0:T(8,128)(2,1)} %copy-done.5), custom_call_target="tpu_custom_call" | custom-call | flops 73728 | bytes 196608 | tf_op jit(solution)/shard_map/pallas_call | solution.py:480
  71.6 12.3 %all_to_all.16.in_ref = bf16[8,96,128]{2,1,0:T(8,128)(2,1)} all-to-all(bf16[8,96,128]{2,1,0:T(8,128)(2,1)} %shard_map.165), channel_id=1, replica_groups=mesh['dp'=4,'seq'=8] {'seq'}, dimensions={0} | all-to-all | bytes 393216 | tf_op jit(solution)/shard_map/all_to_all | solution.py:387
  83.9 3.5 %all-to-all-start.1 = ((bf16[8,128,256]{2,1,0:T(8,128)(2,1)}), bf16[8,128,256]{2,1,0:T(8,128)(2,1)S(1)}, u32[]{:S(2)}, u32[]{:S(2)}) async-start(bf16[8,128,256]{2,1,0:T(8,128)(2,1)} %get-tuple-element.20.refs_12_), calls=%async_computation.1 | async-start | bytes 1048576 | tf_op jit(solution)/shard_map/all_to_all | solution.py:387
  87.4 1.7 %shard_map.166 = (f32[128,384]{1,0:T(8,128)}, f32[128,128]{1,0:T(8,128)}, f32[3,384]{1,0:T(4,128)}, f32[1,128]{1,0:T(1,128)}, f32[1,128]{1,0:T(1,128)}, /*index=5*/f32[8,512]{1,0:T(8,128)}, f32[8,512]{1,0:T(8,128)}) custom-call(bf16[8,96,128]{2,1,0:T(8,128)(2,1)} %all_to_all.16.in_ref), custom_call_target="tpu_custom_call" | custom-call | flops 98304 | bytes 196608 | tf_op jit(solution)/shard_map/pallas_call | solution.py:496
  89.2 13.5 %all-to-all-done.1.in_ref = bf16[8,128,256]{2,1,0:T(8,128)(2,1)S(1)} async-done(((bf16[8,128,256]{2,1,0:T(8,128)(2,1)}), bf16[8,128,256]{2,1,0:T(8,128)(2,1)S(1)}, u32[]{:S(2)}, u32[]{:S(2)}) %all-to-all-start.1) | async-done | bytes 524320 | tf_op jit(solution)/shard_map/all_to_all | solution.py:387
  102.7 0.8 copy-done
  103.5 2.1 %shard_map.163 = (bf16[1,512,128]{2,1,0:T(8,128)(2,1)}, bf16[1,512,128]{2,1,0:T(8,128)(2,1)}) custom-call(bf16[8,128,256]{2,1,0:T(8,128)(2,1)} %copy-done, bf16[128,384]{1,0:T(8,128)(2,1)} %w_in_ref.1, bf16[128,128]{1,0:T(8,128)(2,1)} %w_out_ref.1), custom_call_target="tpu_custom_call" | custom-call | flops 67108864 | bytes 786432 | tf_op jit(solution)/shard_map/pallas_call | solution.py:489
  (35 shorter events, 0.5 us)
Async XLA Ops:
  0.6 9.6 %collective-permute-start = (bf16[512,128]{1,0:T(8,128)(2,1)}, bf16[512,128]{1,0:T(8,128)(2,1)S(1)}, u32[]{:S(2)}, u32[]{:S(2)}) collective-permute-start(bf16[512,128]{1,0:T(8,128)(2,1)} %bitcast.10), channel_id=1, source_target_pairs={{0,2},{1,3},{2,4},{3,5},{4,6},{5,7},{6,0},{7,1},{8,10},{9,11},{10,... | collective-permute-start | bytes 393224 | tf_op jit(solution)/shard_map/ppermute | solution.py:391
  3.7 8.5 %collective-permute-start.5 = (bf16[512,128]{1,0:T(8,128)(2,1)}, bf16[512,128]{1,0:T(8,128)(2,1)S(1)}, u32[]{:S(2)}, u32[]{:S(2)}) collective-permute-start(bf16[512,128]{1,0:T(8,128)(2,1)} %bitcast.13), channel_id=1, source_target_pairs={{0,2},{1,3},{2,4},{3,5},{4,6},{5,7},{6,0},{7,1},{8,10},{9,11},{10,... | collective-permute-start | bytes 393224 | tf_op jit(solution)/shard_map/ppermute | solution.py:391
  10.3 36.2 %copy-start.1 = (bf16[512,128]{1,0:T(8,128)(2,1)}, bf16[512,128]{1,0:T(8,128)(2,1)S(1)}, u32[]{:S(2)}) copy-start(bf16[512,128]{1,0:T(8,128)(2,1)S(1)} %collective-permute-done.refs_1_) | copy-start | bytes 393220
  10.3 7.9 %collective-permute-start.1 = (bf16[512,128]{1,0:T(8,128)(2,1)S(1)}, bf16[512,128]{1,0:T(8,128)(2,1)S(1)}, u32[]{:S(2)}, u32[]{:S(2)}) collective-permute-start(bf16[512,128]{1,0:T(8,128)(2,1)S(1)} %collective-permute-done.refs_1_), channel_id=1, source_target_pairs={{0,2},{1,3},{2,4},{3,5},{4,6},{5,7},{6,0},{7,1},{8,10},{9,11},{10,... | collective-permute-start | bytes 393224 | tf_op jit(solution)/shard_map/ppermute | solution.py:391
  12.3 34.2 %copy-start.2 = (bf16[512,128]{1,0:T(8,128)(2,1)}, bf16[512,128]{1,0:T(8,128)(2,1)S(1)}, u32[]{:S(2)}) copy-start(bf16[512,128]{1,0:T(8,128)(2,1)S(1)} %collective-permute-done.5.refs_7_) | copy-start | bytes 393220
  12.3 7.6 %collective-permute-start.6 = (bf16[512,128]{1,0:T(8,128)(2,1)S(1)}, bf16[512,128]{1,0:T(8,128)(2,1)S(1)}, u32[]{:S(2)}, u32[]{:S(2)}) collective-permute-start(bf16[512,128]{1,0:T(8,128)(2,1)S(1)} %collective-permute-done.5.refs_7_), channel_id=1, source_target_pairs={{0,2},{1,3},{2,4},{3,5},{4,6},{5,7},{6,0},{7,1},{8,10},{9,11},{10,... | collective-permute-start | bytes 393224 | tf_op jit(solution)/shard_map/ppermute | solution.py:391
  18.2 28.3 %copy-start.3 = (bf16[512,128]{1,0:T(8,128)(2,1)}, bf16[512,128]{1,0:T(8,128)(2,1)S(1)}, u32[]{:S(2)}) copy-start(bf16[512,128]{1,0:T(8,128)(2,1)S(1)} %collective-permute-done.1.refs_2_) | copy-start | bytes 393220
  19.2 27.3 %collective-permute-start.3 = (bf16[3,512,128]{2,1,0:T(8,128)(2,1)S(1)}, bf16[3,512,128]{2,1,0:T(8,128)(2,1)S(1)}, u32[]{:S(2)}, u32[]{:S(2)}) collective-permute-start(bf16[3,512,128]{2,1,0:T(8,128)(2,1)S(1)} %pad_maximum_fusion), channel_id=1, source_target_pairs={{0,1},{1,0},{2,3},{3,2},{4,5},{5,4},{6,7},{7,6},{8,9},{9,8},{10,11... | collective-permute-start | bytes 1179656 | tf_op jit(solution)/shard_map/ppermute | solution.py:391
  19.9 26.6 %copy-start.4 = (bf16[512,128]{1,0:T(8,128)(2,1)}, bf16[512,128]{1,0:T(8,128)(2,1)S(1)}, u32[]{:S(2)}) copy-start(bf16[512,128]{1,0:T(8,128)(2,1)S(1)} %collective-permute-done.6.refs_8_) | copy-start | bytes 393220
  20.9 25.6 %collective-permute-start.8 = (bf16[3,512,128]{2,1,0:T(8,128)(2,1)S(1)}, bf16[3,512,128]{2,1,0:T(8,128)(2,1)S(1)}, u32[]{:S(2)}, u32[]{:S(2)}) collective-permute-start(bf16[3,512,128]{2,1,0:T(8,128)(2,1)S(1)} %pad_maximum_fusion.1), channel_id=1, source_target_pairs={{0,1},{1,0},{2,3},{3,2},{4,5},{5,4},{6,7},{7,6},{8,9},{9,8},{10,11... | collective-permute-start | bytes 1179656 | tf_op jit(solution)/shard_map/ppermute | solution.py:391
  20.9 8.1 %collective-permute-start.2 = (bf16[512,128]{1,0:T(8,128)(2,1)S(1)}, bf16[512,128]{1,0:T(8,128)(2,1)S(1)}, u32[]{:S(2)}, u32[]{:S(2)}) collective-permute-start(bf16[512,128]{1,0:T(8,128)(2,1)S(1)} %collective-permute-done.1.refs_2_), channel_id=1, source_target_pairs={{0,2},{1,3},{2,4},{3,5},{4,6},{5,7},{6,0},{7,1},{8,10},{9,11},{10,... | collective-permute-start | bytes 393224 | tf_op jit(solution)/shard_map/ppermute | solution.py:391
  21.0 10.4 %collective-permute-start.7 = (bf16[512,128]{1,0:T(8,128)(2,1)S(1)}, bf16[512,128]{1,0:T(8,128)(2,1)S(1)}, u32[]{:S(2)}, u32[]{:S(2)}) collective-permute-start(bf16[512,128]{1,0:T(8,128)(2,1)S(1)} %collective-permute-done.6.refs_8_), channel_id=1, source_target_pairs={{0,2},{1,3},{2,4},{3,5},{4,6},{5,7},{6,0},{7,1},{8,10},{9,11},{10,... | collective-permute-start | bytes 393224 | tf_op jit(solution)/shard_map/ppermute | solution.py:391
  29.1 17.4 %copy-start.10 = (bf16[512,128]{1,0:T(8,128)(2,1)}, bf16[512,128]{1,0:T(8,128)(2,1)S(1)}, u32[]{:S(2)}) copy-start(bf16[512,128]{1,0:T(8,128)(2,1)S(1)} %collective-permute-done.2.refs_3_) | copy-start | bytes 393220
  29.1 17.3 %collective-permute-start.4 = (bf16[512,128]{1,0:T(8,128)(2,1)S(1)}, bf16[512,128]{1,0:T(8,128)(2,1)S(1)}, u32[]{:S(2)}, u32[]{:S(2)}) collective-permute-start(bf16[512,128]{1,0:T(8,128)(2,1)S(1)} %collective-permute-done.2.refs_3_), channel_id=1, source_target_pairs={{0,1},{1,0},{2,3},{3,2},{4,5},{5,4},{6,7},{7,6},{8,9},{9,8},{10,11... | collective-permute-start | bytes 393224 | tf_op jit(solution)/shard_map/ppermute | solution.py:391
  31.4 15.1 %copy-start.11 = (bf16[512,128]{1,0:T(8,128)(2,1)}, bf16[512,128]{1,0:T(8,128)(2,1)S(1)}, u32[]{:S(2)}) copy-start(bf16[512,128]{1,0:T(8,128)(2,1)S(1)} %collective-permute-done.7.refs_9_) | copy-start | bytes 393220
  31.4 15.0 %collective-permute-start.9 = (bf16[512,128]{1,0:T(8,128)(2,1)S(1)}, bf16[512,128]{1,0:T(8,128)(2,1)S(1)}, u32[]{:S(2)}, u32[]{:S(2)}) collective-permute-start(bf16[512,128]{1,0:T(8,128)(2,1)S(1)} %collective-permute-done.7.refs_9_), channel_id=1, source_target_pairs={{0,1},{1,0},{2,3},{3,2},{4,5},{5,4},{6,7},{7,6},{8,9},{9,8},{10,11... | collective-permute-start | bytes 393224 | tf_op jit(solution)/shard_map/ppermute | solution.py:391
  46.4 0.6 copy-start.12
  46.4 0.7 copy-start.13
  46.4 0.8 copy-start.8
  46.5 0.9 copy-start.9
  61.4 4.4 %collective-permute-start.12 = (bf16[144,128]{1,0:T(8,128)(2,1)}, bf16[144,128]{1,0:T(8,128)(2,1)S(1)}, u32[]{:S(2)}, u32[]{:S(2)}) collective-permute-start(bf16[144,128]{1,0:T(8,128)(2,1)} %shard_map.164.refs_0_), channel_id=1, source_target_pairs={{0,24},{8,0},{16,8},{24,16},{1,25},{9,1},{17,9},{25,17},{2,26},{10... | collective-permute-start | bytes 110600 | tf_op jit(solution)/shard_map/ppermute | solution.py:391
  63.9 4.2 %collective-permute-start.11 = (bf16[144,128]{1,0:T(8,128)(2,1)}, bf16[144,128]{1,0:T(8,128)(2,1)S(1)}, u32[]{:S(2)}, u32[]{:S(2)}) collective-permute-start(bf16[144,128]{1,0:T(8,128)(2,1)} %shard_map.164.refs_0_), channel_id=1, source_target_pairs={{0,16},{8,24},{16,0},{24,8},{1,17},{9,25},{17,1},{25,9},{2,18},{10... | collective-permute-start | bytes 110600 | tf_op jit(solution)/shard_map/ppermute | solution.py:391
  64.4 5.1 %collective-permute-start.10 = (bf16[144,128]{1,0:T(8,128)(2,1)}, bf16[144,128]{1,0:T(8,128)(2,1)S(1)}, u32[]{:S(2)}, u32[]{:S(2)}) collective-permute-start(bf16[144,128]{1,0:T(8,128)(2,1)} %shard_map.164.refs_0_), channel_id=1, source_target_pairs={{0,8},{8,16},{16,24},{24,0},{1,9},{9,17},{17,25},{25,1},{2,10},{10... | collective-permute-start | bytes 110600 | tf_op jit(solution)/shard_map/ppermute | solution.py:391
  65.8 3.6 %copy-start.5 = (bf16[144,128]{1,0:T(8,128)(2,1)}, bf16[144,128]{1,0:T(8,128)(2,1)S(1)}, u32[]{:S(2)}) copy-start(bf16[144,128]{1,0:T(8,128)(2,1)S(1)} %collective-permute-done.12.refs_3_) | copy-start | bytes 110596
  68.1 1.4 %copy-start.6 = (bf16[144,128]{1,0:T(8,128)(2,1)}, bf16[144,128]{1,0:T(8,128)(2,1)S(1)}, u32[]{:S(2)}) copy-start(bf16[144,128]{1,0:T(8,128)(2,1)S(1)} %collective-permute-done.11.refs_2_) | copy-start | bytes 110596
  69.5 0.6 copy-start.7
  83.9 18.8 %all-to-all-start.1 = ((bf16[8,128,256]{2,1,0:T(8,128)(2,1)}), bf16[8,128,256]{2,1,0:T(8,128)(2,1)S(1)}, u32[]{:S(2)}, u32[]{:S(2)}) async-start(bf16[8,128,256]{2,1,0:T(8,128)(2,1)} %get-tuple-element.20.refs_12_), calls=%async_computation.1 | async-start | bytes 1048576 | tf_op jit(solution)/shard_map/all_to_all | solution.py:387
  102.7 0.8 copy-start

commit v4 on v3

v4 whole, which is shorter than its diff:
```python
import functools
import math

import jax
import jax.numpy as jnp
from jax import lax
from jax.experimental import pallas as pl
from jax.experimental.pallas import tpu as pltpu
from jax.sharding import PartitionSpec as P

W = 256
F32 = jnp.float32
BF16 = jnp.bfloat16
NT = (((1,), (1,)), ((), ()))
VMEM_LIMIT = 56 * 1024 * 1024


def call(body, out_shape, scratch=(), flops=0, moved=0):
    return pl.pallas_call(
        body,
        out_shape=out_shape,
        scratch_shapes=list(scratch),
        compiler_params=pltpu.CompilerParams(vmem_limit_bytes=VMEM_LIMIT),
        cost_estimate=pl.CostEstimate(flops=flops, bytes_accessed=moved, transcendentals=0),
    )


def dot(a, b):
    return jnp.dot(a, b, preferred_element_type=F32)


def dot_nt(a, b):
    return lax.dot_general(a, b, NT, preferred_element_type=F32)


def slice_kernel(units, one_ref, two_ref, *out_refs):
    filters, block = one_ref.shape
    rows, width = out_refs[0].shape
    row = lax.broadcasted_iota(jnp.int32, (filters, block), 0)
    me = lax.axis_index("seq")
    for d, out_ref in enumerate(out_refs):
        f = lax.rem(jnp.bitwise_xor(me, d), units) // (units // filters)
        for order, ref in enumerate((one_ref, two_ref)):
            line = jnp.sum(jnp.where(row == f, ref[...], 0.0), axis=0, keepdims=True)
            for q in range(rows // 2):
                at = order * rows // 2 + q
                out_ref[at : at + 1, :] = line[:, q * width : (q + 1) * width]


def toeplitz_kernel(*refs):
    lines_refs, (toep_ref, base_ref) = refs[:-2], refs[-2:]
    rows, width = lines_refs[0].shape
    me = lax.axis_index("seq")
    _, blocks, _, _ = toep_ref.shape
    slots = rows // 2
    length = blocks * W
    half = W // 2
    row = lax.broadcasted_iota(jnp.int32, (8, length), 0)
    lane = lax.broadcasted_iota(jnp.int32, (16, W), 1)
    channel = lax.broadcasted_iota(jnp.int32, (16, W), 0)
    for m in range(2):
        for d, ref in enumerate(lines_refs):
            for q in range(slots):
                at = pl.multiple_of((jnp.bitwise_xor(me, d) * slots + q) * width, width)
                base_ref[:, pl.ds(at, width)] = jnp.broadcast_to(
                    ref[m * slots + q : m * slots + q + 1, :], (8, width)
                )
        base = base_ref[...]
        for bit in (1, 2, 4):
            base = jnp.where((row & bit) != 0, pltpu.roll(base, bit, 1), base)
        for q in range(half // 16):
            low = pltpu.roll(base, 16 * q, 1) if q else base
            both = jnp.concatenate([low, pltpu.roll(base, 16 * q + 8, 1)], axis=0)
            first = jnp.where(lane >= channel + 16 * q, both[:, :W], 0.0)
            both = jnp.concatenate([first, both[:, W:]], axis=1).astype(BF16)
            at = 16 * q
            moved = jnp.concatenate([jnp.zeros((16, half), BF16), both[:, :-half]], axis=1)
            for d in range(blocks):
                toep_ref[m, d, at : at + 16, :] = both[:, d * W : (d + 1) * W]
                toep_ref[m, d, half + at : half + at + 16, :] = moved[:, d * W : (d + 1) * W]


def earlier(field, j, group):
    if j == 0:
        return field
    turned = pltpu.roll(field, j, 1)
    above = jnp.concatenate([jnp.zeros((group, W), F32), turned[:-group]], axis=0)
    lane = lax.broadcasted_iota(jnp.int32, field.shape, 1)
    return jnp.where(lane < j, above, turned)


def later(field, j, group):
    if j == 0:
        return field
    turned = pltpu.roll(field, W - j, 1)
    below = jnp.concatenate([turned[group:], jnp.zeros((group, W), F32)], axis=0)
    lane = lax.broadcasted_iota(jnp.int32, field.shape, 1)
    return jnp.where(lane >= W - j, below, turned)


def own_lanes(f, group, width):
    lane = lax.broadcasted_iota(jnp.int32, (group, width), 1)
    channel = lax.broadcasted_iota(jnp.int32, (group, width), 0)
    return lane == f * group + channel


def places(gathered):
    m = len(gathered) // 2
    me = lax.axis_index("seq")
    row, core = me // 2, lax.rem(me, 2)
    for k in range(m):
        place = 2 * lax.rem(row - k + m, m)
        yield place + core, gathered[k]
        yield place + 1 - core, gathered[m + k]


def project(raw_ref, kinds, matrix, gathered):
    group = matrix.shape[0] // len(kinds)
    for place, block in places(gathered):
        parts = block.shape[0] // W
        for p in range(parts):
            field = dot_nt(matrix, block[p * W : (p + 1) * W, :])
            at = pl.multiple_of((place * parts + p) * group, group)
            for i, kind in enumerate(kinds):
                raw_ref[kind, pl.ds(at, group), :] = field[i * group : (i + 1) * group]


def columns(mine):
    def column(values):
        col = jnp.sum(jnp.where(mine, values, 0.0), axis=1, keepdims=True)
        return jnp.broadcast_to(col, (mine.shape[0], W))

    return column


def scaled(field, col):
    group = col.shape[0]
    return (field.reshape(-1, group, W) * col[None]).reshape(field.shape)


def tap_columns(column, taps_ref):
    width = taps_ref.shape[1] // 3
    return [
        [column(taps_ref[j : j + 1, kind * width : (kind + 1) * width]) for j in range(3)]
        for kind in range(3)
    ]


def forward_kernel(units, *refs):
    sources = len(refs) - 11
    series = refs[:sources]
    toep_ref, w_in_ref, taps_ref, skip_one_ref, skip_two_ref = refs[sources : sources + 5]
    kept_ref, wide_ref, product_ref, pad_ref, raw_ref, turned_ref = refs[sources + 5 :]
    _, rows, _ = kept_ref.shape
    width = series[0].shape[1]
    group = width // units
    blocks = rows // group
    u = lax.rem(lax.axis_index("seq"), units)
    column = columns(own_lanes(u, group, width))

    turned_ref[...] = w_in_ref[...].astype(F32).T
    w_in = [
        turned_ref[pl.ds(pl.multiple_of(kind * width + u * group, group), group), :]
        for kind in range(3)
    ]
    project(raw_ref, (0, 1, 2), jnp.concatenate(w_in, axis=0).astype(BF16), series)

    pad_ref[0:rows, :] = jnp.zeros((rows, W), BF16)

    def causal(order, field):
        low = field.astype(BF16)
        kept_ref[order] = low
        pad_ref[rows : 2 * rows, :] = low
        left = jnp.concatenate(
            [pad_ref[rows - group * d : 2 * rows - group * d, :] for d in range(blocks)], axis=1
        )
        return dot(left, toep_ref[order].reshape(blocks * W, W))

    tap = tap_columns(column, taps_ref)

    def short(kind):
        field = raw_ref[kind]
        kept_ref[2 + kind] = field.astype(BF16)
        total = scaled(field, tap[kind][0])
        for j in (1, 2):
            total = total + scaled(earlier(field, j, group), tap[kind][j])
        return total

    value = short(0)
    y_one = causal(0, value) + scaled(value, column(skip_one_ref[...]))
    wide_ref[0] = y_one
    gate_one = short(1)
    wide_ref[1] = gate_one
    mid = gate_one * y_one
    y_two = causal(1, mid) + scaled(mid, column(skip_two_ref[...]))
    wide_ref[2] = y_two
    gate_two = short(2)
    wide_ref[3] = gate_two
    product_ref[...] = (gate_two * y_two).astype(BF16)


def backward_kernel(units, *refs):
    sources = (len(refs) - 12) // 2
    cot = refs[:sources]
    toep_ref, w_out_ref, taps_ref, skip_one_ref, skip_two_ref, wide_ref, product_ref = refs[
        sources : sources + 7
    ]
    kept_ref, sent_ref = refs[sources + 7 : sources + 9]
    block_refs = refs[sources + 9 : 2 * sources + 9]
    pad_ref, raw_ref, turned_ref = refs[2 * sources + 9 :]
    _, rows, _ = kept_ref.shape
    width = cot[0].shape[1]
    group = width // units
    blocks = rows // group
    me = lax.axis_index("seq")
    u = lax.rem(me, units)
    column = columns(own_lanes(u, group, width))

    turned_ref[...] = w_out_ref[...].astype(F32)
    w_out = turned_ref[pl.ds(pl.multiple_of(u * group, group), group), :].astype(BF16)
    project(raw_ref, (0,), w_out, cot)

    pad_ref[rows : 2 * rows, :] = jnp.zeros((rows, W), BF16)

    def anticausal(order, field):
        low = field.astype(BF16)
        kept_ref[order] = low
        pad_ref[0:rows, :] = low
        left = jnp.concatenate(
            [pad_ref[group * d : rows + group * d, :] for d in range(blocks)], axis=1
        )
        right = jnp.concatenate([toep_ref[order, d] for d in range(blocks)], axis=1)
        return dot_nt(left, right)

    tap = tap_columns(column, taps_ref)

    def send_back(kind, field):
        kept_ref[2 + kind] = field.astype(BF16)
        total = scaled(field, tap[kind][0])
        for j in (1, 2):
            total = total + scaled(later(field, j, group), tap[kind][j])
        send(kind, total.astype(BF16))

    each = rows // sources

    def send(kind, field):
        sent_ref[:, kind * each : (kind + 1) * each, :] = field.reshape(sources, each, W)

    send(3, product_ref[...])
    d_product = raw_ref[0]
    grad_two = d_product * wide_ref[3]
    d_mid = anticausal(1, grad_two) + scaled(grad_two, column(skip_two_ref[...]))
    send_back(2, d_product * wide_ref[2])
    grad_one = d_mid * wide_ref[1]
    d_value = anticausal(0, grad_one) + scaled(grad_one, column(skip_one_ref[...]))
    send_back(1, d_mid * wide_ref[0])
    send_back(0, d_value)
    for d, ref in enumerate(block_refs):
        ref[...] = sent_ref[jnp.bitwise_xor(me, d)]


def gradient_kernel(units, *refs):
    sources = (len(refs) - 7) // 2
    series = refs[:sources]
    cot = refs[sources : 2 * sources]
    fore_ref, back_ref, sent_ref, out_ref = refs[2 * sources : 2 * sources + 4]
    pad_ref, corr_ref, total_ref = refs[2 * sources + 4 :]
    _, rows, _ = back_ref.shape
    _, length = corr_ref.shape
    width = out_ref.shape[1]
    blocks = length // W
    group = rows // blocks
    parts = blocks // sources
    half = W // 2
    u = lax.rem(lax.axis_index("seq"), units)
    mine = own_lanes(u, group, width)
    slots = length // width // sources

    def weights(kinds, gathered):
        left, right = [], []
        for place, block in places(gathered):
            right.append(block[...])
            for p in range(parts):
                at = [(kind * parts + p) * group for kind in kinds]
                left.append(jnp.concatenate([sent_ref[place, i : i + group, :] for i in at], axis=0))
        return dot(jnp.concatenate(left, axis=1), jnp.concatenate(right, axis=0))

    total_ref[0 : 3 * group, :] = weights((0, 1, 2), series)
    total_ref[3 * group : 4 * group, :] = weights((3,), cot)

    pad_ref[rows : 2 * rows, :] = jnp.zeros((rows, W), BF16)
    row8 = lax.broadcasted_iota(jnp.int32, (8, length), 0)
    b = lax.broadcasted_iota(jnp.int32, (W, W), 0)
    r = lax.broadcasted_iota(jnp.int32, (W, W), 1)
    for order in range(2):
        pad_ref[0:rows, :] = back_ref[order]
        right = jnp.concatenate(
            [pad_ref[group * d : rows + group * d, :] for d in range(blocks)], axis=1
        )
        held = fore_ref[order].astype(F32).T.astype(BF16)
        corr_ref[...] = dot(held, right)
        corr_ref[:, 0:W] = jnp.where(r >= b, corr_ref[:, 0:W], 0.0)
        total = None
        for q in range(half // 8):
            upper = corr_ref[half + 8 * q : half + 8 * q + 8, :]
            upper = jnp.concatenate([upper[:, half:], jnp.zeros((8, half), F32)], axis=1)
            both = corr_ref[8 * q : 8 * q + 8, :] + upper
            if q:
                both = pltpu.roll(both, length - 8 * q, 1)
            total = both if total is None else total + both
        for bit in (1, 2, 4):
            total = jnp.where((row8 & bit) != 0, pltpu.roll(total, length - bit, 1), total)
        line = jnp.sum(total, axis=0, keepdims=True)
        for q in range(sources * slots):
            at = 4 * group + (q // slots * 2 + order) * slots + q % slots
            total_ref[at : at + 1, :] = line[:, q * width : (q + 1) * width]

    def spread(products):
        by_channel = jnp.sum(products.reshape(blocks, group, W), axis=0)
        col = jnp.sum(by_channel, axis=1, keepdims=True)
        return jnp.sum(jnp.where(mine, col, 0.0), axis=0, keepdims=True)

    small = []
    for j in range(3):
        for kind in range(3):
            field = fore_ref[2 + kind].astype(F32)
            small.append(spread(back_ref[2 + kind].astype(F32) * earlier(field, j, group)))
    for order in range(2):
        small.append(spread(back_ref[order].astype(F32) * fore_ref[order].astype(F32)))
    total_ref[4 * group + 2 * sources * slots :, :] = jnp.concatenate(
        small + [jnp.zeros((16 - len(small), width), F32)], axis=0
    )
    out_ref[...] = total_ref[...].astype(BF16)


def spread_kernel(copies, *refs):
    in_refs, out_refs, sum_ref = refs[:copies], refs[copies:-1], refs[-1]
    targets = len(out_refs)
    sent, width = out_refs[0].shape
    total = in_refs[0][...].astype(F32)
    for ref in in_refs[1:]:
        total = total + ref[...].astype(F32)
    sum_ref[...] = total
    base = sent - 32
    each = (total.shape[0] - base - 16) // targets
    weights = sum_ref[0:base, :].astype(BF16)
    small = sum_ref[base + targets * each :, :]
    spare = jnp.zeros((16 - each, width), F32)
    me = lax.axis_index("seq")
    for d in range(targets):
        at = pl.multiple_of(base + jnp.bitwise_xor(me, d) * each, each)
        out_refs[d][0:base, :] = weights
        rest = jnp.concatenate([small, sum_ref[pl.ds(at, each), :], spare], axis=0)
        out_refs[d][base:, :] = rest.astype(BF16)


def parameter_kernel(units, scale, *refs):
    in_refs = refs[:-8]
    w_in_ref, w_out_ref, taps_ref, skip_one_ref, skip_two_ref, one_ref, two_ref, rows_ref = refs[-8:]
    sources = len(in_refs)
    width = w_in_ref.shape[0]
    group = width // units
    filters, block = one_ref.shape
    slots = block // width
    me = lax.axis_index("seq")
    small = 0.0
    sums = [0.0] * (2 * slots)
    row = lax.broadcasted_iota(jnp.int32, (filters, width), 0)
    for d in range(sources):
        u = jnp.bitwise_xor(me, d)
        for kind in range(4):
            at = pl.multiple_of(kind * width + u * group, group)
            rows_ref[pl.ds(at, group), :] = (
                in_refs[d][kind * group : (kind + 1) * group, :].astype(F32) * scale
            )
        rest = in_refs[d][4 * group :, :].astype(F32) * scale
        small = small + rest[0:16]
        for q in range(2 * slots):
            sums[q] += jnp.where(row == u // (units // filters), rest[16 + q : 17 + q], 0.0)
    for q in range(slots):
        one_ref[:, q * width : (q + 1) * width] = sums[q]
        two_ref[:, q * width : (q + 1) * width] = sums[slots + q]
    for kind in range(3):
        lanes = slice(kind * width, (kind + 1) * width)
        w_in_ref[:, lanes] = rows_ref[lanes, :].T
        for j in range(3):
            n = 3 * j + kind
            taps_ref[j : j + 1, lanes] = small[n : n + 1]
    w_out_ref[...] = rows_ref[3 * width :, :]
    skip_one_ref[...] = small[9:10]
    skip_two_ref[...] = small[10:11]


def output_kernel(*refs):
    in_refs = refs[:-5]
    w_in_ref, w_out_ref, out_ref, d_series_ref, field_ref = refs[-5:]
    _, block, width = out_ref.shape
    group = width // len(in_refs)
    parts = block // W
    w_in = w_in_ref[...]
    w_out_t = w_out_ref[...].T
    me = lax.axis_index("seq")
    for d, ref in enumerate(in_refs):
        u = jnp.bitwise_xor(me, d)
        for kind in range(4):
            at = pl.multiple_of(kind * width + u * group, group)
            for part in range(parts):
                start = (kind * parts + part) * group
                field = ref[start : start + group, :].astype(field_ref.dtype)
                field_ref[part, pl.ds(at, group), :] = field
    for part in range(parts):
        rows = pl.ds(part * W, W)
        product = field_ref[part, 3 * width :, :].astype(BF16)
        out_ref[0, rows, :] = dot(w_out_t, product).T.astype(BF16)
        grads = field_ref[part, 0 : 3 * width, :].astype(BF16)
        d_series_ref[0, rows, :] = dot(w_in, grads).T.astype(BF16)


def exchange(blocks, axis):
    devices = range(len(blocks))
    return [blocks[0]] + [
        lax.ppermute(blocks[d], axis, [(i, i ^ d) for i in devices]) for d in devices if d
    ]


def swapped(block):
    return lax.ppermute(block, "seq", [(i, i ^ 1) for i in range(lax.axis_size("seq"))])


def onward(block):
    devices = lax.axis_size("seq")
    return lax.ppermute(block, "seq", [(i, (i + 2) % devices) for i in range(devices)])


after = lax.optimization_barrier


def shards(series, cotangent, w_in, w_out, taps, skip_one, skip_two, filter_one, filter_two):
    count, block, width = series.shape
    filters = filter_one.shape[0]
    sources = lax.axis_size("seq")
    copies = lax.axis_size("dp")
    length = block * sources
    units = sources // count
    group = width // units
    assert count == 1 and units % filters == 0 and block % W == 0
    assert sources % 2 == 0
    blocks = length // W
    rows = blocks * group
    scale = 1.0 / math.sqrt(count * copies * length)
    shape = jax.ShapeDtypeStruct
    m = sources // 2

    own_series, own_cot = [series.reshape(block, width)], [cotangent.reshape(block, width)]
    own_series.append(onward(own_series[0]))
    slices = call(
        functools.partial(slice_kernel, units),
        [shape((2 * block // width, width), F32)] * sources,
        flops=1000,
        moved=4 * 4 * filters * block,
    )(filter_one, filter_two)
    lines = exchange(slices, "seq")
    own_series[1], own_cot[0] = after((own_series[1], own_cot[0]))
    toeplitz = None
    for k in range(1, m):
        if k + 1 < m:
            own_series.append(onward(own_series[k]))
        own_cot.append(onward(own_cot[k - 1]))
        if k == 1:
            toeplitz = call(
                toeplitz_kernel,
                shape((2, blocks, W, W), BF16),
                [pltpu.VMEM((8, length), F32)],
                flops=2 * W * length * 200,
                moved=2 * W * length * 2,
            )(*lines)
        if k + 1 < m:
            tied = after((own_series[k + 1], own_cot[k], toeplitz))
            own_series[k + 1], own_cot[k], toeplitz = tied
    all_series = own_series + [swapped(part) for part in own_series]
    all_cot = own_cot + [swapped(part) for part in own_cot]

    skips = (skip_one.reshape(1, width), skip_two.reshape(1, width))
    fore, wide, product = call(
        functools.partial(forward_kernel, units),
        (shape((5, rows, W), BF16), shape((4, rows, W), F32), shape((rows, W), BF16)),
        [
            pltpu.VMEM((2 * rows, W), BF16),
            pltpu.VMEM((3, rows, W), F32),
            pltpu.VMEM((3 * width, width), F32),
        ],
        flops=2 * 2 * rows * length * W,
        moved=W * length * 2 * 2,
    )(*all_series, toeplitz, w_in, taps, *skips)

    each = rows // sources
    back, sent, *blocks_back = call(
        functools.partial(backward_kernel, units),
        [shape((5, rows, W), BF16), shape((sources, 4 * each, W), BF16)]
        + [shape((4 * each, W), BF16)] * sources,
        [
            pltpu.VMEM((2 * rows, W), BF16),
            pltpu.VMEM((1, rows, W), F32),
            pltpu.VMEM((width, width), F32),
        ],
        flops=2 * 2 * rows * length * W,
        moved=W * length * 2 * 2,
    )(*all_cot, toeplitz, w_out, taps, *skips, wide, product)
    blocks_back = exchange(blocks_back, "seq")

    total_rows = 4 * group + 2 * (length // width) + 16
    total = call(
        functools.partial(gradient_kernel, units),
        shape((total_rows, width), BF16),
        [
            pltpu.VMEM((2 * rows, W), BF16),
            pltpu.VMEM((W, length), F32),
            pltpu.VMEM((total_rows, width), F32),
        ],
        flops=2 * 2 * rows * length * W,
        moved=2 * length * width * 2,
    )(*all_series, *all_cot, fore, back, sent)
    totals = exchange([total] * copies, "dp")
    blocks_back, totals = after((blocks_back, totals))

    spread_rows = 4 * group + 32
    sums = call(
        functools.partial(spread_kernel, copies),
        [shape((spread_rows, width), BF16)] * sources,
        [pltpu.VMEM((total_rows, width), F32)],
        flops=copies * total_rows * width,
        moved=2 * sources * spread_rows * width,
    )(*totals)
    sums = exchange(sums, "seq")

    output, d_series = call(
        output_kernel,
        (shape(series.shape, BF16), shape(series.shape, BF16)),
        [pltpu.VMEM((block // W, 4 * width, W), F32 if group % 16 else BF16)],
        flops=2 * count * block * width * 4 * width,
        moved=2 * count * block * width * 6,
    )(*blocks_back, w_in, w_out)

    grads = call(
        functools.partial(parameter_kernel, units, scale),
        (
            shape(w_in.shape, F32),
            shape(w_out.shape, F32),
            shape(taps.shape, F32),
            shape((1, width), F32),
            shape((1, width), F32),
            shape(filter_one.shape, F32),
            shape(filter_two.shape, F32),
        ),
        [pltpu.VMEM((4 * width, width), F32)],
        flops=sources * spread_rows * width,
        moved=2 * sources * spread_rows * width,
    )(*sums)
    grad_w_in, grad_w_out, grad_taps, grad_skip_one, grad_skip_two, grad_one, grad_two = grads
    return (
        output,
        d_series,
        grad_w_in,
        grad_w_out,
        grad_taps,
        grad_skip_one.reshape(width),
        grad_skip_two.reshape(width),
        grad_one,
        grad_two,
    )


def solution(mesh):
    specs = (
        P("dp", "seq", None),
        P("dp", "seq", None),
        P(),
        P(),
        P(),
        P(),
        P(),
        P(None, "seq"),
        P(None, "seq"),
    )
    return jax.shard_map(shards, mesh=mesh, in_specs=specs, out_specs=specs, check_vma=False)
```

time: 106 us -> 104 us (0.981)
  starting transfers between devices: 12.1 us -> 36.1 us
  blocking collectives: 22 us -> 0 us
  waiting for transfers between devices: 41.8 us -> 33.6 us
  Pallas kernels: 24.7 us -> 29.7 us
  other arithmetic: 1.99 us -> 0 us
    ppermute x13 -> x38, starting transfers between devices: 8.6 us -> 36.1 us  [the longest x24 29.5 us: exchange(): lax.ppermute(blocks[d], axis, [(i, i ^ d) for i in devices])]
    all_to_all x2 -> x0, blocking collectives: 22 us -> none  [all_to_all(): return lax.all_to_all(blocks, axis, split_axis=0, concat_axis=0, tiled=True)]
    all_to_all x1 -> x0, waiting for transfers between devices: 13.5 us -> none  [all_to_all(): return lax.all_to_all(blocks, axis, split_axis=0, concat_axis=0, tiled=True)]
    ppermute x13 -> x38, waiting for transfers between devices: 28.2 us -> 33.6 us  [the longest x6 20.4 us: onward(): lax.ppermute(block, 'seq', [(i, (i + 2) % devices) for i in range(devices)])]
    pallas_call x5 -> x6, Pallas kernels: 19.1 us -> 24.1 us  [the longest x1 6.9 us: shards(): call(functools.partial(backward_kernel, units), [shape((5, rows, W), BF16...]
    all_to_all x1 -> x0, starting transfers between devices: 3.49 us -> none  [all_to_all(): return lax.all_to_all(blocks, axis, split_axis=0, concat_axis=0, tiled=True)]
    another operation x2 -> x0, other arithmetic: 1.99 us -> none  [ring(): other = passed(jnp.stack(own[:-1]), 'seq', swap)]
    unnamed x28 -> x80, local copies, waits for them, and re-layouts: 2.33 us -> 2.57 us
  transfers between devices with their start and end apart: 14 -> 38, of which waited for: 10 -> 12; matrix products, arithmetic and copies ran while one was open for 2% -> 0% of each run, Pallas kernels for 7% -> 19%
where the time goes in v4:
time: 104 us; the launch traced here: 103 us
  starting transfers between devices  36.1 us (35%)
  waiting for transfers between devices  33.6 us (32%)
  Pallas kernels  29.7 us (29%)
  local copies, waits for them, and re-layouts  2.57 us (2%)
  between operations  1.07 us (1%)
    ppermute x24, starting transfers between devices, exchange(): lax.ppermute(blocks[d], axis, [(i, i ^ d) for i in devices])  29.5 us
    ppermute x6, waiting for transfers between devices, onward(): lax.ppermute(block, 'seq', [(i, (i + 2) % devices) for i in range(devices)])  20.4 us
    ppermute x24, waiting for transfers between devices, exchange(): lax.ppermute(blocks[d], axis, [(i, i ^ d) for i in devices])  13.2 us
    pallas_call x1, Pallas kernels, shards(): call(functools.partial(backward_kernel, units), [shape((5, rows, W), BF16...  6.9 us
    pallas_call x1, Pallas kernels, shards(): call(functools.partial(forward_kernel, units), (shape((5, rows, W), BF16)...  6.74 us
    pallas_call x1, Pallas kernels, shards(): call(functools.partial(gradient_kernel, units), shape((total_rows, width)...  5.25 us
    ppermute x6, starting transfers between devices, onward(): lax.ppermute(block, 'seq', [(i, (i + 2) % devices) for i in range(devices)])  4.99 us
    pallas_call x1, Pallas kernels, shards(): call(toeplitz_kernel, shape((2, blocks, W, W), BF16), [pltpu.VMEM((8, len...  3.97 us
  transfers between devices with their start and end apart: 38, of which 12 were waited for; matrix products, arithmetic and copies ran while one was open for 0% of the time, Pallas kernels for 19%

profile of v4, /device:TPU:0, one launch (start us, length us, event | category | flops | bytes accessed | tf_op | source)
XLA Modules:
  0.0 103.1 jit_solution(13332949467871400070)
XLA Ops:
  0.7 3.1 %collective-permute-start = (bf16[512,128]{1,0:T(8,128)(2,1)}, bf16[512,128]{1,0:T(8,128)(2,1)S(1)}, u32[]{:S(2)}, u32[]{:S(2)}) collective-permute-start(bf16[512,128]{1,0:T(8,128)(2,1)} %bitcast.10), channel_id=1, source_target_pairs={{0,2},{1,3},{2,4},{3,5},{4,6},{5,7},{6,0},{7,1},{8,10},{9,11},{10,... | collective-permute-start | bytes 393224 | tf_op jit(solution)/shard_map/ppermute | solution.py:432
  3.7 5.7 %collective-permute-done.refs_1_ = bf16[512,128]{1,0:T(8,128)(2,1)S(1)} collective-permute-done((bf16[512,128]{1,0:T(8,128)(2,1)}, bf16[512,128]{1,0:T(8,128)(2,1)S(1)}, u32[]{:S(2)}, u32[]{:S(2)}) %collective-permute-start) | collective-permute-done | bytes 131104 | tf_op jit(solution)/shard_map/ppermute | solution.py:432
  9.5 1.3 %collective-permute-start.1 = (bf16[512,128]{1,0:T(8,128)(2,1)S(1)}, bf16[512,128]{1,0:T(8,128)(2,1)S(1)}, u32[]{:S(2)}, u32[]{:S(2)}) collective-permute-start(bf16[512,128]{1,0:T(8,128)(2,1)S(1)} %collective-permute-done.refs_1_), channel_id=1, source_target_pairs={{0,2},{1,3},{2,4},{3,5},{4,6},{5,7},{6,0},{7,1},{8,10},{9,11},{10,... | collective-permute-start | bytes 393224 | tf_op jit(solution)/shard_map/ppermute | solution.py:432
  10.8 1.4 %shard_map.160 = (f32[8,128]{1,0:T(8,128)}, f32[8,128]{1,0:T(8,128)}, f32[8,128]{1,0:T(8,128)}, f32[8,128]{1,0:T(8,128)}, f32[8,128]{1,0:T(8,128)}, /*index=5*/f...) custom-call(f32[8,512]{1,0:T(8,128)} %one_ref.1, f32[8,512]{1,0:T(8,128)} %two_ref.1), custom_call_target="tpu_custom_call" | custom-call | flops 1000 | bytes 65536 | tf_op jit(solution)/shard_map/pallas_call | solution.py:456
  12.2 1.6 %collective-permute-start.4 = (f32[8,128]{1,0:T(8,128)}, f32[8,128]{1,0:T(8,128)S(1)}, u32[]{:S(2)}, u32[]{:S(2)}) collective-permute-start(f32[8,128]{1,0:T(8,128)} %get-tuple-element.71), channel_id=1, source_target_pairs={{0,2},{1,3},{2,0},{3,1},{4,6},{5,7},{6,4},{7,5},{8,10},{9,11},{10,... | collective-permute-start | bytes 12296 | tf_op jit(solution)/shard_map/ppermute | solution.py:422
  14.0 3.1 %collective-permute-start.6 = (f32[8,128]{1,0:T(8,128)}, f32[8,128]{1,0:T(8,128)S(1)}, u32[]{:S(2)}, u32[]{:S(2)}) collective-permute-start(f32[8,128]{1,0:T(8,128)} %get-tuple-element.73), channel_id=1, source_target_pairs={{0,4},{1,5},{2,6},{3,7},{4,0},{5,1},{6,2},{7,3},{8,12},{9,13},{10,... | collective-permute-start | bytes 12296 | tf_op jit(solution)/shard_map/ppermute | solution.py:422
  17.1 1.0 collective-permute-start.7
  18.2 1.1 %collective-permute-done.5.refs_3_ = f32[8,128]{1,0:T(8,128)S(1)} collective-permute-done((f32[8,128]{1,0:T(8,128)}, f32[8,128]{1,0:T(8,128)S(1)}, u32[]{:S(2)}, u32[]{:S(2)}) %collective-permute-start.5) | collective-permute-done | bytes 4128 | tf_op jit(solution)/shard_map/ppermute | solution.py:422
  20.0 2.9 %collective-permute-start.9 = (f32[8,128]{1,0:T(8,128)}, f32[8,128]{1,0:T(8,128)S(1)}, u32[]{:S(2)}, u32[]{:S(2)}) collective-permute-start(f32[8,128]{1,0:T(8,128)} %get-tuple-element.76), channel_id=1, source_target_pairs={{0,7},{1,6},{2,5},{3,4},{4,3},{5,2},{6,1},{7,0},{8,15},{9,14},{10,... | collective-permute-start | bytes 12296 | tf_op jit(solution)/shard_map/ppermute | solution.py:422
  23.0 1.9 %collective-permute-done.8.refs_6_ = f32[8,128]{1,0:T(8,128)S(1)} collective-permute-done((f32[8,128]{1,0:T(8,128)}, f32[8,128]{1,0:T(8,128)S(1)}, u32[]{:S(2)}, u32[]{:S(2)}) %collective-permute-start.8) | collective-permute-done | bytes 4128 | tf_op jit(solution)/shard_map/ppermute | solution.py:422
  25.7 4.0 %shard_map.161.refs_8_ = bf16[2,16,256,256]{3,2,1,0:T(8,128)(2,1)} custom-call(f32[8,128]{1,0:T(8,128)} %get-tuple-element.69.refs_0_, f32[8,128]{1,0:T(8,128)} %copy-done.33, f32[8,128]{1,0:T(8,128)} %copy-done.34, f32[8,128]{1,0:T(8,128)} %copy-done.35, f32[8,128]{1,0:T(8,128)} %copy-done.36, f32[8,128]{1,0:T(8,128)} %copy-done.37, f32[8,128]{1,0:T(8,128)} %copy-done.38, ...), custom_call_target="tpu_custom_call" | custom-call | flops 419430400 | bytes 4194304 | tf_op jit(solution)/shard_map/pallas_call | solution.py:470
  30.8 7.1 %collective-permute-done.11.refs_2_.refs_10_ = bf16[512,128]{1,0:T(8,128)(2,1)S(1)} collective-permute-done((bf16[512,128]{1,0:T(8,128)(2,1)S(1)}, bf16[512,128]{1,0:T(8,128)(2,1)S(1)}, u32[]{:S(2)}, u32[]{:S(2)}) %collective-permute-start.11) | collective-permute-done | bytes 131104 | tf_op jit(solution)/shard_map/ppermute | solution.py:432
  37.9 2.0 %collective-permute-done.10.refs_3_ = bf16[512,128]{1,0:T(8,128)(2,1)S(1)} collective-permute-done((bf16[512,128]{1,0:T(8,128)(2,1)S(1)}, bf16[512,128]{1,0:T(8,128)(2,1)S(1)}, u32[]{:S(2)}, u32[]{:S(2)}) %collective-permute-start.10) | collective-permute-done | bytes 131104 | tf_op jit(solution)/shard_map/ppermute | solution.py:432
  40.9 5.7 %collective-permute-done.12.refs_3_.refs_11_ = bf16[512,128]{1,0:T(8,128)(2,1)S(1)} collective-permute-done((bf16[512,128]{1,0:T(8,128)(2,1)S(1)}, bf16[512,128]{1,0:T(8,128)(2,1)S(1)}, u32[]{:S(2)}, u32[]{:S(2)}) %collective-permute-start.12) | collective-permute-done | bytes 131104 | tf_op jit(solution)/shard_map/ppermute | solution.py:432
  47.3 6.7 %shard_map.162 = (bf16[5,256,256]{2,1,0:T(8,128)(2,1)}, f32[4,256,256]{2,1,0:T(8,128)}, bf16[256,256]{1,0:T(8,128)(2,1)}) custom-call(bf16[512,128]{1,0:T(8,128)(2,1)} %bitcast.11, bf16[512,128]{1,0:T(8,128)(2,1)} %copy-done.2, bf16[512,128]{1,0:T(8,128)(2,1)} %copy-done.4, bf16[512,128]{1,0:T(8,128)(2,1)} %copy-done.6, bf16[512,128]{1,0:T(8,128)(2,1)} %copy-done.7, ...), custom_call_target="tpu_custom_call" | custom-call | flops 1073741824 | bytes 4194304 | tf_op jit(solution)/shard_map/pallas_call | solution.py:484
  54.8 6.9 %shard_map.163 = (bf16[5,256,256]{2,1,0:T(8,128)(2,1)}, bf16[8,128,256]{2,1,0:T(8,128)(2,1)}, bf16[128,256]{1,0:T(8,128)(2,1)}, bf16[128,256]{1,0:T(8,128)(2,1)}...) custom-call(bf16[512,128]{1,0:T(8,128)(2,1)} %bitcast.7, ...), custom_call_target="tpu_custom_call" | custom-call | flops 1073741824 | bytes 4194304 | tf_op jit(solution)/shard_map/pallas_call | solution.py:497
  62.3 5.2 %shard_map.164.refs_0_ = bf16[144,128]{1,0:T(8,128)(2,1)} custom-call(bf16[512,128]{1,0:T(8,128)(2,1)} %bitcast.12, bf16[512,128]{1,0:T(8,128)(2,1)} %copy-done.2, bf16[512,128]{1,0:T(8,128)(2,1)} %copy-done.4, bf16[512,128]{1,0:T(8,128)(2,1)} %copy-done.6, bf16[512,128]{1,0:T(8,128)(2,1)} %copy-done.7, bf16[512,128]{1,0:T(8,128)(2,1)} %copy-done.8, ...), custom_call_target="tpu_custom_call" | custom-call | flops 1073741824 | bytes 2097152 | tf_op jit(solution)/shard_map/pallas_call | solution.py:512
  67.5 2.5 %collective-permute-start.30 = (bf16[144,128]{1,0:T(8,128)(2,1)}, bf16[144,128]{1,0:T(8,128)(2,1)S(1)}, u32[]{:S(2)}, u32[]{:S(2)}) collective-permute-start(bf16[144,128]{1,0:T(8,128)(2,1)} %shard_map.164.refs_0_), channel_id=1, source_target_pairs={{0,24},{8,16},{16,8},{24,0},{1,25},{9,17},{17,9},{25,1},{2,26},{10... | collective-permute-start | bytes 110600 | tf_op jit(solution)/shard_map/ppermute | solution.py:422
  71.0 1.6 %collective-permute-done.30.refs_3_ = bf16[144,128]{1,0:T(8,128)(2,1)S(1)} collective-permute-done((bf16[144,128]{1,0:T(8,128)(2,1)}, bf16[144,128]{1,0:T(8,128)(2,1)S(1)}, u32[]{:S(2)}, u32[]{:S(2)}) %collective-permute-start.30) | collective-permute-done | bytes 36896 | tf_op jit(solution)/shard_map/ppermute | solution.py:422
  72.9 1.3 %collective-permute-done.29.refs_2_ = bf16[144,128]{1,0:T(8,128)(2,1)S(1)} collective-permute-done((bf16[144,128]{1,0:T(8,128)(2,1)}, bf16[144,128]{1,0:T(8,128)(2,1)S(1)}, u32[]{:S(2)}, u32[]{:S(2)}) %collective-permute-start.29) | collective-permute-done | bytes 36896 | tf_op jit(solution)/shard_map/ppermute | solution.py:422
  74.7 2.4 %collective-permute-start.25 = (bf16[128,256]{1,0:T(8,128)(2,1)}, bf16[128,256]{1,0:T(8,128)(2,1)S(1)}, u32[]{:S(2)}, u32[]{:S(2)}) collective-permute-start(bf16[128,256]{1,0:T(8,128)(2,1)} %get-tuple-element.90), channel_id=1, source_target_pairs={{0,5},{1,4},{2,7},{3,6},{4,1},{5,0},{6,3},{7,2},{8,13},{9,12},{10,... | collective-permute-start | bytes 196616 | tf_op jit(solution)/shard_map/ppermute | solution.py:422
  77.0 1.6 %collective-permute-start.26 = (bf16[128,256]{1,0:T(8,128)(2,1)}, bf16[128,256]{1,0:T(8,128)(2,1)S(1)}, u32[]{:S(2)}, u32[]{:S(2)}) collective-permute-start(bf16[128,256]{1,0:T(8,128)(2,1)} %get-tuple-element.91), channel_id=1, source_target_pairs={{0,6},{1,7},{2,4},{3,5},{4,2},{5,3},{6,0},{7,1},{8,14},{9,15},{10,... | collective-permute-start | bytes 196616 | tf_op jit(solution)/shard_map/ppermute | solution.py:422
  78.6 1.7 %collective-permute-start.27 = (bf16[128,256]{1,0:T(8,128)(2,1)}, bf16[128,256]{1,0:T(8,128)(2,1)S(1)}, u32[]{:S(2)}, u32[]{:S(2)}) collective-permute-start(bf16[128,256]{1,0:T(8,128)(2,1)} %get-tuple-element.92), channel_id=1, source_target_pairs={{0,7},{1,6},{2,5},{3,4},{4,3},{5,2},{6,1},{7,0},{8,15},{9,14},{10,... | collective-permute-start | bytes 196616 | tf_op jit(solution)/shard_map/ppermute | solution.py:422
  80.4 5.9 %collective-permute-done.25.refs_5_ = bf16[128,256]{1,0:T(8,128)(2,1)S(1)} collective-permute-done((bf16[128,256]{1,0:T(8,128)(2,1)}, bf16[128,256]{1,0:T(8,128)(2,1)S(1)}, u32[]{:S(2)}, u32[]{:S(2)}) %collective-permute-start.25) | collective-permute-done | bytes 65568 | tf_op jit(solution)/shard_map/ppermute | solution.py:422
  86.3 1.6 %shard_map.166 = (bf16[96,128]{1,0:T(8,128)(2,1)}, bf16[96,128]{1,0:T(8,128)(2,1)}, bf16[96,128]{1,0:T(8,128)(2,1)}, bf16[96,128]{1,0:T(8,128)(2,1)}, bf16[96,12...) custom-call(bf16[144,128]{1,0:T(8,128)(2,1)} %shard_map.164.refs_0_, ...), custom_call_target="tpu_custom_call" | custom-call | flops 73728 | bytes 196608 | tf_op jit(solution)/shard_map/pallas_call | solution.py:527
  88.0 3.4 %collective-permute-start.32 = (bf16[96,128]{1,0:T(8,128)(2,1)}, bf16[96,128]{1,0:T(8,128)(2,1)S(1)}, u32[]{:S(2)}, u32[]{:S(2)}) collective-permute-start(bf16[96,128]{1,0:T(8,128)(2,1)} %get-tuple-element.112), channel_id=1, source_target_pairs={{0,2},{1,3},{2,0},{3,1},{4,6},{5,7},{6,4},{7,5},{8,10},{9,11},{10,... | collective-permute-start | bytes 73736 | tf_op jit(solution)/shard_map/ppermute | solution.py:422
  91.4 1.8 %collective-permute-start.34 = (bf16[96,128]{1,0:T(8,128)(2,1)}, bf16[96,128]{1,0:T(8,128)(2,1)S(1)}, u32[]{:S(2)}, u32[]{:S(2)}) collective-permute-start(bf16[96,128]{1,0:T(8,128)(2,1)} %get-tuple-element.114), channel_id=1, source_target_pairs={{0,4},{1,5},{2,6},{3,7},{4,0},{5,1},{6,2},{7,3},{8,12},{9,13},{10,... | collective-permute-start | bytes 73736 | tf_op jit(solution)/shard_map/ppermute | solution.py:422
  93.8 1.7 %collective-permute-start.36 = (bf16[96,128]{1,0:T(8,128)(2,1)}, bf16[96,128]{1,0:T(8,128)(2,1)S(1)}, u32[]{:S(2)}, u32[]{:S(2)}) collective-permute-start(bf16[96,128]{1,0:T(8,128)(2,1)} %get-tuple-element.116), channel_id=1, source_target_pairs={{0,6},{1,7},{2,4},{3,5},{4,2},{5,3},{6,0},{7,1},{8,14},{9,15},{10,... | collective-permute-start | bytes 73736 | tf_op jit(solution)/shard_map/ppermute | solution.py:422
  95.5 2.1 %collective-permute-start.37 = (bf16[96,128]{1,0:T(8,128)(2,1)}, bf16[96,128]{1,0:T(8,128)(2,1)S(1)}, u32[]{:S(2)}, u32[]{:S(2)}) collective-permute-start(bf16[96,128]{1,0:T(8,128)(2,1)} %get-tuple-element.117), channel_id=1, source_target_pairs={{0,7},{1,6},{2,5},{3,4},{4,3},{5,2},{6,1},{7,0},{8,15},{9,14},{10,... | collective-permute-start | bytes 73736 | tf_op jit(solution)/shard_map/ppermute | solution.py:422
  97.6 2.2 %shard_map.165 = (bf16[1,512,128]{2,1,0:T(8,128)(2,1)}, bf16[1,512,128]{2,1,0:T(8,128)(2,1)}) custom-call(bf16[128,256]{1,0:T(8,128)(2,1)} %get-tuple-element.96.refs_0_, bf16[128,256]{1,0:T(8,128)(2,1)} %copy-done.16, bf16[128,256]{1,0:T(8,128)(2,1)} %copy-done.17, bf16[128,256]{1,0:T(8,128)(2,1)} %copy-done.18, bf16[128,256]{1,0:T(8,128)(2,1)} %copy-done.19, ...), custom_call_target="tpu_custom_call" | custom-call | flops 67108864 | bytes 786432 | tf_op jit(solution)/shard_map/pallas_call | solution.py:536
  99.9 0.9 collective-permute-done.37.refs_7_
  101.4 1.7 %shard_map.167 = (f32[128,384]{1,0:T(8,128)}, f32[128,128]{1,0:T(8,128)}, f32[3,384]{1,0:T(4,128)}, f32[1,128]{1,0:T(1,128)}, f32[1,128]{1,0:T(1,128)}, /*index=5*/f32[8,512]{1,0:T(8,128)}, f32[8,512]{1,0:T(8,128)}) custom-call(bf16[96,128]{1,0:T(8,128)(2,1)} %get-tuple-element.110.refs_0_, bf16[96,128]{1,0:T(8,128)(2,1)} %copy-done.26, ...), custom_call_target="tpu_custom_call" | custom-call | flops 98304 | bytes 196608 | tf_op jit(solution)/shard_map/pallas_call | solution.py:544
  (132 shorter events, 9.2 us)
Async XLA Ops:
  0.7 8.8 %collective-permute-start = (bf16[512,128]{1,0:T(8,128)(2,1)}, bf16[512,128]{1,0:T(8,128)(2,1)S(1)}, u32[]{:S(2)}, u32[]{:S(2)}) collective-permute-start(bf16[512,128]{1,0:T(8,128)(2,1)} %bitcast.10), channel_id=1, source_target_pairs={{0,2},{1,3},{2,4},{3,5},{4,6},{5,7},{6,0},{7,1},{8,10},{9,11},{10,... | collective-permute-start | bytes 393224 | tf_op jit(solution)/shard_map/ppermute | solution.py:432
  9.5 20.2 %collective-permute-start.2 = (bf16[512,128]{1,0:T(8,128)(2,1)}, bf16[512,128]{1,0:T(8,128)(2,1)S(1)}, u32[]{:S(2)}, u32[]{:S(2)}) collective-permute-start(bf16[512,128]{1,0:T(8,128)(2,1)} %bitcast.6), channel_id=1, source_target_pairs={{0,2},{1,3},{2,4},{3,5},{4,6},{5,7},{6,0},{7,1},{8,10},{9,11},{10,... | collective-permute-start | bytes 393224 | tf_op jit(solution)/shard_map/ppermute | solution.py:432
  9.5 20.2 %collective-permute-start.1 = (bf16[512,128]{1,0:T(8,128)(2,1)S(1)}, bf16[512,128]{1,0:T(8,128)(2,1)S(1)}, u32[]{:S(2)}, u32[]{:S(2)}) collective-permute-start(bf16[512,128]{1,0:T(8,128)(2,1)S(1)} %collective-permute-done.refs_1_), channel_id=1, source_target_pairs={{0,2},{1,3},{2,4},{3,5},{4,6},{5,7},{6,0},{7,1},{8,10},{9,11},{10,... | collective-permute-start | bytes 393224 | tf_op jit(solution)/shard_map/ppermute | solution.py:432
  13.8 5.4 %collective-permute-start.5 = (f32[8,128]{1,0:T(8,128)}, f32[8,128]{1,0:T(8,128)S(1)}, u32[]{:S(2)}, u32[]{:S(2)}) collective-permute-start(f32[8,128]{1,0:T(8,128)} %get-tuple-element.72), channel_id=1, source_target_pairs={{0,3},{1,2},{2,1},{3,0},{4,7},{5,6},{6,5},{7,4},{8,11},{9,10},{10,... | collective-permute-start | bytes 12296 | tf_op jit(solution)/shard_map/ppermute | solution.py:422
  14.0 6.0 %collective-permute-start.6 = (f32[8,128]{1,0:T(8,128)}, f32[8,128]{1,0:T(8,128)S(1)}, u32[]{:S(2)}, u32[]{:S(2)}) collective-permute-start(f32[8,128]{1,0:T(8,128)} %get-tuple-element.73), channel_id=1, source_target_pairs={{0,4},{1,5},{2,6},{3,7},{4,0},{5,1},{6,2},{7,3},{8,12},{9,13},{10,... | collective-permute-start | bytes 12296 | tf_op jit(solution)/shard_map/ppermute | solution.py:422
  17.1 5.8 %collective-permute-start.7 = (f32[8,128]{1,0:T(8,128)}, f32[8,128]{1,0:T(8,128)S(1)}, u32[]{:S(2)}, u32[]{:S(2)}) collective-permute-start(f32[8,128]{1,0:T(8,128)} %get-tuple-element.74), channel_id=1, source_target_pairs={{0,5},{1,4},{2,7},{3,6},{4,1},{5,0},{6,3},{7,2},{8,13},{9,12},{10,... | collective-permute-start | bytes 12296 | tf_op jit(solution)/shard_map/ppermute | solution.py:422
  19.2 5.6 %collective-permute-start.8 = (f32[8,128]{1,0:T(8,128)}, f32[8,128]{1,0:T(8,128)S(1)}, u32[]{:S(2)}, u32[]{:S(2)}) collective-permute-start(f32[8,128]{1,0:T(8,128)} %get-tuple-element.75), channel_id=1, source_target_pairs={{0,6},{1,7},{2,4},{3,5},{4,2},{5,3},{6,0},{7,1},{8,14},{9,15},{10,... | collective-permute-start | bytes 12296 | tf_op jit(solution)/shard_map/ppermute | solution.py:422
  29.7 8.2 %collective-permute-start.11 = (bf16[512,128]{1,0:T(8,128)(2,1)S(1)}, bf16[512,128]{1,0:T(8,128)(2,1)S(1)}, u32[]{:S(2)}, u32[]{:S(2)}) collective-permute-start(bf16[512,128]{1,0:T(8,128)(2,1)S(1)} %collective-permute-done.2.refs_1_.refs_9_), channel_id=1, source_target_pairs={{0,2},{1,3},{2,4},{3,5},{4,6},{5,7},{6,0},{7,1},{8,10},{9,11},{10,... | collective-permute-start | bytes 393224 | tf_op jit(solution)/shard_map/ppermute | solution.py:432
  29.7 10.1 %collective-permute-start.10 = (bf16[512,128]{1,0:T(8,128)(2,1)S(1)}, bf16[512,128]{1,0:T(8,128)(2,1)S(1)}, u32[]{:S(2)}, u32[]{:S(2)}) collective-permute-start(bf16[512,128]{1,0:T(8,128)(2,1)S(1)} %collective-permute-done.1.refs_2_), channel_id=1, source_target_pairs={{0,2},{1,3},{2,4},{3,5},{4,6},{5,7},{6,0},{7,1},{8,10},{9,11},{10,... | collective-permute-start | bytes 393224 | tf_op jit(solution)/shard_map/ppermute | solution.py:432
  30.3 9.6 %collective-permute-start.17 = (bf16[512,128]{1,0:T(8,128)(2,1)S(1)}, bf16[512,128]{1,0:T(8,128)(2,1)S(1)}, u32[]{:S(2)}, u32[]{:S(2)}) collective-permute-start(bf16[512,128]{1,0:T(8,128)(2,1)S(1)} %bitcast.13), channel_id=1, source_target_pairs={{0,1},{1,0},{2,3},{3,2},{4,5},{5,4},{6,7},{7,6},{8,9},{9,8},{10,11... | collective-permute-start | bytes 393224 | tf_op jit(solution)/shard_map/ppermute | solution.py:427
  30.3 10.1 %collective-permute-start.18 = (bf16[512,128]{1,0:T(8,128)(2,1)S(1)}, bf16[512,128]{1,0:T(8,128)(2,1)S(1)}, u32[]{:S(2)}, u32[]{:S(2)}) collective-permute-start(bf16[512,128]{1,0:T(8,128)(2,1)S(1)} %collective-permute-done.refs_1_), channel_id=1, source_target_pairs={{0,1},{1,0},{2,3},{3,2},{4,5},{5,4},{6,7},{7,6},{8,9},{9,8},{10,11... | collective-permute-start | bytes 393224 | tf_op jit(solution)/shard_map/ppermute | solution.py:427
  30.8 9.7 %collective-permute-start.19 = (bf16[512,128]{1,0:T(8,128)(2,1)S(1)}, bf16[512,128]{1,0:T(8,128)(2,1)S(1)}, u32[]{:S(2)}, u32[]{:S(2)}) collective-permute-start(bf16[512,128]{1,0:T(8,128)(2,1)S(1)} %collective-permute-done.1.refs_2_), channel_id=1, source_target_pairs={{0,1},{1,0},{2,3},{3,2},{4,5},{5,4},{6,7},{7,6},{8,9},{9,8},{10,11... | collective-permute-start | bytes 393224 | tf_op jit(solution)/shard_map/ppermute | solution.py:427
  39.8 6.8 %collective-permute-start.12 = (bf16[512,128]{1,0:T(8,128)(2,1)S(1)}, bf16[512,128]{1,0:T(8,128)(2,1)S(1)}, u32[]{:S(2)}, u32[]{:S(2)}) collective-permute-start(bf16[512,128]{1,0:T(8,128)(2,1)S(1)} %collective-permute-done.11.refs_2_.refs_10_), channel_id=1, source_target_pairs={{0,2},{1,3},{2,4},{3,5},{4,6},{5,7},{6,0},{7,1},{8,10},{9,11},{10,... | collective-permute-start | bytes 393224 | tf_op jit(solution)/shard_map/ppermute | solution.py:432
  39.8 6.8 %collective-permute-start.20 = (bf16[512,128]{1,0:T(8,128)(2,1)S(1)}, bf16[512,128]{1,0:T(8,128)(2,1)S(1)}, u32[]{:S(2)}, u32[]{:S(2)}) collective-permute-start(bf16[512,128]{1,0:T(8,128)(2,1)S(1)} %collective-permute-done.10.refs_3_), channel_id=1, source_target_pairs={{0,1},{1,0},{2,3},{3,2},{4,5},{5,4},{6,7},{7,6},{8,9},{9,8},{10,11... | collective-permute-start | bytes 393224 | tf_op jit(solution)/shard_map/ppermute | solution.py:427
  39.9 14.2 %collective-permute-start.13 = (bf16[512,128]{1,0:T(8,128)(2,1)S(1)}, bf16[512,128]{1,0:T(8,128)(2,1)S(1)}, u32[]{:S(2)}, u32[]{:S(2)}) collective-permute-start(bf16[512,128]{1,0:T(8,128)(2,1)S(1)} %bitcast.9), channel_id=1, source_target_pairs={{0,1},{1,0},{2,3},{3,2},{4,5},{5,4},{6,7},{7,6},{8,9},{9,8},{10,11... | collective-permute-start | bytes 393224 | tf_op jit(solution)/shard_map/ppermute | solution.py:427
  40.4 13.6 %collective-permute-start.14 = (bf16[512,128]{1,0:T(8,128)(2,1)S(1)}, bf16[512,128]{1,0:T(8,128)(2,1)S(1)}, u32[]{:S(2)}, u32[]{:S(2)}) collective-permute-start(bf16[512,128]{1,0:T(8,128)(2,1)S(1)} %collective-permute-done.2.refs_1_.refs_9_), channel_id=1, source_target_pairs={{0,1},{1,0},{2,3},{3,2},{4,5},{5,4},{6,7},{7,6},{8,9},{9,8},{10,11... | collective-permute-start | bytes 393224 | tf_op jit(solution)/shard_map/ppermute | solution.py:427
  40.5 13.5 %collective-permute-start.15 = (bf16[512,128]{1,0:T(8,128)(2,1)S(1)}, bf16[512,128]{1,0:T(8,128)(2,1)S(1)}, u32[]{:S(2)}, u32[]{:S(2)}) collective-permute-start(bf16[512,128]{1,0:T(8,128)(2,1)S(1)} %collective-permute-done.11.refs_2_.refs_10_), channel_id=1, source_target_pairs={{0,1},{1,0},{2,3},{3,2},{4,5},{5,4},{6,7},{7,6},{8,9},{9,8},{10,11... | collective-permute-start | bytes 393224 | tf_op jit(solution)/shard_map/ppermute | solution.py:427
  46.6 7.5 %collective-permute-start.16 = (bf16[512,128]{1,0:T(8,128)(2,1)S(1)}, bf16[512,128]{1,0:T(8,128)(2,1)S(1)}, u32[]{:S(2)}, u32[]{:S(2)}) collective-permute-start(bf16[512,128]{1,0:T(8,128)(2,1)S(1)} %collective-permute-done.12.refs_3_.refs_11_), channel_id=1, source_target_pairs={{0,1},{1,0},{2,3},{3,2},{4,5},{5,4},{6,7},{7,6},{8,9},{9,8},{10,11... | collective-permute-start | bytes 393224 | tf_op jit(solution)/shard_map/ppermute | solution.py:427
  61.8 15.3 %collective-permute-start.21 = (bf16[128,256]{1,0:T(8,128)(2,1)}, bf16[128,256]{1,0:T(8,128)(2,1)S(1)}, u32[]{:S(2)}, u32[]{:S(2)}) collective-permute-start(bf16[128,256]{1,0:T(8,128)(2,1)} %get-tuple-element.86), channel_id=1, source_target_pairs={{0,1},{1,0},{2,3},{3,2},{4,5},{5,4},{6,7},{7,6},{8,9},{9,8},{10,11... | collective-permute-start | bytes 196616 | tf_op jit(solution)/shard_map/ppermute | solution.py:422
  62.3 16.4 %collective-permute-start.22 = (bf16[128,256]{1,0:T(8,128)(2,1)}, bf16[128,256]{1,0:T(8,128)(2,1)S(1)}, u32[]{:S(2)}, u32[]{:S(2)}) collective-permute-start(bf16[128,256]{1,0:T(8,128)(2,1)} %get-tuple-element.87), channel_id=1, source_target_pairs={{0,2},{1,3},{2,0},{3,1},{4,6},{5,7},{6,4},{7,5},{8,10},{9,11},{10,... | collective-permute-start | bytes 196616 | tf_op jit(solution)/shard_map/ppermute | solution.py:422
  72.6 7.8 %collective-permute-start.23 = (bf16[128,256]{1,0:T(8,128)(2,1)}, bf16[128,256]{1,0:T(8,128)(2,1)S(1)}, u32[]{:S(2)}, u32[]{:S(2)}) collective-permute-start(bf16[128,256]{1,0:T(8,128)(2,1)} %get-tuple-element.88), channel_id=1, source_target_pairs={{0,3},{1,2},{2,1},{3,0},{4,7},{5,6},{6,5},{7,4},{8,11},{9,10},{10,... | collective-permute-start | bytes 196616 | tf_op jit(solution)/shard_map/ppermute | solution.py:422
  74.2 6.2 %collective-permute-start.24 = (bf16[128,256]{1,0:T(8,128)(2,1)}, bf16[128,256]{1,0:T(8,128)(2,1)S(1)}, u32[]{:S(2)}, u32[]{:S(2)}) collective-permute-start(bf16[128,256]{1,0:T(8,128)(2,1)} %get-tuple-element.89), channel_id=1, source_target_pairs={{0,4},{1,5},{2,6},{3,7},{4,0},{5,1},{6,2},{7,3},{8,12},{9,13},{10,... | collective-permute-start | bytes 196616 | tf_op jit(solution)/shard_map/ppermute | solution.py:422
  74.7 11.6 %collective-permute-start.25 = (bf16[128,256]{1,0:T(8,128)(2,1)}, bf16[128,256]{1,0:T(8,128)(2,1)S(1)}, u32[]{:S(2)}, u32[]{:S(2)}) collective-permute-start(bf16[128,256]{1,0:T(8,128)(2,1)} %get-tuple-element.90), channel_id=1, source_target_pairs={{0,5},{1,4},{2,7},{3,6},{4,1},{5,0},{6,3},{7,2},{8,13},{9,12},{10,... | collective-permute-start | bytes 196616 | tf_op jit(solution)/shard_map/ppermute | solution.py:422
  77.0 9.2 %collective-permute-start.26 = (bf16[128,256]{1,0:T(8,128)(2,1)}, bf16[128,256]{1,0:T(8,128)(2,1)S(1)}, u32[]{:S(2)}, u32[]{:S(2)}) collective-permute-start(bf16[128,256]{1,0:T(8,128)(2,1)} %get-tuple-element.91), channel_id=1, source_target_pairs={{0,6},{1,7},{2,4},{3,5},{4,2},{5,3},{6,0},{7,1},{8,14},{9,15},{10,... | collective-permute-start | bytes 196616 | tf_op jit(solution)/shard_map/ppermute | solution.py:422
  78.6 7.6 %collective-permute-start.27 = (bf16[128,256]{1,0:T(8,128)(2,1)}, bf16[128,256]{1,0:T(8,128)(2,1)S(1)}, u32[]{:S(2)}, u32[]{:S(2)}) collective-permute-start(bf16[128,256]{1,0:T(8,128)(2,1)} %get-tuple-element.92), channel_id=1, source_target_pairs={{0,7},{1,6},{2,5},{3,4},{4,3},{5,2},{6,1},{7,0},{8,15},{9,14},{10,... | collective-permute-start | bytes 196616 | tf_op jit(solution)/shard_map/ppermute | solution.py:422
  87.9 5.9 %collective-permute-start.31 = (bf16[96,128]{1,0:T(8,128)(2,1)}, bf16[96,128]{1,0:T(8,128)(2,1)S(1)}, u32[]{:S(2)}, u32[]{:S(2)}) collective-permute-start(bf16[96,128]{1,0:T(8,128)(2,1)} %get-tuple-element.111), channel_id=1, source_target_pairs={{0,1},{1,0},{2,3},{3,2},{4,5},{5,4},{6,7},{7,6},{8,9},{9,8},{10,11... | collective-permute-start | bytes 73736 | tf_op jit(solution)/shard_map/ppermute | solution.py:422
  88.0 7.5 %collective-permute-start.32 = (bf16[96,128]{1,0:T(8,128)(2,1)}, bf16[96,128]{1,0:T(8,128)(2,1)S(1)}, u32[]{:S(2)}, u32[]{:S(2)}) collective-permute-start(bf16[96,128]{1,0:T(8,128)(2,1)} %get-tuple-element.112), channel_id=1, source_target_pairs={{0,2},{1,3},{2,0},{3,1},{4,6},{5,7},{6,4},{7,5},{8,10},{9,11},{10,... | collective-permute-start | bytes 73736 | tf_op jit(solution)/shard_map/ppermute | solution.py:422
  91.4 8.5 %collective-permute-start.33 = (bf16[96,128]{1,0:T(8,128)(2,1)}, bf16[96,128]{1,0:T(8,128)(2,1)S(1)}, u32[]{:S(2)}, u32[]{:S(2)}) collective-permute-start(bf16[96,128]{1,0:T(8,128)(2,1)} %get-tuple-element.113), channel_id=1, source_target_pairs={{0,3},{1,2},{2,1},{3,0},{4,7},{5,6},{6,5},{7,4},{8,11},{9,10},{10,... | collective-permute-start | bytes 73736 | tf_op jit(solution)/shard_map/ppermute | solution.py:422
  91.4 8.5 %collective-permute-start.34 = (bf16[96,128]{1,0:T(8,128)(2,1)}, bf16[96,128]{1,0:T(8,128)(2,1)S(1)}, u32[]{:S(2)}, u32[]{:S(2)}) collective-permute-start(bf16[96,128]{1,0:T(8,128)(2,1)} %get-tuple-element.114), channel_id=1, source_target_pairs={{0,4},{1,5},{2,6},{3,7},{4,0},{5,1},{6,2},{7,3},{8,12},{9,13},{10,... | collective-permute-start | bytes 73736 | tf_op jit(solution)/shard_map/ppermute | solution.py:422
  93.2 6.7 %collective-permute-start.35 = (bf16[96,128]{1,0:T(8,128)(2,1)}, bf16[96,128]{1,0:T(8,128)(2,1)S(1)}, u32[]{:S(2)}, u32[]{:S(2)}) collective-permute-start(bf16[96,128]{1,0:T(8,128)(2,1)} %get-tuple-element.115), channel_id=1, source_target_pairs={{0,5},{1,4},{2,7},{3,6},{4,1},{5,0},{6,3},{7,2},{8,13},{9,12},{10,... | collective-permute-start | bytes 73736 | tf_op jit(solution)/shard_map/ppermute | solution.py:422
  93.8 6.1 %collective-permute-start.36 = (bf16[96,128]{1,0:T(8,128)(2,1)}, bf16[96,128]{1,0:T(8,128)(2,1)S(1)}, u32[]{:S(2)}, u32[]{:S(2)}) collective-permute-start(bf16[96,128]{1,0:T(8,128)(2,1)} %get-tuple-element.116), channel_id=1, source_target_pairs={{0,6},{1,7},{2,4},{3,5},{4,2},{5,3},{6,0},{7,1},{8,14},{9,15},{10,... | collective-permute-start | bytes 73736 | tf_op jit(solution)/shard_map/ppermute | solution.py:422
  95.5 5.3 %collective-permute-start.37 = (bf16[96,128]{1,0:T(8,128)(2,1)}, bf16[96,128]{1,0:T(8,128)(2,1)S(1)}, u32[]{:S(2)}, u32[]{:S(2)}) collective-permute-start(bf16[96,128]{1,0:T(8,128)(2,1)} %get-tuple-element.117), channel_id=1, source_target_pairs={{0,7},{1,6},{2,5},{3,4},{4,3},{5,2},{6,1},{7,0},{8,15},{9,14},{10,... | collective-permute-start | bytes 73736 | tf_op jit(solution)/shard_map/ppermute | solution.py:422
  (46 other events, 421.4 us)

commit v5 on v2

--- a/solution.py
+++ b/solution.py
@@ -238,8 +238,6 @@
     group = rows // blocks
     received = 4 * rows // sources
     half = W // 2
-    u = lax.rem(lax.axis_index("seq"), units)
-    mine = own_lanes(u, group, width)
     lines = length // width
 
     pad_ref[rows : 2 * rows, :] = jnp.zeros((rows, W), BF16)
@@ -269,47 +267,42 @@
             at = m * lines + q
             out_ref[at : at + 1, :] = line[:, q * width : (q + 1) * width]
 
-    def spread(products):
+    lane = lax.broadcasted_iota(jnp.int32, (group, width), 1)
+    channel = lax.broadcasted_iota(jnp.int32, (group, width), 0)
+    small = [jnp.zeros((1, width), F32)] * 16
+
+    def put(n, products):
         by_channel = jnp.sum(products.reshape(blocks, group, W), axis=0)
         col = jnp.sum(by_channel, axis=1, keepdims=True)
-        return jnp.sum(jnp.where(mine, col, 0.0), axis=0, keepdims=True)
-
-    small = []
+        mine = lane == n % units * group + channel
+        small[n // units] += jnp.sum(jnp.where(mine, col, 0.0), axis=0, keepdims=True)
+
     for j in range(3):
         for kind in range(3):
             field = pick(fields_ref, kind, received)
-            small.append(spread(kept_ref[4 + kind].astype(F32) * earlier(field, j, group)))
+            put(3 * j + kind, kept_ref[4 + kind].astype(F32) * earlier(field, j, group))
     for m in range(2):
-        small.append(spread(kept_ref[2 + m].astype(F32) * kept_ref[m].astype(F32)))
-    out_ref[2 * lines : 2 * lines + 16, :] = jnp.concatenate(
-        small + [jnp.zeros((16 - len(small), width), F32)], axis=0
-    )
-
-
-def output_kernel(
-    units, in_ref, w_in_ref, w_out_ref, series_ref, cot_ref, own_ref, out_ref, d_series_ref, part_ref
-):
-    count, block, width = out_ref.shape
+        put(9 + m, kept_ref[2 + m].astype(F32) * kept_ref[m].astype(F32))
+    out_ref[2 * lines : 2 * lines + 16, :] = jnp.concatenate(small, axis=0)
+
+
+def received_field(in_ref, units, group, parts, e, kind, part):
+    at = (kind * parts + part) * group
+    return in_ref[e * units : (e + 1) * units, at : at + group, :].reshape(units * group, W)
+
+
+def partial_kernel(units, in_ref, series_ref, cot_ref, own_ref, part_ref):
+    count, block, width = series_ref.shape
     group = width // units
     parts = block // W
-    w_in = w_in_ref[...]
-    w_out_t = w_out_ref[...].T
-
-    def field(e, kind, part):
-        at = (kind * parts + part) * group
-        return in_ref[e * units : (e + 1) * units, at : at + group, :].reshape(width, W)
-
     w_in_part = 0.0
     w_out_part = 0.0
     for e in range(count):
         for part in range(parts):
             rows = pl.ds(part * W, W)
-            product = field(e, 3, part)
-            out_ref[e, rows, :] = dot(w_out_t, product).T.astype(BF16)
-            grads = jnp.concatenate([field(e, kind, part) for kind in range(3)], axis=0)
-            d_series_ref[e, rows, :] = dot(w_in, grads).T.astype(BF16)
-            w_in_part += dot(grads, series_ref[e, rows, :])
-            w_out_part += dot(product, cot_ref[e, rows, :])
+            field = [received_field(in_ref, units, group, parts, e, k, part) for k in range(4)]
+            w_in_part += dot(jnp.concatenate(field[:3], axis=0), series_ref[e, rows, :])
+            w_out_part += dot(field[3], cot_ref[e, rows, :])
 
     weights = jnp.concatenate([w_in_part, w_out_part], axis=0)
     targets, sent, _ = part_ref.shape
@@ -317,61 +310,91 @@
     sources = in_ref.shape[0]
     lines = (own_ref.shape[0] - 16) // 2
     slots = lines // sources
-    spare = jnp.zeros((sent - each - 2 * slots - 1, width), F32)
+    small = -(-11 // units)
+    spare = jnp.zeros((sent - each - 2 * slots - small, width), F32)
     for g in range(targets):
         s = g % sources
-        small = 2 * lines + g * 16 // targets
         part_ref[g] = jnp.concatenate(
             [
                 weights[g * each : (g + 1) * each],
                 own_ref[s * slots : (s + 1) * slots, :],
                 own_ref[lines + s * slots : lines + (s + 1) * slots, :],
-                own_ref[small : small + 1, :],
+                own_ref[2 * lines : 2 * lines + small, :],
                 spare,
             ],
             axis=0,
         ).astype(BF16)
 
 
-def sum_kernel(units, each, scale, in_ref, out_ref, one_ref, two_ref):
+def output_kernel(units, in_ref, w_in_ref, w_out_ref, out_ref, d_series_ref):
+    count, block, width = out_ref.shape
+    group = width // units
+    parts = block // W
+    w_in = w_in_ref[...]
+    w_out_t = w_out_ref[...].T
+    for e in range(count):
+        for part in range(parts):
+            rows = pl.ds(part * W, W)
+            field = [received_field(in_ref, units, group, parts, e, k, part) for k in range(4)]
+            out_ref[e, rows, :] = dot(w_out_t, field[3]).T.astype(BF16)
+            grads = jnp.concatenate(field[:3], axis=0)
+            d_series_ref[e, rows, :] = dot(w_in, grads).T.astype(BF16)
+
+
+def sum_kernel(in_ref, out_ref):
+    targets, each, _ = out_ref.shape
+    total = in_ref[0, 0:each, :].astype(F32)
+    for g in range(1, targets):
+        total = total + in_ref[g, 0:each, :].astype(F32)
+    total = total.astype(BF16)
+    for g in range(targets):
+        out_ref[g] = total
+
+
+def small_kernel(units, each, scale, in_ref, one_ref, two_ref, taps_ref, skip_one_ref, skip_two_ref):
     targets, _, width = in_ref.shape
     filters, block = one_ref.shape
     slots = block // width
-    total = in_ref[0].astype(F32)
-    for g in range(1, targets):
-        total = total + in_ref[g].astype(F32)
-    weights = total[:each]
-    small = total[each + 2 * slots : each + 2 * slots + 1]
-    spare = jnp.zeros((out_ref.shape[1] - each - 1, width), F32)
-    total = jnp.concatenate([weights, small, spare], axis=0).astype(BF16)
-    for g in range(targets):
-        out_ref[g] = total
+    group = width // units
+    by_unit = []
+    for u in range(units):
+        sums = 0.0
+        for g in range(u, targets, units):
+            sums += in_ref[g, each:, :].astype(F32)
+        by_unit.append(sums * scale)
     repeat = units // filters
-    for row in range(filters):
-        sums = 0.0
-        for g in range(targets):
-            if g % units // repeat == row:
-                sums += in_ref[g, each : each + 2 * slots, :].astype(F32)
+    for f in range(filters):
+        sums = by_unit[f * repeat]
+        for u in range(f * repeat + 1, (f + 1) * repeat):
+            sums = sums + by_unit[u]
         for q in range(slots):
-            one_ref[row : row + 1, q * width : (q + 1) * width] = sums[q : q + 1] * scale
-            two_ref[row : row + 1, q * width : (q + 1) * width] = sums[slots + q : slots + q + 1] * scale
-
-
-def weight_kernel(each, scale, in_ref, w_in_ref, w_out_ref, taps_ref, skip_one_ref, skip_two_ref):
-    targets, _, width = in_ref.shape
-    weights = jnp.concatenate([in_ref[g, 0:each, :].astype(F32) for g in range(targets)], axis=0) * scale
+            one_ref[f : f + 1, q * width : (q + 1) * width] = sums[q : q + 1]
+            two_ref[f : f + 1, q * width : (q + 1) * width] = sums[slots + q : slots + q + 1]
+
+    row = lax.broadcasted_iota(jnp.int32, (units, width), 0)
+    lane = lax.broadcasted_iota(jnp.int32, (units, width), 1)
+    small = []
+    for r in range(-(-11 // units)):
+        held = jnp.concatenate([sums[2 * slots + r : 2 * slots + r + 1] for sums in by_unit], axis=0)
+        turned = 0.0
+        for shift in range(units):
+            moved = pltpu.roll(held, shift * group, 1) if shift else held
+            moved = jnp.where(lane // group == row, moved, 0.0)
+            turned += pltpu.roll(moved, units - shift, 0) if shift else moved
+        small += [turned[n : n + 1] for n in range(units)]
+    for j in range(3):
+        for kind in range(3):
+            taps_ref[j : j + 1, kind * width : (kind + 1) * width] = small[3 * j + kind]
+    skip_one_ref[...] = small[9]
+    skip_two_ref[...] = small[10]
+
+
+def weight_kernel(scale, in_ref, w_in_ref, w_out_ref):
+    targets, each, width = in_ref.shape
+    weights = jnp.concatenate([in_ref[g].astype(F32) for g in range(targets)], axis=0) * scale
     for kind in range(3):
         w_in_ref[:, kind * width : (kind + 1) * width] = weights[kind * width : (kind + 1) * width].T
     w_out_ref[...] = weights[3 * width :]
-
-    def small(n):
-        return in_ref[n * targets // 16, each : each + 1, :].astype(F32) * scale
-
-    for j in range(3):
-        for kind in range(3):
-            taps_ref[j : j + 1, kind * width : (kind + 1) * width] = small(3 * j + kind)
-    skip_one_ref[...] = small(9)
-    skip_two_ref[...] = small(10)
 
 
 def all_to_all(blocks, axis):
@@ -425,42 +448,47 @@
     )(fields, kept)
 
     each = 4 * width // devices
-    sent_rows = -(-(each + 2 * (block // width) + 1) // 16) * 16
-    output, d_series, partial = call(
+    sent_rows = -(-(each + 2 * (block // width) + -(-11 // units)) // 16) * 16
+    partial = call(
+        functools.partial(partial_kernel, units),
+        shape((devices, sent_rows, width), BF16),
+        flops=2 * count * block * width * 4 * width,
+        moved=2 * count * block * width * 6,
+    )(back, series, cotangent, own)
+    partial = all_to_all(partial, ("dp", "seq"))
+
+    output, d_series = call(
         functools.partial(output_kernel, units),
+        (shape(series.shape, BF16), shape(series.shape, BF16)),
+        flops=2 * count * block * width * 4 * width,
+        moved=2 * count * block * width * 6,
+    )(back, w_in, w_out)
+
+    sums = call(
+        sum_kernel,
+        shape((devices, each, width), BF16),
+        flops=devices * each * width,
+        moved=4 * devices * each * width,
+    )(partial)
+    sums = all_to_all(sums, ("dp", "seq"))
+
+    grad_one, grad_two, grad_taps, grad_skip_one, grad_skip_two = call(
+        functools.partial(small_kernel, units, each, scale),
         (
-            shape(series.shape, BF16),
-            shape(series.shape, BF16),
-            shape((devices, sent_rows, width), BF16),
-        ),
-        flops=2 * count * block * width * 8 * width,
-        moved=2 * count * block * width * 6,
-    )(back, w_in, w_out, series, cotangent, own)
-    partial = all_to_all(partial, ("dp", "seq"))
-
-    sums, grad_one, grad_two = call(
-        functools.partial(sum_kernel, units, each, scale),
-        (
-            shape((devices, -(-(each + 1) // 16) * 16, width), BF16),
             shape(filter_one.shape, F32),
             shape(filter_two.shape, F32),
-        ),
-        flops=devices * sent_rows * width,
-        moved=4 * devices * sent_rows * width,
-    )(partial)
-    sums = all_to_all(sums, ("dp", "seq"))
-
-    grad_w_in, grad_w_out, grad_taps, grad_skip_one, grad_skip_two = call(
-        functools.partial(weight_kernel, each, scale),
-        (
-            shape(w_in.shape, F32),
-            shape(w_out.shape, F32),
             shape(taps.shape, F32),
             shape((1, width), F32),
             shape((1, width), F32),
         ),
         flops=devices * sent_rows * width,
-        moved=2 * devices * sent_rows * width,
+        moved=4 * devices * sent_rows * width,
+    )(partial)
+    grad_w_in, grad_w_out = call(
+        functools.partial(weight_kernel, scale),
+        (shape(w_in.shape, F32), shape(w_out.shape, F32)),
+        flops=devices * each * width,
+        moved=2 * devices * each * width,
     )(sums)
     return (
         output,

time: 87.2 us -> 84.6 us (0.970)
  blocking collectives: 50.8 us -> 37.2 us
  waiting for transfers between devices: 10.8 us -> 15.1 us
  Pallas kernels: 20.1 us -> 23.6 us
  starting transfers between devices: 3.49 us -> 6.07 us
    all_to_all x3 -> x2, blocking collectives: 50.8 us -> 37.2 us  [all_to_all(): return lax.all_to_all(blocks, axis, split_axis=0, concat_axis=0, tiled=True)]
    all_to_all x1 -> x2, waiting for transfers between devices: 10.8 us -> 15.1 us  [all_to_all(): return lax.all_to_all(blocks, axis, split_axis=0, concat_axis=0, tiled=True)]
    pallas_call x2 -> x4, Pallas kernels: 3.48 us -> 7.16 us  [the longest x1 2.13 us: shards(): call(functools.partial(partial_kernel, units), shape((devices, sent_rows,...]
    all_to_all x1 -> x2, starting transfers between devices: 3.49 us -> 6.07 us  [all_to_all(): return lax.all_to_all(blocks, axis, split_axis=0, concat_axis=0, tiled=True)]
  transfers between devices with their start and end apart: 1 -> 2, of which waited for: 1 -> 2; matrix products, arithmetic and copies ran while one was open for 0% -> 0% of each run, Pallas kernels for 5% -> 10%
where the time goes in v5:
time: 84.6 us; the launch traced here: 84 us
  blocking collectives  37.2 us (44%)
  Pallas kernels  23.6 us (28%)
  waiting for transfers between devices  15.1 us (18%)
  starting transfers between devices  6.07 us (7%)
  local copies, waits for them, and re-layouts  1.44 us (2%)
    all_to_all x2, blocking collectives, all_to_all(): return lax.all_to_all(blocks, axis, split_axis=0, concat_axis=0, tiled=True)  37.2 us
    all_to_all x2, waiting for transfers between devices, all_to_all(): return lax.all_to_all(blocks, axis, split_axis=0, concat_axis=0, tiled=True)  15.1 us
    pallas_call x1, Pallas kernels, shards(): call(functools.partial(operator_kernel, units), (shape((sources, packed,...  7.55 us
    all_to_all x2, starting transfers between devices, all_to_all(): return lax.all_to_all(blocks, axis, split_axis=0, concat_axis=0, tiled=True)  6.07 us
    pallas_call x1, Pallas kernels, shards(): call(functools.partial(gradient_kernel, units), shape((2 * (length // wid...  4.52 us
    pallas_call x1, Pallas kernels, shards(): call(functools.partial(project_kernel, units), shape((sources, packed + 1...  2.18 us
    pallas_call x1, Pallas kernels, shards(): call(functools.partial(output_kernel, units), (shape(series.shape, BF16),...  2.15 us
    pallas_call x1, Pallas kernels, shards(): call(functools.partial(partial_kernel, units), shape((devices, sent_rows,...  2.13 us
  transfers between devices with their start and end apart: 2, of which 2 were waited for; matrix products, arithmetic and copies ran while one was open for 0% of the time, Pallas kernels for 10%

profile of v5, /device:TPU:0, one launch (start us, length us, event | category | flops | bytes accessed | tf_op | source)
XLA Modules:
  0.0 84.0 jit_solution(17252834355576618582)
XLA Ops:
  0.6 2.2 %shard_map.160 = bf16[8,144,256]{2,1,0:T(8,128)(2,1)} custom-call(bf16[1,512,128]{2,1,0:T(8,128)(2,1)} %series_ref.3, bf16[1,512,128]{2,1,0:T(8,128)(2,1)} %cot_ref.3, bf16[128,384]{1,0:T(8,128)(2,1)} %w_in_ref.3, bf16[128,128]{1,0:T(8,128)(2,1)} %w_out_ref.3, f32[8,512]{1,0:T(8,128)} %one_ref.1, f32[8,512]{1,0:T(8,128)} %two_ref.1), custom_call_target="tpu_custom_call" | custom-call | flops 67108864 | bytes 2097152 | tf_op jit(solution)/shard_map/pallas_call | solution.py:420
  2.8 23.2 %all_to_all.20.fields_ref = bf16[8,144,256]{2,1,0:T(8,128)(2,1)} all-to-all(bf16[8,144,256]{2,1,0:T(8,128)(2,1)} %shard_map.160), channel_id=1, replica_groups=mesh['dp'=4,'seq'=8] {'seq'}, dimensions={0} | all-to-all | bytes 1179648 | tf_op jit(solution)/shard_map/all_to_all | solution.py:401
  26.0 7.6 %shard_map.161 = (bf16[8,128,256]{2,1,0:T(8,128)(2,1)}, bf16[7,256,256]{2,1,0:T(8,128)(2,1)}) custom-call(bf16[8,144,256]{2,1,0:T(8,128)(2,1)} %all_to_all.20.fields_ref, f32[3,384]{1,0:T(4,128)} %taps_ref.1, f32[1,128]{1,0:T(1,128)} %bitcast.4, f32[1,128]{1,0:T(1,128)} %bitcast.5), custom_call_target="tpu_custom_call" | custom-call | flops 2147483648 | bytes 8388608 | tf_op jit(solution)/shard_map/pallas_call | solution.py:428
  33.6 3.5 %all-to-all-start.1 = ((bf16[8,128,256]{2,1,0:T(8,128)(2,1)}), bf16[8,128,256]{2,1,0:T(8,128)(2,1)S(1)}, u32[]{:S(2)}, u32[]{:S(2)}) async-start(bf16[8,128,256]{2,1,0:T(8,128)(2,1)} %get-tuple-element.20), calls=%async_computation.1 | async-start | bytes 1048576 | tf_op jit(solution)/shard_map/all_to_all | solution.py:401
  37.1 4.5 %shard_map.163.own_ref = f32[80,128]{1,0:T(8,128)} custom-call(bf16[8,144,256]{2,1,0:T(8,128)(2,1)} %all_to_all.20.fields_ref, bf16[7,256,256]{2,1,0:T(8,128)(2,1)} %get-tuple-element.23.kept_ref), custom_call_target="tpu_custom_call" | custom-call | flops 1073741824 | bytes 2097152 | tf_op jit(solution)/shard_map/pallas_call | solution.py:442
  41.6 10.8 %all-to-all-done.1.in_ref = bf16[8,128,256]{2,1,0:T(8,128)(2,1)S(1)} async-done(((bf16[8,128,256]{2,1,0:T(8,128)(2,1)}), bf16[8,128,256]{2,1,0:T(8,128)(2,1)S(1)}, u32[]{:S(2)}, u32[]{:S(2)}) %all-to-all-start.1) | async-done | bytes 524320 | tf_op jit(solution)/shard_map/all_to_all | solution.py:401
  52.3 0.0 copy-start
  52.3 0.8 copy-done
  53.1 2.1 %shard_map.164 = bf16[32,32,128]{2,1,0:T(8,128)(2,1)} custom-call(bf16[8,128,256]{2,1,0:T(8,128)(2,1)} %copy-done, bf16[1,512,128]{2,1,0:T(8,128)(2,1)} %series_ref.3, bf16[1,512,128]{2,1,0:T(8,128)(2,1)} %cot_ref.3, f32[80,128]{1,0:T(8,128)} %shard_map.163.own_ref), custom_call_target="tpu_custom_call" | custom-call | flops 67108864 | bytes 786432 | tf_op jit(solution)/shard_map/pallas_call | solution.py:452
  55.3 14.0 %all_to_all.21.in_ref = bf16[32,32,128]{2,1,0:T(8,128)(2,1)} all-to-all(bf16[32,32,128]{2,1,0:T(8,128)(2,1)} %shard_map.164), channel_id=1, replica_groups=mesh['dp'=4,'seq'=8] {'dp','seq'}, dimensions={0} | all-to-all | bytes 524288 | tf_op jit(solution)/shard_map/all_to_all | solution.py:401
  69.3 1.6 %shard_map.165 = bf16[32,16,128]{2,1,0:T(8,128)(2,1)} custom-call(bf16[32,32,128]{2,1,0:T(8,128)(2,1)} %all_to_all.21.in_ref), custom_call_target="tpu_custom_call" | custom-call | flops 65536 | bytes 262144 | tf_op jit(solution)/shard_map/pallas_call | solution.py:467
  70.9 2.6 %all-to-all-start.3 = ((bf16[32,16,128]{2,1,0:T(8,128)(2,1)}), bf16[32,16,128]{2,1,0:T(8,128)(2,1)S(1)}, u32[]{:S(2)}, u32[]{:S(2)}) async-start(bf16[32,16,128]{2,1,0:T(8,128)(2,1)} %shard_map.165), calls=%async_computation.3 | async-start | bytes 262144 | tf_op jit(solution)/shard_map/all_to_all | solution.py:401
  73.5 2.2 %shard_map.162 = (bf16[1,512,128]{2,1,0:T(8,128)(2,1)}, bf16[1,512,128]{2,1,0:T(8,128)(2,1)}) custom-call(bf16[8,128,256]{2,1,0:T(8,128)(2,1)} %copy-done, bf16[128,384]{1,0:T(8,128)(2,1)} %w_in_ref.3, bf16[128,128]{1,0:T(8,128)(2,1)} %w_out_ref.3), custom_call_target="tpu_custom_call" | custom-call | flops 67108864 | bytes 786432 | tf_op jit(solution)/shard_map/pallas_call | solution.py:460
  75.6 1.7 %shard_map.167 = (f32[8,512]{1,0:T(8,128)}, f32[8,512]{1,0:T(8,128)}, f32[3,384]{1,0:T(4,128)}, f32[1,128]{1,0:T(1,128)}, f32[1,128]{1,0:T(1,128)}) custom-call(bf16[32,32,128]{2,1,0:T(8,128)(2,1)} %all_to_all.21.in_ref), custom_call_target="tpu_custom_call" | custom-call | flops 131072 | bytes 524288 | tf_op jit(solution)/shard_map/pallas_call | solution.py:475
  77.3 4.4 %all-to-all-done.3.in_ref = bf16[32,16,128]{2,1,0:T(8,128)(2,1)S(1)} async-done(((bf16[32,16,128]{2,1,0:T(8,128)(2,1)}), bf16[32,16,128]{2,1,0:T(8,128)(2,1)S(1)}, u32[]{:S(2)}, u32[]{:S(2)}) %all-to-all-start.3) | async-done | bytes 131104 | tf_op jit(solution)/shard_map/all_to_all | solution.py:401
  81.7 0.0 copy-start.1
  81.7 0.6 copy-done.1
  82.3 1.7 %shard_map.166 = (f32[128,384]{1,0:T(8,128)}, f32[128,128]{1,0:T(8,128)}) custom-call(bf16[32,16,128]{2,1,0:T(8,128)(2,1)} %copy-done.1), custom_call_target="tpu_custom_call" | custom-call | flops 65536 | bytes 131072 | tf_op jit(solution)/shard_map/pallas_call | solution.py:487
Async XLA Ops:
  33.6 18.8 %all-to-all-start.1 = ((bf16[8,128,256]{2,1,0:T(8,128)(2,1)}), bf16[8,128,256]{2,1,0:T(8,128)(2,1)S(1)}, u32[]{:S(2)}, u32[]{:S(2)}) async-start(bf16[8,128,256]{2,1,0:T(8,128)(2,1)} %get-tuple-element.20), calls=%async_computation.1 | async-start | bytes 1048576 | tf_op jit(solution)/shard_map/all_to_all | solution.py:401
  52.3 0.8 copy-start
  70.9 10.8 %all-to-all-start.3 = ((bf16[32,16,128]{2,1,0:T(8,128)(2,1)}), bf16[32,16,128]{2,1,0:T(8,128)(2,1)S(1)}, u32[]{:S(2)}, u32[]{:S(2)}) async-start(bf16[32,16,128]{2,1,0:T(8,128)(2,1)} %shard_map.165), calls=%async_computation.3 | async-start | bytes 262144 | tf_op jit(solution)/shard_map/all_to_all | solution.py:401
  81.7 0.6 copy-start.1

commit v6 on v2

--- a/solution.py
+++ b/solution.py
@@ -229,14 +229,44 @@
     send_back(0, d_value)
 
 
-def gradient_kernel(units, fields_ref, kept_ref, out_ref, pad_ref, corr_ref):
-    sources, _, _ = fields_ref.shape
+def places(gathered):
+    m = len(gathered) // 2
+    me = lax.axis_index("seq")
+    row, core = me // 2, lax.rem(me, 2)
+    for k in range(m):
+        place = 2 * lax.rem(row - k + m, m)
+        yield place + core, gathered[k]
+        yield place + 1 - core, gathered[m + k]
+
+def weight_kernel(units, *refs):
+    sources = (len(refs) - 2) // 2
+    series = refs[:sources]
+    cot = refs[sources : 2 * sources]
+    sent_ref, out_ref = refs[2 * sources :]
+    width = out_ref.shape[1]
+    group = width // units
+    parts = sent_ref.shape[1] // 4 // group
+
+    def weights(kinds, gathered):
+        left, right = [], []
+        for place, block in places(gathered):
+            right.append(block[...])
+            for p in range(parts):
+                at = [(kind * parts + p) * group for kind in kinds]
+                left.append(jnp.concatenate([sent_ref[place, i : i + group, :] for i in at], axis=0))
+        return dot(jnp.concatenate(left, axis=1), jnp.concatenate(right, axis=0))
+
+    total = jnp.concatenate([weights((0, 1, 2), series), weights((3,), cot)], axis=0)
+    out_ref[...] = total.astype(BF16)
+
+
+def gradient_kernel(units, fields_ref, kept_ref, low_ref, pad_ref, corr_ref, out_ref):
+    sources, received, _ = fields_ref.shape
     _, rows, _ = kept_ref.shape
     _, length = corr_ref.shape
     width = out_ref.shape[1]
     blocks = length // W
     group = rows // blocks
-    received = 4 * rows // sources
     half = W // 2
     u = lax.rem(lax.axis_index("seq"), units)
     mine = own_lanes(u, group, width)
@@ -246,12 +276,12 @@
     row8 = lax.broadcasted_iota(jnp.int32, (8, length), 0)
     b = lax.broadcasted_iota(jnp.int32, (W, W), 0)
     r = lax.broadcasted_iota(jnp.int32, (W, W), 1)
-    for m in range(2):
-        pad_ref[0:rows, :] = kept_ref[2 + m]
+    for order in range(2):
+        pad_ref[0:rows, :] = kept_ref[2 + order]
         right = jnp.concatenate(
             [pad_ref[group * d : rows + group * d, :] for d in range(blocks)], axis=1
         )
-        held = kept_ref[m].astype(F32).T.astype(BF16)
+        held = kept_ref[order].astype(F32).T.astype(BF16)
         corr_ref[...] = dot(held, right)
         corr_ref[:, 0:W] = jnp.where(r >= b, corr_ref[:, 0:W], 0.0)
         total = None
@@ -266,7 +296,7 @@
             total = jnp.where((row8 & bit) != 0, pltpu.roll(total, length - bit, 1), total)
         line = jnp.sum(total, axis=0, keepdims=True)
         for q in range(lines):
-            at = m * lines + q
+            at = order * lines + q
             out_ref[at : at + 1, :] = line[:, q * width : (q + 1) * width]
 
     def spread(products):
@@ -277,18 +307,81 @@
     small = []
     for j in range(3):
         for kind in range(3):
-            field = pick(fields_ref, kind, received)
+            field = pick(fields_ref, kind, 4 * rows // sources)
             small.append(spread(kept_ref[4 + kind].astype(F32) * earlier(field, j, group)))
-    for m in range(2):
-        small.append(spread(kept_ref[2 + m].astype(F32) * kept_ref[m].astype(F32)))
-    out_ref[2 * lines : 2 * lines + 16, :] = jnp.concatenate(
+    for order in range(2):
+        small.append(spread(kept_ref[2 + order].astype(F32) * kept_ref[order].astype(F32)))
+    out_ref[2 * lines :, :] = jnp.concatenate(
         small + [jnp.zeros((16 - len(small), width), F32)], axis=0
     )
-
-
-def output_kernel(
-    units, in_ref, w_in_ref, w_out_ref, series_ref, cot_ref, own_ref, out_ref, d_series_ref, part_ref
+    low_ref[...] = out_ref[...].astype(BF16)
+
+
+def spread_kernel(copies, *refs):
+    weight_refs, rest_refs = refs[:copies], refs[copies : 2 * copies]
+    out_ref, sum_ref = refs[2 * copies :]
+    targets, _, width = out_ref.shape
+
+    def total(parts):
+        result = parts[0][...].astype(F32)
+        for ref in parts[1:]:
+            result = result + ref[...].astype(F32)
+        return result
+
+    weights = total(weight_refs).astype(BF16)
+    base = weights.shape[0]
+    sum_ref[...] = total(rest_refs)
+    lines = (sum_ref.shape[0] - 16) // 2
+    each = lines // targets
+    for s in range(targets):
+        out_ref[s, 0:base, :] = weights
+        out_ref[s, base:, :] = jnp.concatenate(
+            [
+                sum_ref[s * each : (s + 1) * each, :],
+                sum_ref[lines + s * each : lines + (s + 1) * each, :],
+                sum_ref[2 * lines :, :],
+                jnp.zeros((16 - 2 * each, width), F32),
+            ],
+            axis=0,
+        ).astype(BF16)
+
+
+def parameter_kernel(
+    units, scale, in_ref, w_in_ref, w_out_ref, taps_ref, skip_one_ref, skip_two_ref, one_ref, two_ref
 ):
+    sources, _, width = in_ref.shape
+    group = width // units
+    count = sources // units
+    each = one_ref.shape[1] // width
+
+    def total(first, last):
+        parts = [in_ref[e * units : (e + 1) * units, first:last, :] for e in range(count)]
+        result = parts[0].astype(F32)
+        for part in parts[1:]:
+            result = result + part.astype(F32)
+        return result
+
+    blocks = total(0, 4 * group) * scale
+    for kind in range(3):
+        rows = blocks[:, kind * group : (kind + 1) * group, :].reshape(width, width)
+        w_in_ref[:, kind * width : (kind + 1) * width] = rows.T
+    w_out_ref[...] = blocks[:, 3 * group : 4 * group, :].reshape(width, width)
+    rest = total(4 * group, in_ref.shape[1]) * scale
+    filters = one_ref.shape[0]
+    for q in range(each):
+        for ref, at in ((one_ref, q), (two_ref, each + q)):
+            by_unit = rest[:, at, :].reshape(filters, units // filters, width)
+            ref[:, q * width : (q + 1) * width] = jnp.sum(by_unit, axis=1)
+    small = jnp.sum(rest[:, 2 * each : 2 * each + 16, :], axis=0)
+    for j in range(3):
+        for kind in range(3):
+            n = 3 * j + kind
+            taps_ref[j : j + 1, kind * width : (kind + 1) * width] = small[n : n + 1]
+    skip_one_ref[...] = small[9:10]
+    skip_two_ref[...] = small[10:11]
+
+
+def output_kernel(units, in_ref, w_in_ref, w_out_ref, out_ref, d_series_ref):
     count, block, width = out_ref.shape
     group = width // units
     parts = block // W
@@ -299,83 +392,32 @@
         at = (kind * parts + part) * group
         return in_ref[e * units : (e + 1) * units, at : at + group, :].reshape(width, W)
 
-    w_in_part = 0.0
-    w_out_part = 0.0
     for e in range(count):
         for part in range(parts):
             rows = pl.ds(part * W, W)
-            product = field(e, 3, part)
-            out_ref[e, rows, :] = dot(w_out_t, product).T.astype(BF16)
+            out_ref[e, rows, :] = dot(w_out_t, field(e, 3, part)).T.astype(BF16)
             grads = jnp.concatenate([field(e, kind, part) for kind in range(3)], axis=0)
             d_series_ref[e, rows, :] = dot(w_in, grads).T.astype(BF16)
-            w_in_part += dot(grads, series_ref[e, rows, :])
-            w_out_part += dot(product, cot_ref[e, rows, :])
-
-    weights = jnp.concatenate([w_in_part, w_out_part], axis=0)
-    targets, sent, _ = part_ref.shape
-    each = weights.shape[0] // targets
-    sources = in_ref.shape[0]
-    lines = (own_ref.shape[0] - 16) // 2
-    slots = lines // sources
-    spare = jnp.zeros((sent - each - 2 * slots - 1, width), F32)
-    for g in range(targets):
-        s = g % sources
-        small = 2 * lines + g * 16 // targets
-        part_ref[g] = jnp.concatenate(
-            [
-                weights[g * each : (g + 1) * each],
-                own_ref[s * slots : (s + 1) * slots, :],
-                own_ref[lines + s * slots : lines + (s + 1) * slots, :],
-                own_ref[small : small + 1, :],
-                spare,
-            ],
-            axis=0,
-        ).astype(BF16)
-
-
-def sum_kernel(units, each, scale, in_ref, out_ref, one_ref, two_ref):
-    targets, _, width = in_ref.shape
-    filters, block = one_ref.shape
-    slots = block // width
-    total = in_ref[0].astype(F32)
-    for g in range(1, targets):
-        total = total + in_ref[g].astype(F32)
-    weights = total[:each]
-    small = total[each + 2 * slots : each + 2 * slots + 1]
-    spare = jnp.zeros((out_ref.shape[1] - each - 1, width), F32)
-    total = jnp.concatenate([weights, small, spare], axis=0).astype(BF16)
-    for g in range(targets):
-        out_ref[g] = total
-    repeat = units // filters
-    for row in range(filters):
-        sums = 0.0
-        for g in range(targets):
-            if g % units // repeat == row:
-                sums += in_ref[g, each : each + 2 * slots, :].astype(F32)
-        for q in range(slots):
-            one_ref[row : row + 1, q * width : (q + 1) * width] = sums[q : q + 1] * scale
-            two_ref[row : row + 1, q * width : (q + 1) * width] = sums[slots + q : slots + q + 1] * scale
-
-
-def weight_kernel(each, scale, in_ref, w_in_ref, w_out_ref, taps_ref, skip_one_ref, skip_two_ref):
-    targets, _, width = in_ref.shape
-    weights = jnp.concatenate([in_ref[g, 0:each, :].astype(F32) for g in range(targets)], axis=0) * scale
-    for kind in range(3):
-        w_in_ref[:, kind * width : (kind + 1) * width] = weights[kind * width : (kind + 1) * width].T
-    w_out_ref[...] = weights[3 * width :]
-
-    def small(n):
-        return in_ref[n * targets // 16, each : each + 1, :].astype(F32) * scale
-
-    for j in range(3):
-        for kind in range(3):
-            taps_ref[j : j + 1, kind * width : (kind + 1) * width] = small(3 * j + kind)
-    skip_one_ref[...] = small(9)
-    skip_two_ref[...] = small(10)
 
 
 def all_to_all(blocks, axis):
     return lax.all_to_all(blocks, axis, split_axis=0, concat_axis=0, tiled=True)
+
+
+def exchange(block, axis, routes):
+    devices = lax.axis_size(axis)
+    return [lax.ppermute(block, axis, [(i, route(i) % devices) for i in range(devices)]) for route in routes]
+
+
+def onward(block):
+    return exchange(block, "seq", [lambda i: i + 2])[0]
+
+
+def swap(block):
+    return exchange(block, "seq", [lambda i: i ^ 1])[0]
+
+
+after = lax.optimization_barrier
 
 
 def shards(series, cotangent, w_in, w_out, taps, skip_one, skip_two, filter_one, filter_two):
@@ -386,13 +428,13 @@
     length = block * sources
     units = sources // count
     group = width // units
-    assert sources == count * units and units % filters == 0 and block % W == 0
+    assert count == 1 and units % filters == 0 and block % W == 0
     blocks = length // W
     rows = blocks * group
     scale = 1.0 / math.sqrt(count * copies * length)
     shape = jax.ShapeDtypeStruct
-
-    devices = sources * copies
+    m = sources // 2
+
     packed = 4 * (block // W) * group
     fields = call(
         functools.partial(project_kernel, units),
@@ -401,6 +443,17 @@
         moved=8 * count * block * width * 4,
     )(series, cotangent, w_in, w_out, filter_one, filter_two)
     fields = all_to_all(fields, "seq")
+
+    own_series, own_cot = [series.reshape(block, width)], [cotangent.reshape(block, width)]
+
+    def turn():
+        own_series.append(onward(own_series[-1]))
+        own_cot.append(onward(own_cot[-1]))
+
+    turn()
+    tied = after((own_series[-1], own_cot[-1], fields))
+    own_series[-1], own_cot[-1], fields = tied
+    turn()
 
     sent, kept = call(
         functools.partial(operator_kernel, units),
@@ -414,54 +467,69 @@
         moved=2 * W * length * 2 * 2,
     )(fields, taps, skip_one.reshape(1, width), skip_two.reshape(1, width))
 
+    tied = after((own_series[-1], own_cot[-1], sent))
+    own_series[-1], own_cot[-1], sent = tied
+    while len(own_series) < m:
+        turn()
+    all_series = own_series + [swap(part) for part in own_series]
+    all_cot = own_cot + [swap(part) for part in own_cot]
     back = all_to_all(sent, "seq")
 
-    own = call(
+    around = [lambda i, d=d: i + d for d in range(1, copies)]
+    rest_rows = 2 * (length // width) + 16
+    rest = call(
         functools.partial(gradient_kernel, units),
-        shape((2 * (length // width) + 16, width), F32),
-        [pltpu.VMEM((2 * rows, W), BF16), pltpu.VMEM((W, length), F32)],
+        shape((rest_rows, width), BF16),
+        [
+            pltpu.VMEM((2 * rows, W), BF16),
+            pltpu.VMEM((W, length), F32),
+            pltpu.VMEM((rest_rows, width), F32),
+        ],
         flops=2 * 2 * rows * length * W,
         moved=2 * length * width * 2,
     )(fields, kept)
-
-    each = 4 * width // devices
-    sent_rows = -(-(each + 2 * (block // width) + 1) // 16) * 16
-    output, d_series, partial = call(
+    rests = [rest] + exchange(rest, "dp", around)
+    weights = call(
+        functools.partial(weight_kernel, units),
+        shape((4 * group, width), BF16),
+        flops=2 * length * width * 4 * group,
+        moved=2 * length * width * 2,
+    )(*all_series, *all_cot, sent)
+    weights = [weights] + exchange(weights, "dp", around)
+
+    spread_rows = 4 * group + 32
+    sums = call(
+        functools.partial(spread_kernel, copies),
+        shape((sources, spread_rows, width), BF16),
+        [pltpu.VMEM((rest_rows, width), F32)],
+        flops=copies * spread_rows * width,
+        moved=2 * sources * spread_rows * width,
+    )(*weights, *rests)
+    sums, back = after((sums, back))
+    sums = all_to_all(sums, "seq")
+
+    output, d_series = call(
         functools.partial(output_kernel, units),
-        (
-            shape(series.shape, BF16),
-            shape(series.shape, BF16),
-            shape((devices, sent_rows, width), BF16),
-        ),
-        flops=2 * count * block * width * 8 * width,
+        (shape(series.shape, BF16), shape(series.shape, BF16)),
+        flops=2 * count * block * width * 4 * width,
         moved=2 * count * block * width * 6,
-    )(back, w_in, w_out, series, cotangent, own)
-    partial = all_to_all(partial, ("dp", "seq"))
-
-    sums, grad_one, grad_two = call(
-        functools.partial(sum_kernel, units, each, scale),
-        (
-            shape((devices, -(-(each + 1) // 16) * 16, width), BF16),
-            shape(filter_one.shape, F32),
-            shape(filter_two.shape, F32),
-        ),
-        flops=devices * sent_rows * width,
-        moved=4 * devices * sent_rows * width,
-    )(partial)
-    sums = all_to_all(sums, ("dp", "seq"))
-
-    grad_w_in, grad_w_out, grad_taps, grad_skip_one, grad_skip_two = call(
-        functools.partial(weight_kernel, each, scale),
+    )(back, w_in, w_out)
+
+    grads = call(
+        functools.partial(parameter_kernel, units, scale),
         (
             shape(w_in.shape, F32),
             shape(w_out.shape, F32),
             shape(taps.shape, F32),
             shape((1, width), F32),
             shape((1, width), F32),
+            shape(filter_one.shape, F32),
+            shape(filter_two.shape, F32),
         ),
-        flops=devices * sent_rows * width,
-        moved=2 * devices * sent_rows * width,
+        flops=sources * spread_rows * width,
+        moved=2 * sources * spread_rows * width,
     )(sums)
+    grad_w_in, grad_w_out, grad_taps, grad_skip_one, grad_skip_two, grad_one, grad_two = grads
     return (
         output,
         d_series,

time: 87.2 us -> 102 us (1.17)
  blocking collectives: 50.8 us -> 0 us
  waiting for transfers between devices: 10.8 us -> 45.2 us
  starting transfers between devices: 3.49 us -> 30.4 us
  Pallas kernels: 20.1 us -> 22.6 us
  local copies, waits for them, and re-layouts: 0.79 us -> 2.63 us
    all_to_all x3 -> x0, blocking collectives: 50.8 us -> none  [all_to_all(): return lax.all_to_all(blocks, axis, split_axis=0, concat_axis=0, tiled=True)]
    ppermute x0 -> x20, waiting for transfers between devices: none -> 36.9 us  [exchange(): lax.ppermute(block, axis, [(i, route(i) % devices) for i in range(devices)])]
    ppermute x0 -> x20, starting transfers between devices: none -> 16.8 us  [exchange(): lax.ppermute(block, axis, [(i, route(i) % devices) for i in range(devices)])]
    all_to_all x1 -> x3, starting transfers between devices: 3.49 us -> 13.6 us  [all_to_all(): return lax.all_to_all(blocks, axis, split_axis=0, concat_axis=0, tiled=True)]
    pallas_call x3 -> x4, Pallas kernels: 8 us -> 10.7 us  [the longest x1 4.56 us: shards(): call(functools.partial(gradient_kernel, units), shape((rest_rows, width),...]
    all_to_all x1 -> x3, waiting for transfers between devices: 10.8 us -> 8.31 us  [all_to_all(): return lax.all_to_all(blocks, axis, split_axis=0, concat_axis=0, tiled=True)]
    unnamed x2 -> x50, local copies, waits for them, and re-layouts: 0.79 us -> 2.63 us
  transfers between devices with their start and end apart: 1 -> 23, of which waited for: 1 -> 10; matrix products, arithmetic and copies ran while one was open for 0% -> 0% of each run, Pallas kernels for 5% -> 18%
where the time goes in v6:
time: 102 us
  waiting for transfers between devices  45.2 us (44%)
  starting transfers between devices  30.4 us (30%)
  Pallas kernels  22.6 us (22%)
  local copies, waits for them, and re-layouts  2.63 us (3%)
    ppermute x20, waiting for transfers between devices, exchange(): lax.ppermute(block, axis, [(i, route(i) % devices) for i in range(devices)])  36.9 us
    ppermute x20, starting transfers between devices, exchange(): lax.ppermute(block, axis, [(i, route(i) % devices) for i in range(devices)])  16.8 us
    all_to_all x3, starting transfers between devices, all_to_all(): return lax.all_to_all(blocks, axis, split_axis=0, concat_axis=0, tiled=True)  13.6 us
    all_to_all x3, waiting for transfers between devices, all_to_all(): return lax.all_to_all(blocks, axis, split_axis=0, concat_axis=0, tiled=True)  8.31 us
    pallas_call x1, Pallas kernels, shards(): call(functools.partial(operator_kernel, units), (shape((sources, packed,...  7.56 us
    pallas_call x1, Pallas kernels, shards(): call(functools.partial(gradient_kernel, units), shape((rest_rows, width),...  4.56 us
    pallas_call x1, Pallas kernels, shards(): call(functools.partial(weight_kernel, units), shape((4 * group, width), B...  2.83 us
    unnamed x50, local copies, waits for them, and re-layouts  2.63 us
  transfers between devices with their start and end apart: 23, of which 10 were waited for; matrix products, arithmetic and copies ran while one was open for 0% of the time, Pallas kernels for 18%

profile of v6, /device:TPU:0, one launch (start us, length us, event | category | flops | bytes accessed | tf_op | source)
XLA Modules:
  0.0 101.7 jit_solution(5016638186449864478)
XLA Ops:
  0.6 2.2 %shard_map.160 = bf16[8,144,256]{2,1,0:T(8,128)(2,1)} custom-call(bf16[1,512,128]{2,1,0:T(8,128)(2,1)} %series_ref.1, bf16[1,512,128]{2,1,0:T(8,128)(2,1)} %cot_ref.1, bf16[128,384]{1,0:T(8,128)(2,1)} %w_in_ref.3, bf16[128,128]{1,0:T(8,128)(2,1)} %w_out_ref.3, f32[8,512]{1,0:T(8,128)} %one_ref.1, f32[8,512]{1,0:T(8,128)} %two_ref.1), custom_call_target="tpu_custom_call" | custom-call | flops 67108864 | bytes 2097152 | tf_op jit(solution)/shard_map/pallas_call | solution.py:439
  2.8 6.5 %all-to-all-start = ((bf16[8,144,256]{2,1,0:T(8,128)(2,1)}), bf16[8,144,256]{2,1,0:T(8,128)(2,1)S(1)}, u32[]{:S(2)}, u32[]{:S(2)}) async-start(bf16[8,144,256]{2,1,0:T(8,128)(2,1)} %shard_map.160), calls=%async_computation | async-start | bytes 1179648 | tf_op jit(solution)/shard_map/all_to_all | solution.py:404
  9.3 2.0 %collective-permute-start = (bf16[512,128]{1,0:T(8,128)(2,1)S(1)}, bf16[512,128]{1,0:T(8,128)(2,1)S(1)}, u32[]{:S(2)}, u32[]{:S(2)}) collective-permute-start(bf16[512,128]{1,0:T(8,128)(2,1)S(1)} %bitcast.7), channel_id=1, source_target_pairs={{0,2},{1,3},{2,4},{3,5},{4,6},{5,7},{6,0},{7,1},{8,10},{9,11},{10,... | collective-permute-start | bytes 393224 | tf_op jit(solution)/shard_map/ppermute | solution.py:409
  11.3 1.5 %collective-permute-start.1 = (bf16[512,128]{1,0:T(8,128)(2,1)S(1)}, bf16[512,128]{1,0:T(8,128)(2,1)S(1)}, u32[]{:S(2)}, u32[]{:S(2)}) collective-permute-start(bf16[512,128]{1,0:T(8,128)(2,1)S(1)} %bitcast.10), channel_id=1, source_target_pairs={{0,2},{1,3},{2,4},{3,5},{4,6},{5,7},{6,0},{7,1},{8,10},{9,11},{10,... | collective-permute-start | bytes 393224 | tf_op jit(solution)/shard_map/ppermute | solution.py:409
  12.8 14.4 %collective-permute-done.refs_1_ = bf16[512,128]{1,0:T(8,128)(2,1)S(1)} collective-permute-done((bf16[512,128]{1,0:T(8,128)(2,1)S(1)}, bf16[512,128]{1,0:T(8,128)(2,1)S(1)}, u32[]{:S(2)}, u32[]{:S(2)}) %collective-permute-start) | collective-permute-done | bytes 131104 | tf_op jit(solution)/shard_map/ppermute | solution.py:409
  27.2 2.3 %collective-permute-done.1.refs_9_ = bf16[512,128]{1,0:T(8,128)(2,1)S(1)} collective-permute-done((bf16[512,128]{1,0:T(8,128)(2,1)S(1)}, bf16[512,128]{1,0:T(8,128)(2,1)S(1)}, u32[]{:S(2)}, u32[]{:S(2)}) %collective-permute-start.1) | collective-permute-done | bytes 131104 | tf_op jit(solution)/shard_map/ppermute | solution.py:409
  29.5 2.1 %all-to-all-done.fields_ref = bf16[8,144,256]{2,1,0:T(8,128)(2,1)S(1)} async-done(((bf16[8,144,256]{2,1,0:T(8,128)(2,1)}), bf16[8,144,256]{2,1,0:T(8,128)(2,1)S(1)}, u32[]{:S(2)}, u32[]{:S(2)}) %all-to-all-start) | async-done | bytes 589856 | tf_op jit(solution)/shard_map/all_to_all | solution.py:404
  31.7 1.0 %collective-permute-start.3 = (bf16[512,128]{1,0:T(8,128)(2,1)S(1)}, bf16[512,128]{1,0:T(8,128)(2,1)S(1)}, u32[]{:S(2)}, u32[]{:S(2)}) collective-permute-start(bf16[512,128]{1,0:T(8,128)(2,1)S(1)} %collective-permute-done.1.refs_9_), channel_id=1, source_target_pairs={{0,2},{1,3},{2,4},{3,5},{4,6},{5,7},{6,0},{7,1},{8,10},{9,11},{10,... | collective-permute-start | bytes 393224 | tf_op jit(solution)/shard_map/ppermute | solution.py:409
  32.7 7.6 %shard_map.161 = (bf16[8,128,256]{2,1,0:T(8,128)(2,1)}, bf16[7,256,256]{2,1,0:T(8,128)(2,1)}) custom-call(bf16[8,144,256]{2,1,0:T(8,128)(2,1)} %copy-done.2, f32[3,384]{1,0:T(4,128)} %taps_ref.1, f32[1,128]{1,0:T(1,128)} %bitcast.12, f32[1,128]{1,0:T(1,128)} %bitcast.13), custom_call_target="tpu_custom_call" | custom-call | flops 2147483648 | bytes 8388608 | tf_op jit(solution)/shard_map/pallas_call | solution.py:458
  40.3 1.1 %collective-permute-done.3.refs_10_ = bf16[512,128]{1,0:T(8,128)(2,1)S(1)} collective-permute-done((bf16[512,128]{1,0:T(8,128)(2,1)S(1)}, bf16[512,128]{1,0:T(8,128)(2,1)S(1)}, u32[]{:S(2)}, u32[]{:S(2)}) %collective-permute-start.3) | collective-permute-done | bytes 131104 | tf_op jit(solution)/shard_map/ppermute | solution.py:409
  41.3 3.6 %all-to-all-start.1 = ((bf16[8,128,256]{2,1,0:T(8,128)(2,1)}), bf16[8,128,256]{2,1,0:T(8,128)(2,1)S(1)}, u32[]{:S(2)}, u32[]{:S(2)}) async-start(bf16[8,128,256]{2,1,0:T(8,128)(2,1)} %get-tuple-element.34.refs_16_), calls=%async_computation.1 | async-start | bytes 1048576 | tf_op jit(solution)/shard_map/all_to_all | solution.py:404
  46.0 1.7 %collective-permute-start.4 = (bf16[512,128]{1,0:T(8,128)(2,1)S(1)}, bf16[512,128]{1,0:T(8,128)(2,1)S(1)}, u32[]{:S(2)}, u32[]{:S(2)}) collective-permute-start(bf16[512,128]{1,0:T(8,128)(2,1)S(1)} %collective-permute-done.2.refs_2_), channel_id=1, source_target_pairs={{0,2},{1,3},{2,4},{3,5},{4,6},{5,7},{6,0},{7,1},{8,10},{9,11},{10,... | collective-permute-start | bytes 393224 | tf_op jit(solution)/shard_map/ppermute | solution.py:409
  47.6 1.5 %collective-permute-start.9 = (bf16[512,128]{1,0:T(8,128)(2,1)S(1)}, bf16[512,128]{1,0:T(8,128)(2,1)S(1)}, u32[]{:S(2)}, u32[]{:S(2)}) collective-permute-start(bf16[512,128]{1,0:T(8,128)(2,1)S(1)} %collective-permute-done.3.refs_10_), channel_id=1, source_target_pairs={{0,2},{1,3},{2,4},{3,5},{4,6},{5,7},{6,0},{7,1},{8,10},{9,11},{10,... | collective-permute-start | bytes 393224 | tf_op jit(solution)/shard_map/ppermute | solution.py:409
  49.9 11.9 %collective-permute-done.4.refs_3_ = bf16[512,128]{1,0:T(8,128)(2,1)S(1)} collective-permute-done((bf16[512,128]{1,0:T(8,128)(2,1)S(1)}, bf16[512,128]{1,0:T(8,128)(2,1)S(1)}, u32[]{:S(2)}, u32[]{:S(2)}) %collective-permute-start.4) | collective-permute-done | bytes 131104 | tf_op jit(solution)/shard_map/ppermute | solution.py:409
  61.8 2.3 %collective-permute-done.9.refs_11_ = bf16[512,128]{1,0:T(8,128)(2,1)S(1)} collective-permute-done((bf16[512,128]{1,0:T(8,128)(2,1)S(1)}, bf16[512,128]{1,0:T(8,128)(2,1)S(1)}, u32[]{:S(2)}, u32[]{:S(2)}) %collective-permute-start.9) | collective-permute-done | bytes 131104 | tf_op jit(solution)/shard_map/ppermute | solution.py:409
  64.1 4.6 %shard_map.163.refs_4_ = bf16[80,128]{1,0:T(8,128)(2,1)} custom-call(bf16[8,144,256]{2,1,0:T(8,128)(2,1)} %copy-done.2, bf16[7,256,256]{2,1,0:T(8,128)(2,1)} %get-tuple-element.35.kept_ref), custom_call_target="tpu_custom_call" | custom-call | flops 1073741824 | bytes 2097152 | tf_op jit(solution)/shard_map/pallas_call | solution.py:480
  68.7 2.5 %collective-permute-start.19 = (bf16[80,128]{1,0:T(8,128)(2,1)}, bf16[80,128]{1,0:T(8,128)(2,1)S(1)}, u32[]{:S(2)}, u32[]{:S(2)}) collective-permute-start(bf16[80,128]{1,0:T(8,128)(2,1)} %shard_map.163.refs_4_), channel_id=1, source_target_pairs={{0,24},{8,0},{16,8},{24,16},{1,25},{9,1},{17,9},{25,17},{2,26},{10... | collective-permute-start | bytes 61448 | tf_op jit(solution)/shard_map/ppermute | solution.py:409
  71.8 0.6 collective-permute-start.17
  72.4 0.6 copy-done.17
  73.0 0.6 copy-done.18
  73.7 2.8 %shard_map.162.refs_0_ = bf16[64,128]{1,0:T(8,128)(2,1)} custom-call(bf16[512,128]{1,0:T(8,128)(2,1)} %bitcast.6, bf16[512,128]{1,0:T(8,128)(2,1)} %copy-done.5, bf16[512,128]{1,0:T(8,128)(2,1)} %copy-done.7, bf16[512,128]{1,0:T(8,128)(2,1)} %copy-done.12, bf16[512,128]{1,0:T(8,128)(2,1)} %copy-done.9, bf16[512,128]{1,0:T(8,128)(2,1)} %copy-done.11, ...), custom_call_target="tpu_custom_call" | custom-call | flops 67108864 | bytes 2097152 | tf_op jit(solution)/shard_map/pallas_call | solution.py:492
  76.5 2.3 %collective-permute-start.16 = (bf16[64,128]{1,0:T(8,128)(2,1)}, bf16[64,128]{1,0:T(8,128)(2,1)S(1)}, u32[]{:S(2)}, u32[]{:S(2)}) collective-permute-start(bf16[64,128]{1,0:T(8,128)(2,1)} %shard_map.162.refs_0_), channel_id=1, source_target_pairs={{0,24},{8,0},{16,8},{24,16},{1,25},{9,1},{17,9},{25,17},{2,26},{10... | collective-permute-start | bytes 49160 | tf_op jit(solution)/shard_map/ppermute | solution.py:409
  78.8 1.5 %collective-permute-start.15 = (bf16[64,128]{1,0:T(8,128)(2,1)}, bf16[64,128]{1,0:T(8,128)(2,1)S(1)}, u32[]{:S(2)}, u32[]{:S(2)}) collective-permute-start(bf16[64,128]{1,0:T(8,128)(2,1)} %shard_map.162.refs_0_), channel_id=1, source_target_pairs={{0,16},{8,24},{16,0},{24,8},{1,17},{9,25},{17,1},{25,9},{2,18},{10... | collective-permute-start | bytes 49160 | tf_op jit(solution)/shard_map/ppermute | solution.py:409
  80.8 2.0 %collective-permute-done.15.refs_2_ = bf16[64,128]{1,0:T(8,128)(2,1)S(1)} collective-permute-done((bf16[64,128]{1,0:T(8,128)(2,1)}, bf16[64,128]{1,0:T(8,128)(2,1)S(1)}, u32[]{:S(2)}, u32[]{:S(2)}) %collective-permute-start.15) | collective-permute-done | bytes 16416 | tf_op jit(solution)/shard_map/ppermute | solution.py:409
  82.8 2.4 %collective-permute-done.14.refs_1_ = bf16[64,128]{1,0:T(8,128)(2,1)S(1)} collective-permute-done((bf16[64,128]{1,0:T(8,128)(2,1)}, bf16[64,128]{1,0:T(8,128)(2,1)S(1)}, u32[]{:S(2)}, u32[]{:S(2)}) %collective-permute-start.14) | collective-permute-done | bytes 16416 | tf_op jit(solution)/shard_map/ppermute | solution.py:409
  85.3 0.6 copy-done.24
  85.8 1.6 %shard_map.164 = bf16[8,96,128]{2,1,0:T(8,128)(2,1)} custom-call(bf16[64,128]{1,0:T(8,128)(2,1)} %shard_map.162.refs_0_, bf16[64,128]{1,0:T(8,128)(2,1)} %copy-done.24, bf16[64,128]{1,0:T(8,128)(2,1)} %copy-done.23, bf16[64,128]{1,0:T(8,128)(2,1)} %copy-done.22, bf16[80,128]{1,0:T(8,128)(2,1)} %shard_map.163.refs_4_, bf16[80,128]{1,0:T(8,128)(2,1)} %copy-done.21, ...), custom_call_target="tpu_custom_call" | custom-call | flops 49152 | bytes 196608 | tf_op jit(solution)/shard_map/pallas_call | solution.py:501
  87.4 3.5 %all-to-all-start.2 = ((bf16[8,96,128]{2,1,0:T(8,128)(2,1)}), bf16[8,96,128]{2,1,0:T(8,128)(2,1)S(1)}, u32[]{:S(2)}, u32[]{:S(2)}) async-start(bf16[8,96,128]{2,1,0:T(8,128)(2,1)} %shard_map.164), calls=%async_computation.2 | async-start | bytes 393216 | tf_op jit(solution)/shard_map/all_to_all | solution.py:404
  90.9 2.2 %shard_map.165 = (bf16[1,512,128]{2,1,0:T(8,128)(2,1)}, bf16[1,512,128]{2,1,0:T(8,128)(2,1)}) custom-call(bf16[8,128,256]{2,1,0:T(8,128)(2,1)} %copy-done, bf16[128,384]{1,0:T(8,128)(2,1)} %w_in_ref.3, bf16[128,128]{1,0:T(8,128)(2,1)} %w_out_ref.3), custom_call_target="tpu_custom_call" | custom-call | flops 67108864 | bytes 786432 | tf_op jit(solution)/shard_map/pallas_call | solution.py:511
  93.1 6.2 %all-to-all-done.2.in_ref = bf16[8,96,128]{2,1,0:T(8,128)(2,1)S(1)} async-done(((bf16[8,96,128]{2,1,0:T(8,128)(2,1)}), bf16[8,96,128]{2,1,0:T(8,128)(2,1)S(1)}, u32[]{:S(2)}, u32[]{:S(2)}) %all-to-all-start.2) | async-done | bytes 196640 | tf_op jit(solution)/shard_map/all_to_all | solution.py:404
  99.2 0.7 copy-done.1
  99.9 1.7 %shard_map.166 = (f32[128,384]{1,0:T(8,128)}, f32[128,128]{1,0:T(8,128)}, f32[3,384]{1,0:T(4,128)}, f32[1,128]{1,0:T(1,128)}, f32[1,128]{1,0:T(1,128)}, /*index=5*/f32[8,512]{1,0:T(8,128)}, f32[8,512]{1,0:T(8,128)}) custom-call(bf16[8,96,128]{2,1,0:T(8,128)(2,1)} %copy-done.1), custom_call_target="tpu_custom_call" | custom-call | flops 98304 | bytes 196608 | tf_op jit(solution)/shard_map/pallas_call | solution.py:518
  (71 shorter events, 2.8 us)
Async XLA Ops:
  2.8 8.5 %copy-start.4 = (bf16[1,512,128]{2,1,0:T(8,128)(2,1)S(1)}, bf16[1,512,128]{2,1,0:T(8,128)(2,1)}, u32[]{:S(2)}) copy-start(bf16[1,512,128]{2,1,0:T(8,128)(2,1)} %cot_ref.1) | copy-start | bytes 393220
  2.8 28.8 %all-to-all-start = ((bf16[8,144,256]{2,1,0:T(8,128)(2,1)}), bf16[8,144,256]{2,1,0:T(8,128)(2,1)S(1)}, u32[]{:S(2)}, u32[]{:S(2)}) async-start(bf16[8,144,256]{2,1,0:T(8,128)(2,1)} %shard_map.160), calls=%async_computation | async-start | bytes 1179648 | tf_op jit(solution)/shard_map/all_to_all | solution.py:404
  9.3 17.9 %collective-permute-start = (bf16[512,128]{1,0:T(8,128)(2,1)S(1)}, bf16[512,128]{1,0:T(8,128)(2,1)S(1)}, u32[]{:S(2)}, u32[]{:S(2)}) collective-permute-start(bf16[512,128]{1,0:T(8,128)(2,1)S(1)} %bitcast.7), channel_id=1, source_target_pairs={{0,2},{1,3},{2,4},{3,5},{4,6},{5,7},{6,0},{7,1},{8,10},{9,11},{10,... | collective-permute-start | bytes 393224 | tf_op jit(solution)/shard_map/ppermute | solution.py:409
  11.3 18.2 %collective-permute-start.1 = (bf16[512,128]{1,0:T(8,128)(2,1)S(1)}, bf16[512,128]{1,0:T(8,128)(2,1)S(1)}, u32[]{:S(2)}, u32[]{:S(2)}) collective-permute-start(bf16[512,128]{1,0:T(8,128)(2,1)S(1)} %bitcast.10), channel_id=1, source_target_pairs={{0,2},{1,3},{2,4},{3,5},{4,6},{5,7},{6,0},{7,1},{8,10},{9,11},{10,... | collective-permute-start | bytes 393224 | tf_op jit(solution)/shard_map/ppermute | solution.py:409
  27.2 18.2 %copy-start.5 = (bf16[512,128]{1,0:T(8,128)(2,1)}, bf16[512,128]{1,0:T(8,128)(2,1)S(1)}, u32[]{:S(2)}) copy-start(bf16[512,128]{1,0:T(8,128)(2,1)S(1)} %collective-permute-done.refs_1_) | copy-start | bytes 393220
  29.5 19.6 %copy-start.6 = (bf16[512,128]{1,0:T(8,128)(2,1)}, bf16[512,128]{1,0:T(8,128)(2,1)S(1)}, u32[]{:S(2)}) copy-start(bf16[512,128]{1,0:T(8,128)(2,1)S(1)} %collective-permute-done.1.refs_9_) | copy-start | bytes 393220
  31.7 8.6 %collective-permute-start.2 = (bf16[512,128]{1,0:T(8,128)(2,1)S(1)}, bf16[512,128]{1,0:T(8,128)(2,1)S(1)}, u32[]{:S(2)}, u32[]{:S(2)}) collective-permute-start(bf16[512,128]{1,0:T(8,128)(2,1)S(1)} %collective-permute-done.refs_1_), channel_id=1, source_target_pairs={{0,2},{1,3},{2,4},{3,5},{4,6},{5,7},{6,0},{7,1},{8,10},{9,11},{10,... | collective-permute-start | bytes 393224 | tf_op jit(solution)/shard_map/ppermute | solution.py:409
  31.7 9.6 %collective-permute-start.3 = (bf16[512,128]{1,0:T(8,128)(2,1)S(1)}, bf16[512,128]{1,0:T(8,128)(2,1)S(1)}, u32[]{:S(2)}, u32[]{:S(2)}) collective-permute-start(bf16[512,128]{1,0:T(8,128)(2,1)S(1)} %collective-permute-done.1.refs_9_), channel_id=1, source_target_pairs={{0,2},{1,3},{2,4},{3,5},{4,6},{5,7},{6,0},{7,1},{8,10},{9,11},{10,... | collective-permute-start | bytes 393224 | tf_op jit(solution)/shard_map/ppermute | solution.py:409
  40.3 8.9 %copy-start.7 = (bf16[512,128]{1,0:T(8,128)(2,1)}, bf16[512,128]{1,0:T(8,128)(2,1)S(1)}, u32[]{:S(2)}) copy-start(bf16[512,128]{1,0:T(8,128)(2,1)S(1)} %collective-permute-done.2.refs_2_) | copy-start | bytes 393220
  41.3 8.4 %copy-start.8 = (bf16[512,128]{1,0:T(8,128)(2,1)}, bf16[512,128]{1,0:T(8,128)(2,1)S(1)}, u32[]{:S(2)}) copy-start(bf16[512,128]{1,0:T(8,128)(2,1)S(1)} %collective-permute-done.3.refs_10_) | copy-start | bytes 393220
  41.3 46.1 %all-to-all-start.1 = ((bf16[8,128,256]{2,1,0:T(8,128)(2,1)}), bf16[8,128,256]{2,1,0:T(8,128)(2,1)S(1)}, u32[]{:S(2)}, u32[]{:S(2)}) async-start(bf16[8,128,256]{2,1,0:T(8,128)(2,1)} %get-tuple-element.34.refs_16_), calls=%async_computation.1 | async-start | bytes 1048576 | tf_op jit(solution)/shard_map/all_to_all | solution.py:404
  44.9 4.2 %collective-permute-start.5 = (bf16[512,128]{1,0:T(8,128)(2,1)S(1)}, bf16[512,128]{1,0:T(8,128)(2,1)S(1)}, u32[]{:S(2)}, u32[]{:S(2)}) collective-permute-start(bf16[512,128]{1,0:T(8,128)(2,1)S(1)} %bitcast.8), channel_id=1, source_target_pairs={{0,1},{1,0},{2,3},{3,2},{4,5},{5,4},{6,7},{7,6},{8,9},{9,8},{10,11... | collective-permute-start | bytes 393224 | tf_op jit(solution)/shard_map/ppermute | solution.py:409
  45.4 3.7 %collective-permute-start.10 = (bf16[512,128]{1,0:T(8,128)(2,1)S(1)}, bf16[512,128]{1,0:T(8,128)(2,1)S(1)}, u32[]{:S(2)}, u32[]{:S(2)}) collective-permute-start(bf16[512,128]{1,0:T(8,128)(2,1)S(1)} %bitcast.11), channel_id=1, source_target_pairs={{0,1},{1,0},{2,3},{3,2},{4,5},{5,4},{6,7},{7,6},{8,9},{9,8},{10,11... | collective-permute-start | bytes 393224 | tf_op jit(solution)/shard_map/ppermute | solution.py:409
  45.5 4.3 %collective-permute-start.6 = (bf16[512,128]{1,0:T(8,128)(2,1)S(1)}, bf16[512,128]{1,0:T(8,128)(2,1)S(1)}, u32[]{:S(2)}, u32[]{:S(2)}) collective-permute-start(bf16[512,128]{1,0:T(8,128)(2,1)S(1)} %collective-permute-done.refs_1_), channel_id=1, source_target_pairs={{0,1},{1,0},{2,3},{3,2},{4,5},{5,4},{6,7},{7,6},{8,9},{9,8},{10,11... | collective-permute-start | bytes 393224 | tf_op jit(solution)/shard_map/ppermute | solution.py:409
  46.0 15.8 %collective-permute-start.4 = (bf16[512,128]{1,0:T(8,128)(2,1)S(1)}, bf16[512,128]{1,0:T(8,128)(2,1)S(1)}, u32[]{:S(2)}, u32[]{:S(2)}) collective-permute-start(bf16[512,128]{1,0:T(8,128)(2,1)S(1)} %collective-permute-done.2.refs_2_), channel_id=1, source_target_pairs={{0,2},{1,3},{2,4},{3,5},{4,6},{5,7},{6,0},{7,1},{8,10},{9,11},{10,... | collective-permute-start | bytes 393224 | tf_op jit(solution)/shard_map/ppermute | solution.py:409
  47.6 16.5 %collective-permute-start.9 = (bf16[512,128]{1,0:T(8,128)(2,1)S(1)}, bf16[512,128]{1,0:T(8,128)(2,1)S(1)}, u32[]{:S(2)}, u32[]{:S(2)}) collective-permute-start(bf16[512,128]{1,0:T(8,128)(2,1)S(1)} %collective-permute-done.3.refs_10_), channel_id=1, source_target_pairs={{0,2},{1,3},{2,4},{3,5},{4,6},{5,7},{6,0},{7,1},{8,10},{9,11},{10,... | collective-permute-start | bytes 393224 | tf_op jit(solution)/shard_map/ppermute | solution.py:409
  49.1 19.6 %copy-start.9 = (bf16[512,128]{1,0:T(8,128)(2,1)}, bf16[512,128]{1,0:T(8,128)(2,1)S(1)}, u32[]{:S(2)}) copy-start(bf16[512,128]{1,0:T(8,128)(2,1)S(1)} %collective-permute-done.5.refs_4_) | copy-start | bytes 393220
  49.1 19.6 %collective-permute-start.11 = (bf16[512,128]{1,0:T(8,128)(2,1)S(1)}, bf16[512,128]{1,0:T(8,128)(2,1)S(1)}, u32[]{:S(2)}, u32[]{:S(2)}) collective-permute-start(bf16[512,128]{1,0:T(8,128)(2,1)S(1)} %collective-permute-done.1.refs_9_), channel_id=1, source_target_pairs={{0,1},{1,0},{2,3},{3,2},{4,5},{5,4},{6,7},{7,6},{8,9},{9,8},{10,11... | collective-permute-start | bytes 393224 | tf_op jit(solution)/shard_map/ppermute | solution.py:409
  49.2 19.5 %copy-start.10 = (bf16[512,128]{1,0:T(8,128)(2,1)}, bf16[512,128]{1,0:T(8,128)(2,1)S(1)}, u32[]{:S(2)}) copy-start(bf16[512,128]{1,0:T(8,128)(2,1)S(1)} %collective-permute-done.10.refs_12_) | copy-start | bytes 393220
  49.2 22.0 %collective-permute-start.7 = (bf16[512,128]{1,0:T(8,128)(2,1)S(1)}, bf16[512,128]{1,0:T(8,128)(2,1)S(1)}, u32[]{:S(2)}, u32[]{:S(2)}) collective-permute-start(bf16[512,128]{1,0:T(8,128)(2,1)S(1)} %collective-permute-done.2.refs_2_), channel_id=1, source_target_pairs={{0,1},{1,0},{2,3},{3,2},{4,5},{5,4},{6,7},{7,6},{8,9},{9,8},{10,11... | collective-permute-start | bytes 393224 | tf_op jit(solution)/shard_map/ppermute | solution.py:409
  49.8 19.0 %copy-start.11 = (bf16[512,128]{1,0:T(8,128)(2,1)}, bf16[512,128]{1,0:T(8,128)(2,1)S(1)}, u32[]{:S(2)}) copy-start(bf16[512,128]{1,0:T(8,128)(2,1)S(1)} %collective-permute-done.6.refs_5_) | copy-start | bytes 393220
  49.8 22.0 %collective-permute-start.12 = (bf16[512,128]{1,0:T(8,128)(2,1)S(1)}, bf16[512,128]{1,0:T(8,128)(2,1)S(1)}, u32[]{:S(2)}, u32[]{:S(2)}) collective-permute-start(bf16[512,128]{1,0:T(8,128)(2,1)S(1)} %collective-permute-done.3.refs_10_), channel_id=1, source_target_pairs={{0,1},{1,0},{2,3},{3,2},{4,5},{5,4},{6,7},{7,6},{8,9},{9,8},{10,11... | collective-permute-start | bytes 393224 | tf_op jit(solution)/shard_map/ppermute | solution.py:409
  61.8 6.9 %copy-start.12 = (bf16[512,128]{1,0:T(8,128)(2,1)}, bf16[512,128]{1,0:T(8,128)(2,1)S(1)}, u32[]{:S(2)}) copy-start(bf16[512,128]{1,0:T(8,128)(2,1)S(1)} %collective-permute-done.4.refs_3_) | copy-start | bytes 393220
  61.8 10.6 %collective-permute-start.8 = (bf16[512,128]{1,0:T(8,128)(2,1)S(1)}, bf16[512,128]{1,0:T(8,128)(2,1)S(1)}, u32[]{:S(2)}, u32[]{:S(2)}) collective-permute-start(bf16[512,128]{1,0:T(8,128)(2,1)S(1)} %collective-permute-done.4.refs_3_), channel_id=1, source_target_pairs={{0,1},{1,0},{2,3},{3,2},{4,5},{5,4},{6,7},{7,6},{8,9},{9,8},{10,11... | collective-permute-start | bytes 393224 | tf_op jit(solution)/shard_map/ppermute | solution.py:409
  64.1 8.2 %collective-permute-start.13 = (bf16[512,128]{1,0:T(8,128)(2,1)S(1)}, bf16[512,128]{1,0:T(8,128)(2,1)S(1)}, u32[]{:S(2)}, u32[]{:S(2)}) collective-permute-start(bf16[512,128]{1,0:T(8,128)(2,1)S(1)} %collective-permute-done.9.refs_11_), channel_id=1, source_target_pairs={{0,1},{1,0},{2,3},{3,2},{4,5},{5,4},{6,7},{7,6},{8,9},{9,8},{10,11... | collective-permute-start | bytes 393224 | tf_op jit(solution)/shard_map/ppermute | solution.py:409
  68.7 11.6 %collective-permute-start.19 = (bf16[80,128]{1,0:T(8,128)(2,1)}, bf16[80,128]{1,0:T(8,128)(2,1)S(1)}, u32[]{:S(2)}, u32[]{:S(2)}) collective-permute-start(bf16[80,128]{1,0:T(8,128)(2,1)} %shard_map.163.refs_4_), channel_id=1, source_target_pairs={{0,24},{8,0},{16,8},{24,16},{1,25},{9,1},{17,9},{25,17},{2,26},{10... | collective-permute-start | bytes 61448 | tf_op jit(solution)/shard_map/ppermute | solution.py:409
  71.2 9.1 %collective-permute-start.18 = (bf16[80,128]{1,0:T(8,128)(2,1)}, bf16[80,128]{1,0:T(8,128)(2,1)S(1)}, u32[]{:S(2)}, u32[]{:S(2)}) collective-permute-start(bf16[80,128]{1,0:T(8,128)(2,1)} %shard_map.163.refs_4_), channel_id=1, source_target_pairs={{0,16},{8,24},{16,0},{24,8},{1,17},{9,25},{17,1},{25,9},{2,18},{10... | collective-permute-start | bytes 61448 | tf_op jit(solution)/shard_map/ppermute | solution.py:409
  71.8 8.6 %collective-permute-start.17 = (bf16[80,128]{1,0:T(8,128)(2,1)}, bf16[80,128]{1,0:T(8,128)(2,1)S(1)}, u32[]{:S(2)}, u32[]{:S(2)}) collective-permute-start(bf16[80,128]{1,0:T(8,128)(2,1)} %shard_map.163.refs_4_), channel_id=1, source_target_pairs={{0,8},{8,16},{16,24},{24,0},{1,9},{9,17},{17,25},{25,1},{2,10},{10... | collective-permute-start | bytes 61448 | tf_op jit(solution)/shard_map/ppermute | solution.py:409
  76.5 4.3 %collective-permute-start.16 = (bf16[64,128]{1,0:T(8,128)(2,1)}, bf16[64,128]{1,0:T(8,128)(2,1)S(1)}, u32[]{:S(2)}, u32[]{:S(2)}) collective-permute-start(bf16[64,128]{1,0:T(8,128)(2,1)} %shard_map.162.refs_0_), channel_id=1, source_target_pairs={{0,24},{8,0},{16,8},{24,16},{1,25},{9,1},{17,9},{25,17},{2,26},{10... | collective-permute-start | bytes 49160 | tf_op jit(solution)/shard_map/ppermute | solution.py:409
  78.8 3.9 %collective-permute-start.15 = (bf16[64,128]{1,0:T(8,128)(2,1)}, bf16[64,128]{1,0:T(8,128)(2,1)S(1)}, u32[]{:S(2)}, u32[]{:S(2)}) collective-permute-start(bf16[64,128]{1,0:T(8,128)(2,1)} %shard_map.162.refs_0_), channel_id=1, source_target_pairs={{0,16},{8,24},{16,0},{24,8},{1,17},{9,25},{17,1},{25,9},{2,18},{10... | collective-permute-start | bytes 49160 | tf_op jit(solution)/shard_map/ppermute | solution.py:409
  80.4 4.8 %collective-permute-start.14 = (bf16[64,128]{1,0:T(8,128)(2,1)}, bf16[64,128]{1,0:T(8,128)(2,1)S(1)}, u32[]{:S(2)}, u32[]{:S(2)}) collective-permute-start(bf16[64,128]{1,0:T(8,128)(2,1)} %shard_map.162.refs_0_), channel_id=1, source_target_pairs={{0,8},{8,16},{16,24},{24,0},{1,9},{9,17},{17,25},{25,1},{2,10},{10... | collective-permute-start | bytes 49160 | tf_op jit(solution)/shard_map/ppermute | solution.py:409
  87.4 11.8 %all-to-all-start.2 = ((bf16[8,96,128]{2,1,0:T(8,128)(2,1)}), bf16[8,96,128]{2,1,0:T(8,128)(2,1)S(1)}, u32[]{:S(2)}, u32[]{:S(2)}) async-start(bf16[8,96,128]{2,1,0:T(8,128)(2,1)} %shard_map.164), calls=%async_computation.2 | async-start | bytes 393216 | tf_op jit(solution)/shard_map/all_to_all | solution.py:404
  (16 other events, 44.9 us)

commit v7 on v5

--- a/solution.py
+++ b/solution.py
@@ -33,41 +33,100 @@
     return lax.dot_general(a, b, NT, preferred_element_type=F32)
 
 
-def project_kernel(units, series_ref, cot_ref, w_in_ref, w_out_ref, one_ref, two_ref, out_ref):
-    count, block, width = series_ref.shape
+def lanes_of(field):
+    return lax.broadcasted_iota(jnp.int32, field.shape, field.ndim - 1)
+
+
+def turned(field, shift):
+    return pltpu.roll(field, shift, field.ndim - 1)
+
+
+def earlier_parts(parts, j, before):
+    result = []
+    for held in parts:
+        result.append(jnp.where(lanes_of(held) < j, turned(before, j), turned(held, j)))
+        before = held
+    return result
+
+
+def later_parts(parts, j, behind):
+    result = []
+    for held, following in zip(parts, parts[1:] + [behind]):
+        edge = lanes_of(held) >= W - j
+        result.append(jnp.where(edge, turned(following, W - j), turned(held, W - j)))
+    return result
+
+
+def gate_taps(taps_ref):
+    width = taps_ref.shape[1] // 3
+    rows = jnp.concatenate([taps_ref[:, 2 * width :], jnp.zeros((5, width), F32)], axis=0)
+    cols = jnp.concatenate([rows] * (width // 8), axis=0).T
+    return [cols[:, j : j + 1] for j in range(3)]
+
+
+def gate_local(second, cols):
+    zeros = jnp.zeros_like(second[0])
+    total = [cols[0] * held for held in second]
+    for j in (1, 2):
+        moved = earlier_parts(second, j, zeros)
+        total = [have + cols[j] * held for have, held in zip(total, moved)]
+    return total
+
+
+def project_kernel(units, series_ref, cot_ref, w_in_ref, w_out_ref, taps_ref, one_ref, two_ref, out_ref):
+    _, block, width = series_ref.shape
     group = width // units
     parts = block // W
     w_in_t = w_in_ref[...].T
     w_out = w_out_ref[...]
-    for e in range(count):
-        for part in range(parts):
-            rows = pl.ds(part * W, W)
-            proj = dot_nt(w_in_t, series_ref[e, rows, :]).astype(BF16)
-            d_prod = dot_nt(w_out, cot_ref[e, rows, :]).astype(BF16)
-            for kind in range(4):
-                field = proj[kind * width : (kind + 1) * width] if kind < 3 else d_prod
-                out_ref[
-                    e * units : (e + 1) * units,
-                    (kind * parts + part) * group : (kind * parts + part + 1) * group,
-                    :,
-                ] = field.reshape(units, group, W)
+    proj = [dot_nt(w_in_t, series_ref[0, p * W : (p + 1) * W, :]) for p in range(parts)]
+    d_prod = [dot_nt(w_out, cot_ref[0, p * W : (p + 1) * W, :]) for p in range(parts)]
+    second = [held[2 * width :] for held in proj]
+    gate = gate_local(second, gate_taps(taps_ref))
+    for p in range(parts):
+        fields = [proj[p][:width], proj[p][width : 2 * width], d_prod[p] * gate[p]]
+        for kind, field in enumerate(fields):
+            at = (kind * parts + p) * group
+            out_ref[:, at : at + group, :] = field.astype(BF16).reshape(units, group, W)
+
+    lane = lanes_of(second[0])
+    edges = jnp.where((lane >= 128) & (lane < 130), turned(second[-1], 130), 0.0)
+    edges = jnp.where((lane >= 130) & (lane < 132), turned(d_prod[0], 130), edges)
     lines = [
-        ref[:, part * W : (part + 1) * W] for ref in (one_ref, two_ref) for part in range(parts)
+        ref[:, q * width : (q + 1) * width]
+        for ref in (one_ref, two_ref)
+        for q in range(block // width)
     ]
     repeat = units // one_ref.shape[0]
-    start = 4 * parts * group
-    spare = jnp.zeros((out_ref.shape[1] - start - len(lines), W), F32)
     for u in range(units):
         row = u // repeat
-        field = jnp.concatenate([line[row : row + 1] for line in lines] + [spare], axis=0)
-        for e in range(count):
-            out_ref[e * units + u, start:, :] = field.astype(BF16)
+        held = jnp.concatenate([line[row : row + 1] for line in lines], axis=0)
+        held = jnp.concatenate([held, jnp.zeros((held.shape[0], W - width), F32)], axis=1)
+        held = jnp.concatenate([held, jnp.zeros((16 - held.shape[0], W), F32)], axis=0)
+        edge = edges[u * group : (u + 1) * group]
+        if group < 16:
+            edge = jnp.concatenate([edge, jnp.zeros((16 - group, W), F32)], axis=0)
+        out_ref[u, 3 * parts * group :, :] = (held + edge).astype(BF16)
+
+
+def gate_kernel(series_ref, cot_ref, w_in_ref, w_out_ref, taps_ref, out_ref):
+    _, block, width = series_ref.shape
+    parts = block // W
+    w_two_t = w_in_ref[:, 2 * width :].T
+    w_out = w_out_ref[...]
+    second = [dot_nt(w_two_t, series_ref[0, p * W : (p + 1) * W, :]) for p in range(parts)]
+    gate = gate_local(second, gate_taps(taps_ref))
+    for p in range(parts):
+        out_ref[0, p] = second[p]
+        out_ref[1, p] = gate[p]
+        out_ref[2, p] = dot_nt(w_out, cot_ref[0, p * W : (p + 1) * W, :])
 
 
 def build_toeplitz(fields_ref, start, toep_ref, base_ref):
     sources = fields_ref.shape[0]
     _, blocks, _, _ = toep_ref.shape
-    parts = blocks // sources
+    width = W // 2
+    slots = blocks // sources * W // width
     length = blocks * W
     half = W // 2
     row = lax.broadcasted_iota(jnp.int32, (8, length), 0)
@@ -76,10 +135,10 @@
     for m in range(2):
         for s in range(sources):
             lines = fields_ref[s, start : start + 16, :].astype(F32)
-            for p in range(parts):
-                at = (s * parts + p) * W
-                base_ref[:, at : at + W] = jnp.broadcast_to(
-                    lines[m * parts + p : m * parts + p + 1, :], (8, W)
+            for q in range(slots):
+                at = (s * slots + q) * width
+                base_ref[:, at : at + width] = jnp.broadcast_to(
+                    lines[m * slots + q : m * slots + q + 1, :width], (8, width)
                 )
         base = base_ref[...]
         for bit in (1, 2, 4):
@@ -121,7 +180,7 @@
 
 
 def pick(ref, kind, received):
-    rows = received // 4
+    rows = received
     field = ref[:, kind * rows : (kind + 1) * rows, :]
     return field.reshape(field.shape[0] * rows, W).astype(F32)
 
@@ -138,14 +197,16 @@
     toep_ref,
     base_ref,
 ):
-    sources, received, _ = out_ref.shape
-    build_toeplitz(fields_ref, received, toep_ref, base_ref)
+    sources, _, _ = out_ref.shape
+    _, rows, _ = kept_ref.shape
+    each = rows // sources
+    start = 3 * each
+    build_toeplitz(fields_ref, start, toep_ref, base_ref)
     width = taps_ref.shape[1] // 3
     group = width // units
-    rows = sources * received // 4
     blocks = rows // group
-    f = lax.rem(lax.axis_index("seq"), units)
-    mine = own_lanes(f, group, width)
+    u = lax.rem(lax.axis_index("seq"), units)
+    mine = own_lanes(u, group, width)
 
     def column(values):
         col = jnp.sum(jnp.where(mine, values, 0.0), axis=1, keepdims=True)
@@ -184,7 +245,7 @@
     skip_two = column(skip_two_ref[...])
 
     def short(kind):
-        field = pick(fields_ref, kind, received)
+        field = pick(fields_ref, kind, each)
         total = scaled(field, tap[kind][0])
         for j in (1, 2):
             total = total + scaled(earlier(field, j, group), tap[kind][j])
@@ -196,10 +257,7 @@
         return low
 
     def send(kind, field):
-        part_rows = received // 4
-        out_ref[:, kind * part_rows : (kind + 1) * part_rows, :] = field.astype(BF16).reshape(
-            sources, part_rows, W
-        )
+        out_ref[:, kind * each : (kind + 1) * each, :] = field.astype(BF16).reshape(sources, each, W)
 
     def send_back(kind, field):
         total = scaled(field, tap[kind][0])
@@ -207,18 +265,31 @@
             total = total + scaled(later(field, j, group), tap[kind][j])
         send(kind, total)
 
+    edges = fields_ref[:, start : start + 16, :].astype(F32)[:, :group]
+    none = jnp.zeros((1, group, W), F32)
+    before = jnp.concatenate([none, edges[:-1]], axis=0)
+    following = jnp.concatenate([edges[1:], none], axis=0)
+    lane = lanes_of(edges)
+    reach = tap[2][2] * turned(before, 128)
+    reach = reach + jnp.where(lane < 1, tap[2][1] * turned(before, 127), 0.0)
+    reach = jnp.where(lane < 2, turned(edges, 126) * reach, 0.0)
+    grad_two = pick(fields_ref, 2, each).reshape(sources, each, W)
+    grad_two = jnp.concatenate([grad_two[:, :group] + reach, grad_two[:, group:]], axis=1)
+    grad_two = grad_two.reshape(rows, W)
+
     value = short(0)
     y_one = causal(0, keep(0, value)) + scaled(value, skip_one)
     gate_one = short(1)
     mid = gate_one * y_one
     y_two = causal(1, keep(1, mid)) + scaled(mid, skip_two)
-    gate_two = short(2)
-    send(3, gate_two * y_two)
-    d_product = pick(fields_ref, 3, received)
-    grad_two = d_product * gate_two
-    d_gate_two = d_product * y_two
-    keep(6, d_gate_two)
-    send_back(2, d_gate_two)
+    send(2, y_two)
+    heads = y_two.reshape(sources, each, W)[1:, :group]
+    heads = jnp.concatenate([heads, none], axis=0)
+    edges = jnp.where(lane < 4, turned(following, 128) * turned(heads, 2), 0.0)
+    edges = jnp.where(lane < 2, turned(before, 128), edges)
+    if group < 16:
+        edges = jnp.concatenate([edges, jnp.zeros((sources, 16 - group, W), F32)], axis=1)
+    out_ref[:, start:, :] = edges.astype(BF16)
     d_mid = anticausal(1, keep(3, grad_two)) + scaled(grad_two, skip_two)
     grad_one = d_mid * gate_one
     d_gate_one = d_mid * y_one
@@ -236,7 +307,7 @@
     width = out_ref.shape[1]
     blocks = length // W
     group = rows // blocks
-    received = 4 * rows // sources
+    each = rows // sources
     half = W // 2
     lines = length // width
 
@@ -278,31 +349,58 @@
         small[n // units] += jnp.sum(jnp.where(mine, col, 0.0), axis=0, keepdims=True)
 
     for j in range(3):
-        for kind in range(3):
-            field = pick(fields_ref, kind, received)
-            put(3 * j + kind, kept_ref[4 + kind].astype(F32) * earlier(field, j, group))
+        for kind in range(2):
+            field = pick(fields_ref, kind, each)
+            put(2 * j + kind, kept_ref[4 + kind].astype(F32) * earlier(field, j, group))
     for m in range(2):
-        put(9 + m, kept_ref[2 + m].astype(F32) * kept_ref[m].astype(F32))
+        put(6 + m, kept_ref[2 + m].astype(F32) * kept_ref[m].astype(F32))
     out_ref[2 * lines : 2 * lines + 16, :] = jnp.concatenate(small, axis=0)
 
 
-def received_field(in_ref, units, group, parts, e, kind, part):
+def received_field(in_ref, units, group, parts, kind, part):
     at = (kind * parts + part) * group
-    return in_ref[e * units : (e + 1) * units, at : at + group, :].reshape(units * group, W)
-
-
-def partial_kernel(units, in_ref, series_ref, cot_ref, own_ref, part_ref):
-    count, block, width = series_ref.shape
+    return in_ref[:, at : at + group, :].reshape(units * group, W)
+
+
+def partial_kernel(
+    units, in_ref, held_ref, taps_ref, series_ref, cot_ref, own_ref, part_ref, product_ref, grads_ref
+):
+    _, block, width = series_ref.shape
     group = width // units
     parts = block // W
+    cols = gate_taps(taps_ref)
+    edges = in_ref[:, 3 * parts * group :, :].astype(F32)[:, :group].reshape(width, W)
+    lane = lanes_of(edges)
+    second = [held_ref[0, p] for p in range(parts)]
+    gate = [held_ref[1, p] for p in range(parts)]
+    gate[0] += jnp.where(lane < 2, cols[2] * edges, 0.0)
+    gate[0] += jnp.where(lane < 1, cols[1] * turned(edges, W - 1), 0.0)
+    around = turned(edges, W - 2)
+    y_two = [received_field(in_ref, units, group, parts, 2, p).astype(F32) for p in range(parts)]
+    d_gate = [held_ref[2, p] * y_two[p] for p in range(parts)]
+    grads = [cols[0] * held for held in d_gate]
+    for j in (1, 2):
+        grads = [
+            have + cols[j] * held for have, held in zip(grads, later_parts(d_gate, j, around))
+        ]
     w_in_part = 0.0
     w_out_part = 0.0
-    for e in range(count):
-        for part in range(parts):
-            rows = pl.ds(part * W, W)
-            field = [received_field(in_ref, units, group, parts, e, k, part) for k in range(4)]
-            w_in_part += dot(jnp.concatenate(field[:3], axis=0), series_ref[e, rows, :])
-            w_out_part += dot(field[3], cot_ref[e, rows, :])
+    for p in range(parts):
+        rows = pl.ds(p * W, W)
+        product = (gate[p] * y_two[p]).astype(BF16)
+        product_ref[p] = product
+        low = grads[p].astype(BF16)
+        grads_ref[p] = low
+        field = [received_field(in_ref, units, group, parts, k, p) for k in range(2)] + [low]
+        w_in_part += dot(jnp.concatenate(field, axis=0), series_ref[0, rows, :])
+        w_out_part += dot(product, cot_ref[0, rows, :])
+
+    small = jnp.zeros((width, width), F32)
+    for j in range(3):
+        moved = earlier_parts(second, j, around) if j else second
+        col = sum(jnp.sum(d * held, axis=1, keepdims=True) for d, held in zip(d_gate, moved))
+        small = jnp.where(lanes_of(small) == j, col, small)
+    small = small.T[0:3]
 
     weights = jnp.concatenate([w_in_part, w_out_part], axis=0)
     targets, sent, _ = part_ref.shape
@@ -310,8 +408,8 @@
     sources = in_ref.shape[0]
     lines = (own_ref.shape[0] - 16) // 2
     slots = lines // sources
-    small = -(-11 // units)
-    spare = jnp.zeros((sent - each - 2 * slots - small, width), F32)
+    rest = sent - each - 2 * slots - 4
+    spare = [jnp.zeros((rest, width), F32)] if rest else []
     for g in range(targets):
         s = g % sources
         part_ref[g] = jnp.concatenate(
@@ -319,26 +417,26 @@
                 weights[g * each : (g + 1) * each],
                 own_ref[s * slots : (s + 1) * slots, :],
                 own_ref[lines + s * slots : lines + (s + 1) * slots, :],
-                own_ref[2 * lines : 2 * lines + small, :],
-                spare,
-            ],
+                own_ref[2 * lines : 2 * lines + 1, :],
+                small,
+            ]
+            + spare,
             axis=0,
         ).astype(BF16)
 
 
-def output_kernel(units, in_ref, w_in_ref, w_out_ref, out_ref, d_series_ref):
-    count, block, width = out_ref.shape
+def output_kernel(units, in_ref, product_ref, grads_ref, w_in_ref, w_out_ref, out_ref, d_series_ref):
+    _, block, width = out_ref.shape
     group = width // units
     parts = block // W
     w_in = w_in_ref[...]
     w_out_t = w_out_ref[...].T
-    for e in range(count):
-        for part in range(parts):
-            rows = pl.ds(part * W, W)
-            field = [received_field(in_ref, units, group, parts, e, k, part) for k in range(4)]
-            out_ref[e, rows, :] = dot(w_out_t, field[3]).T.astype(BF16)
-            grads = jnp.concatenate(field[:3], axis=0)
-            d_series_ref[e, rows, :] = dot(w_in, grads).T.astype(BF16)
+    for p in range(parts):
+        rows = pl.ds(p * W, W)
+        out_ref[0, rows, :] = dot(w_out_t, product_ref[p]).T.astype(BF16)
+        field = [received_field(in_ref, units, group, parts, k, p) for k in range(2)]
+        grads = jnp.concatenate(field + [grads_ref[p]], axis=0)
+        d_series_ref[0, rows, :] = dot(w_in, grads).T.astype(BF16)
 
 
 def sum_kernel(in_ref, out_ref):
@@ -373,20 +471,20 @@
 
     row = lax.broadcasted_iota(jnp.int32, (units, width), 0)
     lane = lax.broadcasted_iota(jnp.int32, (units, width), 1)
-    small = []
-    for r in range(-(-11 // units)):
-        held = jnp.concatenate([sums[2 * slots + r : 2 * slots + r + 1] for sums in by_unit], axis=0)
-        turned = 0.0
-        for shift in range(units):
-            moved = pltpu.roll(held, shift * group, 1) if shift else held
-            moved = jnp.where(lane // group == row, moved, 0.0)
-            turned += pltpu.roll(moved, units - shift, 0) if shift else moved
-        small += [turned[n : n + 1] for n in range(units)]
+    held = jnp.concatenate([sums[2 * slots : 2 * slots + 1] for sums in by_unit], axis=0)
+    small = 0.0
+    for shift in range(units):
+        moved = pltpu.roll(held, shift * group, 1) if shift else held
+        moved = jnp.where(lane // group == row, moved, 0.0)
+        small += pltpu.roll(moved, units - shift, 0) if shift else moved
+    gate = sum(by_unit)[2 * slots + 1 : 2 * slots + 4]
     for j in range(3):
-        for kind in range(3):
-            taps_ref[j : j + 1, kind * width : (kind + 1) * width] = small[3 * j + kind]
-    skip_one_ref[...] = small[9]
-    skip_two_ref[...] = small[10]
+        for kind in range(2):
+            n = 2 * j + kind
+            taps_ref[j : j + 1, kind * width : (kind + 1) * width] = small[n : n + 1]
+    taps_ref[:, 2 * width :] = gate
+    skip_one_ref[...] = small[6:7]
+    skip_two_ref[...] = small[7:8]
 
 
 def weight_kernel(scale, in_ref, w_in_ref, w_out_ref):
@@ -409,21 +507,27 @@
     length = block * sources
     units = sources // count
     group = width // units
-    assert sources == count * units and units % filters == 0 and block % W == 0
+    assert count == 1 and units >= 8 and 2 * block // width <= 16 and units % filters == 0 and block % W == 0
     blocks = length // W
     rows = blocks * group
     scale = 1.0 / math.sqrt(count * copies * length)
     shape = jax.ShapeDtypeStruct
 
     devices = sources * copies
-    packed = 4 * (block // W) * group
+    packed = 3 * (block // W) * group + 16
     fields = call(
         functools.partial(project_kernel, units),
-        shape((sources, packed + 16, W), BF16),
-        flops=2 * count * block * width * 4 * width,
-        moved=8 * count * block * width * 4,
-    )(series, cotangent, w_in, w_out, filter_one, filter_two)
+        shape((sources, packed, W), BF16),
+        flops=2 * block * width * 4 * width,
+        moved=8 * block * width * 4,
+    )(series, cotangent, w_in, w_out, taps, filter_one, filter_two)
     fields = all_to_all(fields, "seq")
+    held = call(
+        gate_kernel,
+        shape((3, block // W, width, W), F32),
+        flops=2 * block * width * 2 * width,
+        moved=4 * 4 * block * width,
+    )(series, cotangent, w_in, w_out, taps)
 
     sent, kept = call(
         functools.partial(operator_kernel, units),
@@ -448,21 +552,25 @@
     )(fields, kept)
 
     each = 4 * width // devices
-    sent_rows = -(-(each + 2 * (block // width) + -(-11 // units)) // 16) * 16
-    partial = call(
+    sent_rows = -(-(each + 2 * (block // width) + 4) // 16) * 16
+    partial, product, grads = call(
         functools.partial(partial_kernel, units),
-        shape((devices, sent_rows, width), BF16),
-        flops=2 * count * block * width * 4 * width,
-        moved=2 * count * block * width * 6,
-    )(back, series, cotangent, own)
+        (
+            shape((devices, sent_rows, width), BF16),
+            shape((block // W, width, W), BF16),
+            shape((block // W, width, W), BF16),
+        ),
+        flops=2 * block * width * 4 * width,
+        moved=2 * block * width * 6,
+    )(back, held, taps, series, cotangent, own)
     partial = all_to_all(partial, ("dp", "seq"))
 
     output, d_series = call(
         functools.partial(output_kernel, units),
         (shape(series.shape, BF16), shape(series.shape, BF16)),
-        flops=2 * count * block * width * 4 * width,
-        moved=2 * count * block * width * 6,
-    )(back, w_in, w_out)
+        flops=2 * block * width * 4 * width,
+        moved=2 * block * width * 6,
+    )(back, product, grads, w_in, w_out)
 
     sums = call(
         sum_kernel,

time: 84.6 us -> 81.1 us (0.959)
  waiting for transfers between devices: 15.1 us -> 11.6 us
  blocking collectives: 37.2 us -> 34.3 us
  Pallas kernels: 23.6 us -> 26.4 us
    all_to_all x2, waiting for transfers between devices: 15.1 us -> 11.6 us  [all_to_all(): return lax.all_to_all(blocks, axis, split_axis=0, concat_axis=0, tiled=True)]
    pallas_call x2 -> x3, Pallas kernels: 4.3 us -> 7.61 us  [the longest x1 2.89 us: shards(): call(functools.partial(partial_kernel, units), (shape((devices, sent_rows...]
    all_to_all x2, blocking collectives: 37.2 us -> 34.3 us  [all_to_all(): return lax.all_to_all(blocks, axis, split_axis=0, concat_axis=0, tiled=True)]
  transfers between devices with their start and end apart: 2 -> 2, of which waited for: 2 -> 2; matrix products, arithmetic and copies ran while one was open for 0% -> 0% of each run, Pallas kernels for 10% -> 13%
where the time goes in v7:
time: 81.1 us; the launch traced here: 80.5 us
  blocking collectives  34.3 us (42%)
  Pallas kernels  26.4 us (33%)
  waiting for transfers between devices  11.6 us (14%)
  starting transfers between devices  6.03 us (7%)
  local copies, waits for them, and re-layouts  1.41 us (2%)
    all_to_all x2, blocking collectives, all_to_all(): return lax.all_to_all(blocks, axis, split_axis=0, concat_axis=0, tiled=True)  34.3 us
    all_to_all x2, waiting for transfers between devices, all_to_all(): return lax.all_to_all(blocks, axis, split_axis=0, concat_axis=0, tiled=True)  11.6 us
    pallas_call x1, Pallas kernels, shards(): call(functools.partial(operator_kernel, units), (shape((sources, packed,...  7.42 us
    all_to_all x2, starting transfers between devices, all_to_all(): return lax.all_to_all(blocks, axis, split_axis=0, concat_axis=0, tiled=True)  6.03 us
    pallas_call x1, Pallas kernels, shards(): call(functools.partial(gradient_kernel, units), shape((2 * (length // wid...  4.17 us
    pallas_call x1, Pallas kernels, shards(): call(functools.partial(partial_kernel, units), (shape((devices, sent_rows...  2.89 us
    pallas_call x1, Pallas kernels, shards(): call(gate_kernel, shape((3, block // W, width, W), F32), flops=2 * block...  2.39 us
    pallas_call x1, Pallas kernels, shards(): call(functools.partial(project_kernel, units), shape((sources, packed, W)...  2.32 us
  transfers between devices with their start and end apart: 2, of which 2 were waited for; matrix products, arithmetic and copies ran while one was open for 0% of the time, Pallas kernels for 13%

profile of v7, /device:TPU:0, one launch (start us, length us, event | category | flops | bytes accessed | tf_op | source)
XLA Modules:
  0.0 80.5 jit_solution(16747985600434156320)
XLA Ops:
  0.6 2.3 %shard_map.160 = bf16[8,112,256]{2,1,0:T(8,128)(2,1)} custom-call(bf16[1,512,128]{2,1,0:T(8,128)(2,1)} %series_ref.5, bf16[1,512,128]{2,1,0:T(8,128)(2,1)} %cot_ref.5, bf16[128,384]{1,0:T(8,128)(2,1)} %w_in_ref.5, bf16[128,128]{1,0:T(8,128)(2,1)} %w_out_ref.5, f32[3,384]{1,0:T(4,128)} %taps_ref.7, f32[8,512]{1,0:T(8,128)} %one_ref.1, f32[8,512]{1,0:T(8,128)} %two_ref.1), custom_call_target="tpu_custom_call" | custom-call | flops 67108864 | bytes 2097152 | tf_op jit(solution)/shard_map/pallas_call | solution.py:518
  3.0 20.4 %all_to_all.20.fields_ref = bf16[8,112,256]{2,1,0:T(8,128)(2,1)} all-to-all(bf16[8,112,256]{2,1,0:T(8,128)(2,1)} %shard_map.160), channel_id=1, replica_groups=mesh['dp'=4,'seq'=8] {'seq'}, dimensions={0} | all-to-all | bytes 917504 | tf_op jit(solution)/shard_map/all_to_all | solution.py:499
  23.3 7.4 %shard_map.161 = (bf16[8,112,256]{2,1,0:T(8,128)(2,1)}, bf16[7,256,256]{2,1,0:T(8,128)(2,1)}) custom-call(bf16[8,112,256]{2,1,0:T(8,128)(2,1)} %all_to_all.20.fields_ref, f32[3,384]{1,0:T(4,128)} %taps_ref.7, f32[1,128]{1,0:T(1,128)} %bitcast.4, f32[1,128]{1,0:T(1,128)} %bitcast.5), custom_call_target="tpu_custom_call" | custom-call | flops 2147483648 | bytes 8388608 | tf_op jit(solution)/shard_map/pallas_call | solution.py:532
  30.8 3.5 %all-to-all-start.1 = ((bf16[8,112,256]{2,1,0:T(8,128)(2,1)}), bf16[8,112,256]{2,1,0:T(8,128)(2,1)S(1)}, u32[]{:S(2)}, u32[]{:S(2)}) async-start(bf16[8,112,256]{2,1,0:T(8,128)(2,1)} %get-tuple-element.23), calls=%async_computation.1 | async-start | bytes 917504 | tf_op jit(solution)/shard_map/all_to_all | solution.py:499
  34.2 2.4 %shard_map.162.held_ref = f32[3,2,128,256]{3,2,1,0:T(8,128)} custom-call(bf16[1,512,128]{2,1,0:T(8,128)(2,1)} %series_ref.5, bf16[1,512,128]{2,1,0:T(8,128)(2,1)} %cot_ref.5, bf16[128,384]{1,0:T(8,128)(2,1)} %w_in_ref.5, bf16[128,128]{1,0:T(8,128)(2,1)} %w_out_ref.5, f32[3,384]{1,0:T(4,128)} %taps_ref.7), custom_call_target="tpu_custom_call" | custom-call | flops 33554432 | bytes 1048576 | tf_op jit(solution)/shard_map/pallas_call | solution.py:525
  36.6 4.2 %shard_map.163.own_ref = f32[80,128]{1,0:T(8,128)} custom-call(bf16[8,112,256]{2,1,0:T(8,128)(2,1)} %all_to_all.20.fields_ref, bf16[7,256,256]{2,1,0:T(8,128)(2,1)} %get-tuple-element.24.kept_ref), custom_call_target="tpu_custom_call" | custom-call | flops 1073741824 | bytes 2097152 | tf_op jit(solution)/shard_map/pallas_call | solution.py:546
  40.8 7.3 %all-to-all-done.1.in_ref = bf16[8,112,256]{2,1,0:T(8,128)(2,1)S(1)} async-done(((bf16[8,112,256]{2,1,0:T(8,128)(2,1)}), bf16[8,112,256]{2,1,0:T(8,128)(2,1)S(1)}, u32[]{:S(2)}, u32[]{:S(2)}) %all-to-all-start.1) | async-done | bytes 458784 | tf_op jit(solution)/shard_map/all_to_all | solution.py:499
  48.1 0.0 copy-start
  48.1 0.8 copy-done
  48.9 2.9 %shard_map.164 = (bf16[32,32,128]{2,1,0:T(8,128)(2,1)}, bf16[2,128,256]{2,1,0:T(8,128)(2,1)}, bf16[2,128,256]{2,1,0:T(8,128)(2,1)}) custom-call(bf16[8,112,256]{2,1,0:T(8,128)(2,1)} %copy-done, f32[3,2,128,256]{3,2,1,0:T(8,128)} %shard_map.162.held_ref, f32[3,384]{1,0:T(4,128)} %taps_ref.7, bf16[1,512,128]{2,1,0:T(8,128)(2,1)} %series_ref.5, ...), custom_call_target="tpu_custom_call" | custom-call | flops 67108864 | bytes 786432 | tf_op jit(solution)/shard_map/pallas_call | solution.py:556
  51.8 14.0 %all_to_all.21.in_ref = bf16[32,32,128]{2,1,0:T(8,128)(2,1)} all-to-all(bf16[32,32,128]{2,1,0:T(8,128)(2,1)} %get-tuple-element.29), channel_id=1, replica_groups=mesh['dp'=4,'seq'=8] {'dp','seq'}, dimensions={0} | all-to-all | bytes 524288 | tf_op jit(solution)/shard_map/all_to_all | solution.py:499
  65.7 1.6 %shard_map.166 = bf16[32,16,128]{2,1,0:T(8,128)(2,1)} custom-call(bf16[32,32,128]{2,1,0:T(8,128)(2,1)} %all_to_all.21.in_ref), custom_call_target="tpu_custom_call" | custom-call | flops 65536 | bytes 262144 | tf_op jit(solution)/shard_map/pallas_call | solution.py:575
  67.4 2.6 %all-to-all-start.3 = ((bf16[32,16,128]{2,1,0:T(8,128)(2,1)}), bf16[32,16,128]{2,1,0:T(8,128)(2,1)S(1)}, u32[]{:S(2)}, u32[]{:S(2)}) async-start(bf16[32,16,128]{2,1,0:T(8,128)(2,1)} %shard_map.166), calls=%async_computation.3 | async-start | bytes 262144 | tf_op jit(solution)/shard_map/all_to_all | solution.py:499
  70.0 2.2 %shard_map.165 = (bf16[1,512,128]{2,1,0:T(8,128)(2,1)}, bf16[1,512,128]{2,1,0:T(8,128)(2,1)}) custom-call(bf16[8,112,256]{2,1,0:T(8,128)(2,1)} %copy-done, bf16[2,128,256]{2,1,0:T(8,128)(2,1)} %get-tuple-element.25.product_ref, bf16[2,128,256]{2,1,0:T(8,128)(2,1)} %get-tuple-element.26.grads_ref, bf16[128,384]{1,0:T(8,128)(2,1)} %w_in_ref.5, ...), custom_call_target="tpu_custom_call" | custom-call | flops 67108864 | bytes 786432 | tf_op jit(solution)/shard_map/pallas_call | solution.py:568
  72.2 1.7 %shard_map.168 = (f32[8,512]{1,0:T(8,128)}, f32[8,512]{1,0:T(8,128)}, f32[3,384]{1,0:T(4,128)}, f32[1,128]{1,0:T(1,128)}, f32[1,128]{1,0:T(1,128)}) custom-call(bf16[32,32,128]{2,1,0:T(8,128)(2,1)} %all_to_all.21.in_ref), custom_call_target="tpu_custom_call" | custom-call | flops 131072 | bytes 524288 | tf_op jit(solution)/shard_map/pallas_call | solution.py:583
  73.8 4.3 %all-to-all-done.3.in_ref = bf16[32,16,128]{2,1,0:T(8,128)(2,1)S(1)} async-done(((bf16[32,16,128]{2,1,0:T(8,128)(2,1)}), bf16[32,16,128]{2,1,0:T(8,128)(2,1)S(1)}, u32[]{:S(2)}, u32[]{:S(2)}) %all-to-all-start.3) | async-done | bytes 131104 | tf_op jit(solution)/shard_map/all_to_all | solution.py:499
  78.1 0.0 copy-start.1
  78.1 0.6 copy-done.1
  78.8 1.7 %shard_map.167 = (f32[128,384]{1,0:T(8,128)}, f32[128,128]{1,0:T(8,128)}) custom-call(bf16[32,16,128]{2,1,0:T(8,128)(2,1)} %copy-done.1), custom_call_target="tpu_custom_call" | custom-call | flops 65536 | bytes 131072 | tf_op jit(solution)/shard_map/pallas_call | solution.py:595
Async XLA Ops:
  30.8 17.4 %all-to-all-start.1 = ((bf16[8,112,256]{2,1,0:T(8,128)(2,1)}), bf16[8,112,256]{2,1,0:T(8,128)(2,1)S(1)}, u32[]{:S(2)}, u32[]{:S(2)}) async-start(bf16[8,112,256]{2,1,0:T(8,128)(2,1)} %get-tuple-element.23), calls=%async_computation.1 | async-start | bytes 917504 | tf_op jit(solution)/shard_map/all_to_all | solution.py:499
  48.1 0.8 copy-start
  67.4 10.7 %all-to-all-start.3 = ((bf16[32,16,128]{2,1,0:T(8,128)(2,1)}), bf16[32,16,128]{2,1,0:T(8,128)(2,1)S(1)}, u32[]{:S(2)}, u32[]{:S(2)}) async-start(bf16[32,16,128]{2,1,0:T(8,128)(2,1)} %shard_map.166), calls=%async_computation.3 | async-start | bytes 262144 | tf_op jit(solution)/shard_map/all_to_all | solution.py:499
  78.1 0.6 copy-start.1

commit v8 on v7

--- a/solution.py
+++ b/solution.py
@@ -9,6 +9,7 @@
 from jax.sharding import PartitionSpec as P
 
 W = 256
+TILE = 128
 F32 = jnp.float32
 BF16 = jnp.bfloat16
 NT = (((1,), (1,)), ((), ()))
@@ -41,20 +42,27 @@
     return pltpu.roll(field, shift, field.ndim - 1)
 
 
+def tiles_of(parts):
+    return [held[:, at : at + TILE] for held in parts for at in range(0, W, TILE)]
+
+
+def parts_of(tiles):
+    each = W // TILE
+    return [jnp.concatenate(tiles[at : at + each], axis=1) for at in range(0, len(tiles), each)]
+
+
 def earlier_parts(parts, j, before):
-    result = []
-    for held in parts:
-        result.append(jnp.where(lanes_of(held) < j, turned(before, j), turned(held, j)))
-        before = held
-    return result
+    moved = [turned(tile, j) for tile in tiles_of([before] + parts)]
+    moved = moved[W // TILE - 1 :]
+    edge = lanes_of(moved[0]) < j
+    return parts_of([jnp.where(edge, ahead, tile) for ahead, tile in zip(moved, moved[1:])])
 
 
 def later_parts(parts, j, behind):
-    result = []
-    for held, following in zip(parts, parts[1:] + [behind]):
-        edge = lanes_of(held) >= W - j
-        result.append(jnp.where(edge, turned(following, W - j), turned(held, W - j)))
-    return result
+    moved = [turned(tile, TILE - j) for tile in tiles_of(parts + [behind])]
+    moved = moved[: len(moved) - W // TILE + 1]
+    edge = lanes_of(moved[0]) >= TILE - j
+    return parts_of([jnp.where(edge, following, tile) for tile, following in zip(moved, moved[1:])])
 
 
 def gate_taps(taps_ref):
@@ -125,52 +133,57 @@
 def build_toeplitz(fields_ref, start, toep_ref, base_ref):
     sources = fields_ref.shape[0]
     _, blocks, _, _ = toep_ref.shape
-    width = W // 2
-    slots = blocks // sources * W // width
-    length = blocks * W
-    half = W // 2
-    row = lax.broadcasted_iota(jnp.int32, (8, length), 0)
-    lane = lax.broadcasted_iota(jnp.int32, (16, W), 1)
-    channel = lax.broadcasted_iota(jnp.int32, (16, W), 0)
+    slots = blocks // sources * (W // TILE)
+    tiles = sources * slots
+    lane = lax.broadcasted_iota(jnp.int32, (tiles * 16, TILE), 1)
+    row = lax.rem(lax.broadcasted_iota(jnp.int32, (tiles * 16, TILE), 0), 16)
     for m in range(2):
         for s in range(sources):
             lines = fields_ref[s, start : start + 16, :].astype(F32)
             for q in range(slots):
-                at = (s * slots + q) * width
-                base_ref[:, at : at + width] = jnp.broadcast_to(
-                    lines[m * slots + q : m * slots + q + 1, :width], (8, width)
-                )
-        base = base_ref[...]
-        for bit in (1, 2, 4):
-            base = jnp.where((row & bit) != 0, pltpu.roll(base, bit, 1), base)
-        for q in range(half // 16):
-            low = pltpu.roll(base, 16 * q, 1) if q else base
-            both = jnp.concatenate([low, pltpu.roll(base, 16 * q + 8, 1)], axis=0)
-            first = jnp.where(lane >= channel + 16 * q, both[:, :W], 0.0)
-            both = jnp.concatenate([first, both[:, W:]], axis=1).astype(BF16)
+                line = lines[m * slots + q : m * slots + q + 1, :TILE]
+                at = (s * slots + q) * 16
+                base_ref[at : at + 16, :] = jnp.broadcast_to(line, (16, TILE))
+        base = base_ref[...].astype(BF16)
+        none = jnp.zeros((16, TILE), BF16)
+        for bit in (1, 2, 4, 8):
+            moved = pltpu.roll(base, bit, 1)
+            ahead = jnp.concatenate([none, moved[:-16]], axis=0)
+            moved = jnp.where(lane < bit, ahead, moved)
+            base = jnp.where((row & bit) != 0, moved, base)
+        for q in range(TILE // 16):
+            moved = base
+            if q:
+                moved = pltpu.roll(base, 16 * q, 1)
+                ahead = jnp.concatenate([none, moved[:-16]], axis=0)
+                moved = jnp.where(lane < 16 * q, ahead, moved)
+            moved = moved.reshape(blocks, 2, 16, TILE)
             at = 16 * q
-            moved = jnp.concatenate([jnp.zeros((16, half), BF16), both[:, :-half]], axis=1)
-            for d in range(blocks):
-                toep_ref[m, d, at : at + 16, :] = both[:, d * W : (d + 1) * W]
-                toep_ref[m, d, half + at : half + at + 16, :] = moved[:, d * W : (d + 1) * W]
+            low = moved[:, 0]
+            high = moved[:, 1]
+            shifted = jnp.concatenate([jnp.zeros((1, 16, TILE), BF16), high[:-1]], axis=0)
+            toep_ref[m, :, at : at + 16, 0:TILE] = low
+            toep_ref[m, :, at : at + 16, TILE:] = high
+            toep_ref[m, :, TILE + at : TILE + at + 16, 0:TILE] = shifted
+            toep_ref[m, :, TILE + at : TILE + at + 16, TILE:] = low
 
 
 def earlier(field, j, group):
     if j == 0:
         return field
-    turned = pltpu.roll(field, j, 1)
-    above = jnp.concatenate([jnp.zeros((group, W), F32), turned[:-group]], axis=0)
-    lane = lax.broadcasted_iota(jnp.int32, field.shape, 1)
-    return jnp.where(lane < j, above, turned)
+    low, high = pltpu.roll(field[:, :TILE], j, 1), pltpu.roll(field[:, TILE:], j, 1)
+    above = jnp.concatenate([jnp.zeros((group, TILE), F32), high[:-group]], axis=0)
+    edge = lanes_of(low) < j
+    return jnp.concatenate([jnp.where(edge, above, low), jnp.where(edge, low, high)], axis=1)
 
 
 def later(field, j, group):
     if j == 0:
         return field
-    turned = pltpu.roll(field, W - j, 1)
-    below = jnp.concatenate([turned[group:], jnp.zeros((group, W), F32)], axis=0)
-    lane = lax.broadcasted_iota(jnp.int32, field.shape, 1)
-    return jnp.where(lane >= W - j, below, turned)
+    low, high = pltpu.roll(field[:, :TILE], TILE - j, 1), pltpu.roll(field[:, TILE:], TILE - j, 1)
+    below = jnp.concatenate([low[group:], jnp.zeros((group, TILE), F32)], axis=0)
+    edge = lanes_of(low) >= TILE - j
+    return jnp.concatenate([jnp.where(edge, high, low), jnp.where(edge, below, high)], axis=1)
 
 
 def own_lanes(f, group, width):
@@ -535,7 +548,7 @@
         [
             pltpu.VMEM((3 * rows, W), BF16),
             pltpu.VMEM((2, blocks, W, W), BF16),
-            pltpu.VMEM((8, length), F32),
+            pltpu.VMEM((length // TILE * 16, TILE), F32),
         ],
         flops=4 * 2 * rows * length * W,
         moved=2 * W * length * 2 * 2,

time: 81.1 us -> 81.4 us (level)
  no operation moved by 1% of the time
where the time goes in v8:
time: 81.4 us; the launch traced here: 80.8 us
  blocking collectives  34.4 us (42%)
  Pallas kernels  26.7 us (33%)
  waiting for transfers between devices  11.6 us (14%)
  starting transfers between devices  6.03 us (7%)
  local copies, waits for them, and re-layouts  1.41 us (2%)
    all_to_all x2, blocking collectives, all_to_all(): return lax.all_to_all(blocks, axis, split_axis=0, concat_axis=0, tiled=True)  34.4 us
    all_to_all x2, waiting for transfers between devices, all_to_all(): return lax.all_to_all(blocks, axis, split_axis=0, concat_axis=0, tiled=True)  11.6 us
    pallas_call x1, Pallas kernels, shards(): call(functools.partial(operator_kernel, units), (shape((sources, packed,...  7.76 us
    all_to_all x2, starting transfers between devices, all_to_all(): return lax.all_to_all(blocks, axis, split_axis=0, concat_axis=0, tiled=True)  6.03 us
    pallas_call x1, Pallas kernels, shards(): call(functools.partial(gradient_kernel, units), shape((2 * (length // wid...  4.14 us
    pallas_call x1, Pallas kernels, shards(): call(functools.partial(partial_kernel, units), (shape((devices, sent_rows...  2.85 us
    pallas_call x1, Pallas kernels, shards(): call(gate_kernel, shape((3, block // W, width, W), F32), flops=2 * block...  2.39 us
    pallas_call x1, Pallas kernels, shards(): call(functools.partial(project_kernel, units), shape((sources, packed, W)...  2.32 us
  transfers between devices with their start and end apart: 2, of which 2 were waited for; matrix products, arithmetic and copies ran while one was open for 0% of the time, Pallas kernels for 13%

profile of v8, /device:TPU:0, one launch (start us, length us, event | category | flops | bytes accessed | tf_op | source)
XLA Modules:
  0.0 80.8 jit_solution(17596775510176780820)
XLA Ops:
  0.6 2.3 %shard_map.160 = bf16[8,112,256]{2,1,0:T(8,128)(2,1)} custom-call(bf16[1,512,128]{2,1,0:T(8,128)(2,1)} %series_ref.5, bf16[1,512,128]{2,1,0:T(8,128)(2,1)} %cot_ref.5, bf16[128,384]{1,0:T(8,128)(2,1)} %w_in_ref.5, bf16[128,128]{1,0:T(8,128)(2,1)} %w_out_ref.5, f32[3,384]{1,0:T(4,128)} %taps_ref.7, f32[8,512]{1,0:T(8,128)} %one_ref.1, f32[8,512]{1,0:T(8,128)} %two_ref.1), custom_call_target="tpu_custom_call" | custom-call | flops 67108864 | bytes 2097152 | tf_op jit(solution)/shard_map/pallas_call | solution.py:531
  3.0 20.4 %all_to_all.20.fields_ref = bf16[8,112,256]{2,1,0:T(8,128)(2,1)} all-to-all(bf16[8,112,256]{2,1,0:T(8,128)(2,1)} %shard_map.160), channel_id=1, replica_groups=mesh['dp'=4,'seq'=8] {'seq'}, dimensions={0} | all-to-all | bytes 917504 | tf_op jit(solution)/shard_map/all_to_all | solution.py:512
  23.3 7.8 %shard_map.161 = (bf16[8,112,256]{2,1,0:T(8,128)(2,1)}, bf16[7,256,256]{2,1,0:T(8,128)(2,1)}) custom-call(bf16[8,112,256]{2,1,0:T(8,128)(2,1)} %all_to_all.20.fields_ref, f32[3,384]{1,0:T(4,128)} %taps_ref.7, f32[1,128]{1,0:T(1,128)} %bitcast.4, f32[1,128]{1,0:T(1,128)} %bitcast.5), custom_call_target="tpu_custom_call" | custom-call | flops 2147483648 | bytes 8388608 | tf_op jit(solution)/shard_map/pallas_call | solution.py:545
  31.1 3.5 %all-to-all-start.1 = ((bf16[8,112,256]{2,1,0:T(8,128)(2,1)}), bf16[8,112,256]{2,1,0:T(8,128)(2,1)S(1)}, u32[]{:S(2)}, u32[]{:S(2)}) async-start(bf16[8,112,256]{2,1,0:T(8,128)(2,1)} %get-tuple-element.23), calls=%async_computation.1 | async-start | bytes 917504 | tf_op jit(solution)/shard_map/all_to_all | solution.py:512
  34.6 2.4 %shard_map.162.held_ref = f32[3,2,128,256]{3,2,1,0:T(8,128)} custom-call(bf16[1,512,128]{2,1,0:T(8,128)(2,1)} %series_ref.5, bf16[1,512,128]{2,1,0:T(8,128)(2,1)} %cot_ref.5, bf16[128,384]{1,0:T(8,128)(2,1)} %w_in_ref.5, bf16[128,128]{1,0:T(8,128)(2,1)} %w_out_ref.5, f32[3,384]{1,0:T(4,128)} %taps_ref.7), custom_call_target="tpu_custom_call" | custom-call | flops 33554432 | bytes 1048576 | tf_op jit(solution)/shard_map/pallas_call | solution.py:538
  37.0 4.1 %shard_map.163.own_ref = f32[80,128]{1,0:T(8,128)} custom-call(bf16[8,112,256]{2,1,0:T(8,128)(2,1)} %all_to_all.20.fields_ref, bf16[7,256,256]{2,1,0:T(8,128)(2,1)} %get-tuple-element.24.kept_ref), custom_call_target="tpu_custom_call" | custom-call | flops 1073741824 | bytes 2097152 | tf_op jit(solution)/shard_map/pallas_call | solution.py:559
  41.1 7.3 %all-to-all-done.1.in_ref = bf16[8,112,256]{2,1,0:T(8,128)(2,1)S(1)} async-done(((bf16[8,112,256]{2,1,0:T(8,128)(2,1)}), bf16[8,112,256]{2,1,0:T(8,128)(2,1)S(1)}, u32[]{:S(2)}, u32[]{:S(2)}) %all-to-all-start.1) | async-done | bytes 458784 | tf_op jit(solution)/shard_map/all_to_all | solution.py:512
  48.5 0.0 copy-start
  48.5 0.8 copy-done
  49.2 2.9 %shard_map.164 = (bf16[32,32,128]{2,1,0:T(8,128)(2,1)}, bf16[2,128,256]{2,1,0:T(8,128)(2,1)}, bf16[2,128,256]{2,1,0:T(8,128)(2,1)}) custom-call(bf16[8,112,256]{2,1,0:T(8,128)(2,1)} %copy-done, f32[3,2,128,256]{3,2,1,0:T(8,128)} %shard_map.162.held_ref, f32[3,384]{1,0:T(4,128)} %taps_ref.7, bf16[1,512,128]{2,1,0:T(8,128)(2,1)} %series_ref.5, ...), custom_call_target="tpu_custom_call" | custom-call | flops 67108864 | bytes 786432 | tf_op jit(solution)/shard_map/pallas_call | solution.py:569
  52.1 14.0 %all_to_all.21.in_ref = bf16[32,32,128]{2,1,0:T(8,128)(2,1)} all-to-all(bf16[32,32,128]{2,1,0:T(8,128)(2,1)} %get-tuple-element.29), channel_id=1, replica_groups=mesh['dp'=4,'seq'=8] {'dp','seq'}, dimensions={0} | all-to-all | bytes 524288 | tf_op jit(solution)/shard_map/all_to_all | solution.py:512
  66.1 1.6 %shard_map.166 = bf16[32,16,128]{2,1,0:T(8,128)(2,1)} custom-call(bf16[32,32,128]{2,1,0:T(8,128)(2,1)} %all_to_all.21.in_ref), custom_call_target="tpu_custom_call" | custom-call | flops 65536 | bytes 262144 | tf_op jit(solution)/shard_map/pallas_call | solution.py:588
  67.7 2.6 %all-to-all-start.3 = ((bf16[32,16,128]{2,1,0:T(8,128)(2,1)}), bf16[32,16,128]{2,1,0:T(8,128)(2,1)S(1)}, u32[]{:S(2)}, u32[]{:S(2)}) async-start(bf16[32,16,128]{2,1,0:T(8,128)(2,1)} %shard_map.166), calls=%async_computation.3 | async-start | bytes 262144 | tf_op jit(solution)/shard_map/all_to_all | solution.py:512
  70.3 2.2 %shard_map.165 = (bf16[1,512,128]{2,1,0:T(8,128)(2,1)}, bf16[1,512,128]{2,1,0:T(8,128)(2,1)}) custom-call(bf16[8,112,256]{2,1,0:T(8,128)(2,1)} %copy-done, bf16[2,128,256]{2,1,0:T(8,128)(2,1)} %get-tuple-element.25.product_ref, bf16[2,128,256]{2,1,0:T(8,128)(2,1)} %get-tuple-element.26.grads_ref, bf16[128,384]{1,0:T(8,128)(2,1)} %w_in_ref.5, ...), custom_call_target="tpu_custom_call" | custom-call | flops 67108864 | bytes 786432 | tf_op jit(solution)/shard_map/pallas_call | solution.py:581
  72.5 1.7 %shard_map.168 = (f32[8,512]{1,0:T(8,128)}, f32[8,512]{1,0:T(8,128)}, f32[3,384]{1,0:T(4,128)}, f32[1,128]{1,0:T(1,128)}, f32[1,128]{1,0:T(1,128)}) custom-call(bf16[32,32,128]{2,1,0:T(8,128)(2,1)} %all_to_all.21.in_ref), custom_call_target="tpu_custom_call" | custom-call | flops 131072 | bytes 524288 | tf_op jit(solution)/shard_map/pallas_call | solution.py:596
  74.2 4.3 %all-to-all-done.3.in_ref = bf16[32,16,128]{2,1,0:T(8,128)(2,1)S(1)} async-done(((bf16[32,16,128]{2,1,0:T(8,128)(2,1)}), bf16[32,16,128]{2,1,0:T(8,128)(2,1)S(1)}, u32[]{:S(2)}, u32[]{:S(2)}) %all-to-all-start.3) | async-done | bytes 131104 | tf_op jit(solution)/shard_map/all_to_all | solution.py:512
  78.4 0.0 copy-start.1
  78.5 0.6 copy-done.1
  79.1 1.7 %shard_map.167 = (f32[128,384]{1,0:T(8,128)}, f32[128,128]{1,0:T(8,128)}) custom-call(bf16[32,16,128]{2,1,0:T(8,128)(2,1)} %copy-done.1), custom_call_target="tpu_custom_call" | custom-call | flops 65536 | bytes 131072 | tf_op jit(solution)/shard_map/pallas_call | solution.py:608
Async XLA Ops:
  31.1 17.4 %all-to-all-start.1 = ((bf16[8,112,256]{2,1,0:T(8,128)(2,1)}), bf16[8,112,256]{2,1,0:T(8,128)(2,1)S(1)}, u32[]{:S(2)}, u32[]{:S(2)}) async-start(bf16[8,112,256]{2,1,0:T(8,128)(2,1)} %get-tuple-element.23), calls=%async_computation.1 | async-start | bytes 917504 | tf_op jit(solution)/shard_map/all_to_all | solution.py:512
  48.5 0.8 copy-start
  67.7 10.7 %all-to-all-start.3 = ((bf16[32,16,128]{2,1,0:T(8,128)(2,1)}), bf16[32,16,128]{2,1,0:T(8,128)(2,1)S(1)}, u32[]{:S(2)}, u32[]{:S(2)}) async-start(bf16[32,16,128]{2,1,0:T(8,128)(2,1)} %shard_map.166), calls=%async_computation.3 | async-start | bytes 262144 | tf_op jit(solution)/shard_map/all_to_all | solution.py:512
  78.4 0.6 copy-start.1

commit v9 on v8

--- a/solution.py
+++ b/solution.py
@@ -130,42 +130,43 @@
         out_ref[2, p] = dot_nt(w_out, cot_ref[0, p * W : (p + 1) * W, :])
 
 
-def build_toeplitz(fields_ref, start, toep_ref, base_ref):
+def build_toeplitz(fields_ref, start, toep_ref):
     sources = fields_ref.shape[0]
     _, blocks, _, _ = toep_ref.shape
     slots = blocks // sources * (W // TILE)
-    tiles = sources * slots
-    lane = lax.broadcasted_iota(jnp.int32, (tiles * 16, TILE), 1)
-    row = lax.rem(lax.broadcasted_iota(jnp.int32, (tiles * 16, TILE), 0), 16)
+    lane = lax.broadcasted_iota(jnp.int32, (16, TILE), 1)
+    row = lax.broadcasted_iota(jnp.int32, (16, TILE), 0)
+    none = jnp.zeros((16, TILE), F32)
     for m in range(2):
+        behind = {}
+
+        def shifted(tile, shift):
+            moved = pltpu.roll(tile, shift, 1) if shift else tile
+            ahead, behind[shift] = behind.get(shift, none), moved
+            return jnp.where(lane < shift, ahead, moved) if shift else moved
+
+        for q in range(TILE // 16):
+            at = TILE + 16 * q
+            toep_ref[m, 0, at : at + 16, 0:TILE] = none.astype(BF16)
+        held = {}
         for s in range(sources):
             lines = fields_ref[s, start : start + 16, :].astype(F32)
-            for q in range(slots):
-                line = lines[m * slots + q : m * slots + q + 1, :TILE]
-                at = (s * slots + q) * 16
-                base_ref[at : at + 16, :] = jnp.broadcast_to(line, (16, TILE))
-        base = base_ref[...].astype(BF16)
-        none = jnp.zeros((16, TILE), BF16)
-        for bit in (1, 2, 4, 8):
-            moved = pltpu.roll(base, bit, 1)
-            ahead = jnp.concatenate([none, moved[:-16]], axis=0)
-            moved = jnp.where(lane < bit, ahead, moved)
-            base = jnp.where((row & bit) != 0, moved, base)
-        for q in range(TILE // 16):
-            moved = base
-            if q:
-                moved = pltpu.roll(base, 16 * q, 1)
-                ahead = jnp.concatenate([none, moved[:-16]], axis=0)
-                moved = jnp.where(lane < 16 * q, ahead, moved)
-            moved = moved.reshape(blocks, 2, 16, TILE)
-            at = 16 * q
-            low = moved[:, 0]
-            high = moved[:, 1]
-            shifted = jnp.concatenate([jnp.zeros((1, 16, TILE), BF16), high[:-1]], axis=0)
-            toep_ref[m, :, at : at + 16, 0:TILE] = low
-            toep_ref[m, :, at : at + 16, TILE:] = high
-            toep_ref[m, :, TILE + at : TILE + at + 16, 0:TILE] = shifted
-            toep_ref[m, :, TILE + at : TILE + at + 16, TILE:] = low
+            for i in range(slots):
+                d, part = divmod(s * slots + i, W // TILE)
+                line = lines[m * slots + i : m * slots + i + 1, :TILE]
+                tile = jnp.broadcast_to(line, (16, TILE))
+                for bit in (1, 2, 4, 8):
+                    moved = pltpu.roll(tile, bit, 1)
+                    ahead, held[bit] = held.get(bit, none), moved
+                    tile = jnp.where((row & bit) != 0, jnp.where(lane < bit, ahead, moved), tile)
+                for q in range(TILE // 16):
+                    low = shifted(tile, 16 * q).astype(BF16)
+                    at = 16 * q
+                    toep_ref[m, d, at : at + 16, part * TILE : (part + 1) * TILE] = low
+                    if part == 0:
+                        toep_ref[m, d, TILE + at : TILE + at + 16, TILE:] = low
+                    elif d + 1 < blocks:
+                        toep_ref[m, d + 1, TILE + at : TILE + at + 16, 0:TILE] = low
 
 
 def earlier(field, j, group):
@@ -175,15 +176,6 @@
     above = jnp.concatenate([jnp.zeros((group, TILE), F32), high[:-group]], axis=0)
     edge = lanes_of(low) < j
     return jnp.concatenate([jnp.where(edge, above, low), jnp.where(edge, low, high)], axis=1)
-
-
-def later(field, j, group):
-    if j == 0:
-        return field
-    low, high = pltpu.roll(field[:, :TILE], TILE - j, 1), pltpu.roll(field[:, TILE:], TILE - j, 1)
-    below = jnp.concatenate([low[group:], jnp.zeros((group, TILE), F32)], axis=0)
-    edge = lanes_of(low) >= TILE - j
-    return jnp.concatenate([jnp.where(edge, high, low), jnp.where(edge, below, high)], axis=1)
 
 
 def own_lanes(f, group, width):
@@ -207,45 +199,30 @@
     out_ref,
     kept_ref,
     pad_ref,
+    back_ref,
     toep_ref,
-    base_ref,
+    wide_ref,
 ):
     sources, _, _ = out_ref.shape
     _, rows, _ = kept_ref.shape
     each = rows // sources
     start = 3 * each
-    build_toeplitz(fields_ref, start, toep_ref, base_ref)
+    build_toeplitz(fields_ref, start, toep_ref)
     width = taps_ref.shape[1] // 3
     group = width // units
     blocks = rows // group
     u = lax.rem(lax.axis_index("seq"), units)
     mine = own_lanes(u, group, width)
+    value_ref, gate_ref, y_ref, mid_ref, grad_ref, first_ref, second_ref = [
+        wide_ref.at[i] for i in range(7)
+    ]
 
     def column(values):
         col = jnp.sum(jnp.where(mine, values, 0.0), axis=1, keepdims=True)
         return jnp.broadcast_to(col, (group, W))
 
     def scaled(field, col):
-        return (field.reshape(blocks, group, W) * col[None]).reshape(rows, W)
-
-    zeros = jnp.zeros((rows, W), BF16)
-    pad_ref[0:rows, :] = zeros
-    pad_ref[2 * rows : 3 * rows, :] = zeros
-
-    def causal(m, field):
-        pad_ref[rows : 2 * rows, :] = field
-        left = jnp.concatenate(
-            [pad_ref[rows - group * d : 2 * rows - group * d, :] for d in range(blocks)], axis=1
-        )
-        return dot(left, toep_ref[m].reshape(blocks * W, W))
-
-    def anticausal(m, field):
-        pad_ref[rows : 2 * rows, :] = field
-        left = jnp.concatenate(
-            [pad_ref[rows + group * d : 2 * rows + group * d, :] for d in range(blocks)], axis=1
-        )
-        right = jnp.concatenate([toep_ref[m, d] for d in range(blocks)], axis=1)
-        return dot_nt(left, right)
+        return (field.reshape(-1, group, W) * col[None]).reshape(field.shape)
 
     tap = [
         [
@@ -256,27 +233,46 @@
     ]
     skip_one = column(skip_one_ref[...])
     skip_two = column(skip_two_ref[...])
-
-    def short(kind):
-        field = pick(fields_ref, kind, each)
-        total = scaled(field, tap[kind][0])
+    chunks = [slice(s * each, (s + 1) * each) for s in range(sources)]
+
+    zeros = jnp.zeros((rows, W), BF16)
+    pad_ref[0:rows, :] = zeros
+    back_ref[rows : 2 * rows, :] = zeros
+
+    def causal(order, into_ref):
+        left = jnp.concatenate(
+            [pad_ref[rows - group * d : 2 * rows - group * d, :] for d in range(blocks)], axis=1
+        )
+        into_ref[...] = dot(left, toep_ref[order].reshape(blocks * W, W))
+
+    def anticausal(order, into_ref):
+        left = jnp.concatenate(
+            [back_ref[group * d : rows + group * d, :] for d in range(blocks)], axis=1
+        )
+        right = jnp.concatenate([toep_ref[order, d] for d in range(blocks)], axis=1)
+        into_ref[...] = dot_nt(left, right)
+
+    def put(slot, s, field, into_ref=None, at=0):
+        low = field.astype(BF16)
+        kept_ref[slot, chunks[s], :] = low
+        if into_ref is not None:
+            into_ref[at + s * each : at + (s + 1) * each, :] = low
+
+    def short(kind, s):
+        held = fields_ref[s, kind * each : (kind + 1) * each, :].astype(F32)
+        if s:
+            last = fields_ref[s - 1, (kind + 1) * each - group : (kind + 1) * each, :].astype(F32)
+        else:
+            last = jnp.zeros((group, W), F32)
+        total = scaled(held, tap[kind][0])
+        low, high = held[:, :TILE], held[:, TILE:]
         for j in (1, 2):
-            total = total + scaled(earlier(field, j, group), tap[kind][j])
+            low_j, high_j = pltpu.roll(low, j, 1), pltpu.roll(high, j, 1)
+            above = jnp.concatenate([pltpu.roll(last[:, TILE:], j, 1), high_j[:-group]], axis=0)
+            edge = lanes_of(low) < j
+            moved = [jnp.where(edge, above, low_j), jnp.where(edge, low_j, high_j)]
+            total = total + scaled(jnp.concatenate(moved, axis=1), tap[kind][j])
         return total
-
-    def keep(slot, field):
-        low = field.astype(BF16)
-        kept_ref[slot] = low
-        return low
-
-    def send(kind, field):
-        out_ref[:, kind * each : (kind + 1) * each, :] = field.astype(BF16).reshape(sources, each, W)
-
-    def send_back(kind, field):
-        total = scaled(field, tap[kind][0])
-        for j in (1, 2):
-            total = total + scaled(later(field, j, group), tap[kind][j])
-        send(kind, total)
 
     edges = fields_ref[:, start : start + 16, :].astype(F32)[:, :group]
     none = jnp.zeros((1, group, W), F32)
@@ -286,31 +282,70 @@
     reach = tap[2][2] * turned(before, 128)
     reach = reach + jnp.where(lane < 1, tap[2][1] * turned(before, 127), 0.0)
     reach = jnp.where(lane < 2, turned(edges, 126) * reach, 0.0)
-    grad_two = pick(fields_ref, 2, each).reshape(sources, each, W)
-    grad_two = jnp.concatenate([grad_two[:, :group] + reach, grad_two[:, group:]], axis=1)
-    grad_two = grad_two.reshape(rows, W)
-
-    value = short(0)
-    y_one = causal(0, keep(0, value)) + scaled(value, skip_one)
-    gate_one = short(1)
-    mid = gate_one * y_one
-    y_two = causal(1, keep(1, mid)) + scaled(mid, skip_two)
-    send(2, y_two)
-    heads = y_two.reshape(sources, each, W)[1:, :group]
-    heads = jnp.concatenate([heads, none], axis=0)
+    for s in range(sources):
+        held = fields_ref[s, 2 * each : 3 * each, :].astype(F32)
+        held = jnp.concatenate([held[:group] + reach[s], held[group:]], axis=0)
+        grad_ref[chunks[s], :] = held
+        put(3, s, held, back_ref)
+        value = short(0, s)
+        value_ref[chunks[s], :] = value
+        put(0, s, value, pad_ref, rows)
+        gate_ref[chunks[s], :] = short(1, s)
+
+    causal(0, first_ref)
+    anticausal(1, second_ref)
+    for s in range(sources):
+        at = chunks[s]
+        y_one = first_ref[at, :] + scaled(value_ref[at, :], skip_one)
+        y_ref[at, :] = y_one
+        mid = gate_ref[at, :] * y_one
+        mid_ref[at, :] = mid
+        put(1, s, mid, pad_ref, rows)
+    causal(1, first_ref)
+    for s in range(sources):
+        at = chunks[s]
+        d_mid = second_ref[at, :] + scaled(grad_ref[at, :], skip_two)
+        grad_one = d_mid * gate_ref[at, :]
+        grad_ref[at, :] = grad_one
+        put(2, s, grad_one, back_ref)
+        d_gate = d_mid * y_ref[at, :]
+        y_ref[at, :] = d_gate
+        put(5, s, d_gate)
+    anticausal(0, second_ref)
+    heads = []
+    for s in range(sources):
+        at = chunks[s]
+        y_two = first_ref[at, :] + scaled(mid_ref[at, :], skip_two)
+        out_ref[s, 2 * each : 3 * each, :] = y_two.astype(BF16)
+        heads.append(y_two[:group])
+    heads = jnp.stack(heads[1:] + [none[0]])
     edges = jnp.where(lane < 4, turned(following, 128) * turned(heads, 2), 0.0)
     edges = jnp.where(lane < 2, turned(before, 128), edges)
     if group < 16:
         edges = jnp.concatenate([edges, jnp.zeros((sources, 16 - group, W), F32)], axis=1)
     out_ref[:, start:, :] = edges.astype(BF16)
-    d_mid = anticausal(1, keep(3, grad_two)) + scaled(grad_two, skip_two)
-    grad_one = d_mid * gate_one
-    d_gate_one = d_mid * y_one
-    keep(5, d_gate_one)
-    send_back(1, d_gate_one)
-    d_value = anticausal(0, keep(2, grad_one)) + scaled(grad_one, skip_one)
-    keep(4, d_value)
-    send_back(0, d_value)
+    for s in range(sources):
+        at = chunks[s]
+        d_value = second_ref[at, :] + scaled(grad_ref[at, :], skip_one)
+        value_ref[at, :] = d_value
+        put(4, s, d_value)
+
+    for s in range(sources):
+        for kind, ref in ((0, value_ref), (1, y_ref)):
+            held = ref[chunks[s], :]
+            if s + 1 < sources:
+                first = ref[(s + 1) * each : (s + 1) * each + group, :]
+            else:
+                first = jnp.zeros((group, W), F32)
+            total = scaled(held, tap[kind][0])
+            low, high = held[:, :TILE], held[:, TILE:]
+            for j in (1, 2):
+                low_j, high_j = pltpu.roll(low, TILE - j, 1), pltpu.roll(high, TILE - j, 1)
+                below = jnp.concatenate([low_j[group:], pltpu.roll(first[:, :TILE], TILE - j, 1)], axis=0)
+                edge = lanes_of(low) >= TILE - j
+                moved = [jnp.where(edge, high_j, low_j), jnp.where(edge, below, high_j)]
+                total = total + scaled(jnp.concatenate(moved, axis=1), tap[kind][j])
+            out_ref[s, kind * each : (kind + 1) * each, :] = total.astype(BF16)
 
 
 def gradient_kernel(units, fields_ref, kept_ref, out_ref, pad_ref, corr_ref):
@@ -421,21 +456,20 @@
     sources = in_ref.shape[0]
     lines = (own_ref.shape[0] - 16) // 2
     slots = lines // sources
-    rest = sent - each - 2 * slots - 4
-    spare = [jnp.zeros((rest, width), F32)] if rest else []
+    spare = sent - each - 2 * slots - 4
+    spare = [jnp.zeros((spare, width), F32)] if spare else []
+    rests = []
+    for s in range(sources):
+        rows = [
+            own_ref[s * slots : (s + 1) * slots, :],
+            own_ref[lines + s * slots : lines + (s + 1) * slots, :],
+            own_ref[2 * lines : 2 * lines + 1, :],
+            small,
+        ]
+        rests.append(jnp.concatenate(rows + spare, axis=0))
     for g in range(targets):
-        s = g % sources
-        part_ref[g] = jnp.concatenate(
-            [
-                weights[g * each : (g + 1) * each],
-                own_ref[s * slots : (s + 1) * slots, :],
-                own_ref[lines + s * slots : lines + (s + 1) * slots, :],
-                own_ref[2 * lines : 2 * lines + 1, :],
-                small,
-            ]
-            + spare,
-            axis=0,
-        ).astype(BF16)
+        block = [weights[g * each : (g + 1) * each], rests[g % sources]]
+        part_ref[g] = jnp.concatenate(block, axis=0).astype(BF16)
 
 
 def output_kernel(units, in_ref, product_ref, grads_ref, w_in_ref, w_out_ref, out_ref, d_series_ref):
@@ -546,9 +580,10 @@
         functools.partial(operator_kernel, units),
         (shape((sources, packed, W), BF16), shape((7, rows, W), BF16)),
         [
-            pltpu.VMEM((3 * rows, W), BF16),
+            pltpu.VMEM((2 * rows, W), BF16),
+            pltpu.VMEM((2 * rows, W), BF16),
             pltpu.VMEM((2, blocks, W, W), BF16),
-            pltpu.VMEM((length // TILE * 16, TILE), F32),
+            pltpu.VMEM((7, rows, W), F32),
         ],
         flops=4 * 2 * rows * length * W,
         moved=2 * W * length * 2 * 2,

time: 81.4 us -> 79.9 us (0.982)
  Pallas kernels: 26.7 us -> 25.2 us
    pallas_call x1, Pallas kernels: 7.76 us -> 6.2 us  [shards(): call(functools.partial(operator_kernel, units), (shape((sources, packed,...]
where the time goes in v9:
time: 79.9 us; the launch traced here: 79.2 us
  blocking collectives  34.4 us (43%)
  Pallas kernels  25.2 us (32%)
  waiting for transfers between devices  11.6 us (15%)
  starting transfers between devices  6.03 us (8%)
  local copies, waits for them, and re-layouts  1.41 us (2%)
    all_to_all x2, blocking collectives, all_to_all(): return lax.all_to_all(blocks, axis, split_axis=0, concat_axis=0, tiled=True)  34.4 us
    all_to_all x2, waiting for transfers between devices, all_to_all(): return lax.all_to_all(blocks, axis, split_axis=0, concat_axis=0, tiled=True)  11.6 us
    pallas_call x1, Pallas kernels, shards(): call(functools.partial(operator_kernel, units), (shape((sources, packed,...  6.2 us
    all_to_all x2, starting transfers between devices, all_to_all(): return lax.all_to_all(blocks, axis, split_axis=0, concat_axis=0, tiled=True)  6.03 us
    pallas_call x1, Pallas kernels, shards(): call(functools.partial(gradient_kernel, units), shape((2 * (length // wid...  4.15 us
    pallas_call x1, Pallas kernels, shards(): call(functools.partial(partial_kernel, units), (shape((devices, sent_rows...  2.85 us
    pallas_call x1, Pallas kernels, shards(): call(gate_kernel, shape((3, block // W, width, W), F32), flops=2 * block...  2.39 us
    pallas_call x1, Pallas kernels, shards(): call(functools.partial(project_kernel, units), shape((sources, packed, W)...  2.32 us
  transfers between devices with their start and end apart: 2, of which 2 were waited for; matrix products, arithmetic and copies ran while one was open for 0% of the time, Pallas kernels for 13%

profile of v9, /device:TPU:0, one launch (start us, length us, event | category | flops | bytes accessed | tf_op | source)
XLA Modules:
  0.0 79.2 jit_solution(14309366593164382009)
XLA Ops:
  0.6 2.3 %shard_map.160 = bf16[8,112,256]{2,1,0:T(8,128)(2,1)} custom-call(bf16[1,512,128]{2,1,0:T(8,128)(2,1)} %series_ref.5, bf16[1,512,128]{2,1,0:T(8,128)(2,1)} %cot_ref.5, bf16[128,384]{1,0:T(8,128)(2,1)} %w_in_ref.5, bf16[128,128]{1,0:T(8,128)(2,1)} %w_out_ref.5, f32[3,384]{1,0:T(4,128)} %taps_ref.7, f32[8,512]{1,0:T(8,128)} %one_ref.1, f32[8,512]{1,0:T(8,128)} %two_ref.1), custom_call_target="tpu_custom_call" | custom-call | flops 67108864 | bytes 2097152 | tf_op jit(solution)/shard_map/pallas_call | solution.py:565
  3.0 20.4 %all_to_all.20.fields_ref = bf16[8,112,256]{2,1,0:T(8,128)(2,1)} all-to-all(bf16[8,112,256]{2,1,0:T(8,128)(2,1)} %shard_map.160), channel_id=1, replica_groups=mesh['dp'=4,'seq'=8] {'seq'}, dimensions={0} | all-to-all | bytes 917504 | tf_op jit(solution)/shard_map/all_to_all | solution.py:546
  23.3 6.2 %shard_map.161 = (bf16[8,112,256]{2,1,0:T(8,128)(2,1)}, bf16[7,256,256]{2,1,0:T(8,128)(2,1)}) custom-call(bf16[8,112,256]{2,1,0:T(8,128)(2,1)} %all_to_all.20.fields_ref, f32[3,384]{1,0:T(4,128)} %taps_ref.7, f32[1,128]{1,0:T(1,128)} %bitcast.4, f32[1,128]{1,0:T(1,128)} %bitcast.5), custom_call_target="tpu_custom_call" | custom-call | flops 2147483648 | bytes 8388608 | tf_op jit(solution)/shard_map/pallas_call | solution.py:579
  29.5 3.5 %all-to-all-start.1 = ((bf16[8,112,256]{2,1,0:T(8,128)(2,1)}), bf16[8,112,256]{2,1,0:T(8,128)(2,1)S(1)}, u32[]{:S(2)}, u32[]{:S(2)}) async-start(bf16[8,112,256]{2,1,0:T(8,128)(2,1)} %get-tuple-element.23), calls=%async_computation.1 | async-start | bytes 917504 | tf_op jit(solution)/shard_map/all_to_all | solution.py:546
  33.0 2.4 %shard_map.162.held_ref = f32[3,2,128,256]{3,2,1,0:T(8,128)} custom-call(bf16[1,512,128]{2,1,0:T(8,128)(2,1)} %series_ref.5, bf16[1,512,128]{2,1,0:T(8,128)(2,1)} %cot_ref.5, bf16[128,384]{1,0:T(8,128)(2,1)} %w_in_ref.5, bf16[128,128]{1,0:T(8,128)(2,1)} %w_out_ref.5, f32[3,384]{1,0:T(4,128)} %taps_ref.7), custom_call_target="tpu_custom_call" | custom-call | flops 33554432 | bytes 1048576 | tf_op jit(solution)/shard_map/pallas_call | solution.py:572
  35.4 4.2 %shard_map.163.own_ref = f32[80,128]{1,0:T(8,128)} custom-call(bf16[8,112,256]{2,1,0:T(8,128)(2,1)} %all_to_all.20.fields_ref, bf16[7,256,256]{2,1,0:T(8,128)(2,1)} %get-tuple-element.24.kept_ref), custom_call_target="tpu_custom_call" | custom-call | flops 1073741824 | bytes 2097152 | tf_op jit(solution)/shard_map/pallas_call | solution.py:594
  39.6 7.3 %all-to-all-done.1.in_ref = bf16[8,112,256]{2,1,0:T(8,128)(2,1)S(1)} async-done(((bf16[8,112,256]{2,1,0:T(8,128)(2,1)}), bf16[8,112,256]{2,1,0:T(8,128)(2,1)S(1)}, u32[]{:S(2)}, u32[]{:S(2)}) %all-to-all-start.1) | async-done | bytes 458784 | tf_op jit(solution)/shard_map/all_to_all | solution.py:546
  46.9 0.0 copy-start
  46.9 0.8 copy-done
  47.7 2.9 %shard_map.164 = (bf16[32,32,128]{2,1,0:T(8,128)(2,1)}, bf16[2,128,256]{2,1,0:T(8,128)(2,1)}, bf16[2,128,256]{2,1,0:T(8,128)(2,1)}) custom-call(bf16[8,112,256]{2,1,0:T(8,128)(2,1)} %copy-done, f32[3,2,128,256]{3,2,1,0:T(8,128)} %shard_map.162.held_ref, f32[3,384]{1,0:T(4,128)} %taps_ref.7, bf16[1,512,128]{2,1,0:T(8,128)(2,1)} %series_ref.5, ...), custom_call_target="tpu_custom_call" | custom-call | flops 67108864 | bytes 786432 | tf_op jit(solution)/shard_map/pallas_call | solution.py:604
  50.5 14.0 %all_to_all.21.in_ref = bf16[32,32,128]{2,1,0:T(8,128)(2,1)} all-to-all(bf16[32,32,128]{2,1,0:T(8,128)(2,1)} %get-tuple-element.29), channel_id=1, replica_groups=mesh['dp'=4,'seq'=8] {'dp','seq'}, dimensions={0} | all-to-all | bytes 524288 | tf_op jit(solution)/shard_map/all_to_all | solution.py:546
  64.5 1.6 %shard_map.166 = bf16[32,16,128]{2,1,0:T(8,128)(2,1)} custom-call(bf16[32,32,128]{2,1,0:T(8,128)(2,1)} %all_to_all.21.in_ref), custom_call_target="tpu_custom_call" | custom-call | flops 65536 | bytes 262144 | tf_op jit(solution)/shard_map/pallas_call | solution.py:623
  66.1 2.6 %all-to-all-start.3 = ((bf16[32,16,128]{2,1,0:T(8,128)(2,1)}), bf16[32,16,128]{2,1,0:T(8,128)(2,1)S(1)}, u32[]{:S(2)}, u32[]{:S(2)}) async-start(bf16[32,16,128]{2,1,0:T(8,128)(2,1)} %shard_map.166), calls=%async_computation.3 | async-start | bytes 262144 | tf_op jit(solution)/shard_map/all_to_all | solution.py:546
  68.7 2.2 %shard_map.165 = (bf16[1,512,128]{2,1,0:T(8,128)(2,1)}, bf16[1,512,128]{2,1,0:T(8,128)(2,1)}) custom-call(bf16[8,112,256]{2,1,0:T(8,128)(2,1)} %copy-done, bf16[2,128,256]{2,1,0:T(8,128)(2,1)} %get-tuple-element.25.product_ref, bf16[2,128,256]{2,1,0:T(8,128)(2,1)} %get-tuple-element.26.grads_ref, bf16[128,384]{1,0:T(8,128)(2,1)} %w_in_ref.5, ...), custom_call_target="tpu_custom_call" | custom-call | flops 67108864 | bytes 786432 | tf_op jit(solution)/shard_map/pallas_call | solution.py:616
  70.9 1.7 %shard_map.168 = (f32[8,512]{1,0:T(8,128)}, f32[8,512]{1,0:T(8,128)}, f32[3,384]{1,0:T(4,128)}, f32[1,128]{1,0:T(1,128)}, f32[1,128]{1,0:T(1,128)}) custom-call(bf16[32,32,128]{2,1,0:T(8,128)(2,1)} %all_to_all.21.in_ref), custom_call_target="tpu_custom_call" | custom-call | flops 131072 | bytes 524288 | tf_op jit(solution)/shard_map/pallas_call | solution.py:631
  72.6 4.3 %all-to-all-done.3.in_ref = bf16[32,16,128]{2,1,0:T(8,128)(2,1)S(1)} async-done(((bf16[32,16,128]{2,1,0:T(8,128)(2,1)}), bf16[32,16,128]{2,1,0:T(8,128)(2,1)S(1)}, u32[]{:S(2)}, u32[]{:S(2)}) %all-to-all-start.3) | async-done | bytes 131104 | tf_op jit(solution)/shard_map/all_to_all | solution.py:546
  76.9 0.0 copy-start.1
  76.9 0.6 copy-done.1
  77.5 1.7 %shard_map.167 = (f32[128,384]{1,0:T(8,128)}, f32[128,128]{1,0:T(8,128)}) custom-call(bf16[32,16,128]{2,1,0:T(8,128)(2,1)} %copy-done.1), custom_call_target="tpu_custom_call" | custom-call | flops 65536 | bytes 131072 | tf_op jit(solution)/shard_map/pallas_call | solution.py:643
Async XLA Ops:
  29.5 17.4 %all-to-all-start.1 = ((bf16[8,112,256]{2,1,0:T(8,128)(2,1)}), bf16[8,112,256]{2,1,0:T(8,128)(2,1)S(1)}, u32[]{:S(2)}, u32[]{:S(2)}) async-start(bf16[8,112,256]{2,1,0:T(8,128)(2,1)} %get-tuple-element.23), calls=%async_computation.1 | async-start | bytes 917504 | tf_op jit(solution)/shard_map/all_to_all | solution.py:546
  46.9 0.8 copy-start
  66.1 10.7 %all-to-all-start.3 = ((bf16[32,16,128]{2,1,0:T(8,128)(2,1)}), bf16[32,16,128]{2,1,0:T(8,128)(2,1)S(1)}, u32[]{:S(2)}, u32[]{:S(2)}) async-start(bf16[32,16,128]{2,1,0:T(8,128)(2,1)} %shard_map.166), calls=%async_computation.3 | async-start | bytes 262144 | tf_op jit(solution)/shard_map/all_to_all | solution.py:546
  76.9 0.6 copy-start.1

commit v10 on v9

--- a/solution.py
+++ b/solution.py
@@ -13,7 +13,7 @@
 F32 = jnp.float32
 BF16 = jnp.bfloat16
 NT = (((1,), (1,)), ((), ()))
-VMEM_LIMIT = 56 * 1024 * 1024
+VMEM_LIMIT = 24 * 1024 * 1024
 
 
 def call(body, out_shape, scratch=(), flops=0, moved=0):

time: 79.9 us -> 77.4 us (0.969)
  Pallas kernels: 25.2 us -> 12.2 us
  waiting for transfers between devices: 11.6 us -> 17.6 us
  local copies, waits for them, and re-layouts: 1.41 us -> 6.27 us
    all_to_all x2, waiting for transfers between devices: 11.6 us -> 17.6 us  [all_to_all(): return lax.all_to_all(blocks, axis, split_axis=0, concat_axis=0, tiled=True)]
    unnamed x4 -> x28, local copies, waits for them, and re-layouts: 1.41 us -> 6.27 us
    pallas_call x1, Pallas kernels: 2.85 us -> 0.81 us  [shards(): call(functools.partial(partial_kernel, units), (shape((devices, sent_rows...]
    pallas_call x1, Pallas kernels: 2.39 us -> 0.42 us  [shards(): call(gate_kernel, shape((3, block // W, width, W), F32), flops=2 * block...]
    pallas_call x1, Pallas kernels: 4.15 us -> 2.21 us  [shards(): call(functools.partial(gradient_kernel, units), shape((2 * (length // wid...]
    pallas_call x1, Pallas kernels: 2.32 us -> 0.5 us  [shards(): call(functools.partial(project_kernel, units), shape((sources, packed, W)...]
    pallas_call x1, Pallas kernels: 6.2 us -> 5.03 us  [shards(): call(functools.partial(operator_kernel, units), (shape((sources, packed,...]
    pallas_call x1, Pallas kernels: 2.21 us -> 1.05 us  [shards(): call(functools.partial(output_kernel, units), (shape(series.shape, BF16),...]
  transfers between devices with their start and end apart: 2 -> 2, of which waited for: 2 -> 2; matrix products, arithmetic and copies ran while one was open for 0% -> 0% of each run, Pallas kernels for 13% -> 6%
where the time goes in v10:
time: 77.4 us; the launch traced here: 76.8 us
  blocking collectives  33.7 us (44%)
  waiting for transfers between devices  17.6 us (23%)
  Pallas kernels  12.2 us (16%)
  local copies, waits for them, and re-layouts  6.27 us (8%)
  starting transfers between devices  6.19 us (8%)
    all_to_all x2, blocking collectives, all_to_all(): return lax.all_to_all(blocks, axis, split_axis=0, concat_axis=0, tiled=True)  33.7 us
    all_to_all x2, waiting for transfers between devices, all_to_all(): return lax.all_to_all(blocks, axis, split_axis=0, concat_axis=0, tiled=True)  17.6 us
    unnamed x28, local copies, waits for them, and re-layouts  6.27 us
    all_to_all x2, starting transfers between devices, all_to_all(): return lax.all_to_all(blocks, axis, split_axis=0, concat_axis=0, tiled=True)  6.19 us
    pallas_call x1, Pallas kernels, shards(): call(functools.partial(operator_kernel, units), (shape((sources, packed,...  5.03 us
    pallas_call x1, Pallas kernels, shards(): call(functools.partial(gradient_kernel, units), shape((2 * (length // wid...  2.21 us
  transfers between devices with their start and end apart: 2, of which 2 were waited for; matrix products, arithmetic and copies ran while one was open for 0% of the time, Pallas kernels for 6%

profile of v10, /device:TPU:0, one launch (start us, length us, event | category | flops | bytes accessed | tf_op | source)
XLA Modules:
  0.0 76.8 jit_solution(12694909824562379515)
XLA Ops:
  0.6 0.0 copy-start
  0.7 0.9 %copy-done = bf16[1,512,128]{2,1,0:T(8,128)(2,1)S(1)} copy-done((bf16[1,512,128]{2,1,0:T(8,128)(2,1)S(1)}, bf16[1,512,128]{2,1,0:T(8,128)(2,1)}, u32[]{:S(2)}) %copy-start) | copy-done | bytes 131096
  1.5 0.0 copy-start.2
  1.6 0.9 %copy-done.2 = bf16[1,512,128]{2,1,0:T(8,128)(2,1)S(1)} copy-done((bf16[1,512,128]{2,1,0:T(8,128)(2,1)S(1)}, bf16[1,512,128]{2,1,0:T(8,128)(2,1)}, u32[]{:S(2)}) %copy-start.2) | copy-done | bytes 131096
  2.5 0.9 %copy-done.4 = bf16[128,384]{1,0:T(8,128)(2,1)S(1)} copy-done((bf16[128,384]{1,0:T(8,128)(2,1)S(1)}, bf16[128,384]{1,0:T(8,128)(2,1)}, u32[]{:S(2)}) %copy-start.4) | copy-done | bytes 98328
  3.3 0.8 copy-done.6
  4.1 0.7 copy-done.8
  4.8 0.7 copy-done.10
  5.5 0.7 copy-done.11
  6.2 0.5 shard_map.160
  6.7 20.1 %all_to_all.20.fields_ref = bf16[8,112,256]{2,1,0:T(8,128)(2,1)S(1)} all-to-all(bf16[8,112,256]{2,1,0:T(8,128)(2,1)S(1)} %shard_map.160), channel_id=1, replica_groups=mesh['dp'=4,'seq'=8] {'seq'}, dimensions={0} | all-to-all | bytes 917504 | tf_op jit(solution)/shard_map/all_to_all | solution.py:546
  26.8 0.7 copy-done.12
  27.5 0.0 copy-done.13
  27.5 5.0 %shard_map.161 = (bf16[8,112,256]{2,1,0:T(8,128)(2,1)}, bf16[7,256,256]{2,1,0:T(8,128)(2,1)S(1)}) custom-call(bf16[8,112,256]{2,1,0:T(8,128)(2,1)S(1)} %all_to_all.20.fields_ref, f32[3,384]{1,0:T(4,128)S(1)} %copy-done.8, f32[1,128]{1,0:T(1,128)S(1)} %bitcast.4, f32[1,128]{1,0:T(1,128)S(1)} %bitcast.5), custom_call_target="tpu_custom_call" | custom-call | flops 2147483648 | bytes 8388608 | tf_op jit(solution)/shard_map/pallas_call | solution.py:579
  32.5 0.0 copy-start.9
  32.5 3.6 %all-to-all-start.1 = ((bf16[8,112,256]{2,1,0:T(8,128)(2,1)}), bf16[8,112,256]{2,1,0:T(8,128)(2,1)S(1)}, u32[]{:S(2)}, u32[]{:S(2)}) async-start(bf16[8,112,256]{2,1,0:T(8,128)(2,1)} %get-tuple-element.23), calls=%async_computation.1 | async-start | bytes 917504 | tf_op jit(solution)/shard_map/all_to_all | solution.py:546
  36.2 0.0 copy-done.1
  36.2 0.0 copy-done.3
  36.2 0.0 copy-done.5
  36.2 0.0 copy-done.7
  36.2 0.0 copy-done.9
  36.2 0.4 shard_map.162.held_ref
  36.6 2.2 %shard_map.163.own_ref = f32[80,128]{1,0:T(8,128)S(1)} custom-call(bf16[8,112,256]{2,1,0:T(8,128)(2,1)S(1)} %all_to_all.20.fields_ref, bf16[7,256,256]{2,1,0:T(8,128)(2,1)S(1)} %get-tuple-element.24.kept_ref), custom_call_target="tpu_custom_call" | custom-call | flops 1073741824 | bytes 2097152 | tf_op jit(solution)/shard_map/pallas_call | solution.py:594
  38.8 11.2 %all-to-all-done.1.in_ref = bf16[8,112,256]{2,1,0:T(8,128)(2,1)S(1)} async-done(((bf16[8,112,256]{2,1,0:T(8,128)(2,1)}), bf16[8,112,256]{2,1,0:T(8,128)(2,1)S(1)}, u32[]{:S(2)}, u32[]{:S(2)}) %all-to-all-start.1) | async-done | bytes 458784 | tf_op jit(solution)/shard_map/all_to_all | solution.py:546
  50.0 0.8 %shard_map.164 = (bf16[32,32,128]{2,1,0:T(8,128)(2,1)S(1)}, bf16[2,128,256]{2,1,0:T(8,128)(2,1)S(1)}, bf16[2,128,256]{2,1,0:T(8,128)(2,1)S(1)}) custom-call(bf16[8,112,256]{2,1,0:T(8,128)(2,1)S(1)} %all-to-all-done.1.in_ref, f32[3,2,128,256]{3,2,1,0:T(8,128)S(1)} %shard_map.162.held_ref, f32[3,384]{1,0:T(4,128)S(1)} %copy-done.9, ...), custom_call_target="tpu_custom_call" | custom-call | flops 67108864 | bytes 786432 | tf_op jit(solution)/shard_map/pallas_call | solution.py:604
  50.8 13.7 %all_to_all.21.in_ref = bf16[32,32,128]{2,1,0:T(8,128)(2,1)S(1)} all-to-all(bf16[32,32,128]{2,1,0:T(8,128)(2,1)S(1)} %get-tuple-element.29), channel_id=1, replica_groups=mesh['dp'=4,'seq'=8] {'dp','seq'}, dimensions={0} | all-to-all | bytes 524288 | tf_op jit(solution)/shard_map/all_to_all | solution.py:546
  64.5 0.7 shard_map.166
  65.2 2.6 %all-to-all-start.3 = ((bf16[32,16,128]{2,1,0:T(8,128)(2,1)}), bf16[32,16,128]{2,1,0:T(8,128)(2,1)S(1)}, u32[]{:S(2)}, u32[]{:S(2)}) async-start(bf16[32,16,128]{2,1,0:T(8,128)(2,1)} %shard_map.166), calls=%async_computation.3 | async-start | bytes 262144 | tf_op jit(solution)/shard_map/all_to_all | solution.py:546
  67.8 1.1 %shard_map.165 = (bf16[1,512,128]{2,1,0:T(8,128)(2,1)}, bf16[1,512,128]{2,1,0:T(8,128)(2,1)}) custom-call(bf16[8,112,256]{2,1,0:T(8,128)(2,1)S(1)} %all-to-all-done.1.in_ref, bf16[2,128,256]{2,1,0:T(8,128)(2,1)S(1)} %get-tuple-element.25.product_ref, bf16[2,128,256]{2,1,0:T(8,128)(2,1)S(1)} %get-tuple-element.26.grads_ref, bf16[128,384]{1,0:T(8,128)(2,1)S(1)} %copy-done.5, ...), custom_call_target="tpu_custom_call" | custom-call | flops 67108864 | bytes 786432 | tf_op jit(solution)/shard_map/pallas_call | solution.py:616
  68.9 0.7 shard_map.168
  69.6 6.4 %all-to-all-done.3.in_ref = bf16[32,16,128]{2,1,0:T(8,128)(2,1)S(1)} async-done(((bf16[32,16,128]{2,1,0:T(8,128)(2,1)}), bf16[32,16,128]{2,1,0:T(8,128)(2,1)S(1)}, u32[]{:S(2)}, u32[]{:S(2)}) %all-to-all-start.3) | async-done | bytes 131104 | tf_op jit(solution)/shard_map/all_to_all | solution.py:546
  76.0 0.8 %shard_map.167 = (f32[128,384]{1,0:T(8,128)}, f32[128,128]{1,0:T(8,128)}) custom-call(bf16[32,16,128]{2,1,0:T(8,128)(2,1)S(1)} %all-to-all-done.3.in_ref), custom_call_target="tpu_custom_call" | custom-call | flops 65536 | bytes 131072 | tf_op jit(solution)/shard_map/pallas_call | solution.py:643
  (11 shorter events, 0.0 us)
Async XLA Ops:
  0.6 0.9 %copy-start = (bf16[1,512,128]{2,1,0:T(8,128)(2,1)S(1)}, bf16[1,512,128]{2,1,0:T(8,128)(2,1)}, u32[]{:S(2)}) copy-start(bf16[1,512,128]{2,1,0:T(8,128)(2,1)} %series_ref.5) | copy-start | bytes 393220
  1.5 0.9 %copy-start.2 = (bf16[1,512,128]{2,1,0:T(8,128)(2,1)S(1)}, bf16[1,512,128]{2,1,0:T(8,128)(2,1)}, u32[]{:S(2)}) copy-start(bf16[1,512,128]{2,1,0:T(8,128)(2,1)} %cot_ref.5) | copy-start | bytes 393220
  2.5 0.9 %copy-start.4 = (bf16[128,384]{1,0:T(8,128)(2,1)S(1)}, bf16[128,384]{1,0:T(8,128)(2,1)}, u32[]{:S(2)}) copy-start(bf16[128,384]{1,0:T(8,128)(2,1)} %w_in_ref.5) | copy-start | bytes 294916
  3.3 0.8 copy-start.6
  4.1 0.7 copy-start.8
  4.8 0.7 copy-start.10
  5.5 0.7 copy-start.11
  26.8 0.7 copy-start.12
  26.8 0.7 copy-start.13
  32.5 3.6 %copy-start.1 = (bf16[1,512,128]{2,1,0:T(8,128)(2,1)S(1)}, bf16[1,512,128]{2,1,0:T(8,128)(2,1)}, u32[]{:S(2)}) copy-start(bf16[1,512,128]{2,1,0:T(8,128)(2,1)} %series_ref.5) | copy-start | bytes 393220
  32.5 3.7 %copy-start.3 = (bf16[1,512,128]{2,1,0:T(8,128)(2,1)S(1)}, bf16[1,512,128]{2,1,0:T(8,128)(2,1)}, u32[]{:S(2)}) copy-start(bf16[1,512,128]{2,1,0:T(8,128)(2,1)} %cot_ref.5) | copy-start | bytes 393220
  32.5 3.7 %copy-start.5 = (bf16[128,384]{1,0:T(8,128)(2,1)S(1)}, bf16[128,384]{1,0:T(8,128)(2,1)}, u32[]{:S(2)}) copy-start(bf16[128,384]{1,0:T(8,128)(2,1)} %w_in_ref.5) | copy-start | bytes 294916
  32.5 3.7 %copy-start.7 = (bf16[128,128]{1,0:T(8,128)(2,1)S(1)}, bf16[128,128]{1,0:T(8,128)(2,1)}, u32[]{:S(2)}) copy-start(bf16[128,128]{1,0:T(8,128)(2,1)} %w_out_ref.5) | copy-start | bytes 98308
  32.5 3.7 %copy-start.9 = (f32[3,384]{1,0:T(4,128)S(1)}, f32[3,384]{1,0:T(4,128)}, u32[]{:S(2)}) copy-start(f32[3,384]{1,0:T(4,128)} %taps_ref.7) | copy-start | bytes 13828
  32.5 17.5 %all-to-all-start.1 = ((bf16[8,112,256]{2,1,0:T(8,128)(2,1)}), bf16[8,112,256]{2,1,0:T(8,128)(2,1)S(1)}, u32[]{:S(2)}, u32[]{:S(2)}) async-start(bf16[8,112,256]{2,1,0:T(8,128)(2,1)} %get-tuple-element.23), calls=%async_computation.1 | async-start | bytes 917504 | tf_op jit(solution)/shard_map/all_to_all | solution.py:546
  65.2 10.8 %all-to-all-start.3 = ((bf16[32,16,128]{2,1,0:T(8,128)(2,1)}), bf16[32,16,128]{2,1,0:T(8,128)(2,1)S(1)}, u32[]{:S(2)}, u32[]{:S(2)}) async-start(bf16[32,16,128]{2,1,0:T(8,128)(2,1)} %shard_map.166), calls=%async_computation.3 | async-start | bytes 262144 | tf_op jit(solution)/shard_map/all_to_all | solution.py:546

commit v11 on v10

--- a/solution.py
+++ b/solution.py
@@ -14,14 +14,15 @@
 BF16 = jnp.bfloat16
 NT = (((1,), (1,)), ((), ()))
 VMEM_LIMIT = 24 * 1024 * 1024
-
-
-def call(body, out_shape, scratch=(), flops=0, moved=0):
+VMEM_ALL = 56 * 1024 * 1024
+
+
+def call(body, out_shape, scratch=(), flops=0, moved=0, limit=VMEM_LIMIT):
     return pl.pallas_call(
         body,
         out_shape=out_shape,
         scratch_shapes=list(scratch),
-        compiler_params=pltpu.CompilerParams(vmem_limit_bytes=VMEM_LIMIT),
+        compiler_params=pltpu.CompilerParams(vmem_limit_bytes=limit),
         cost_estimate=pl.CostEstimate(flops=flops, bytes_accessed=moved, transcendentals=0),
     )
 
@@ -67,7 +68,7 @@
 
 def gate_taps(taps_ref):
     width = taps_ref.shape[1] // 3
-    rows = jnp.concatenate([taps_ref[:, 2 * width :], jnp.zeros((5, width), F32)], axis=0)
+    rows = jnp.concatenate([taps_ref[0:3, 2 * width :], jnp.zeros((5, width), F32)], axis=0)
     cols = jnp.concatenate([rows] * (width // 8), axis=0).T
     return [cols[:, j : j + 1] for j in range(3)]
 
@@ -81,10 +82,27 @@
     return total
 
 
-def project_kernel(units, series_ref, cot_ref, w_in_ref, w_out_ref, taps_ref, one_ref, two_ref, out_ref):
+def project_kernel(
+    units,
+    series_ref,
+    cot_ref,
+    w_in_ref,
+    w_out_ref,
+    taps_ref,
+    skip_one_ref,
+    skip_two_ref,
+    one_ref,
+    two_ref,
+    out_ref,
+    params_ref,
+):
     _, block, width = series_ref.shape
     group = width // units
     parts = block // W
+    params_ref[...] = jnp.zeros(params_ref.shape, F32)
+    params_ref[0:3, :] = taps_ref[...]
+    params_ref[3:4, 0:width] = skip_one_ref[...]
+    params_ref[4:5, 0:width] = skip_two_ref[...]
     w_in_t = w_in_ref[...].T
     w_out = w_out_ref[...]
     proj = [dot_nt(w_in_t, series_ref[0, p * W : (p + 1) * W, :]) for p in range(parts)]
@@ -194,8 +212,6 @@
     units,
     fields_ref,
     taps_ref,
-    skip_one_ref,
-    skip_two_ref,
     out_ref,
     kept_ref,
     pad_ref,
@@ -231,8 +247,8 @@
         ]
         for kind in range(3)
     ]
-    skip_one = column(skip_one_ref[...])
-    skip_two = column(skip_two_ref[...])
+    skip_one = column(taps_ref[3:4, 0:width])
+    skip_two = column(taps_ref[4:5, 0:width])
     chunks = [slice(s * each, (s + 1) * each) for s in range(sources)]
 
     zeros = jnp.zeros((rows, W), BF16)
@@ -562,19 +578,21 @@
 
     devices = sources * copies
     packed = 3 * (block // W) * group + 16
-    fields = call(
+    skips = (skip_one.reshape(1, width), skip_two.reshape(1, width))
+    fields, params = call(
         functools.partial(project_kernel, units),
-        shape((sources, packed, W), BF16),
+        (shape((sources, packed, W), BF16), shape((8, 3 * width), F32)),
         flops=2 * block * width * 4 * width,
         moved=8 * block * width * 4,
-    )(series, cotangent, w_in, w_out, taps, filter_one, filter_two)
+        limit=VMEM_ALL,
+    )(series, cotangent, w_in, w_out, taps, *skips, filter_one, filter_two)
     fields = all_to_all(fields, "seq")
     held = call(
         gate_kernel,
         shape((3, block // W, width, W), F32),
         flops=2 * block * width * 2 * width,
         moved=4 * 4 * block * width,
-    )(series, cotangent, w_in, w_out, taps)
+    )(series, cotangent, w_in, w_out, params)
 
     sent, kept = call(
         functools.partial(operator_kernel, units),
@@ -587,7 +605,7 @@
         ],
         flops=4 * 2 * rows * length * W,
         moved=2 * W * length * 2 * 2,
-    )(fields, taps, skip_one.reshape(1, width), skip_two.reshape(1, width))
+    )(fields, params)
 
     back = all_to_all(sent, "seq")
 
@@ -610,7 +628,7 @@
         ),
         flops=2 * block * width * 4 * width,
         moved=2 * block * width * 6,
-    )(back, held, taps, series, cotangent, own)
+    )(back, held, params, series, cotangent, own)
     partial = all_to_all(partial, ("dp", "seq"))
 
     output, d_series = call(

time: 77.4 us -> 73.1 us (0.944)
  local copies, waits for them, and re-layouts: 6.27 us -> 0.02 us
  Pallas kernels: 12.2 us -> 14.1 us
    unnamed x28 -> x10, local copies, waits for them, and re-layouts: 6.27 us -> 0.02 us
    pallas_call x1, Pallas kernels: 0.5 us -> 2.34 us  [shards(): call(functools.partial(project_kernel, units), (shape((sources, packed, W...]
where the time goes in v11:
time: 73.1 us; the launch traced here: 72.7 us
  blocking collectives  34.1 us (47%)
  waiting for transfers between devices  17.6 us (24%)
  Pallas kernels  14.1 us (19%)
  starting transfers between devices  6.19 us (8%)
    all_to_all x2, blocking collectives, all_to_all(): return lax.all_to_all(blocks, axis, split_axis=0, concat_axis=0, tiled=True)  34.1 us
    all_to_all x2, waiting for transfers between devices, all_to_all(): return lax.all_to_all(blocks, axis, split_axis=0, concat_axis=0, tiled=True)  17.6 us
    all_to_all x2, starting transfers between devices, all_to_all(): return lax.all_to_all(blocks, axis, split_axis=0, concat_axis=0, tiled=True)  6.19 us
    pallas_call x1, Pallas kernels, shards(): call(functools.partial(operator_kernel, units), (shape((sources, packed,...  5.04 us
    pallas_call x1, Pallas kernels, shards(): call(functools.partial(project_kernel, units), (shape((sources, packed, W...  2.34 us
    pallas_call x1, Pallas kernels, shards(): call(functools.partial(gradient_kernel, units), shape((2 * (length // wid...  2.23 us
  transfers between devices with their start and end apart: 2, of which 2 were waited for; matrix products, arithmetic and copies ran while one was open for 0% of the time, Pallas kernels for 6%

profile of v11, /device:TPU:0, one launch (start us, length us, event | category | flops | bytes accessed | tf_op | source)
XLA Modules:
  0.0 72.7 jit_solution(10615064443439580774)
XLA Ops:
  0.6 2.3 %shard_map.160 = (bf16[8,112,256]{2,1,0:T(8,128)(2,1)}, f32[8,384]{1,0:T(8,128)}) custom-call(bf16[1,512,128]{2,1,0:T(8,128)(2,1)} %series_ref.5, bf16[1,512,128]{2,1,0:T(8,128)(2,1)} %cot_ref.5, bf16[128,384]{1,0:T(8,128)(2,1)} %w_in_ref.5, bf16[128,128]{1,0:T(8,128)(2,1)} %w_out_ref.5, f32[3,384]{1,0:T(4,128)} %taps_ref.1, f32[1,128]{1,0:T(1,128)} %bitcast.4, ...), custom_call_target="tpu_custom_call" | custom-call | flops 67108864 | bytes 2097152 | tf_op jit(solution)/shard_map/pallas_call | solution.py:582
  3.0 0.0 copy-start.4
  3.0 20.4 %all_to_all.20.fields_ref = bf16[8,112,256]{2,1,0:T(8,128)(2,1)S(1)} all-to-all(bf16[8,112,256]{2,1,0:T(8,128)(2,1)} %get-tuple-element.25), channel_id=1, replica_groups=mesh['dp'=4,'seq'=8] {'seq'}, dimensions={0} | all-to-all | bytes 917504 | tf_op jit(solution)/shard_map/all_to_all | solution.py:562
  23.4 0.0 copy-done.4
  23.4 5.0 %shard_map.161 = (bf16[8,112,256]{2,1,0:T(8,128)(2,1)}, bf16[7,256,256]{2,1,0:T(8,128)(2,1)S(1)}) custom-call(bf16[8,112,256]{2,1,0:T(8,128)(2,1)S(1)} %all_to_all.20.fields_ref, f32[8,384]{1,0:T(8,128)S(1)} %copy-done.4), custom_call_target="tpu_custom_call" | custom-call | flops 2147483648 | bytes 8388608 | tf_op jit(solution)/shard_map/pallas_call | solution.py:597
  28.4 0.0 copy-start
  28.4 0.0 copy-start.1
  28.4 0.0 copy-start.2
  28.4 0.0 copy-start.3
  28.4 3.6 %all-to-all-start.1 = ((bf16[8,112,256]{2,1,0:T(8,128)(2,1)}), bf16[8,112,256]{2,1,0:T(8,128)(2,1)S(1)}, u32[]{:S(2)}, u32[]{:S(2)}) async-start(bf16[8,112,256]{2,1,0:T(8,128)(2,1)} %get-tuple-element.27), calls=%async_computation.1 | async-start | bytes 917504 | tf_op jit(solution)/shard_map/all_to_all | solution.py:562
  32.1 0.0 copy-done
  32.1 0.0 copy-done.1
  32.1 0.0 copy-done.2
  32.1 0.0 copy-done.3
  32.1 0.4 shard_map.162.held_ref
  32.5 2.2 %shard_map.163.own_ref = f32[80,128]{1,0:T(8,128)S(1)} custom-call(bf16[8,112,256]{2,1,0:T(8,128)(2,1)S(1)} %all_to_all.20.fields_ref, bf16[7,256,256]{2,1,0:T(8,128)(2,1)S(1)} %get-tuple-element.28.kept_ref), custom_call_target="tpu_custom_call" | custom-call | flops 1073741824 | bytes 2097152 | tf_op jit(solution)/shard_map/pallas_call | solution.py:612
  34.8 11.2 %all-to-all-done.1.in_ref = bf16[8,112,256]{2,1,0:T(8,128)(2,1)S(1)} async-done(((bf16[8,112,256]{2,1,0:T(8,128)(2,1)}), bf16[8,112,256]{2,1,0:T(8,128)(2,1)S(1)}, u32[]{:S(2)}, u32[]{:S(2)}) %all-to-all-start.1) | async-done | bytes 458784 | tf_op jit(solution)/shard_map/all_to_all | solution.py:562
  45.9 0.8 %shard_map.164 = (bf16[32,32,128]{2,1,0:T(8,128)(2,1)S(1)}, bf16[2,128,256]{2,1,0:T(8,128)(2,1)S(1)}, bf16[2,128,256]{2,1,0:T(8,128)(2,1)S(1)}) custom-call(bf16[8,112,256]{2,1,0:T(8,128)(2,1)S(1)} %all-to-all-done.1.in_ref, f32[3,2,128,256]{3,2,1,0:T(8,128)S(1)} %shard_map.162.held_ref, f32[8,384]{1,0:T(8,128)S(1)} %copy-done.4, ...), custom_call_target="tpu_custom_call" | custom-call | flops 67108864 | bytes 786432 | tf_op jit(solution)/shard_map/pallas_call | solution.py:622
  46.8 13.7 %all_to_all.21.in_ref = bf16[32,32,128]{2,1,0:T(8,128)(2,1)S(1)} all-to-all(bf16[32,32,128]{2,1,0:T(8,128)(2,1)S(1)} %get-tuple-element.33), channel_id=1, replica_groups=mesh['dp'=4,'seq'=8] {'dp','seq'}, dimensions={0} | all-to-all | bytes 524288 | tf_op jit(solution)/shard_map/all_to_all | solution.py:562
  60.4 0.7 shard_map.166
  61.1 2.6 %all-to-all-start.3 = ((bf16[32,16,128]{2,1,0:T(8,128)(2,1)}), bf16[32,16,128]{2,1,0:T(8,128)(2,1)S(1)}, u32[]{:S(2)}, u32[]{:S(2)}) async-start(bf16[32,16,128]{2,1,0:T(8,128)(2,1)} %shard_map.166), calls=%async_computation.3 | async-start | bytes 262144 | tf_op jit(solution)/shard_map/all_to_all | solution.py:562
  63.7 1.1 %shard_map.165 = (bf16[1,512,128]{2,1,0:T(8,128)(2,1)}, bf16[1,512,128]{2,1,0:T(8,128)(2,1)}) custom-call(bf16[8,112,256]{2,1,0:T(8,128)(2,1)S(1)} %all-to-all-done.1.in_ref, bf16[2,128,256]{2,1,0:T(8,128)(2,1)S(1)} %get-tuple-element.29.product_ref, bf16[2,128,256]{2,1,0:T(8,128)(2,1)S(1)} %get-tuple-element.30.grads_ref, bf16[128,384]{1,0:T(8,128)(2,1)S(1)} %copy-done.2, ...), custom_call_target="tpu_custom_call" | custom-call | flops 67108864 | bytes 786432 | tf_op jit(solution)/shard_map/pallas_call | solution.py:634
  64.8 0.7 shard_map.168
  65.5 6.4 %all-to-all-done.3.in_ref = bf16[32,16,128]{2,1,0:T(8,128)(2,1)S(1)} async-done(((bf16[32,16,128]{2,1,0:T(8,128)(2,1)}), bf16[32,16,128]{2,1,0:T(8,128)(2,1)S(1)}, u32[]{:S(2)}, u32[]{:S(2)}) %all-to-all-start.3) | async-done | bytes 131104 | tf_op jit(solution)/shard_map/all_to_all | solution.py:562
  71.9 0.8 %shard_map.167 = (f32[128,384]{1,0:T(8,128)}, f32[128,128]{1,0:T(8,128)}) custom-call(bf16[32,16,128]{2,1,0:T(8,128)(2,1)S(1)} %all-to-all-done.3.in_ref), custom_call_target="tpu_custom_call" | custom-call | flops 65536 | bytes 131072 | tf_op jit(solution)/shard_map/pallas_call | solution.py:661
Async XLA Ops:
  3.0 20.4 %copy-start.4 = (f32[8,384]{1,0:T(8,128)S(1)}, f32[8,384]{1,0:T(8,128)}, u32[]{:S(2)}) copy-start(f32[8,384]{1,0:T(8,128)} %get-tuple-element.26.taps_ref) | copy-start | bytes 36868
  28.4 3.6 %copy-start = (bf16[1,512,128]{2,1,0:T(8,128)(2,1)S(1)}, bf16[1,512,128]{2,1,0:T(8,128)(2,1)}, u32[]{:S(2)}) copy-start(bf16[1,512,128]{2,1,0:T(8,128)(2,1)} %series_ref.5) | copy-start | bytes 393220
  28.4 3.6 %copy-start.1 = (bf16[1,512,128]{2,1,0:T(8,128)(2,1)S(1)}, bf16[1,512,128]{2,1,0:T(8,128)(2,1)}, u32[]{:S(2)}) copy-start(bf16[1,512,128]{2,1,0:T(8,128)(2,1)} %cot_ref.5) | copy-start | bytes 393220
  28.4 3.7 %copy-start.2 = (bf16[128,384]{1,0:T(8,128)(2,1)S(1)}, bf16[128,384]{1,0:T(8,128)(2,1)}, u32[]{:S(2)}) copy-start(bf16[128,384]{1,0:T(8,128)(2,1)} %w_in_ref.5) | copy-start | bytes 294916
  28.4 3.7 %copy-start.3 = (bf16[128,128]{1,0:T(8,128)(2,1)S(1)}, bf16[128,128]{1,0:T(8,128)(2,1)}, u32[]{:S(2)}) copy-start(bf16[128,128]{1,0:T(8,128)(2,1)} %w_out_ref.5) | copy-start | bytes 98308
  28.4 17.5 %all-to-all-start.1 = ((bf16[8,112,256]{2,1,0:T(8,128)(2,1)}), bf16[8,112,256]{2,1,0:T(8,128)(2,1)S(1)}, u32[]{:S(2)}, u32[]{:S(2)}) async-start(bf16[8,112,256]{2,1,0:T(8,128)(2,1)} %get-tuple-element.27), calls=%async_computation.1 | async-start | bytes 917504 | tf_op jit(solution)/shard_map/all_to_all | solution.py:562
  61.1 10.8 %all-to-all-start.3 = ((bf16[32,16,128]{2,1,0:T(8,128)(2,1)}), bf16[32,16,128]{2,1,0:T(8,128)(2,1)S(1)}, u32[]{:S(2)}, u32[]{:S(2)}) async-start(bf16[32,16,128]{2,1,0:T(8,128)(2,1)} %shard_map.166), calls=%async_computation.3 | async-start | bytes 262144 | tf_op jit(solution)/shard_map/all_to_all | solution.py:562

commit v12 on v11

--- a/solution.py
+++ b/solution.py
@@ -50,6 +50,18 @@
 def parts_of(tiles):
     each = W // TILE
     return [jnp.concatenate(tiles[at : at + each], axis=1) for at in range(0, len(tiles), each)]
+
+
+def fold(edges):
+    total = edges[..., :8, :]
+    for k in range(1, edges.shape[-2] // 8):
+        total = total + turned(edges[..., 8 * k : 8 * k + 8, :], 64 * k)
+    return total
+
+
+def unfold(edges, group):
+    pieces = [edges] + [turned(edges, W - 64 * k) for k in range(1, group // 8)]
+    return jnp.concatenate(pieces, axis=edges.ndim - 2)
 
 
 def earlier_parts(parts, j, before):
@@ -128,10 +140,7 @@
         row = u // repeat
         held = jnp.concatenate([line[row : row + 1] for line in lines], axis=0)
         held = jnp.concatenate([held, jnp.zeros((held.shape[0], W - width), F32)], axis=1)
-        held = jnp.concatenate([held, jnp.zeros((16 - held.shape[0], W), F32)], axis=0)
-        edge = edges[u * group : (u + 1) * group]
-        if group < 16:
-            edge = jnp.concatenate([edge, jnp.zeros((16 - group, W), F32)], axis=0)
+        edge = fold(edges[u * group : (u + 1) * group])
         out_ref[u, 3 * parts * group :, :] = (held + edge).astype(BF16)
 
 
@@ -168,7 +177,7 @@
             toep_ref[m, 0, at : at + 16, 0:TILE] = none.astype(BF16)
         held = {}
         for s in range(sources):
-            lines = fields_ref[s, start : start + 16, :].astype(F32)
+            lines = fields_ref[s, start:, :].astype(F32)
             for i in range(slots):
                 d, part = divmod(s * slots + i, W // TILE)
                 line = lines[m * slots + i : m * slots + i + 1, :TILE]
@@ -290,7 +299,7 @@
             total = total + scaled(jnp.concatenate(moved, axis=1), tap[kind][j])
         return total
 
-    edges = fields_ref[:, start : start + 16, :].astype(F32)[:, :group]
+    edges = unfold(fields_ref[:, start:, :].astype(F32), group)
     none = jnp.zeros((1, group, W), F32)
     before = jnp.concatenate([none, edges[:-1]], axis=0)
     following = jnp.concatenate([edges[1:], none], axis=0)
@@ -337,9 +346,7 @@
     heads = jnp.stack(heads[1:] + [none[0]])
     edges = jnp.where(lane < 4, turned(following, 128) * turned(heads, 2), 0.0)
     edges = jnp.where(lane < 2, turned(before, 128), edges)
-    if group < 16:
-        edges = jnp.concatenate([edges, jnp.zeros((sources, 16 - group, W), F32)], axis=1)
-    out_ref[:, start:, :] = edges.astype(BF16)
+    out_ref[:, start:, :] = fold(edges).astype(BF16)
     for s in range(sources):
         at = chunks[s]
         d_value = second_ref[at, :] + scaled(grad_ref[at, :], skip_one)
@@ -433,7 +440,7 @@
     group = width // units
     parts = block // W
     cols = gate_taps(taps_ref)
-    edges = in_ref[:, 3 * parts * group :, :].astype(F32)[:, :group].reshape(width, W)
+    edges = unfold(in_ref[:, 3 * parts * group :, :].astype(F32), group).reshape(width, W)
     lane = lanes_of(edges)
     second = [held_ref[0, p] for p in range(parts)]
     gate = [held_ref[1, p] for p in range(parts)]
@@ -577,7 +584,8 @@
     shape = jax.ShapeDtypeStruct
 
     devices = sources * copies
-    packed = 3 * (block // W) * group + 16
+    assert 2 * block // width == 8 and group in (8, 16)
+    packed = 3 * (block // W) * group + 8
     skips = (skip_one.reshape(1, width), skip_two.reshape(1, width))
     fields, params = call(
         functools.partial(project_kernel, units),

time: 73.1 us -> 71.7 us (0.981)
  no operation moved by 1% of the time
where the time goes in v12:
time: 71.7 us; the launch traced here: 71.3 us
  blocking collectives  33.4 us (47%)
  waiting for transfers between devices  16.9 us (24%)
  Pallas kernels  14.1 us (20%)
  starting transfers between devices  6.18 us (9%)
  between operations  0.72 us (1%)
    all_to_all x2, blocking collectives, all_to_all(): return lax.all_to_all(blocks, axis, split_axis=0, concat_axis=0, tiled=True)  33.4 us
    all_to_all x2, waiting for transfers between devices, all_to_all(): return lax.all_to_all(blocks, axis, split_axis=0, concat_axis=0, tiled=True)  16.9 us
    all_to_all x2, starting transfers between devices, all_to_all(): return lax.all_to_all(blocks, axis, split_axis=0, concat_axis=0, tiled=True)  6.18 us
    pallas_call x1, Pallas kernels, shards(): call(functools.partial(operator_kernel, units), (shape((sources, packed,...  4.91 us
    pallas_call x1, Pallas kernels, shards(): call(functools.partial(project_kernel, units), (shape((sources, packed, W...  2.4 us
    pallas_call x1, Pallas kernels, shards(): call(functools.partial(gradient_kernel, units), shape((2 * (length // wid...  2.23 us
  transfers between devices with their start and end apart: 2, of which 2 were waited for; matrix products, arithmetic and copies ran while one was open for 0% of the time, Pallas kernels for 6%

profile of v12, /device:TPU:0, one launch (start us, length us, event | category | flops | bytes accessed | tf_op | source)
XLA Modules:
  0.0 71.3 jit_solution(11424686635734312114)
XLA Ops:
  0.6 2.4 %shard_map.160 = (bf16[8,104,256]{2,1,0:T(8,128)(2,1)}, f32[8,384]{1,0:T(8,128)}) custom-call(bf16[1,512,128]{2,1,0:T(8,128)(2,1)} %series_ref.5, bf16[1,512,128]{2,1,0:T(8,128)(2,1)} %cot_ref.5, bf16[128,384]{1,0:T(8,128)(2,1)} %w_in_ref.5, bf16[128,128]{1,0:T(8,128)(2,1)} %w_out_ref.5, f32[3,384]{1,0:T(4,128)} %taps_ref.1, f32[1,128]{1,0:T(1,128)} %bitcast.4, ...), custom_call_target="tpu_custom_call" | custom-call | flops 67108864 | bytes 2097152 | tf_op jit(solution)/shard_map/pallas_call | solution.py:590
  3.0 0.0 copy-start.4
  3.0 19.7 %all_to_all.20.fields_ref = bf16[8,104,256]{2,1,0:T(8,128)(2,1)S(1)} all-to-all(bf16[8,104,256]{2,1,0:T(8,128)(2,1)} %get-tuple-element.25), channel_id=1, replica_groups=mesh['dp'=4,'seq'=8] {'seq'}, dimensions={0} | all-to-all | bytes 851968 | tf_op jit(solution)/shard_map/all_to_all | solution.py:569
  22.8 0.0 copy-done.4
  22.8 4.9 %shard_map.161 = (bf16[8,104,256]{2,1,0:T(8,128)(2,1)}, bf16[7,256,256]{2,1,0:T(8,128)(2,1)S(1)}) custom-call(bf16[8,104,256]{2,1,0:T(8,128)(2,1)S(1)} %all_to_all.20.fields_ref, f32[8,384]{1,0:T(8,128)S(1)} %copy-done.4), custom_call_target="tpu_custom_call" | custom-call | flops 2147483648 | bytes 8388608 | tf_op jit(solution)/shard_map/pallas_call | solution.py:605
  27.7 0.0 copy-start
  27.7 0.0 copy-start.1
  27.7 0.0 copy-start.2
  27.7 0.0 copy-start.3
  27.7 3.6 %all-to-all-start.1 = ((bf16[8,104,256]{2,1,0:T(8,128)(2,1)}), bf16[8,104,256]{2,1,0:T(8,128)(2,1)S(1)}, u32[]{:S(2)}, u32[]{:S(2)}) async-start(bf16[8,104,256]{2,1,0:T(8,128)(2,1)} %get-tuple-element.27), calls=%async_computation.1 | async-start | bytes 851968 | tf_op jit(solution)/shard_map/all_to_all | solution.py:569
  31.3 0.0 copy-done
  31.3 0.0 copy-done.1
  31.3 0.0 copy-done.2
  31.3 0.0 copy-done.3
  31.3 0.4 shard_map.162.held_ref
  31.8 2.2 %shard_map.163.own_ref = f32[80,128]{1,0:T(8,128)S(1)} custom-call(bf16[8,104,256]{2,1,0:T(8,128)(2,1)S(1)} %all_to_all.20.fields_ref, bf16[7,256,256]{2,1,0:T(8,128)(2,1)S(1)} %get-tuple-element.28.kept_ref), custom_call_target="tpu_custom_call" | custom-call | flops 1073741824 | bytes 2097152 | tf_op jit(solution)/shard_map/pallas_call | solution.py:620
  34.0 10.5 %all-to-all-done.1.in_ref = bf16[8,104,256]{2,1,0:T(8,128)(2,1)S(1)} async-done(((bf16[8,104,256]{2,1,0:T(8,128)(2,1)}), bf16[8,104,256]{2,1,0:T(8,128)(2,1)S(1)}, u32[]{:S(2)}, u32[]{:S(2)}) %all-to-all-start.1) | async-done | bytes 426016 | tf_op jit(solution)/shard_map/all_to_all | solution.py:569
  44.5 0.9 %shard_map.164 = (bf16[32,32,128]{2,1,0:T(8,128)(2,1)S(1)}, bf16[2,128,256]{2,1,0:T(8,128)(2,1)S(1)}, bf16[2,128,256]{2,1,0:T(8,128)(2,1)S(1)}) custom-call(bf16[8,104,256]{2,1,0:T(8,128)(2,1)S(1)} %all-to-all-done.1.in_ref, f32[3,2,128,256]{3,2,1,0:T(8,128)S(1)} %shard_map.162.held_ref, f32[8,384]{1,0:T(8,128)S(1)} %copy-done.4, ...), custom_call_target="tpu_custom_call" | custom-call | flops 67108864 | bytes 786432 | tf_op jit(solution)/shard_map/pallas_call | solution.py:630
  45.3 13.7 %all_to_all.21.in_ref = bf16[32,32,128]{2,1,0:T(8,128)(2,1)S(1)} all-to-all(bf16[32,32,128]{2,1,0:T(8,128)(2,1)S(1)} %get-tuple-element.33), channel_id=1, replica_groups=mesh['dp'=4,'seq'=8] {'dp','seq'}, dimensions={0} | all-to-all | bytes 524288 | tf_op jit(solution)/shard_map/all_to_all | solution.py:569
  59.0 0.7 shard_map.166
  59.7 2.6 %all-to-all-start.3 = ((bf16[32,16,128]{2,1,0:T(8,128)(2,1)}), bf16[32,16,128]{2,1,0:T(8,128)(2,1)S(1)}, u32[]{:S(2)}, u32[]{:S(2)}) async-start(bf16[32,16,128]{2,1,0:T(8,128)(2,1)} %shard_map.166), calls=%async_computation.3 | async-start | bytes 262144 | tf_op jit(solution)/shard_map/all_to_all | solution.py:569
  62.3 1.1 %shard_map.165 = (bf16[1,512,128]{2,1,0:T(8,128)(2,1)}, bf16[1,512,128]{2,1,0:T(8,128)(2,1)}) custom-call(bf16[8,104,256]{2,1,0:T(8,128)(2,1)S(1)} %all-to-all-done.1.in_ref, bf16[2,128,256]{2,1,0:T(8,128)(2,1)S(1)} %get-tuple-element.29.product_ref, bf16[2,128,256]{2,1,0:T(8,128)(2,1)S(1)} %get-tuple-element.30.grads_ref, bf16[128,384]{1,0:T(8,128)(2,1)S(1)} %copy-done.2, ...), custom_call_target="tpu_custom_call" | custom-call | flops 67108864 | bytes 786432 | tf_op jit(solution)/shard_map/pallas_call | solution.py:642
  63.3 0.7 %shard_map.168 = (f32[8,512]{1,0:T(8,128)}, f32[8,512]{1,0:T(8,128)}, f32[3,384]{1,0:T(4,128)}, f32[1,128]{1,0:T(1,128)}, f32[1,128]{1,0:T(1,128)}) custom-call(bf16[32,32,128]{2,1,0:T(8,128)(2,1)S(1)} %all_to_all.21.in_ref), custom_call_target="tpu_custom_call" | custom-call | flops 131072 | bytes 524288 | tf_op jit(solution)/shard_map/pallas_call | solution.py:657
  64.1 6.4 %all-to-all-done.3.in_ref = bf16[32,16,128]{2,1,0:T(8,128)(2,1)S(1)} async-done(((bf16[32,16,128]{2,1,0:T(8,128)(2,1)}), bf16[32,16,128]{2,1,0:T(8,128)(2,1)S(1)}, u32[]{:S(2)}, u32[]{:S(2)}) %all-to-all-start.3) | async-done | bytes 131104 | tf_op jit(solution)/shard_map/all_to_all | solution.py:569
  70.5 0.8 %shard_map.167 = (f32[128,384]{1,0:T(8,128)}, f32[128,128]{1,0:T(8,128)}) custom-call(bf16[32,16,128]{2,1,0:T(8,128)(2,1)S(1)} %all-to-all-done.3.in_ref), custom_call_target="tpu_custom_call" | custom-call | flops 65536 | bytes 131072 | tf_op jit(solution)/shard_map/pallas_call | solution.py:669
Async XLA Ops:
  3.0 19.7 %copy-start.4 = (f32[8,384]{1,0:T(8,128)S(1)}, f32[8,384]{1,0:T(8,128)}, u32[]{:S(2)}) copy-start(f32[8,384]{1,0:T(8,128)} %get-tuple-element.26.taps_ref) | copy-start | bytes 36868
  27.7 3.6 %copy-start = (bf16[1,512,128]{2,1,0:T(8,128)(2,1)S(1)}, bf16[1,512,128]{2,1,0:T(8,128)(2,1)}, u32[]{:S(2)}) copy-start(bf16[1,512,128]{2,1,0:T(8,128)(2,1)} %series_ref.5) | copy-start | bytes 393220
  27.7 3.6 %copy-start.1 = (bf16[1,512,128]{2,1,0:T(8,128)(2,1)S(1)}, bf16[1,512,128]{2,1,0:T(8,128)(2,1)}, u32[]{:S(2)}) copy-start(bf16[1,512,128]{2,1,0:T(8,128)(2,1)} %cot_ref.5) | copy-start | bytes 393220
  27.7 3.6 %copy-start.2 = (bf16[128,384]{1,0:T(8,128)(2,1)S(1)}, bf16[128,384]{1,0:T(8,128)(2,1)}, u32[]{:S(2)}) copy-start(bf16[128,384]{1,0:T(8,128)(2,1)} %w_in_ref.5) | copy-start | bytes 294916
  27.7 3.7 %copy-start.3 = (bf16[128,128]{1,0:T(8,128)(2,1)S(1)}, bf16[128,128]{1,0:T(8,128)(2,1)}, u32[]{:S(2)}) copy-start(bf16[128,128]{1,0:T(8,128)(2,1)} %w_out_ref.5) | copy-start | bytes 98308
  27.7 16.8 %all-to-all-start.1 = ((bf16[8,104,256]{2,1,0:T(8,128)(2,1)}), bf16[8,104,256]{2,1,0:T(8,128)(2,1)S(1)}, u32[]{:S(2)}, u32[]{:S(2)}) async-start(bf16[8,104,256]{2,1,0:T(8,128)(2,1)} %get-tuple-element.27), calls=%async_computation.1 | async-start | bytes 851968 | tf_op jit(solution)/shard_map/all_to_all | solution.py:569
  59.7 10.8 %all-to-all-start.3 = ((bf16[32,16,128]{2,1,0:T(8,128)(2,1)}), bf16[32,16,128]{2,1,0:T(8,128)(2,1)S(1)}, u32[]{:S(2)}, u32[]{:S(2)}) async-start(bf16[32,16,128]{2,1,0:T(8,128)(2,1)} %shard_map.166), calls=%async_computation.3 | async-start | bytes 262144 | tf_op jit(solution)/shard_map/all_to_all | solution.py:569

commit v13 on v12

--- a/solution.py
+++ b/solution.py
@@ -371,7 +371,7 @@
             out_ref[s, kind * each : (kind + 1) * each, :] = total.astype(BF16)
 
 
-def gradient_kernel(units, fields_ref, kept_ref, out_ref, pad_ref, corr_ref):
+def gradient_kernel(units, fields_ref, kept_ref, low_ref, pad_ref, corr_ref, out_ref):
     sources, _, _ = fields_ref.shape
     _, rows, _ = kept_ref.shape
     _, length = corr_ref.shape
@@ -426,6 +426,7 @@
     for m in range(2):
         put(6 + m, kept_ref[2 + m].astype(F32) * kept_ref[m].astype(F32))
     out_ref[2 * lines : 2 * lines + 16, :] = jnp.concatenate(small, axis=0)
+    low_ref[...] = out_ref[...].astype(BF16)
 
 
 def received_field(in_ref, units, group, parts, kind, part):
@@ -433,9 +434,8 @@
     return in_ref[:, at : at + group, :].reshape(units * group, W)
 
 
-def partial_kernel(
-    units, in_ref, held_ref, taps_ref, series_ref, cot_ref, own_ref, part_ref, product_ref, grads_ref
-):
+def partial_kernel(units, copies, in_ref, held_ref, taps_ref, series_ref, cot_ref, *refs):
+    own_refs, (part_ref, product_ref, grads_ref) = refs[:copies], refs[copies:]
     _, block, width = series_ref.shape
     group = width // units
     parts = block // W
@@ -474,21 +474,26 @@
     small = small.T[0:3]
 
     weights = jnp.concatenate([w_in_part, w_out_part], axis=0)
+    own = own_refs[0][...].astype(F32)
+    for ref in own_refs[1:]:
+        own = own + ref[...].astype(F32)
     targets, sent, _ = part_ref.shape
     each = weights.shape[0] // targets
     sources = in_ref.shape[0]
-    lines = (own_ref.shape[0] - 16) // 2
+    lines = (own.shape[0] - 16) // 2
     slots = lines // sources
-    spare = sent - each - 2 * slots - 4
+    share = 2 * slots // copies
+    mine = lax.axis_index("dp")
+    spare = sent - each - share - 4
     spare = [jnp.zeros((spare, width), F32)] if spare else []
     rests = []
     for s in range(sources):
-        rows = [
-            own_ref[s * slots : (s + 1) * slots, :],
-            own_ref[lines + s * slots : lines + (s + 1) * slots, :],
-            own_ref[2 * lines : 2 * lines + 1, :],
-            small,
-        ]
+        rows = [own[order * lines + s * slots + q][None] for order in range(2) for q in range(slots)]
+        held = 0.0
+        for k in range(copies):
+            block = jnp.concatenate(rows[k * share : (k + 1) * share], axis=0)
+            held += jnp.where(mine == k, block, 0.0)
+        rows = [held, own[2 * lines : 2 * lines + 1], small]
         rests.append(jnp.concatenate(rows + spare, axis=0))
     for g in range(targets):
         block = [weights[g * each : (g + 1) * each], rests[g % sources]]
@@ -524,12 +529,15 @@
     filters, block = one_ref.shape
     slots = block // width
     group = width // units
+    share = 2 * slots * units // targets
     by_unit = []
+    gate = 0.0
     for u in range(units):
-        sums = 0.0
-        for g in range(u, targets, units):
-            sums += in_ref[g, each:, :].astype(F32)
-        by_unit.append(sums * scale)
+        rows = [in_ref[g, each:, :].astype(F32) * scale for g in range(u, targets, units)]
+        for held in rows:
+            gate += held[share + 1 : share + 4]
+        shares = [held[:share] for held in rows]
+        by_unit.append(jnp.concatenate(shares + [rows[0][share : share + 1]], axis=0))
     repeat = units // filters
     for f in range(filters):
         sums = by_unit[f * repeat]
@@ -547,7 +555,6 @@
         moved = pltpu.roll(held, shift * group, 1) if shift else held
         moved = jnp.where(lane // group == row, moved, 0.0)
         small += pltpu.roll(moved, units - shift, 0) if shift else moved
-    gate = sum(by_unit)[2 * slots + 1 : 2 * slots + 4]
     for j in range(3):
         for kind in range(2):
             n = 2 * j + kind
@@ -619,16 +626,23 @@
 
     own = call(
         functools.partial(gradient_kernel, units),
-        shape((2 * (length // width) + 16, width), F32),
-        [pltpu.VMEM((2 * rows, W), BF16), pltpu.VMEM((W, length), F32)],
+        shape((2 * (length // width) + 16, width), BF16),
+        [
+            pltpu.VMEM((2 * rows, W), BF16),
+            pltpu.VMEM((W, length), F32),
+            pltpu.VMEM((2 * (length // width) + 16, width), F32),
+        ],
         flops=2 * 2 * rows * length * W,
         moved=2 * length * width * 2,
     )(fields, kept)
 
     each = 4 * width // devices
-    sent_rows = -(-(each + 2 * (block // width) + 4) // 16) * 16
+    around = [[(i, (i + d) % copies) for i in range(copies)] for d in range(1, copies)]
+    owns = [own] + [lax.ppermute(own, "dp", route) for route in around]
+    assert 2 * (block // width) % copies == 0
+    sent_rows = -(-(each + 2 * (block // width) // copies + 4) // 8) * 8
     partial, product, grads = call(
-        functools.partial(partial_kernel, units),
+        functools.partial(partial_kernel, units, copies),
         (
             shape((devices, sent_rows, width), BF16),
             shape((block // W, width, W), BF16),
@@ -636,7 +650,7 @@
         ),
         flops=2 * block * width * 4 * width,
         moved=2 * block * width * 6,
-    )(back, held, params, series, cotangent, own)
+    )(back, held, params, series, cotangent, *owns)
     partial = all_to_all(partial, ("dp", "seq"))
 
     output, d_series = call(

time: 71.7 us -> 70 us (0.976)
  waiting for transfers between devices: 16.9 us -> 12.3 us
  starting transfers between devices: 6.18 us -> 10.7 us
  blocking collectives: 33.4 us -> 31.7 us
    all_to_all x2, waiting for transfers between devices: 16.9 us -> 10.5 us  [all_to_all(): return lax.all_to_all(blocks, axis, split_axis=0, concat_axis=0, tiled=True)]
    ppermute x0 -> x3, starting transfers between devices: none -> 4.52 us  [shards(): owns = [own] + [lax.ppermute(own, 'dp', route) for route in around]]
    ppermute x0 -> x3, waiting for transfers between devices: none -> 1.89 us  [shards(): owns = [own] + [lax.ppermute(own, 'dp', route) for route in around]]
    all_to_all x2, blocking collectives: 33.4 us -> 31.7 us  [all_to_all(): return lax.all_to_all(blocks, axis, split_axis=0, concat_axis=0, tiled=True)]
  transfers between devices with their start and end apart: 2 -> 5, of which waited for: 2 -> 4; matrix products, arithmetic and copies ran while one was open for 0% -> 0% of each run, Pallas kernels for 6% -> 6%
where the time goes in v13:
time: 70 us; the launch traced here: 69.6 us
  blocking collectives  31.7 us (45%)
  Pallas kernels  14 us (20%)
  waiting for transfers between devices  12.3 us (18%)
  starting transfers between devices  10.7 us (15%)
  between operations  0.73 us (1%)
    all_to_all x2, blocking collectives, all_to_all(): return lax.all_to_all(blocks, axis, split_axis=0, concat_axis=0, tiled=True)  31.7 us
    all_to_all x2, waiting for transfers between devices, all_to_all(): return lax.all_to_all(blocks, axis, split_axis=0, concat_axis=0, tiled=True)  10.5 us
    all_to_all x2, starting transfers between devices, all_to_all(): return lax.all_to_all(blocks, axis, split_axis=0, concat_axis=0, tiled=True)  6.18 us
    pallas_call x1, Pallas kernels, shards(): call(functools.partial(operator_kernel, units), (shape((sources, packed,...  4.89 us
    ppermute x3, starting transfers between devices, shards(): owns = [own] + [lax.ppermute(own, 'dp', route) for route in around]  4.52 us
    pallas_call x1, Pallas kernels, shards(): call(functools.partial(project_kernel, units), (shape((sources, packed, W...  2.38 us
    pallas_call x1, Pallas kernels, shards(): call(functools.partial(gradient_kernel, units), shape((2 * (length // wid...  2.21 us
    ppermute x3, waiting for transfers between devices, shards(): owns = [own] + [lax.ppermute(own, 'dp', route) for route in around]  1.89 us
  transfers between devices with their start and end apart: 5, of which 4 were waited for; matrix products, arithmetic and copies ran while one was open for 0% of the time, Pallas kernels for 6%

profile of v13, /device:TPU:0, one launch (start us, length us, event | category | flops | bytes accessed | tf_op | source)
XLA Modules:
  0.0 69.6 jit_solution(7568126426874623159)
XLA Ops:
  0.6 2.4 %shard_map.160 = (bf16[8,104,256]{2,1,0:T(8,128)(2,1)}, f32[8,384]{1,0:T(8,128)}) custom-call(bf16[1,512,128]{2,1,0:T(8,128)(2,1)} %series_ref.5, bf16[1,512,128]{2,1,0:T(8,128)(2,1)} %cot_ref.5, bf16[128,384]{1,0:T(8,128)(2,1)} %w_in_ref.5, bf16[128,128]{1,0:T(8,128)(2,1)} %w_out_ref.5, f32[3,384]{1,0:T(4,128)} %taps_ref.1, f32[1,128]{1,0:T(1,128)} %bitcast.4, ...), custom_call_target="tpu_custom_call" | custom-call | flops 67108864 | bytes 2097152 | tf_op jit(solution)/shard_map/pallas_call | solution.py:597
  3.0 0.0 copy-start.4
  3.0 19.7 %all_to_all.20.fields_ref = bf16[8,104,256]{2,1,0:T(8,128)(2,1)S(1)} all-to-all(bf16[8,104,256]{2,1,0:T(8,128)(2,1)} %get-tuple-element.25), channel_id=1, replica_groups=mesh['dp'=4,'seq'=8] {'seq'}, dimensions={0} | all-to-all | bytes 851968 | tf_op jit(solution)/shard_map/all_to_all | solution.py:576
  22.7 0.0 copy-done.4
  22.7 4.9 %shard_map.161 = (bf16[8,104,256]{2,1,0:T(8,128)(2,1)}, bf16[7,256,256]{2,1,0:T(8,128)(2,1)S(1)}) custom-call(bf16[8,104,256]{2,1,0:T(8,128)(2,1)S(1)} %all_to_all.20.fields_ref, f32[8,384]{1,0:T(8,128)S(1)} %copy-done.4), custom_call_target="tpu_custom_call" | custom-call | flops 2147483648 | bytes 8388608 | tf_op jit(solution)/shard_map/pallas_call | solution.py:612
  27.6 3.5 %all-to-all-start.1 = ((bf16[8,104,256]{2,1,0:T(8,128)(2,1)}), bf16[8,104,256]{2,1,0:T(8,128)(2,1)S(1)}, u32[]{:S(2)}, u32[]{:S(2)}) async-start(bf16[8,104,256]{2,1,0:T(8,128)(2,1)} %get-tuple-element.27), calls=%async_computation.1 | async-start | bytes 851968 | tf_op jit(solution)/shard_map/all_to_all | solution.py:576
  31.1 0.0 copy-start
  31.1 0.0 copy-start.1
  31.1 0.0 copy-start.2
  31.1 0.0 copy-start.3
  31.2 2.2 %shard_map.163.refs_0_ = bf16[80,128]{1,0:T(8,128)(2,1)S(1)} custom-call(bf16[8,104,256]{2,1,0:T(8,128)(2,1)S(1)} %all_to_all.20.fields_ref, bf16[7,256,256]{2,1,0:T(8,128)(2,1)S(1)} %get-tuple-element.28.kept_ref), custom_call_target="tpu_custom_call" | custom-call | flops 1073741824 | bytes 2097152 | tf_op jit(solution)/shard_map/pallas_call | solution.py:627
  33.4 1.6 %collective-permute-start = (bf16[80,128]{1,0:T(8,128)(2,1)S(1)}, bf16[80,128]{1,0:T(8,128)(2,1)S(1)}, u32[]{:S(2)}, u32[]{:S(2)}) collective-permute-start(bf16[80,128]{1,0:T(8,128)(2,1)S(1)} %shard_map.163.refs_0_), channel_id=1, source_target_pairs={{0,8},{8,16},{16,24},{24,0},{1,9},{9,17},{17,25},{25,1},{2,10},{10... | collective-permute-start | bytes 61448 | tf_op jit(solution)/shard_map/ppermute | solution.py:641
  34.9 1.5 %collective-permute-start.1 = (bf16[80,128]{1,0:T(8,128)(2,1)S(1)}, bf16[80,128]{1,0:T(8,128)(2,1)S(1)}, u32[]{:S(2)}, u32[]{:S(2)}) collective-permute-start(bf16[80,128]{1,0:T(8,128)(2,1)S(1)} %shard_map.163.refs_0_), channel_id=1, source_target_pairs={{0,16},{8,24},{16,0},{24,8},{1,17},{9,25},{17,1},{25,9},{2,18},{10... | collective-permute-start | bytes 61448 | tf_op jit(solution)/shard_map/ppermute | solution.py:641
  36.4 1.4 %collective-permute-start.2 = (bf16[80,128]{1,0:T(8,128)(2,1)S(1)}, bf16[80,128]{1,0:T(8,128)(2,1)S(1)}, u32[]{:S(2)}, u32[]{:S(2)}) collective-permute-start(bf16[80,128]{1,0:T(8,128)(2,1)S(1)} %shard_map.163.refs_0_), channel_id=1, source_target_pairs={{0,24},{8,0},{16,8},{24,16},{1,25},{9,1},{17,9},{25,17},{2,26},{10... | collective-permute-start | bytes 61448 | tf_op jit(solution)/shard_map/ppermute | solution.py:641
  37.9 0.0 copy-done
  37.9 0.0 copy-done.1
  37.9 0.0 copy-done.2
  37.9 0.0 copy-done.3
  37.9 0.4 shard_map.162.held_ref
  38.3 0.0 collective-permute-done.refs_1_
  38.3 0.4 collective-permute-done.1.refs_2_
  38.7 1.5 %collective-permute-done.2.refs_3_ = bf16[80,128]{1,0:T(8,128)(2,1)S(1)} collective-permute-done((bf16[80,128]{1,0:T(8,128)(2,1)S(1)}, bf16[80,128]{1,0:T(8,128)(2,1)S(1)}, u32[]{:S(2)}, u32[]{:S(2)}) %collective-permute-start.2) | collective-permute-done | bytes 20512 | tf_op jit(solution)/shard_map/ppermute | solution.py:641
  40.2 4.0 %all-to-all-done.1.in_ref = bf16[8,104,256]{2,1,0:T(8,128)(2,1)S(1)} async-done(((bf16[8,104,256]{2,1,0:T(8,128)(2,1)}), bf16[8,104,256]{2,1,0:T(8,128)(2,1)S(1)}, u32[]{:S(2)}, u32[]{:S(2)}) %all-to-all-start.1) | async-done | bytes 426016 | tf_op jit(solution)/shard_map/all_to_all | solution.py:576
  44.3 0.9 %shard_map.164 = (bf16[32,24,128]{2,1,0:T(8,128)(2,1)S(1)}, bf16[2,128,256]{2,1,0:T(8,128)(2,1)S(1)}, bf16[2,128,256]{2,1,0:T(8,128)(2,1)S(1)}) custom-call(bf16[8,104,256]{2,1,0:T(8,128)(2,1)S(1)} %all-to-all-done.1.in_ref, f32[3,2,128,256]{3,2,1,0:T(8,128)S(1)} %shard_map.162.held_ref, f32[8,384]{1,0:T(8,128)S(1)} %copy-done.4, ...), custom_call_target="tpu_custom_call" | custom-call | flops 67108864 | bytes 786432 | tf_op jit(solution)/shard_map/pallas_call | solution.py:644
  45.1 12.0 %all_to_all.21.in_ref = bf16[32,24,128]{2,1,0:T(8,128)(2,1)S(1)} all-to-all(bf16[32,24,128]{2,1,0:T(8,128)(2,1)S(1)} %get-tuple-element.33), channel_id=1, replica_groups=mesh['dp'=4,'seq'=8] {'dp','seq'}, dimensions={0} | all-to-all | bytes 393216 | tf_op jit(solution)/shard_map/all_to_all | solution.py:576
  57.2 0.7 %shard_map.166 = bf16[32,16,128]{2,1,0:T(8,128)(2,1)} custom-call(bf16[32,24,128]{2,1,0:T(8,128)(2,1)S(1)} %all_to_all.21.in_ref), custom_call_target="tpu_custom_call" | custom-call | flops 65536 | bytes 262144 | tf_op jit(solution)/shard_map/pallas_call | solution.py:663
  57.9 2.7 %all-to-all-start.3 = ((bf16[32,16,128]{2,1,0:T(8,128)(2,1)}), bf16[32,16,128]{2,1,0:T(8,128)(2,1)S(1)}, u32[]{:S(2)}, u32[]{:S(2)}) async-start(bf16[32,16,128]{2,1,0:T(8,128)(2,1)} %shard_map.166), calls=%async_computation.3 | async-start | bytes 262144 | tf_op jit(solution)/shard_map/all_to_all | solution.py:576
  60.6 1.1 %shard_map.165 = (bf16[1,512,128]{2,1,0:T(8,128)(2,1)}, bf16[1,512,128]{2,1,0:T(8,128)(2,1)}) custom-call(bf16[8,104,256]{2,1,0:T(8,128)(2,1)S(1)} %all-to-all-done.1.in_ref, bf16[2,128,256]{2,1,0:T(8,128)(2,1)S(1)} %get-tuple-element.29.product_ref, bf16[2,128,256]{2,1,0:T(8,128)(2,1)S(1)} %get-tuple-element.30.grads_ref, bf16[128,384]{1,0:T(8,128)(2,1)S(1)} %copy-done.2, ...), custom_call_target="tpu_custom_call" | custom-call | flops 67108864 | bytes 786432 | tf_op jit(solution)/shard_map/pallas_call | solution.py:656
  61.7 0.7 %shard_map.168 = (f32[8,512]{1,0:T(8,128)}, f32[8,512]{1,0:T(8,128)}, f32[3,384]{1,0:T(4,128)}, f32[1,128]{1,0:T(1,128)}, f32[1,128]{1,0:T(1,128)}) custom-call(bf16[32,24,128]{2,1,0:T(8,128)(2,1)S(1)} %all_to_all.21.in_ref), custom_call_target="tpu_custom_call" | custom-call | flops 98304 | bytes 393216 | tf_op jit(solution)/shard_map/pallas_call | solution.py:671
  62.4 6.4 %all-to-all-done.3.in_ref = bf16[32,16,128]{2,1,0:T(8,128)(2,1)S(1)} async-done(((bf16[32,16,128]{2,1,0:T(8,128)(2,1)}), bf16[32,16,128]{2,1,0:T(8,128)(2,1)S(1)}, u32[]{:S(2)}, u32[]{:S(2)}) %all-to-all-start.3) | async-done | bytes 131104 | tf_op jit(solution)/shard_map/all_to_all | solution.py:576
  68.8 0.8 %shard_map.167 = (f32[128,384]{1,0:T(8,128)}, f32[128,128]{1,0:T(8,128)}) custom-call(bf16[32,16,128]{2,1,0:T(8,128)(2,1)S(1)} %all-to-all-done.3.in_ref), custom_call_target="tpu_custom_call" | custom-call | flops 65536 | bytes 131072 | tf_op jit(solution)/shard_map/pallas_call | solution.py:683
Async XLA Ops:
  3.0 19.7 %copy-start.4 = (f32[8,384]{1,0:T(8,128)S(1)}, f32[8,384]{1,0:T(8,128)}, u32[]{:S(2)}) copy-start(f32[8,384]{1,0:T(8,128)} %get-tuple-element.26.taps_ref) | copy-start | bytes 36868
  27.6 16.6 %all-to-all-start.1 = ((bf16[8,104,256]{2,1,0:T(8,128)(2,1)}), bf16[8,104,256]{2,1,0:T(8,128)(2,1)S(1)}, u32[]{:S(2)}, u32[]{:S(2)}) async-start(bf16[8,104,256]{2,1,0:T(8,128)(2,1)} %get-tuple-element.27), calls=%async_computation.1 | async-start | bytes 851968 | tf_op jit(solution)/shard_map/all_to_all | solution.py:576
  31.1 6.8 %copy-start = (bf16[1,512,128]{2,1,0:T(8,128)(2,1)S(1)}, bf16[1,512,128]{2,1,0:T(8,128)(2,1)}, u32[]{:S(2)}) copy-start(bf16[1,512,128]{2,1,0:T(8,128)(2,1)} %series_ref.5) | copy-start | bytes 393220
  31.1 6.8 %copy-start.1 = (bf16[1,512,128]{2,1,0:T(8,128)(2,1)S(1)}, bf16[1,512,128]{2,1,0:T(8,128)(2,1)}, u32[]{:S(2)}) copy-start(bf16[1,512,128]{2,1,0:T(8,128)(2,1)} %cot_ref.5) | copy-start | bytes 393220
  31.1 6.8 %copy-start.2 = (bf16[128,384]{1,0:T(8,128)(2,1)S(1)}, bf16[128,384]{1,0:T(8,128)(2,1)}, u32[]{:S(2)}) copy-start(bf16[128,384]{1,0:T(8,128)(2,1)} %w_in_ref.5) | copy-start | bytes 294916
  31.1 6.8 %copy-start.3 = (bf16[128,128]{1,0:T(8,128)(2,1)S(1)}, bf16[128,128]{1,0:T(8,128)(2,1)}, u32[]{:S(2)}) copy-start(bf16[128,128]{1,0:T(8,128)(2,1)} %w_out_ref.5) | copy-start | bytes 98308
  33.4 5.0 %collective-permute-start = (bf16[80,128]{1,0:T(8,128)(2,1)S(1)}, bf16[80,128]{1,0:T(8,128)(2,1)S(1)}, u32[]{:S(2)}, u32[]{:S(2)}) collective-permute-start(bf16[80,128]{1,0:T(8,128)(2,1)S(1)} %shard_map.163.refs_0_), channel_id=1, source_target_pairs={{0,8},{8,16},{16,24},{24,0},{1,9},{9,17},{17,25},{25,1},{2,10},{10... | collective-permute-start | bytes 61448 | tf_op jit(solution)/shard_map/ppermute | solution.py:641
  34.9 3.8 %collective-permute-start.1 = (bf16[80,128]{1,0:T(8,128)(2,1)S(1)}, bf16[80,128]{1,0:T(8,128)(2,1)S(1)}, u32[]{:S(2)}, u32[]{:S(2)}) collective-permute-start(bf16[80,128]{1,0:T(8,128)(2,1)S(1)} %shard_map.163.refs_0_), channel_id=1, source_target_pairs={{0,16},{8,24},{16,0},{24,8},{1,17},{9,25},{17,1},{25,9},{2,18},{10... | collective-permute-start | bytes 61448 | tf_op jit(solution)/shard_map/ppermute | solution.py:641
  36.4 3.8 %collective-permute-start.2 = (bf16[80,128]{1,0:T(8,128)(2,1)S(1)}, bf16[80,128]{1,0:T(8,128)(2,1)S(1)}, u32[]{:S(2)}, u32[]{:S(2)}) collective-permute-start(bf16[80,128]{1,0:T(8,128)(2,1)S(1)} %shard_map.163.refs_0_), channel_id=1, source_target_pairs={{0,24},{8,0},{16,8},{24,16},{1,25},{9,1},{17,9},{25,17},{2,26},{10... | collective-permute-start | bytes 61448 | tf_op jit(solution)/shard_map/ppermute | solution.py:641
  57.9 10.9 %all-to-all-start.3 = ((bf16[32,16,128]{2,1,0:T(8,128)(2,1)}), bf16[32,16,128]{2,1,0:T(8,128)(2,1)S(1)}, u32[]{:S(2)}, u32[]{:S(2)}) async-start(bf16[32,16,128]{2,1,0:T(8,128)(2,1)} %shard_map.166), calls=%async_computation.3 | async-start | bytes 262144 | tf_op jit(solution)/shard_map/all_to_all | solution.py:576

commit v14 on v13

--- a/solution.py
+++ b/solution.py
@@ -17,10 +17,11 @@
 VMEM_ALL = 56 * 1024 * 1024
 
 
-def call(body, out_shape, scratch=(), flops=0, moved=0, limit=VMEM_LIMIT):
+def call(body, out_shape, scratch=(), flops=0, moved=0, limit=VMEM_LIMIT, **specs):
     return pl.pallas_call(
         body,
         out_shape=out_shape,
+        **specs,
         scratch_shapes=list(scratch),
         compiler_params=pltpu.CompilerParams(vmem_limit_bytes=limit),
         cost_estimate=pl.CostEstimate(flops=flops, bytes_accessed=moved, transcendentals=0),
@@ -94,20 +95,17 @@
     return total
 
 
-def project_kernel(
-    units,
-    series_ref,
-    cot_ref,
-    w_in_ref,
-    w_out_ref,
-    taps_ref,
-    skip_one_ref,
-    skip_two_ref,
-    one_ref,
-    two_ref,
-    out_ref,
-    params_ref,
-):
+def project_kernel(units, *refs):
+    given, (out_ref, params_ref), held, sems = refs[:9], refs[9:11], refs[11:20], refs[20]
+    copies = [
+        pltpu.make_async_copy(far, near, sems.at[i]) for i, (far, near) in enumerate(zip(given, held))
+    ]
+    for copy in copies:
+        copy.start()
+    for copy in copies:
+        copy.wait()
+    series_ref, cot_ref, w_in_ref, w_out_ref, taps_ref = held[:5]
+    skip_one_ref, skip_two_ref, one_ref, two_ref = held[5:]
     _, block, width = series_ref.shape
     group = width // units
     parts = block // W
@@ -594,13 +592,16 @@
     assert 2 * block // width == 8 and group in (8, 16)
     packed = 3 * (block // W) * group + 8
     skips = (skip_one.reshape(1, width), skip_two.reshape(1, width))
+    given = (series, cotangent, w_in, w_out, taps, *skips, filter_one, filter_two)
     fields, params = call(
         functools.partial(project_kernel, units),
         (shape((sources, packed, W), BF16), shape((8, 3 * width), F32)),
+        [pltpu.VMEM(x.shape, x.dtype) for x in given] + [pltpu.SemaphoreType.DMA((len(given),))],
         flops=2 * block * width * 4 * width,
         moved=8 * block * width * 4,
         limit=VMEM_ALL,
-    )(series, cotangent, w_in, w_out, taps, *skips, filter_one, filter_two)
+        in_specs=[pl.BlockSpec(memory_space=pl.ANY)] * len(given),
+    )(*given)
     fields = all_to_all(fields, "seq")
     held = call(
         gate_kernel,

time: 70 us -> 69.9 us (level)
  no operation moved by 1% of the time
where the time goes in v14:
time: 69.9 us; the launch traced here: 69.5 us
  blocking collectives  31.6 us (45%)
  Pallas kernels  14.1 us (20%)
  waiting for transfers between devices  12.3 us (18%)
  starting transfers between devices  10.7 us (15%)
  between operations  0.75 us (1%)
    all_to_all x2, blocking collectives, all_to_all(): return lax.all_to_all(blocks, axis, split_axis=0, concat_axis=0, tiled=True)  31.6 us
    all_to_all x2, waiting for transfers between devices, all_to_all(): return lax.all_to_all(blocks, axis, split_axis=0, concat_axis=0, tiled=True)  10.5 us
    all_to_all x2, starting transfers between devices, all_to_all(): return lax.all_to_all(blocks, axis, split_axis=0, concat_axis=0, tiled=True)  6.18 us
    pallas_call x1, Pallas kernels, shards(): call(functools.partial(operator_kernel, units), (shape((sources, packed,...  4.89 us
    ppermute x3, starting transfers between devices, shards(): owns = [own] + [lax.ppermute(own, 'dp', route) for route in around]  4.52 us
    pallas_call x1, Pallas kernels, shards(): call(functools.partial(project_kernel, units), (shape((sources, packed, W...  2.41 us
    pallas_call x1, Pallas kernels, shards(): call(functools.partial(gradient_kernel, units), shape((2 * (length // wid...  2.21 us
    ppermute x3, waiting for transfers between devices, shards(): owns = [own] + [lax.ppermute(own, 'dp', route) for route in around]  1.89 us
  transfers between devices with their start and end apart: 5, of which 4 were waited for; matrix products, arithmetic and copies ran while one was open for 0% of the time, Pallas kernels for 6%

profile of v14, /device:TPU:0, one launch (start us, length us, event | category | flops | bytes accessed | tf_op | source)
XLA Modules:
  0.0 69.5 jit_solution(1640744943943113858)
XLA Ops:
  0.6 2.4 %shard_map.160 = (bf16[8,104,256]{2,1,0:T(8,128)(2,1)}, f32[8,384]{1,0:T(8,128)}) custom-call(bf16[1,512,128]{2,1,0:T(8,128)(2,1)} %series_ref.3, bf16[1,512,128]{2,1,0:T(8,128)(2,1)} %cot_ref.3, bf16[128,384]{1,0:T(8,128)(2,1)} %w_in_ref.3, bf16[128,128]{1,0:T(8,128)(2,1)} %w_out_ref.3, f32[3,384]{1,0:T(4,128)} %refs_4_.1, f32[1,128]{1,0:T(1,128)} %bitcast.4, ...), custom_call_target="tpu_custom_call" | custom-call | flops 67108864 | bytes 2097152 | tf_op jit(solution)/shard_map/pallas_call | solution.py:596
  3.1 0.0 copy-start.4
  3.1 19.6 %all_to_all.20.fields_ref = bf16[8,104,256]{2,1,0:T(8,128)(2,1)S(1)} all-to-all(bf16[8,104,256]{2,1,0:T(8,128)(2,1)} %get-tuple-element.25), channel_id=1, replica_groups=mesh['dp'=4,'seq'=8] {'seq'}, dimensions={0} | all-to-all | bytes 851968 | tf_op jit(solution)/shard_map/all_to_all | solution.py:574
  22.7 0.0 copy-done.4
  22.7 4.9 %shard_map.161 = (bf16[8,104,256]{2,1,0:T(8,128)(2,1)}, bf16[7,256,256]{2,1,0:T(8,128)(2,1)S(1)}) custom-call(bf16[8,104,256]{2,1,0:T(8,128)(2,1)S(1)} %all_to_all.20.fields_ref, f32[8,384]{1,0:T(8,128)S(1)} %copy-done.4), custom_call_target="tpu_custom_call" | custom-call | flops 2147483648 | bytes 8388608 | tf_op jit(solution)/shard_map/pallas_call | solution.py:613
  27.6 3.5 %all-to-all-start.1 = ((bf16[8,104,256]{2,1,0:T(8,128)(2,1)}), bf16[8,104,256]{2,1,0:T(8,128)(2,1)S(1)}, u32[]{:S(2)}, u32[]{:S(2)}) async-start(bf16[8,104,256]{2,1,0:T(8,128)(2,1)} %get-tuple-element.27), calls=%async_computation.1 | async-start | bytes 851968 | tf_op jit(solution)/shard_map/all_to_all | solution.py:574
  31.0 0.0 copy-start
  31.0 0.0 copy-start.1
  31.1 0.0 copy-start.2
  31.1 0.0 copy-start.3
  31.1 2.2 %shard_map.163.refs_0_ = bf16[80,128]{1,0:T(8,128)(2,1)S(1)} custom-call(bf16[8,104,256]{2,1,0:T(8,128)(2,1)S(1)} %all_to_all.20.fields_ref, bf16[7,256,256]{2,1,0:T(8,128)(2,1)S(1)} %get-tuple-element.28.kept_ref), custom_call_target="tpu_custom_call" | custom-call | flops 1073741824 | bytes 2097152 | tf_op jit(solution)/shard_map/pallas_call | solution.py:628
  33.3 1.6 %collective-permute-start = (bf16[80,128]{1,0:T(8,128)(2,1)S(1)}, bf16[80,128]{1,0:T(8,128)(2,1)S(1)}, u32[]{:S(2)}, u32[]{:S(2)}) collective-permute-start(bf16[80,128]{1,0:T(8,128)(2,1)S(1)} %shard_map.163.refs_0_), channel_id=1, source_target_pairs={{0,8},{8,16},{16,24},{24,0},{1,9},{9,17},{17,25},{25,1},{2,10},{10... | collective-permute-start | bytes 61448 | tf_op jit(solution)/shard_map/ppermute | solution.py:642
  34.9 1.5 %collective-permute-start.1 = (bf16[80,128]{1,0:T(8,128)(2,1)S(1)}, bf16[80,128]{1,0:T(8,128)(2,1)S(1)}, u32[]{:S(2)}, u32[]{:S(2)}) collective-permute-start(bf16[80,128]{1,0:T(8,128)(2,1)S(1)} %shard_map.163.refs_0_), channel_id=1, source_target_pairs={{0,16},{8,24},{16,0},{24,8},{1,17},{9,25},{17,1},{25,9},{2,18},{10... | collective-permute-start | bytes 61448 | tf_op jit(solution)/shard_map/ppermute | solution.py:642
  36.4 1.4 %collective-permute-start.2 = (bf16[80,128]{1,0:T(8,128)(2,1)S(1)}, bf16[80,128]{1,0:T(8,128)(2,1)S(1)}, u32[]{:S(2)}, u32[]{:S(2)}) collective-permute-start(bf16[80,128]{1,0:T(8,128)(2,1)S(1)} %shard_map.163.refs_0_), channel_id=1, source_target_pairs={{0,24},{8,0},{16,8},{24,16},{1,25},{9,1},{17,9},{25,17},{2,26},{10... | collective-permute-start | bytes 61448 | tf_op jit(solution)/shard_map/ppermute | solution.py:642
  37.8 0.0 copy-done
  37.8 0.0 copy-done.1
  37.8 0.0 copy-done.2
  37.8 0.0 copy-done.3
  37.8 0.4 shard_map.162.held_ref
  38.3 0.0 collective-permute-done.refs_1_
  38.3 0.4 collective-permute-done.1.refs_2_
  38.6 1.5 %collective-permute-done.2.refs_3_ = bf16[80,128]{1,0:T(8,128)(2,1)S(1)} collective-permute-done((bf16[80,128]{1,0:T(8,128)(2,1)S(1)}, bf16[80,128]{1,0:T(8,128)(2,1)S(1)}, u32[]{:S(2)}, u32[]{:S(2)}) %collective-permute-start.2) | collective-permute-done | bytes 20512 | tf_op jit(solution)/shard_map/ppermute | solution.py:642
  40.2 4.0 %all-to-all-done.1.in_ref = bf16[8,104,256]{2,1,0:T(8,128)(2,1)S(1)} async-done(((bf16[8,104,256]{2,1,0:T(8,128)(2,1)}), bf16[8,104,256]{2,1,0:T(8,128)(2,1)S(1)}, u32[]{:S(2)}, u32[]{:S(2)}) %all-to-all-start.1) | async-done | bytes 426016 | tf_op jit(solution)/shard_map/all_to_all | solution.py:574
  44.2 0.9 %shard_map.164 = (bf16[32,24,128]{2,1,0:T(8,128)(2,1)S(1)}, bf16[2,128,256]{2,1,0:T(8,128)(2,1)S(1)}, bf16[2,128,256]{2,1,0:T(8,128)(2,1)S(1)}) custom-call(bf16[8,104,256]{2,1,0:T(8,128)(2,1)S(1)} %all-to-all-done.1.in_ref, f32[3,2,128,256]{3,2,1,0:T(8,128)S(1)} %shard_map.162.held_ref, f32[8,384]{1,0:T(8,128)S(1)} %copy-done.4, ...), custom_call_target="tpu_custom_call" | custom-call | flops 67108864 | bytes 786432 | tf_op jit(solution)/shard_map/pallas_call | solution.py:645
  45.1 12.0 %all_to_all.21.in_ref = bf16[32,24,128]{2,1,0:T(8,128)(2,1)S(1)} all-to-all(bf16[32,24,128]{2,1,0:T(8,128)(2,1)S(1)} %get-tuple-element.33), channel_id=1, replica_groups=mesh['dp'=4,'seq'=8] {'dp','seq'}, dimensions={0} | all-to-all | bytes 393216 | tf_op jit(solution)/shard_map/all_to_all | solution.py:574
  57.1 0.7 %shard_map.166 = bf16[32,16,128]{2,1,0:T(8,128)(2,1)} custom-call(bf16[32,24,128]{2,1,0:T(8,128)(2,1)S(1)} %all_to_all.21.in_ref), custom_call_target="tpu_custom_call" | custom-call | flops 65536 | bytes 262144 | tf_op jit(solution)/shard_map/pallas_call | solution.py:664
  57.8 2.7 %all-to-all-start.3 = ((bf16[32,16,128]{2,1,0:T(8,128)(2,1)}), bf16[32,16,128]{2,1,0:T(8,128)(2,1)S(1)}, u32[]{:S(2)}, u32[]{:S(2)}) async-start(bf16[32,16,128]{2,1,0:T(8,128)(2,1)} %shard_map.166), calls=%async_computation.3 | async-start | bytes 262144 | tf_op jit(solution)/shard_map/all_to_all | solution.py:574
  60.5 1.1 %shard_map.165 = (bf16[1,512,128]{2,1,0:T(8,128)(2,1)}, bf16[1,512,128]{2,1,0:T(8,128)(2,1)}) custom-call(bf16[8,104,256]{2,1,0:T(8,128)(2,1)S(1)} %all-to-all-done.1.in_ref, bf16[2,128,256]{2,1,0:T(8,128)(2,1)S(1)} %get-tuple-element.29.product_ref, bf16[2,128,256]{2,1,0:T(8,128)(2,1)S(1)} %get-tuple-element.30.grads_ref, bf16[128,384]{1,0:T(8,128)(2,1)S(1)} %copy-done.2, ...), custom_call_target="tpu_custom_call" | custom-call | flops 67108864 | bytes 786432 | tf_op jit(solution)/shard_map/pallas_call | solution.py:657
  61.6 0.7 %shard_map.168 = (f32[8,512]{1,0:T(8,128)}, f32[8,512]{1,0:T(8,128)}, f32[3,384]{1,0:T(4,128)}, f32[1,128]{1,0:T(1,128)}, f32[1,128]{1,0:T(1,128)}) custom-call(bf16[32,24,128]{2,1,0:T(8,128)(2,1)S(1)} %all_to_all.21.in_ref), custom_call_target="tpu_custom_call" | custom-call | flops 98304 | bytes 393216 | tf_op jit(solution)/shard_map/pallas_call | solution.py:672
  62.3 6.4 %all-to-all-done.3.in_ref = bf16[32,16,128]{2,1,0:T(8,128)(2,1)S(1)} async-done(((bf16[32,16,128]{2,1,0:T(8,128)(2,1)}), bf16[32,16,128]{2,1,0:T(8,128)(2,1)S(1)}, u32[]{:S(2)}, u32[]{:S(2)}) %all-to-all-start.3) | async-done | bytes 131104 | tf_op jit(solution)/shard_map/all_to_all | solution.py:574
  68.7 0.8 %shard_map.167 = (f32[128,384]{1,0:T(8,128)}, f32[128,128]{1,0:T(8,128)}) custom-call(bf16[32,16,128]{2,1,0:T(8,128)(2,1)S(1)} %all-to-all-done.3.in_ref), custom_call_target="tpu_custom_call" | custom-call | flops 65536 | bytes 131072 | tf_op jit(solution)/shard_map/pallas_call | solution.py:684
Async XLA Ops:
  3.1 19.6 %copy-start.4 = (f32[8,384]{1,0:T(8,128)S(1)}, f32[8,384]{1,0:T(8,128)}, u32[]{:S(2)}) copy-start(f32[8,384]{1,0:T(8,128)} %get-tuple-element.26.taps_ref) | copy-start | bytes 36868
  27.6 16.6 %all-to-all-start.1 = ((bf16[8,104,256]{2,1,0:T(8,128)(2,1)}), bf16[8,104,256]{2,1,0:T(8,128)(2,1)S(1)}, u32[]{:S(2)}, u32[]{:S(2)}) async-start(bf16[8,104,256]{2,1,0:T(8,128)(2,1)} %get-tuple-element.27), calls=%async_computation.1 | async-start | bytes 851968 | tf_op jit(solution)/shard_map/all_to_all | solution.py:574
  31.0 6.8 %copy-start = (bf16[1,512,128]{2,1,0:T(8,128)(2,1)S(1)}, bf16[1,512,128]{2,1,0:T(8,128)(2,1)}, u32[]{:S(2)}) copy-start(bf16[1,512,128]{2,1,0:T(8,128)(2,1)} %series_ref.3) | copy-start | bytes 393220
  31.0 6.8 %copy-start.1 = (bf16[1,512,128]{2,1,0:T(8,128)(2,1)S(1)}, bf16[1,512,128]{2,1,0:T(8,128)(2,1)}, u32[]{:S(2)}) copy-start(bf16[1,512,128]{2,1,0:T(8,128)(2,1)} %cot_ref.3) | copy-start | bytes 393220
  31.1 6.8 %copy-start.2 = (bf16[128,384]{1,0:T(8,128)(2,1)S(1)}, bf16[128,384]{1,0:T(8,128)(2,1)}, u32[]{:S(2)}) copy-start(bf16[128,384]{1,0:T(8,128)(2,1)} %w_in_ref.3) | copy-start | bytes 294916
  31.1 6.8 %copy-start.3 = (bf16[128,128]{1,0:T(8,128)(2,1)S(1)}, bf16[128,128]{1,0:T(8,128)(2,1)}, u32[]{:S(2)}) copy-start(bf16[128,128]{1,0:T(8,128)(2,1)} %w_out_ref.3) | copy-start | bytes 98308
  33.3 5.0 %collective-permute-start = (bf16[80,128]{1,0:T(8,128)(2,1)S(1)}, bf16[80,128]{1,0:T(8,128)(2,1)S(1)}, u32[]{:S(2)}, u32[]{:S(2)}) collective-permute-start(bf16[80,128]{1,0:T(8,128)(2,1)S(1)} %shard_map.163.refs_0_), channel_id=1, source_target_pairs={{0,8},{8,16},{16,24},{24,0},{1,9},{9,17},{17,25},{25,1},{2,10},{10... | collective-permute-start | bytes 61448 | tf_op jit(solution)/shard_map/ppermute | solution.py:642
  34.9 3.8 %collective-permute-start.1 = (bf16[80,128]{1,0:T(8,128)(2,1)S(1)}, bf16[80,128]{1,0:T(8,128)(2,1)S(1)}, u32[]{:S(2)}, u32[]{:S(2)}) collective-permute-start(bf16[80,128]{1,0:T(8,128)(2,1)S(1)} %shard_map.163.refs_0_), channel_id=1, source_target_pairs={{0,16},{8,24},{16,0},{24,8},{1,17},{9,25},{17,1},{25,9},{2,18},{10... | collective-permute-start | bytes 61448 | tf_op jit(solution)/shard_map/ppermute | solution.py:642
  36.4 3.8 %collective-permute-start.2 = (bf16[80,128]{1,0:T(8,128)(2,1)S(1)}, bf16[80,128]{1,0:T(8,128)(2,1)S(1)}, u32[]{:S(2)}, u32[]{:S(2)}) collective-permute-start(bf16[80,128]{1,0:T(8,128)(2,1)S(1)} %shard_map.163.refs_0_), channel_id=1, source_target_pairs={{0,24},{8,0},{16,8},{24,16},{1,25},{9,1},{17,9},{25,17},{2,26},{10... | collective-permute-start | bytes 61448 | tf_op jit(solution)/shard_map/ppermute | solution.py:642
  57.8 10.9 %all-to-all-start.3 = ((bf16[32,16,128]{2,1,0:T(8,128)(2,1)}), bf16[32,16,128]{2,1,0:T(8,128)(2,1)S(1)}, u32[]{:S(2)}, u32[]{:S(2)}) async-start(bf16[32,16,128]{2,1,0:T(8,128)(2,1)} %shard_map.166), calls=%async_computation.3 | async-start | bytes 262144 | tf_op jit(solution)/shard_map/all_to_all | solution.py:574
